TPU v7x, 32 devices: a whole 2x2x4 slice. The times are simulated.
32 devices in a mesh: space: 8 (over z, y), chan: 4 (over x, core).
Axes of the slice: x: 2, y: 2, z: 4, core: 2. Of those that a mesh axis runs over, the one named last changes fastest.
Arguments:
- features: bfloat16 [16384, 256], P('space', 'chan'), may hold values from -6 to 6
- kernel_map: int32 [8, 27, 16, 3], P('space'), may hold values from 0 to 15, as said below
- block_count: int32 [8], replicated, may hold values from 3 to 16, as said below
- weight_one: bfloat16 [27, 256, 256], P(None, 'chan'), may hold values from -0.078125 to 0.078125
- weight_two: bfloat16 [27, 256, 256], P(None, 'chan'), may hold values from -0.078125 to 0.078125
- cotangent: bfloat16 [16384, 256], P('space', 'chan'), may hold values from -0.026977539 to 0.026977539
Outputs:
- output: bfloat16 [16384, 256], P('space', 'chan')
- grad_one: float32 [27, 256, 256], P(None, 'chan', 'space')
- grad_two: float32 [27, 256, 256], P(None, 'chan', 'space')
Inputs may be any that keep to these rules, and one draw needn't show every extreme that they name: `kernel_map`: column 0 of slab s's entries is s - 1, s or s + 1. Column 1 is a block below block_count of that source slab; from slab s - 1 it is one of that slab's last 2 live blocks, from slab s + 1 one of its first 2. Column 2 lies below 16. Entries stand in offset order, 16 per offset and slab. `block_count`: at least one slab has all 16 blocks live.
All inputs are finite; a program needn't handle non-finite values.
Results may differ from a plain program's by a relative error of at most 0.015.
Values may be sent and summed in bfloat16 or wider, within the bound.
No kernel may reach another device: no remote copies, remote signals or barrier semaphores. Data moves between devices by JAX's collectives and lax.ppermute only.
A program may use at most 64 MiB of HBM per device.

v0:
```python
import jax
import jax.numpy as jnp
from jax import lax
from jax.sharding import PartitionSpec as P

BLK = 128
HB = 2


def padded(shard, sides, width):
    for axis, dim in sides:
        size, length = (lax.axis_size(axis), shard.shape[dim])
        up = [(i, (i + 1) % size) for i in range(size - 1)]
        down = [(j, i) for i, j in up]
        last = lax.slice_in_dim(shard, length - width, length, axis=dim)
        leading = lax.slice_in_dim(shard, 0, width, axis=dim)
        before = lax.ppermute(last, axis, up)
        after = lax.ppermute(leading, axis, down)
        shard = jnp.concatenate([before, shard, after], axis=dim)
    return shard


def local(features, kernel_map, block_count, weight_one, weight_two, cotangent):
    shard = lax.axis_index("space")
    nblocks = features.shape[0] // BLK
    own_count = block_count[shard]
    left_count = block_count[jnp.maximum(shard - 1, 0)]
    entries = kernel_map[0]
    source = entries[..., 0]
    inblock = entries[..., 1]
    target = entries[..., 2]
    position = jnp.where(
        source == shard,
        HB + inblock,
        jnp.where(source < shard, inblock - (left_count - HB), HB + nblocks + inblock),
    )
    live = target < own_count
    select = (target[..., None] == jnp.arange(nblocks, dtype=jnp.int32)) & live[..., None]
    select_f = select.astype(jnp.float32)
    select_b = select.astype(jnp.bfloat16)
    place = (
        (position[..., None] == jnp.arange(nblocks + 2 * HB, dtype=jnp.int32)) & live[..., None]
    ).astype(jnp.float32)

    def widen(feat):
        return lax.all_gather(feat, "chan", axis=1, tiled=True)

    def attach_rims(feat):
        width = feat.shape[1]
        cube = feat.reshape(nblocks, BLK, width)
        first = cube[:HB]
        last = lax.dynamic_slice_in_dim(cube, own_count - HB, HB, 0)
        rims = jnp.concatenate([first, last], 0).reshape(2 * HB * BLK, width)
        outer = padded(rims, (("space", 0),), HB * BLK)
        return jnp.concatenate([outer[: HB * BLK], feat, outer[3 * HB * BLK :]], 0)

    def extend(feat):
        return attach_rims(widen(feat))

    def convolve(wide, weights):
        cube = wide.reshape(-1, BLK, wide.shape[1])

        def convolve_add_offset(total, item):
            index, choose, kernel = item
            picked = cube[index]
            prod = jnp.einsum("erc,dc->erd", picked, kernel, preferred_element_type=jnp.float32)
            return (total + jnp.einsum("eb,erd->brd", choose, prod), None)

        start = jnp.zeros((nblocks, BLK, weights.shape[1]), jnp.float32)
        total, _ = lax.scan(convolve_add_offset, start, (position, select_f, weights))
        return total.reshape(nblocks * BLK, weights.shape[1])

    def weight_grad(wide, grads_cube):
        cube = wide.reshape(-1, BLK, wide.shape[1])

        def one_offset(item):
            index, choose = item
            picked = cube[index]
            chosen = jnp.einsum(
                "eb,brd->erd", choose, grads_cube, preferred_element_type=jnp.float32
            ).astype(jnp.bfloat16)
            return jnp.einsum("erc,erd->dc", picked, chosen, preferred_element_type=jnp.float32)

        return lax.map(one_offset, (position, select_b))

    wide_x = extend(features)
    z_one = convolve(wide_x, weight_one)
    hidden = jax.nn.silu(z_one).astype(jnp.bfloat16)
    wide_h = extend(hidden)
    output = convolve(wide_h, weight_two).astype(jnp.bfloat16)
    grad_cube = cotangent.reshape(nblocks, BLK, -1)
    grad_two = weight_grad(wide_h, grad_cube)
    width = cotangent.shape[1]

    def spread_add_offset(total, item):
        choose, spot, kernel = item
        chosen = jnp.einsum(
            "eb,brd->erd", choose, grad_cube, preferred_element_type=jnp.float32
        ).astype(jnp.bfloat16)
        contrib = jnp.einsum("erd,dc->erc", chosen, kernel, preferred_element_type=jnp.float32)
        return (total + jnp.einsum("ex,erc->xrc", spot, contrib), None)

    start = jnp.zeros((nblocks + 2 * HB, BLK, weight_two.shape[2]), jnp.float32)
    total, _ = lax.scan(spread_add_offset, start, (select_b, place, weight_two))
    partial_value = total.reshape((nblocks + 2 * HB) * BLK, weight_two.shape[2])
    summed = lax.psum_scatter(partial_value, "chan", scatter_dimension=1, tiled=True)
    width = summed.shape[1]
    cube = summed.reshape(-1, BLK, width)
    edges = jnp.concatenate([cube[:HB], cube[HB + nblocks :]], 0).reshape(2 * HB * BLK, width)
    back = padded(edges, (("space", 0),), HB * BLK)
    inner = cube[HB : HB + nblocks]
    from_left = back[: HB * BLK].reshape(HB, BLK, width)
    from_right = back[3 * HB * BLK :].reshape(HB, BLK, width)
    inner = inner.at[:HB].add(from_left)
    tail = lax.dynamic_slice_in_dim(inner, own_count - HB, HB, 0) + from_right
    inner = lax.dynamic_update_slice_in_dim(inner, tail, own_count - HB, 0)
    grad_hidden = inner.reshape(nblocks * BLK, width)
    gate = jax.nn.sigmoid(z_one)
    grad_z = (grad_hidden * gate * (1.0 + z_one * (1.0 - gate))).astype(jnp.bfloat16)
    grad_one = weight_grad(wide_x, grad_z.reshape(nblocks, BLK, -1))
    totals = (
        lax.psum_scatter(grad_one, "space", scatter_dimension=2, tiled=True),
        lax.psum_scatter(grad_two, "space", scatter_dimension=2, tiled=True),
    )
    return (output, totals[0], totals[1])


def solution(mesh):
    return jax.shard_map(
        local,
        mesh=mesh,
        in_specs=(
            P("space", "chan"),
            P("space", None, None, None),
            P(),
            P(None, "chan", None),
            P(None, "chan", None),
            P("space", "chan"),
        ),
        out_specs=(P("space", "chan"), P(None, "chan", "space"), P(None, "chan", "space")),
        check_vma=False,
    )
```

profile of v0, /device:TPU:0, one launch (start us, length us, event | category | flops | bytes accessed | tf_op | source)
XLA Modules:
  0.0 717.4 jit_solution(8535963598169555180)
XLA Ops:
  14.7 14.3 %all-gather.3.cloned.1.call-done = bf16[2048,256]{0,1:T(8,128)(2,1)} async-done(((bf16[2048,64]{0,1:T(8,128)(2,1)}), bf16[2048,256]{0,1:T(8,128)(2,1)}) %all-gather.3.cloned.1.call-update) | async-done | bytes 1048592 | tf_op jit(solution)/shard_map/all_gather | solution.py:46
  30.8 3.4 collective-permute-start
  37.3 4.2 collective-permute-done.1
  45.0 204.1 %while.56 = (s32[]{:T(128)}, f32[16,128,64]{1,0,2:T(8,128)}, bf16[27,16,16]{1,2,0:T(8,128)(2,1)}, s32[27,16]{1,0:T(8,128)S(1)}, bf16[20,128,256]{2,1,0:T(8,128)(...) while((s32[]{:T(128)}, f32[16,128,64]{1,0,2:T(8,128)}, ...), condition=%wide.region_1.2_spmd.clone, body=%wide.region_0.1_spmd.clone.sunk | while | flops 71566384 | bytes 4760931 | solution.py:70
  45.1 2.9 gather_fusion.2
  52.5 2.9 gather_fusion.2
  60.0 2.9 gather_fusion.2
  67.6 2.9 gather_fusion.2
  75.2 2.9 gather_fusion.2
  82.7 2.9 gather_fusion.2
  90.3 2.9 gather_fusion.2
  97.9 2.9 gather_fusion.2
  105.4 2.9 gather_fusion.2
  113.0 2.9 gather_fusion.2
  120.6 2.9 gather_fusion.2
  128.1 2.9 gather_fusion.2
  135.7 2.9 gather_fusion.2
  143.3 2.9 gather_fusion.2
  150.8 2.9 gather_fusion.2
  158.4 2.9 gather_fusion.2
  166.0 2.9 gather_fusion.2
  173.5 2.9 gather_fusion.2
  181.1 2.9 gather_fusion.2
  188.7 2.9 gather_fusion.2
  196.2 2.9 gather_fusion.2
  203.8 2.9 gather_fusion.2
  211.4 2.9 gather_fusion.2
  218.9 2.9 gather_fusion.2
  226.5 2.9 gather_fusion.2
  234.1 2.9 gather_fusion.2
  241.6 2.9 gather_fusion.2
  251.2 157.6 %while.58 = (s32[]{:T(128)}, f32[20,128,256]{2,0,1:T(8,128)S(1)}, bf16[27,16,20]{2,1,0:T(8,128)(2,1)}, bf16[27,16,16]{2,1,0:T(8,128)(2,1)S(1)}, bf16[16,128,64]{...) while((s32[]{:T(128)}, f32[20,128,256]{2,0,1:T(8,128)S(1)}, ...), condition=%wide.region_5.6_spmd.clone, body=%wide.region_4.5_spmd.clone.sunk | while | flops 93716480 | bytes 6857827 | solution.py:104
  254.4 2.6 select_add_fusion.2
  289.5 2.6 select_add_fusion.2
  312.8 2.6 select_add_fusion.2
  336.1 2.6 select_add_fusion.2
  359.5 2.6 select_add_fusion.2
  382.8 2.6 select_add_fusion.2
  411.1 3.2 copy.71
  416.0 4.3 collective-permute-start.2
  422.8 4.4 collective-permute-done.3
  427.3 21.9 %reduce-scatter.10.cloned.1.call-done = f32[64,2560]{1,0:T(8,128)} async-done(((f32[256,2560]{1,0:T(8,128)}), f32[64,2560]{1,0:T(8,128)}) %reduce-scatter.10.cloned.1.call-update) | async-done | bytes 655376
  450.9 4.0 collective-permute-start.4
  458.4 47.3 %while.55 = (s32[]{:T(128)}, f32[27,64,256]{2,1,0:T(8,128)}, bf16[27,16,16]{2,1,0:T(8,128)(2,1)S(1)}, bf16[16,128,64]{1,0,2:T(8,128)(2,1)S(1)}, s32[27,16]{1,0:T...) while((s32[]{:T(128)}, f32[27,64,256]{2,1,0:T(8,128)}, bf16[27,16,16]{2,1,0:T(8,128)(2,1)S(1)}, ...), condition=%wide.region_11.12_spmd, body=%wide.region_10.11_spmd.sunk | while | flops 71435312 | bytes 4006741 | solution.py:84
  505.7 3.4 copy.69
  520.1 106.4 %while.54 = (s32[]{:T(128)}, f32[27,64,256]{2,1,0:T(8,128)}, bf16[27,16,16]{2,1,0:T(8,128)(2,1)S(1)}, bf16[16,128,64]{1,0,2:T(8,128)(2,1)S(1)}, s32[27,16]{1,0:T...) while((s32[]{:T(128)}, f32[27,64,256]{2,1,0:T(8,128)}, bf16[27,16,16]{2,1,0:T(8,128)(2,1)S(1)}, ...), condition=%wide.region_8.9_spmd, body=%wide.region_7.8_spmd.sunk | while | flops 71435312 | bytes 4006741 | solution.py:84
  626.5 3.5 copy.68
  631.0 77.8 %while.57 = (s32[]{:T(128)}, f32[16,128,64]{1,0,2:T(8,128)S(1)}, bf16[27,16,16]{1,2,0:T(8,128)(2,1)}, s32[27,16]{1,0:T(8,128)S(1)}, bf16[20,128,256]{2,1,0:T(8,1...) while((s32[]{:T(128)}, f32[16,128,64]{1,0,2:T(8,128)S(1)}, ...), condition=%wide.region_3.4_spmd.clone, body=%wide.region_2.3_spmd.clone.sunk | while | flops 71566384 | bytes 4760931 | solution.py:70
  (659 shorter events, 537.5 us)
Async XLA Ops:
  7.2 21.8 %all-gather.3.cloned.1.call-start = ((), (), s32[]{:S(2)}) async-start(), calls=%async_computation.3 | async-start | bytes 1310720 | tf_op jit(solution)/shard_map/all_gather | solution.py:46
  7.9 406.6 %all-gather.5.cloned.1.call-start = ((), (), s32[]{:S(2)}) async-start(), calls=%async_computation.4 | async-start | bytes 1310720 | tf_op jit(solution)/shard_map/all_gather | solution.py:46
  29.0 5.2 copy-start.3
  30.8 6.5 collective-permute-start
  34.2 7.2 %collective-permute-start.1 = (bf16[256,256]{0,1:T(8,128)(2,1)S(1)}, bf16[256,256]{0,1:T(8,128)(2,1)S(1)}, u32[]{:S(2)}, u32[]{:S(2)}) collective-permute-start(bf16[256,256]{0,1:T(8,128)(2,1)S(1)} %slice.96), channel_id=1, source_target_pairs={{4,0},{8,4},{12,8},{16,12},{20,16},{24,20},{28,24},{5,1},{9,5},{13... | collective-permute-start | bytes 393224 | tf_op jit(solution)/shard_map/ppermute | solution.py:18
  251.2 198.0 %reduce-scatter.10.cloned.1.call-start = ((), (), s32[]{:S(2)}) async-start(), calls=%async_computation.7 | async-start | bytes 3276800
  414.4 295.3 %reduce-scatter.8.cloned.1.call-start = ((), (), s32[]{:S(2)}) async-start(), calls=%async_computation.6 | async-start | bytes 3981312 | tf_op jit(solution)/shard_map/reduce_scatter | solution.py:123
  416.0 6.8 collective-permute-start.2
  420.3 6.9 collective-permute-start.3
  450.9 61.0 %collective-permute-start.4 = (f32[256,64]{1,0:T(8,128)}, f32[256,64]{1,0:T(8,128)}, u32[]{:S(2)}, u32[]{:S(2)}) collective-permute-start(f32[256,64]{1,0:T(8,128)} %copy.75), channel_id=1, source_target_pairs={{0,4},{4,8},{8,12},{12,16},{16,20},{20,24},{24,28},{1,5},{5,9},{9,... | collective-permute-start | bytes 196616 | tf_op jit(solution)/shard_map/ppermute | solution.py:17
  455.7 57.2 %collective-permute-start.5 = (f32[256,64]{1,0:T(8,128)}, f32[256,64]{1,0:T(8,128)}, u32[]{:S(2)}, u32[]{:S(2)}) collective-permute-start(f32[256,64]{1,0:T(8,128)} %copy.76), channel_id=1, source_target_pairs={{4,0},{8,4},{12,8},{16,12},{20,16},{24,20},{28,24},{5,1},{9,5},{13... | collective-permute-start | bytes 196616 | tf_op jit(solution)/shard_map/ppermute | solution.py:18
  509.2 1.1 copy-start.4
  509.2 201.7 %reduce-scatter.6.cloned.1.call-start = ((), (), s32[]{:S(2)}) async-start(), calls=%async_computation.5 | async-start | bytes 3981312 | tf_op jit(solution)/shard_map/reduce_scatter | solution.py:122
  510.7 6.6 copy-start.1
  513.9 6.2 copy-start
  630.0 1.0 copy-start.2
Sparse Core Ops, SparseCore 0:
  9.6 19.4 all-gather.2
  251.3 16.6 all-gather.4
  414.5 34.6 reduce-scatter.9
  509.3 80.7 reduce-scatter.7
  630.1 80.7 reduce-scatter.5
where the time goes:
time: 726 us; the launch traced here: 717 us
  matrix products  371 us (51%)
  local copies, waits for them, and re-layouts  253 us (35%)
  waiting for transfers between devices  48.9 us (7%)
  between operations  16 us (2%)
  starting transfers between devices  15.8 us (2%)
  other arithmetic  9.87 us (1%)
    dot_general x54, matrix products, convolve_add_offset(): jnp.einsum('erc,dc->erd', picked, kernel, preferred_element_type=jnp.floa...  96.5 us
    gather x54, local copies, waits for them, and re-layouts, convolve_add_offset(): picked = cube[index]  95.7 us
    dot_general x54, matrix products, convolve_add_offset(): return (total + jnp.einsum('eb,erd->brd', choose, prod), None)  87.6 us
    dot_general x54, matrix products, one_offset(): jnp.einsum('erc,erd->dc', picked, chosen, preferred_element_type=jnp.floa...  82.2 us
    dot_general x27, matrix products, spread_add_offset(): return (total + jnp.einsum('ex,erc->xrc', spot, contrib), None)  69.9 us
    convert_element_type x27, local copies, waits for them, and re-layouts, spread_add_offset(): chosen = jnp.einsum('eb,brd->erd', choose, grad_cube, preferred_element_t...  62.5 us
    gather x54, local copies, waits for them, and re-layouts, one_offset(): picked = cube[index]  59.2 us
    dot_general x27, matrix products, spread_add_offset(): jnp.einsum('eb,brd->erd', choose, grad_cube, preferred_element_type=jnp.f...  24.6 us
  transfers between devices with their start and end apart: 11, of which 7 were waited for; matrix products, arithmetic and copies ran while one was open for 58% of the time, Pallas kernels for 0%

commit v1 on v0

v1 whole, which is shorter than its diff:
```python
import functools

import jax
import jax.numpy as jnp
from jax import lax
from jax.experimental import pallas as pl
from jax.experimental.pallas import tpu as pltpu
from jax.sharding import PartitionSpec as P

BLK = 128
HB = 2
RIM = HB * BLK
STEP = 256
F32 = jnp.float32
BF16 = jnp.bfloat16

VMEM = pl.BlockSpec(memory_space=pltpu.VMEM)
SMEM = pl.BlockSpec(memory_space=pltpu.SMEM)


def call(body, outs, ins, scratch=(), flops=0, traffic=0):
    specs = [SMEM if a.dtype == jnp.int32 else VMEM for a in ins]
    return pl.pallas_call(
        body,
        out_shape=[jax.ShapeDtypeStruct(s, t) for s, t in outs],
        in_specs=specs,
        out_specs=[VMEM] * len(outs),
        scratch_shapes=list(scratch),
        compiler_params=pltpu.CompilerParams(vmem_limit_bytes=56 << 20),
        cost_estimate=pl.CostEstimate(flops=flops, bytes_accessed=traffic, transcendentals=0),
    )(*ins)


def chunks(total, step, body):
    whole = total // step

    def one(i, _):
        body(pl.multiple_of(i * step, step), step)
        return 0

    lax.fori_loop(0, whole, one, 0)
    if total % step:
        body(whole * step, total % step)


def cell(code):
    return code >> 6, code & 63


def spread(tab, blocks, sums, spread_ref):
    reach, depth = sums[0].shape[0], sums[0].shape[1]
    offsets = spread_ref.shape[0] // depth
    entries = tab.shape[0] // offsets
    ways = len(sums)

    def some(i, _):
        for acc in sums:
            acc[...] = jnp.zeros_like(acc)
        for e in range(entries):
            for w, acc in enumerate(sums):
                s, t = cell(tab[(i * ways + w) * entries + e])
                acc[s] = acc[s] + blocks[t]
        for w, acc in enumerate(sums):
            rows = pl.ds(pl.multiple_of((i * ways + w) * depth, depth), depth)
            for s in range(reach):
                spread_ref[rows, s * BLK : (s + 1) * BLK] = acc[s].astype(BF16)
        return 0

    lax.fori_loop(0, offsets // ways, some, 0)


def collect(tab, prod, sums, low, high):
    depth = sums[0].shape[1]
    offsets = prod.shape[0] // depth
    entries = tab.shape[0] // offsets
    idle = sums[0].shape[0] - 1
    for acc in sums:
        acc[...] = jnp.zeros_like(acc)

    def some(k, _):
        rows = pl.ds(pl.multiple_of(k * depth, depth), depth)
        for e in range(entries):
            acc = sums[e % len(sums)]
            s, t = cell(tab[k * entries + e])
            inside = (s >= low) & (s < high)
            t = jnp.where(inside, t, idle)
            s = jnp.where(inside, s - low, 0)
            acc[t] = acc[t] + prod[rows, pl.ds(pl.multiple_of(s * BLK, BLK), BLK)]
        return 0

    lax.fori_loop(0, offsets, some, 0)


def input_grad_body(nblocks, tab, info, cot_ref, w_ref, spread_ref, keep_ref, send_ref, blocks, part, *sums):
    depth = cot_ref.shape[0]
    for b in range(nblocks):
        blocks[b] = cot_ref[:, b * BLK : (b + 1) * BLK].astype(F32)
    blocks[nblocks] = jnp.zeros_like(blocks[nblocks])
    spread(tab, blocks, sums, spread_ref)

    def product(start, width):
        cols = pl.ds(start, width)
        res = lax.dot_general(w_ref[...], spread_ref[:, cols], (((0,), (0,)), ((), ())), preferred_element_type=F32)
        part[:, :, cols] = res.astype(BF16).reshape(part.shape[0], depth, width)

    chunks(spread_ref.shape[1], 2 * STEP, product)
    core = info[0]
    for j in range(keep_ref.shape[0]):
        keep_ref[j] = part[2 * j + core]
        send_ref[j] = part[2 * j + 1 - core]


def join_body(pieces, info, *refs):
    wide_ref, first_ref, last_ref = refs[pieces:]
    depth = refs[0].shape[0]
    for i, ref in enumerate(refs[:pieces]):
        place = info[8 + i]
        wide_ref[pl.ds(pl.multiple_of(place * depth, depth), depth), :] = ref[...]
    first_ref[...] = wide_ref[:, :RIM]
    start = pl.multiple_of((info[2] - HB) * BLK, BLK)
    last_ref[...] = wide_ref[:, pl.ds(start, RIM)]


def conv_inner_body(tab, w_ref, wide_ref, z_ref, prod, *sums):
    def product(start, width):
        cols = pl.ds(start, width)
        prod[:, cols] = jnp.dot(w_ref[...], wide_ref[:, cols], preferred_element_type=F32)

    nblocks = z_ref.shape[0]
    chunks(wide_ref.shape[1], STEP, product)
    collect(tab, prod, sums, 0, nblocks)
    for b in range(nblocks):
        total = sums[0][b]
        for acc in sums[1:]:
            total = total + acc[b]
        z_ref[b] = total


def conv_rim_body(layer, tab, w_ref, left_ref, right_ref, part_ref, *refs):
    outs, prod, sums = refs[: 2 if layer == 1 else 1], refs[2 if layer == 1 else 1], refs[3 if layer == 1 else 2 :]
    nblocks = part_ref.shape[0]
    prod[:, :RIM] = jnp.dot(w_ref[...], left_ref[...], preferred_element_type=F32)
    prod[:, RIM:] = jnp.dot(w_ref[...], right_ref[...], preferred_element_type=F32)
    collect(tab, prod, sums, nblocks, nblocks + 2 * HB)
    for b in range(nblocks):
        z = part_ref[b]
        for acc in sums:
            z = z + acc[b]
        cols = slice(b * BLK, (b + 1) * BLK)
        if layer == 1:
            outs[0][:, cols] = z
            outs[1][:, cols] = (z / (1.0 + jnp.exp(-z))).astype(BF16)
        else:
            outs[0][:, cols] = z.astype(BF16)


def halve_body(info, keep_ref, got_ref, mine_ref, *send_refs):
    place = info[1]
    mine_ref[...] = keep_ref[place].astype(F32) + got_ref[place].astype(F32)
    for j, ref in enumerate(send_refs):
        other = place ^ (j + 1)
        ref[...] = (keep_ref[other].astype(F32) + got_ref[other].astype(F32)).astype(BF16)


def rims_body(count, mine_ref, *refs):
    gots, (inner_ref, left_ref, right_ref) = refs[:count], refs[count:]
    total = mine_ref[...]
    for ref in gots:
        total = total + ref[...].astype(F32)
    rows = inner_ref.shape[1]
    inner_ref[...] = total[:, :rows]
    left_ref[...] = total[:, rows : rows + RIM].astype(BF16)
    right_ref[...] = total[:, rows + RIM :].astype(BF16)


def weight_grad(wide_ref, left_ref, right_ref, spread_ref, total, keep_ref, send_ref, parity):
    rows = wide_ref.shape[1]
    shares, width_in = total.shape[0], total.shape[1]
    dims = (((1,), (1,)), ((), ()))

    def product(start, width):
        part = pl.ds(start, width)
        res = lax.dot_general(wide_ref[...], spread_ref[part, :rows], dims, preferred_element_type=F32)
        res += lax.dot_general(left_ref[...], spread_ref[part, rows : rows + RIM], dims, preferred_element_type=F32)
        res += lax.dot_general(right_ref[...], spread_ref[part, rows + RIM :], dims, preferred_element_type=F32)
        total[:, :, part] = res.reshape(shares, width_in, width)

    chunks(spread_ref.shape[0], STEP, product)
    for j in range(shares // 2):
        keep_ref[j] = total[2 * j + parity]
        send_ref[j] = total[2 * j + 1 - parity].astype(BF16)


def grad_two_body(info, wide_ref, left_ref, right_ref, spread_ref, keep_ref, send_ref, total):
    weight_grad(wide_ref, left_ref, right_ref, spread_ref, total, keep_ref, send_ref, info[3])


def grad_one_body(
    tab, info, z_ref, inner_ref, from_left, from_right, wide_ref, left_ref, right_ref,
    keep_ref, send_ref, grads, blocks, spread_ref, total, *sums
):
    grads[...] = inner_ref[...]
    grads[:, :RIM] = grads[:, :RIM] + from_left[...].astype(F32)
    tail = pl.ds(pl.multiple_of((info[2] - HB) * BLK, BLK), RIM)
    grads[:, tail] = grads[:, tail] + from_right[...].astype(F32)
    nblocks = blocks.shape[0] - 1
    for b in range(nblocks):
        cols = slice(b * BLK, (b + 1) * BLK)
        z = z_ref[:, cols]
        gate = 1.0 / (1.0 + jnp.exp(-z))
        value = grads[:, cols] * gate * (1.0 + z * (1.0 - gate))
        blocks[b] = value.astype(BF16).astype(F32)
    blocks[nblocks] = jnp.zeros_like(blocks[nblocks])
    spread(tab, blocks, sums, spread_ref)
    weight_grad(wide_ref, left_ref, right_ref, spread_ref, total, keep_ref, send_ref, info[3])


def finish_body(count, mine_ref, *refs):
    gots, out_ref = refs[:count], refs[count]
    total = mine_ref[...]
    for ref in gots:
        total = total + ref[...].astype(F32)
    depth = out_ref.shape[2]
    for k in range(out_ref.shape[0]):
        out_ref[k] = total[:, k * depth : (k + 1) * depth]


def local(features, kernel_map, block_count, weight_one, weight_two, cotangent):
    shard, place = lax.axis_index("space"), lax.axis_index("chan")
    slabs, parts = lax.axis_size("space"), lax.axis_size("chan")
    pairs = parts // 2
    rows, depth = features.shape
    nblocks = rows // BLK
    reach = nblocks + 2 * HB
    offsets, entries = kernel_map.shape[1:3]
    wide = weight_one.shape[2]
    flat = offsets * depth

    own_count = block_count[shard]
    left_count = block_count[jnp.maximum(shard - 1, 0)]
    source, inblock, target = (kernel_map[0, :, :, i] for i in range(3))
    position = jnp.where(
        source == shard,
        inblock,
        jnp.where(source < shard, nblocks + inblock - (left_count - HB), nblocks + HB + inblock),
    )
    tab = (position * 64 + jnp.where(target < own_count, target, nblocks)).reshape(-1)
    order = [0, 1] + [v for j in range(1, pairs) for v in (2 * j, 2 * j + 1)]
    info = jnp.stack(
        [place % 2, place // 2, own_count, shard % 2, shard // 2, shard * 0, shard * 0, shard * 0]
        + [place ^ v for v in order]
    ).astype(jnp.int32)

    def swap(value, axis, bits):
        return lax.ppermute(value, axis, [(i, i ^ bits) for i in range(lax.axis_size(axis))])

    def up(value):
        return lax.ppermute(value, "space", [(i, i + 1) for i in range(slabs - 1)])

    def down(value):
        return lax.ppermute(value, "space", [(i + 1, i) for i in range(slabs - 1)])

    def gather(shard_t):
        pieces = [shard_t]
        far = [swap(shard_t, "chan", 2 * j) for j in range(1, pairs)]
        pieces.append(swap(shard_t, "chan", 1))
        for got in far:
            pieces += [got, swap(got, "chan", 1)]
        joined, first, last = call(
            functools.partial(join_body, parts),
            [((wide, rows), BF16), ((wide, RIM), BF16), ((wide, RIM), BF16)],
            [info] + pieces,
            traffic=4 << 20,
        )
        return joined, up(last), down(first)

    sum_block = pltpu.VMEM((nblocks + 1, depth, BLK), F32)
    reach_block = pltpu.VMEM((reach, depth, BLK), F32)

    def conv_inner(weights, joined):
        return call(
            conv_inner_body,
            [((nblocks, depth, BLK), F32)],
            [tab, weights, joined],
            [pltpu.VMEM((flat, rows), F32)] + [sum_block] * 4,
            flops=2 * flat * wide * rows,
            traffic=16 << 20,
        )[0]

    def conv_rim(layer, weights, left, right, part):
        return call(
            functools.partial(conv_rim_body, layer),
            [((depth, rows), F32), ((depth, rows), BF16)] if layer == 1 else [((depth, rows), BF16)],
            [tab, weights, left, right, part],
            [pltpu.VMEM((flat, 2 * RIM), F32)] + [sum_block] * 4,
            flops=2 * flat * wide * 2 * RIM,
            traffic=8 << 20,
        )

    def reduce_slabs(keep, send):
        got = swap(send, "space", 1)
        share = wide // slabs
        outs = call(
            halve_body,
            [((share, flat), F32)] + [((share, flat), BF16)] * (slabs // 2 - 1),
            [info_z, keep, got],
            traffic=4 << 20,
        )
        gots = [swap(v, "space", 2 * (j + 1)) for j, v in enumerate(outs[1:])]
        total = call(
            functools.partial(finish_body, len(gots)),
            [((offsets, share, depth), F32)],
            [outs[0]] + gots,
            traffic=2 << 20,
        )[0]
        return total.transpose(0, 2, 1)

    info_z = jnp.stack([shard % 2, shard // 2]).astype(jnp.int32)
    w_one = weight_one.reshape(flat, wide)
    w_two = weight_two.reshape(flat, wide)

    x_wide, x_left, x_right = gather(features.T)

    spread_two, keep, send = call(
        functools.partial(input_grad_body, nblocks),
        [((flat, reach * BLK), BF16), ((pairs, depth, reach * BLK), BF16), ((pairs, depth, reach * BLK), BF16)],
        [tab, info, cotangent.T, w_two],
        [pltpu.VMEM((nblocks + 1, depth, BLK), F32), pltpu.VMEM((parts, depth, reach * BLK), BF16)] + [reach_block] * 3,
        flops=2 * flat * wide * reach * BLK,
        traffic=24 << 20,
    )
    got = swap(send, "chan", 1)
    mine, *sends = call(
        halve_body,
        [((depth, reach * BLK), F32)] + [((depth, reach * BLK), BF16)] * (pairs - 1),
        [info, keep, got],
        traffic=4 << 20,
    )
    gots = [swap(v, "chan", 2 * (j + 1)) for j, v in enumerate(sends)]

    z_part = conv_inner(w_one, x_wide)
    z_one, hidden = conv_rim(1, w_one, x_left, x_right, z_part)
    h_wide, h_left, h_right = gather(hidden)

    inner, to_left, to_right = call(
        functools.partial(rims_body, len(gots)),
        [((depth, rows), F32), ((depth, RIM), BF16), ((depth, RIM), BF16)],
        [mine] + gots,
        traffic=3 << 20,
    )
    from_right, from_left = down(to_left), up(to_right)

    share = wide // slabs
    grad_outs = [((slabs // 2, share, flat), F32), ((slabs // 2, share, flat), BF16)]
    total_scratch = pltpu.VMEM((slabs, share, flat), F32)
    keep_one, send_one = call(
        grad_one_body,
        grad_outs,
        [tab, info, z_one, inner, from_left, from_right, x_wide, x_left, x_right],
        [
            pltpu.VMEM((depth, rows), F32),
            pltpu.VMEM((nblocks + 1, depth, BLK), F32),
            pltpu.VMEM((flat, reach * BLK), BF16),
            total_scratch,
        ]
        + [reach_block] * 3,
        flops=2 * flat * wide * reach * BLK,
        traffic=24 << 20,
    )
    grad_one = reduce_slabs(keep_one, send_one)

    out_part = conv_inner(w_two, h_wide)
    keep_two, send_two = call(
        grad_two_body,
        grad_outs,
        [info, h_wide, h_left, h_right, spread_two],
        [total_scratch],
        flops=2 * flat * wide * reach * BLK,
        traffic=16 << 20,
    )
    grad_two = reduce_slabs(keep_two, send_two)
    (output,) = conv_rim(2, w_two, h_left, h_right, out_part)
    return output.T, grad_one, grad_two


def solution(mesh):
    return jax.shard_map(
        local,
        mesh=mesh,
        in_specs=(
            P("space", "chan"),
            P("space", None, None, None),
            P(),
            P(None, "chan", None),
            P(None, "chan", None),
            P("space", "chan"),
        ),
        out_specs=(P("space", "chan"), P(None, "chan", "space"), P(None, "chan", "space")),
        check_vma=False,
    )
```

time: 726 us -> 144 us (0.20); the launches traced: 717 us -> 144 us
  matrix products: 371 us -> 0 us
  local copies, waits for them, and re-layouts: 253 us -> 14 us
  Pallas kernels: 0 us -> 76.4 us
  waiting for transfers between devices: 48.9 us -> 13.1 us
  starting transfers between devices: 15.8 us -> 36.1 us
  between operations: 16 us -> 1.5 us
  other arithmetic: 9.87 us -> 2.59 us
    dot_general x270 -> x0, matrix products: 371 us -> none  [the longest x54 96.5 us: convolve_add_offset(): jnp.einsum('erc,dc->erd', picked, kernel, preferred_element_type=jnp.floa...]
    gather x108 -> x0, local copies, waits for them, and re-layouts: 155 us -> none  [the longest x54 95.7 us: convolve_add_offset(): picked = cube[index]]
    pallas_call x0 -> x15, Pallas kernels: none -> 76.4 us  [call(): pl.pallas_call(body, out_shape=[jax.ShapeDtypeStruct(s, t) for s, t in ou...]
    convert_element_type x27 -> x0, local copies, waits for them, and re-layouts: 62.5 us -> none  [spread_add_offset(): chosen = jnp.einsum('eb,brd->erd', choose, grad_cube, preferred_element_t...]
    unnamed x6 -> x0, waiting for transfers between devices: 22.7 us -> none
    ppermute x6 -> x22, starting transfers between devices: 15.6 us -> 36.1 us  [the longest x16 19.7 us: swap(): lax.ppermute(value, axis, [(i, i ^ bits) for i in range(lax.axis_size(axi...]
    all_gather x2 -> x0, waiting for transfers between devices: 14.3 us -> none  [widen(): return lax.all_gather(feat, 'chan', axis=1, tiled=True)]
    while x3 -> x0, local copies, waits for them, and re-layouts: 9.27 us -> none  [the longest x2 6.91 us: weight_grad(): return lax.map(one_offset, (position, select_b))]
  transfers between devices with their start and end apart: 11 -> 22, of which waited for: 7 -> 4; matrix products, arithmetic and copies ran while one was open for 58% -> 5% of each run, Pallas kernels for 0% -> 52%
where the time goes in v1:
time: 144 us
  Pallas kernels  76.4 us (53%)
  starting transfers between devices  36.1 us (25%)
  local copies, waits for them, and re-layouts  14 us (10%)
  waiting for transfers between devices  13.1 us (9%)
  other arithmetic  2.59 us (2%)
  between operations  1.5 us (1%)
    pallas_call x15, Pallas kernels, call(): pl.pallas_call(body, out_shape=[jax.ShapeDtypeStruct(s, t) for s, t in ou...  76.4 us
    ppermute x16, starting transfers between devices, swap(): lax.ppermute(value, axis, [(i, i ^ bits) for i in range(lax.axis_size(axi...  19.7 us
    ppermute x16, waiting for transfers between devices, swap(): lax.ppermute(value, axis, [(i, i ^ bits) for i in range(lax.axis_size(axi...  13.1 us
    ppermute x3, starting transfers between devices, up(): return lax.ppermute(value, 'space', [(i, i + 1) for i in range(slabs - 1)])  12.6 us
    unnamed x44, local copies, waits for them, and re-layouts  9.88 us
    ppermute x3, starting transfers between devices, down(): return lax.ppermute(value, 'space', [(i + 1, i) for i in range(slabs - 1)])  3.88 us
  transfers between devices with their start and end apart: 22, of which 4 were waited for; matrix products, arithmetic and copies ran while one was open for 5% of the time, Pallas kernels for 52%

profile of v1, /device:TPU:0, one launch (start us, length us, event | category | flops | bytes accessed | tf_op | source)
XLA Modules:
  0.0 143.7 jit_solution(9329881026026466407)
XLA Ops:
  0.6 3.0 %collective-permute-start.1 = (bf16[64,2048]{1,0:T(8,128)(2,1)}, bf16[64,2048]{1,0:T(8,128)(2,1)S(1)}, u32[]{:S(2)}, u32[]{:S(2)}) collective-permute-start(bf16[64,2048]{1,0:T(8,128)(2,1)} %bitcast.30), channel_id=1, source_target_pairs={{0,2},{1,3},{2,0},{3,1},{4,6},{5,7},{6,4},{7,5},{8,10},{9,11},{10,... | collective-permute-start | bytes 786440 | tf_op jit(solution)/shard_map/ppermute | solution.py:255
  3.6 0.7 fusion.1
  4.5 0.7 slice_compare_fusion
  5.8 1.3 fusion.2
  7.8 1.2 fusion.tab
  9.0 1.3 stack.40.info
  10.3 11.5 %shard_map.91 = (bf16[1728,2560]{1,0:T(8,128)(2,1)}, bf16[2,64,2560]{2,1,0:T(8,128)(2,1)}, bf16[2,64,2560]{2,1,0:T(8,128)(2,1)}) custom-call(s32[432]{0:T(512)} %fusion.tab, s32[12]{0:T(128)} %stack.40.info, bf16[64,2048]{1,0:T(8,128)(2,1)} %bitcast.36, bf16[1728,256]{1,0:T(8,128)(2,1)} %bitcast.25), custom_call_target="tpu_custom_call" | custom-call | flops 2264924160 | bytes 25165824 | tf_op jit(solution)/shard_map/pallas_call | solution.py:23
  22.4 2.5 %collective-permute-done.refs_1_ = bf16[64,2048]{1,0:T(8,128)(2,1)S(1)} collective-permute-done((bf16[64,2048]{1,0:T(8,128)(2,1)}, bf16[64,2048]{1,0:T(8,128)(2,1)S(1)}, u32[]{:S(2)}, u32[]{:S(2)}) %collective-permute-start) | collective-permute-done | bytes 262176 | tf_op jit(solution)/shard_map/ppermute | solution.py:255
  24.9 0.7 copy-done.10
  25.6 0.7 copy-done.11
  26.3 2.3 %shard_map.85 = (bf16[256,2048]{1,0:T(8,128)(2,1)}, bf16[256,256]{1,0:T(8,128)(2,1)}, bf16[256,256]{1,0:T(8,128)(2,1)}) custom-call(s32[12]{0:T(128)} %stack.40.info, bf16[64,2048]{1,0:T(8,128)(2,1)} %bitcast.32, bf16[64,2048]{1,0:T(8,128)(2,1)} %copy-done.10, bf16[64,2048]{1,0:T(8,128)(2,1)} %copy-done.6, bf16[64,2048]{1,0:T(8,128)(2,1)} %copy-done.11), custom_call_target="tpu_custom_call" | custom-call | bytes 4194304 | tf_op jit(solution)/shard_map/pallas_call | solution.py:23
  28.7 3.4 %collective-permute-start.3 = (bf16[256,256]{1,0:T(8,128)(2,1)}, bf16[256,256]{1,0:T(8,128)(2,1)S(1)}, u32[]{:S(2)}, u32[]{:S(2)}) collective-permute-start(bf16[256,256]{1,0:T(8,128)(2,1)} %get-tuple-element.31), channel_id=1, source_target_pairs={{0,4},{4,8},{8,12},{12,16},{16,20},{20,24},{24,28},{1,5},{5,9},{9,... | collective-permute-start | bytes 393224 | tf_op jit(solution)/shard_map/ppermute | solution.py:258
  32.1 1.3 collective-permute-start.4
  33.4 8.4 %shard_map.86.part_ref = f32[16,64,128]{2,1,0:T(8,128)} custom-call(s32[432]{0:T(512)} %fusion.tab, bf16[1728,256]{1,0:T(8,128)(2,1)} %bitcast.34, bf16[256,2048]{1,0:T(8,128)(2,1)} %get-tuple-element.33.wide_ref), custom_call_target="tpu_custom_call" | custom-call | flops 1811939328 | bytes 16777216 | tf_op jit(solution)/shard_map/pallas_call | solution.py:23
  41.8 0.6 copy-done.18
  42.4 0.7 copy-done.19
  43.1 5.8 %shard_map.87 = (f32[64,2048]{1,0:T(8,128)}, bf16[64,2048]{1,0:T(8,128)(2,1)}) custom-call(s32[432]{0:T(512)} %fusion.tab, bf16[1728,256]{1,0:T(8,128)(2,1)} %bitcast.35, bf16[256,256]{1,0:T(8,128)(2,1)} %copy-done.18, bf16[256,256]{1,0:T(8,128)(2,1)} %copy-done.19, f32[16,64,128]{2,1,0:T(8,128)} %shard_map.86.part_ref), custom_call_target="tpu_custom_call" | custom-call | flops 452984832 | bytes 8388608 | tf_op jit(solution)/shard_map/pallas_call | solution.py:23
  49.4 0.8 copy-done
  50.2 2.3 %shard_map.92 = (f32[64,2560]{1,0:T(8,128)}, bf16[64,2560]{1,0:T(8,128)(2,1)}) custom-call(s32[12]{0:T(128)} %stack.40.info, bf16[2,64,2560]{2,1,0:T(8,128)(2,1)} %get-tuple-element.39.keep_ref, bf16[2,64,2560]{2,1,0:T(8,128)(2,1)} %copy-done), custom_call_target="tpu_custom_call" | custom-call | bytes 4194304 | tf_op jit(solution)/shard_map/pallas_call | solution.py:23
  52.5 1.5 %collective-permute-start.11 = (bf16[64,2560]{1,0:T(8,128)(2,1)}, bf16[64,2560]{1,0:T(8,128)(2,1)S(1)}, u32[]{:S(2)}, u32[]{:S(2)}) collective-permute-start(bf16[64,2560]{1,0:T(8,128)(2,1)} %get-tuple-element.42), channel_id=1, source_target_pairs={{0,2},{1,3},{2,0},{3,1},{4,6},{5,7},{6,4},{7,5},{8,10},{9,11},{10,... | collective-permute-start | bytes 983048 | tf_op jit(solution)/shard_map/ppermute | solution.py:255
  54.0 4.2 %collective-permute-done.6.refs_2_ = bf16[64,2048]{1,0:T(8,128)(2,1)S(1)} collective-permute-done((bf16[64,2048]{1,0:T(8,128)(2,1)}, bf16[64,2048]{1,0:T(8,128)(2,1)S(1)}, u32[]{:S(2)}, u32[]{:S(2)}) %collective-permute-start.6) | collective-permute-done | bytes 262176 | tf_op jit(solution)/shard_map/ppermute | solution.py:255
  58.3 5.8 %collective-permute-done.11.refs_0_ = bf16[64,2560]{1,0:T(8,128)(2,1)S(1)} collective-permute-done((bf16[64,2560]{1,0:T(8,128)(2,1)}, bf16[64,2560]{1,0:T(8,128)(2,1)S(1)}, u32[]{:S(2)}, u32[]{:S(2)}) %collective-permute-start.11) | collective-permute-done | bytes 327712 | tf_op jit(solution)/shard_map/ppermute | solution.py:255
  64.1 0.7 copy-done.5
  64.8 2.0 %shard_map.93 = (f32[64,2048]{1,0:T(8,128)}, bf16[64,256]{1,0:T(8,128)(2,1)}, bf16[64,256]{1,0:T(8,128)(2,1)}) custom-call(f32[64,2560]{1,0:T(8,128)} %get-tuple-element.41.mine_ref, bf16[64,2560]{1,0:T(8,128)(2,1)} %copy-done.5), custom_call_target="tpu_custom_call" | custom-call | bytes 3145728 | tf_op jit(solution)/shard_map/pallas_call | solution.py:23
  66.9 4.3 %collective-permute-start.12 = (bf16[64,256]{1,0:T(8,128)(2,1)}, bf16[64,256]{1,0:T(8,128)(2,1)S(1)}, u32[]{:S(2)}, u32[]{:S(2)}) collective-permute-start(bf16[64,256]{1,0:T(8,128)(2,1)} %get-tuple-element.44), channel_id=1, source_target_pairs={{0,4},{4,8},{8,12},{12,16},{16,20},{20,24},{24,28},{1,5},{5,9},{9,... | collective-permute-start | bytes 98312 | tf_op jit(solution)/shard_map/ppermute | solution.py:258
  71.2 1.3 collective-permute-start.13
  72.5 0.7 copy-done.8
  73.2 0.7 copy-done.9
  73.9 2.4 %shard_map.88 = (bf16[256,2048]{1,0:T(8,128)(2,1)}, bf16[256,256]{1,0:T(8,128)(2,1)}, bf16[256,256]{1,0:T(8,128)(2,1)}) custom-call(s32[12]{0:T(128)} %stack.40.info, bf16[64,2048]{1,0:T(8,128)(2,1)} %get-tuple-element.34.refs_0_, bf16[64,2048]{1,0:T(8,128)(2,1)} %copy-done.8, bf16[64,2048]{1,0:T(8,128)(2,1)} %copy-done.7, bf16[64,2048]{1,0:T(8,128)(2,1)} %copy-done.9), custom_call_target="tpu_custom_call" | custom-call | bytes 4194304 | tf_op jit(solution)/shard_map/pallas_call | solution.py:23
  76.3 4.9 %collective-permute-start.8 = (bf16[256,256]{1,0:T(8,128)(2,1)}, bf16[256,256]{1,0:T(8,128)(2,1)S(1)}, u32[]{:S(2)}, u32[]{:S(2)}) collective-permute-start(bf16[256,256]{1,0:T(8,128)(2,1)} %get-tuple-element.35), channel_id=1, source_target_pairs={{0,4},{4,8},{8,12},{12,16},{16,20},{20,24},{24,28},{1,5},{5,9},{9,... | collective-permute-start | bytes 393224 | tf_op jit(solution)/shard_map/ppermute | solution.py:258
  81.2 1.3 collective-permute-start.9
  83.1 10.5 %shard_map.94 = (f32[4,32,1728]{2,1,0:T(8,128)}, bf16[4,32,1728]{2,1,0:T(8,128)(2,1)}) custom-call(s32[432]{0:T(512)} %fusion.tab, s32[12]{0:T(128)} %stack.40.info, f32[64,2048]{1,0:T(8,128)} %get-tuple-element.38.z_ref, f32[64,2048]{1,0:T(8,128)} %get-tuple-element.43.inner_ref, bf16[64,256]{1,0:T(8,128)(2,1)} %copy-done.20, bf16[64,256]{1,0:T(8,128)(2,1)} %copy-done.21, ...), custom_call_target="tpu_custom_call" | custom-call | flops 2264924160 | bytes 25165824 | tf_op jit(solution)/shard_map/pallas_call | solution.py:23
  93.7 3.5 %collective-permute-start.14 = (bf16[4,32,1728]{2,1,0:T(8,128)(2,1)}, bf16[4,32,1728]{2,1,0:T(8,128)(2,1)S(1)}, u32[]{:S(2)}, u32[]{:S(2)}) collective-permute-start(bf16[4,32,1728]{2,1,0:T(8,128)(2,1)} %get-tuple-element.47), channel_id=1, source_target_pairs={{0,4},{4,0},{8,12},{12,8},{16,20},{20,16},{24,28},{28,24},{1,5},{5... | collective-permute-start | bytes 1327112 | tf_op jit(solution)/shard_map/ppermute | solution.py:255
  97.2 0.6 copy-done.1
  97.9 8.8 %shard_map.97 = (f32[4,32,1728]{2,1,0:T(8,128)}, bf16[4,32,1728]{2,1,0:T(8,128)(2,1)}) custom-call(s32[12]{0:T(128)} %stack.40.info, bf16[256,2048]{1,0:T(8,128)(2,1)} %get-tuple-element.37.wide_ref, bf16[256,256]{1,0:T(8,128)(2,1)} %copy-done.1, bf16[256,256]{1,0:T(8,128)(2,1)} %copy-done.2, bf16[1728,2560]{1,0:T(8,128)(2,1)} %get-tuple-element.52.spread_ref), custom_call_target="tpu_custom_call" | custom-call | flops 2264924160 | bytes 16777216 | tf_op jit(solution)/shard_map/pallas_call | solution.py:23
  106.7 0.7 pad_add_fusion.info
  107.4 0.8 copy-done.4
  108.2 2.2 %shard_map.95 = (f32[32,1728]{1,0:T(8,128)}, bf16[32,1728]{1,0:T(8,128)(2,1)}, bf16[32,1728]{1,0:T(8,128)(2,1)}, bf16[32,1728]{1,0:T(8,128)(2,1)}) custom-call(s32[2]{0:T(128)} %pad_add_fusion.info, f32[4,32,1728]{2,1,0:T(8,128)} %get-tuple-element.46.keep_ref, bf16[4,32,1728]{2,1,0:T(8,128)(2,1)} %copy-done.4), custom_call_target="tpu_custom_call" | custom-call | bytes 4194304 | tf_op jit(solution)/shard_map/pallas_call | solution.py:23
  110.3 3.5 %collective-permute-start.15 = (bf16[32,1728]{1,0:T(8,128)(2,1)}, bf16[32,1728]{1,0:T(8,128)(2,1)S(1)}, u32[]{:S(2)}, u32[]{:S(2)}) collective-permute-start(bf16[32,1728]{1,0:T(8,128)(2,1)} %get-tuple-element.49), channel_id=1, source_target_pairs={{0,8},{4,12},{8,0},{12,4},{16,24},{20,28},{24,16},{28,20},{1,9},{5... | collective-permute-start | bytes 331784 | tf_op jit(solution)/shard_map/ppermute | solution.py:255
  113.8 2.6 %collective-permute-start.16 = (bf16[32,1728]{1,0:T(8,128)(2,1)}, bf16[32,1728]{1,0:T(8,128)(2,1)S(1)}, u32[]{:S(2)}, u32[]{:S(2)}) collective-permute-start(bf16[32,1728]{1,0:T(8,128)(2,1)} %get-tuple-element.50), channel_id=1, source_target_pairs={{0,16},{4,20},{8,24},{12,28},{16,0},{20,4},{24,8},{28,12},{1,17},{... | collective-permute-start | bytes 331784 | tf_op jit(solution)/shard_map/ppermute | solution.py:255
  117.0 0.8 copy-done.3
  117.7 2.2 %shard_map.98 = (f32[32,1728]{1,0:T(8,128)}, bf16[32,1728]{1,0:T(8,128)(2,1)}, bf16[32,1728]{1,0:T(8,128)(2,1)}, bf16[32,1728]{1,0:T(8,128)(2,1)}) custom-call(s32[2]{0:T(128)} %pad_add_fusion.info, f32[4,32,1728]{2,1,0:T(8,128)} %get-tuple-element.53.keep_ref, bf16[4,32,1728]{2,1,0:T(8,128)(2,1)} %copy-done.3), custom_call_target="tpu_custom_call" | custom-call | bytes 4194304 | tf_op jit(solution)/shard_map/pallas_call | solution.py:23
  119.9 1.7 %collective-permute-start.19 = (bf16[32,1728]{1,0:T(8,128)(2,1)}, bf16[32,1728]{1,0:T(8,128)(2,1)S(1)}, u32[]{:S(2)}, u32[]{:S(2)}) collective-permute-start(bf16[32,1728]{1,0:T(8,128)(2,1)} %get-tuple-element.56), channel_id=1, source_target_pairs={{0,8},{4,12},{8,0},{12,4},{16,24},{20,28},{24,16},{28,20},{1,9},{5... | collective-permute-start | bytes 331784 | tf_op jit(solution)/shard_map/ppermute | solution.py:255
  121.6 2.6 %collective-permute-start.20 = (bf16[32,1728]{1,0:T(8,128)(2,1)}, bf16[32,1728]{1,0:T(8,128)(2,1)S(1)}, u32[]{:S(2)}, u32[]{:S(2)}) collective-permute-start(bf16[32,1728]{1,0:T(8,128)(2,1)} %get-tuple-element.57), channel_id=1, source_target_pairs={{0,16},{4,20},{8,24},{12,28},{16,0},{20,4},{24,8},{28,12},{1,17},{... | collective-permute-start | bytes 331784 | tf_op jit(solution)/shard_map/ppermute | solution.py:255
  124.3 8.4 %shard_map.89.part_ref = f32[16,64,128]{2,1,0:T(8,128)} custom-call(s32[432]{0:T(512)} %fusion.tab, bf16[1728,256]{1,0:T(8,128)(2,1)} %bitcast.26, bf16[256,2048]{1,0:T(8,128)(2,1)} %get-tuple-element.37.wide_ref), custom_call_target="tpu_custom_call" | custom-call | flops 1811939328 | bytes 16777216 | tf_op jit(solution)/shard_map/pallas_call | solution.py:23
  132.7 5.5 %shard_map.90 = bf16[64,2048]{1,0:T(8,128)(2,1)} custom-call(s32[432]{0:T(512)} %fusion.tab, bf16[1728,256]{1,0:T(8,128)(2,1)} %bitcast.27, bf16[256,256]{1,0:T(8,128)(2,1)} %copy-done.1, bf16[256,256]{1,0:T(8,128)(2,1)} %copy-done.2, f32[16,64,128]{2,1,0:T(8,128)} %shard_map.89.part_ref), custom_call_target="tpu_custom_call" | custom-call | flops 452984832 | bytes 8388608 | tf_op jit(solution)/shard_map/pallas_call | solution.py:23
  138.9 2.0 %shard_map.96 = f32[27,32,64]{2,1,0:T(8,128)} custom-call(f32[32,1728]{1,0:T(8,128)} %get-tuple-element.48.mine_ref, bf16[32,1728]{1,0:T(8,128)(2,1)} %copy-done.12, bf16[32,1728]{1,0:T(8,128)(2,1)} %copy-done.13, bf16[32,1728]{1,0:T(8,128)(2,1)} %copy-done.14), custom_call_target="tpu_custom_call" | custom-call | bytes 2097152 | tf_op jit(solution)/shard_map/pallas_call | solution.py:23
  141.7 2.0 %shard_map.99 = f32[27,32,64]{2,1,0:T(8,128)} custom-call(f32[32,1728]{1,0:T(8,128)} %get-tuple-element.55.mine_ref, bf16[32,1728]{1,0:T(8,128)(2,1)} %copy-done.15, bf16[32,1728]{1,0:T(8,128)(2,1)} %copy-done.16, bf16[32,1728]{1,0:T(8,128)(2,1)} %copy-done.17), custom_call_target="tpu_custom_call" | custom-call | bytes 2097152 | tf_op jit(solution)/shard_map/pallas_call | solution.py:23
  (70 shorter events, 4.5 us)
Async XLA Ops:
  0.6 21.7 %collective-permute-start.1 = (bf16[64,2048]{1,0:T(8,128)(2,1)}, bf16[64,2048]{1,0:T(8,128)(2,1)S(1)}, u32[]{:S(2)}, u32[]{:S(2)}) collective-permute-start(bf16[64,2048]{1,0:T(8,128)(2,1)} %bitcast.30), channel_id=1, source_target_pairs={{0,2},{1,3},{2,0},{3,1},{4,6},{5,7},{6,4},{7,5},{8,10},{9,11},{10,... | collective-permute-start | bytes 786440 | tf_op jit(solution)/shard_map/ppermute | solution.py:255
  21.8 27.5 %collective-permute-start.10 = (bf16[2,64,2560]{2,1,0:T(8,128)(2,1)}, bf16[2,64,2560]{2,1,0:T(8,128)(2,1)S(1)}, u32[]{:S(2)}, u32[]{:S(2)}) collective-permute-start(bf16[2,64,2560]{2,1,0:T(8,128)(2,1)} %get-tuple-element.40), channel_id=1, source_target_pairs={{0,1},{1,0},{2,3},{3,2},{4,5},{5,4},{6,7},{7,6},{8,9},{9,8},{10,11... | collective-permute-start | bytes 1966088 | tf_op jit(solution)/shard_map/ppermute | solution.py:255
  21.9 3.1 %collective-permute-start = (bf16[64,2048]{1,0:T(8,128)(2,1)}, bf16[64,2048]{1,0:T(8,128)(2,1)S(1)}, u32[]{:S(2)}, u32[]{:S(2)}) collective-permute-start(bf16[64,2048]{1,0:T(8,128)(2,1)} %bitcast.31), channel_id=1, source_target_pairs={{0,1},{1,0},{2,3},{3,2},{4,5},{5,4},{6,7},{7,6},{8,9},{9,8},{10,11... | collective-permute-start | bytes 786440 | tf_op jit(solution)/shard_map/ppermute | solution.py:255
  22.4 2.6 %copy-start.6 = (bf16[64,2048]{1,0:T(8,128)(2,1)}, bf16[64,2048]{1,0:T(8,128)(2,1)S(1)}, u32[]{:S(2)}) copy-start(bf16[64,2048]{1,0:T(8,128)(2,1)S(1)} %collective-permute-done.1.refs_2_) | copy-start | bytes 786436
  22.4 2.5 %collective-permute-start.2 = (bf16[64,2048]{1,0:T(8,128)(2,1)S(1)}, bf16[64,2048]{1,0:T(8,128)(2,1)S(1)}, u32[]{:S(2)}, u32[]{:S(2)}) collective-permute-start(bf16[64,2048]{1,0:T(8,128)(2,1)S(1)} %collective-permute-done.1.refs_2_), channel_id=1, source_target_pairs={{0,1},{1,0},{2,3},{3,2},{4,5},{5,4},{6,7},{7,6},{8,9},{9,8},{10,11... | collective-permute-start | bytes 786440 | tf_op jit(solution)/shard_map/ppermute | solution.py:255
  24.9 0.7 copy-start.10
  25.6 0.7 copy-start.11
  28.7 13.1 %collective-permute-start.3 = (bf16[256,256]{1,0:T(8,128)(2,1)}, bf16[256,256]{1,0:T(8,128)(2,1)S(1)}, u32[]{:S(2)}, u32[]{:S(2)}) collective-permute-start(bf16[256,256]{1,0:T(8,128)(2,1)} %get-tuple-element.31), channel_id=1, source_target_pairs={{0,4},{4,8},{8,12},{12,16},{16,20},{20,24},{24,28},{1,5},{5,9},{9,... | collective-permute-start | bytes 393224 | tf_op jit(solution)/shard_map/ppermute | solution.py:258
  32.1 9.7 %collective-permute-start.4 = (bf16[256,256]{1,0:T(8,128)(2,1)}, bf16[256,256]{1,0:T(8,128)(2,1)S(1)}, u32[]{:S(2)}, u32[]{:S(2)}) collective-permute-start(bf16[256,256]{1,0:T(8,128)(2,1)} %get-tuple-element.32), channel_id=1, source_target_pairs={{4,0},{8,4},{12,8},{16,12},{20,16},{24,20},{28,24},{5,1},{9,5},{13... | collective-permute-start | bytes 393224 | tf_op jit(solution)/shard_map/ppermute | solution.py:261
  41.8 0.7 copy-start.18
  42.4 0.7 copy-start.19
  48.9 9.4 %collective-permute-start.6 = (bf16[64,2048]{1,0:T(8,128)(2,1)}, bf16[64,2048]{1,0:T(8,128)(2,1)S(1)}, u32[]{:S(2)}, u32[]{:S(2)}) collective-permute-start(bf16[64,2048]{1,0:T(8,128)(2,1)} %get-tuple-element.34.refs_0_), channel_id=1, source_target_pairs={{0,2},{1,3},{2,0},{3,1},{4,6},{5,7},{6,4},{7,5},{8,10},{9,11},{10,... | collective-permute-start | bytes 786440 | tf_op jit(solution)/shard_map/ppermute | solution.py:255
  49.4 0.8 copy-start
  52.5 11.6 %collective-permute-start.11 = (bf16[64,2560]{1,0:T(8,128)(2,1)}, bf16[64,2560]{1,0:T(8,128)(2,1)S(1)}, u32[]{:S(2)}, u32[]{:S(2)}) collective-permute-start(bf16[64,2560]{1,0:T(8,128)(2,1)} %get-tuple-element.42), channel_id=1, source_target_pairs={{0,2},{1,3},{2,0},{3,1},{4,6},{5,7},{6,4},{7,5},{8,10},{9,11},{10,... | collective-permute-start | bytes 983048 | tf_op jit(solution)/shard_map/ppermute | solution.py:255
  54.0 18.4 %collective-permute-start.5 = (bf16[64,2048]{1,0:T(8,128)(2,1)}, bf16[64,2048]{1,0:T(8,128)(2,1)S(1)}, u32[]{:S(2)}, u32[]{:S(2)}) collective-permute-start(bf16[64,2048]{1,0:T(8,128)(2,1)} %get-tuple-element.34.refs_0_), channel_id=1, source_target_pairs={{0,1},{1,0},{2,3},{3,2},{4,5},{5,4},{6,7},{7,6},{8,9},{9,8},{10,11... | collective-permute-start | bytes 786440 | tf_op jit(solution)/shard_map/ppermute | solution.py:255
  58.3 14.2 %copy-start.7 = (bf16[64,2048]{1,0:T(8,128)(2,1)}, bf16[64,2048]{1,0:T(8,128)(2,1)S(1)}, u32[]{:S(2)}) copy-start(bf16[64,2048]{1,0:T(8,128)(2,1)S(1)} %collective-permute-done.6.refs_2_) | copy-start | bytes 786436
  58.3 14.2 %collective-permute-start.7 = (bf16[64,2048]{1,0:T(8,128)(2,1)S(1)}, bf16[64,2048]{1,0:T(8,128)(2,1)S(1)}, u32[]{:S(2)}, u32[]{:S(2)}) collective-permute-start(bf16[64,2048]{1,0:T(8,128)(2,1)S(1)} %collective-permute-done.6.refs_2_), channel_id=1, source_target_pairs={{0,1},{1,0},{2,3},{3,2},{4,5},{5,4},{6,7},{7,6},{8,9},{9,8},{10,11... | collective-permute-start | bytes 786440 | tf_op jit(solution)/shard_map/ppermute | solution.py:255
  64.1 0.7 copy-start.5
  66.9 15.6 %collective-permute-start.12 = (bf16[64,256]{1,0:T(8,128)(2,1)}, bf16[64,256]{1,0:T(8,128)(2,1)S(1)}, u32[]{:S(2)}, u32[]{:S(2)}) collective-permute-start(bf16[64,256]{1,0:T(8,128)(2,1)} %get-tuple-element.44), channel_id=1, source_target_pairs={{0,4},{4,8},{8,12},{12,16},{16,20},{20,24},{24,28},{1,5},{5,9},{9,... | collective-permute-start | bytes 98312 | tf_op jit(solution)/shard_map/ppermute | solution.py:258
  71.2 11.3 %collective-permute-start.13 = (bf16[64,256]{1,0:T(8,128)(2,1)}, bf16[64,256]{1,0:T(8,128)(2,1)S(1)}, u32[]{:S(2)}, u32[]{:S(2)}) collective-permute-start(bf16[64,256]{1,0:T(8,128)(2,1)} %get-tuple-element.45), channel_id=1, source_target_pairs={{4,0},{8,4},{12,8},{16,12},{20,16},{24,20},{28,24},{5,1},{9,5},{13... | collective-permute-start | bytes 98312 | tf_op jit(solution)/shard_map/ppermute | solution.py:261
  72.5 0.7 copy-start.8
  73.2 0.7 copy-start.9
  76.3 20.9 %collective-permute-start.8 = (bf16[256,256]{1,0:T(8,128)(2,1)}, bf16[256,256]{1,0:T(8,128)(2,1)S(1)}, u32[]{:S(2)}, u32[]{:S(2)}) collective-permute-start(bf16[256,256]{1,0:T(8,128)(2,1)} %get-tuple-element.35), channel_id=1, source_target_pairs={{0,4},{4,8},{8,12},{12,16},{16,20},{20,24},{24,28},{1,5},{5,9},{9,... | collective-permute-start | bytes 393224 | tf_op jit(solution)/shard_map/ppermute | solution.py:258
  81.2 16.0 %collective-permute-start.9 = (bf16[256,256]{1,0:T(8,128)(2,1)}, bf16[256,256]{1,0:T(8,128)(2,1)S(1)}, u32[]{:S(2)}, u32[]{:S(2)}) collective-permute-start(bf16[256,256]{1,0:T(8,128)(2,1)} %get-tuple-element.36), channel_id=1, source_target_pairs={{4,0},{8,4},{12,8},{16,12},{20,16},{24,20},{28,24},{5,1},{9,5},{13... | collective-permute-start | bytes 393224 | tf_op jit(solution)/shard_map/ppermute | solution.py:261
  82.5 0.6 copy-start.20
  82.5 0.6 copy-start.21
  93.7 13.7 %collective-permute-start.14 = (bf16[4,32,1728]{2,1,0:T(8,128)(2,1)}, bf16[4,32,1728]{2,1,0:T(8,128)(2,1)S(1)}, u32[]{:S(2)}, u32[]{:S(2)}) collective-permute-start(bf16[4,32,1728]{2,1,0:T(8,128)(2,1)} %get-tuple-element.47), channel_id=1, source_target_pairs={{0,4},{4,0},{8,12},{12,8},{16,20},{20,16},{24,28},{28,24},{1,5},{5... | collective-permute-start | bytes 1327112 | tf_op jit(solution)/shard_map/ppermute | solution.py:255
  97.2 0.7 copy-start.1
  97.2 0.7 copy-start.2
  106.7 10.2 %collective-permute-start.18 = (bf16[4,32,1728]{2,1,0:T(8,128)(2,1)}, bf16[4,32,1728]{2,1,0:T(8,128)(2,1)S(1)}, u32[]{:S(2)}, u32[]{:S(2)}) collective-permute-start(bf16[4,32,1728]{2,1,0:T(8,128)(2,1)} %get-tuple-element.54), channel_id=1, source_target_pairs={{0,4},{4,0},{8,12},{12,8},{16,20},{20,16},{24,28},{28,24},{1,5},{5... | collective-permute-start | bytes 1327112 | tf_op jit(solution)/shard_map/ppermute | solution.py:255
  107.4 0.8 copy-start.4
  110.3 14.0 %collective-permute-start.15 = (bf16[32,1728]{1,0:T(8,128)(2,1)}, bf16[32,1728]{1,0:T(8,128)(2,1)S(1)}, u32[]{:S(2)}, u32[]{:S(2)}) collective-permute-start(bf16[32,1728]{1,0:T(8,128)(2,1)} %get-tuple-element.49), channel_id=1, source_target_pairs={{0,8},{4,12},{8,0},{12,4},{16,24},{20,28},{24,16},{28,20},{1,9},{5... | collective-permute-start | bytes 331784 | tf_op jit(solution)/shard_map/ppermute | solution.py:255
  113.8 24.4 %collective-permute-start.16 = (bf16[32,1728]{1,0:T(8,128)(2,1)}, bf16[32,1728]{1,0:T(8,128)(2,1)S(1)}, u32[]{:S(2)}, u32[]{:S(2)}) collective-permute-start(bf16[32,1728]{1,0:T(8,128)(2,1)} %get-tuple-element.50), channel_id=1, source_target_pairs={{0,16},{4,20},{8,24},{12,28},{16,0},{20,4},{24,8},{28,12},{1,17},{... | collective-permute-start | bytes 331784 | tf_op jit(solution)/shard_map/ppermute | solution.py:255
  116.4 21.8 %collective-permute-start.17 = (bf16[32,1728]{1,0:T(8,128)(2,1)}, bf16[32,1728]{1,0:T(8,128)(2,1)S(1)}, u32[]{:S(2)}, u32[]{:S(2)}) collective-permute-start(bf16[32,1728]{1,0:T(8,128)(2,1)} %get-tuple-element.51), channel_id=1, source_target_pairs={{0,24},{4,28},{8,16},{12,20},{16,8},{20,12},{24,0},{28,4},{1,25},{... | collective-permute-start | bytes 331784 | tf_op jit(solution)/shard_map/ppermute | solution.py:255
  117.0 0.8 copy-start.3
  119.9 21.0 %collective-permute-start.19 = (bf16[32,1728]{1,0:T(8,128)(2,1)}, bf16[32,1728]{1,0:T(8,128)(2,1)S(1)}, u32[]{:S(2)}, u32[]{:S(2)}) collective-permute-start(bf16[32,1728]{1,0:T(8,128)(2,1)} %get-tuple-element.56), channel_id=1, source_target_pairs={{0,8},{4,12},{8,0},{12,4},{16,24},{20,28},{24,16},{28,20},{1,9},{5... | collective-permute-start | bytes 331784 | tf_op jit(solution)/shard_map/ppermute | solution.py:255
  121.6 19.3 %collective-permute-start.20 = (bf16[32,1728]{1,0:T(8,128)(2,1)}, bf16[32,1728]{1,0:T(8,128)(2,1)S(1)}, u32[]{:S(2)}, u32[]{:S(2)}) collective-permute-start(bf16[32,1728]{1,0:T(8,128)(2,1)} %get-tuple-element.57), channel_id=1, source_target_pairs={{0,16},{4,20},{8,24},{12,28},{16,0},{20,4},{24,8},{28,12},{1,17},{... | collective-permute-start | bytes 331784 | tf_op jit(solution)/shard_map/ppermute | solution.py:255
  124.3 14.0 %copy-start.12 = (bf16[32,1728]{1,0:T(8,128)(2,1)}, bf16[32,1728]{1,0:T(8,128)(2,1)S(1)}, u32[]{:S(2)}) copy-start(bf16[32,1728]{1,0:T(8,128)(2,1)S(1)} %collective-permute-done.15.refs_0_) | copy-start | bytes 331780
  124.3 16.7 %collective-permute-start.21 = (bf16[32,1728]{1,0:T(8,128)(2,1)}, bf16[32,1728]{1,0:T(8,128)(2,1)S(1)}, u32[]{:S(2)}, u32[]{:S(2)}) collective-permute-start(bf16[32,1728]{1,0:T(8,128)(2,1)} %get-tuple-element.58), channel_id=1, source_target_pairs={{0,24},{4,28},{8,16},{12,20},{16,8},{20,12},{24,0},{28,4},{1,25},{... | collective-permute-start | bytes 331784 | tf_op jit(solution)/shard_map/ppermute | solution.py:255
  138.2 0.6 copy-start.13
  138.2 0.7 copy-start.14
  140.9 0.7 copy-start.15
  140.9 0.7 copy-start.16
  141.0 0.7 copy-start.17

commit v2 on v1

v2 whole, which is shorter than its diff:
```python
import functools

import jax
import jax.numpy as jnp
from jax import lax
from jax.experimental import pallas as pl
from jax.experimental.pallas import tpu as pltpu
from jax.sharding import PartitionSpec as P

BLK = 128
HB = 2
RIM = HB * BLK
STEP = 256
F32 = jnp.float32
BF16 = jnp.bfloat16

VMEM = pl.BlockSpec(memory_space=pltpu.VMEM)
SMEM = pl.BlockSpec(memory_space=pltpu.SMEM)


def held(value):
    return pltpu.with_memory_space_constraint(value, pltpu.VMEM)


def call(body, outs, ins, scratch=(), flops=0, traffic=0, vmem=40):
    specs = [SMEM if a.dtype == jnp.int32 and a.ndim < 3 else VMEM for a in ins]
    return pl.pallas_call(
        body,
        out_shape=outs,
        in_specs=specs,
        out_specs=[VMEM] * len(outs),
        scratch_shapes=list(scratch),
        compiler_params=pltpu.CompilerParams(vmem_limit_bytes=vmem << 20),
        cost_estimate=pl.CostEstimate(flops=flops, bytes_accessed=traffic, transcendentals=0),
    )(*ins)


def chunks(total, step, body):
    whole = total // step

    def one(i, _):
        body(pl.multiple_of(i * step, step), step)
        return 0

    lax.fori_loop(0, whole, one, 0)
    if total % step:
        body(whole * step, total % step)


def cell(code):
    return code >> 6, code & 63


def near_rim(counts):
    shard = lax.axis_index("space")
    tail = (counts[shard] - HB) * BLK
    even = shard % 2 == 0
    return pl.multiple_of(jnp.where(even, tail, 0), BLK), pl.multiple_of(jnp.where(even, 0, tail), BLK)


def table(counts, map_ref, nblocks):
    shard = lax.axis_index("space")
    even = shard % 2 == 0
    own_count, left_count = counts[shard], counts[jnp.maximum(shard - 1, 0)]
    source, inblock, target = map_ref[0], map_ref[1], map_ref[2]
    left = jnp.where(even, nblocks + HB, nblocks) - (left_count - HB)
    right = jnp.where(even, nblocks, nblocks + HB)
    position = inblock + jnp.where(source == shard, 0, jnp.where(source < shard, left, right))
    code = position * 64 + jnp.where(target < own_count, target, nblocks)
    entries = code.shape[0]
    index = lax.broadcasted_iota(jnp.int32, code.shape, 0)
    rank = jnp.zeros_like(code)
    for e in range(entries):
        row = code[e : e + 1]
        rank += ((row < code) | ((row == code) & (e < index))).astype(jnp.int32)
    rows = [jnp.sum(jnp.where(rank == e, code, 0), axis=0, keepdims=True) for e in range(entries)]
    return jnp.concatenate(rows, axis=0)


def spread(tab, blocks, spread_ref):
    depth = blocks.shape[1]
    entries, offsets = tab.shape

    def one(k, _):
        rows = pl.ds(pl.multiple_of(k * depth, depth), depth)
        spread_ref[rows, :] = jnp.zeros((depth, spread_ref.shape[1]), BF16)
        before, acc = -1, jnp.zeros((depth, BLK), F32)
        for e in range(entries):
            s, t = cell(tab[e, k])
            acc = jnp.where(s == before, acc, 0.0) + blocks[t]
            spread_ref[rows, pl.ds(pl.multiple_of(s * BLK, BLK), BLK)] = acc.astype(BF16)
            before = s
        return 0

    lax.fori_loop(0, offsets, one, 0)


def collect(tab, prod, sums):
    depth = sums[0].shape[1]
    entries, offsets = tab.shape
    for acc in sums:
        acc[...] = jnp.zeros_like(acc)

    def one(k, _):
        rows = pl.ds(pl.multiple_of(k * depth, depth), depth)
        for e in range(entries):
            acc = sums[e % len(sums)]
            s, t = cell(tab[e, k])
            acc[t] = acc[t] + prod[rows, pl.ds(pl.multiple_of(s * BLK, BLK), BLK)]
        return 0

    lax.fori_loop(0, offsets, one, 0)


def extend(ext_ref, wide_ref, a_ref, b_ref):
    rows = wide_ref.shape[1]
    ext_ref[:, :rows] = wide_ref[...]
    ext_ref[:, rows : rows + RIM] = a_ref[...]
    ext_ref[:, rows + RIM :] = b_ref[...]


def input_grad_body(counts, map_ref, cot_ref, w_ref, tab_ref, spread_ref, keep_ref, send_ref, blocks, part, tab, sem):
    depth, rows = cot_ref.shape
    nblocks = rows // BLK
    tab_ref[...] = table(counts, map_ref, nblocks)
    copy = pltpu.make_async_copy(tab_ref, tab, sem)
    copy.start()
    for b in range(nblocks):
        blocks[b] = cot_ref[:, b * BLK : (b + 1) * BLK].astype(F32)
    blocks[nblocks] = jnp.zeros_like(blocks[nblocks])
    copy.wait()
    spread(tab, blocks, spread_ref)

    def product(start, width):
        cols = pl.ds(start, width)
        res = lax.dot_general(w_ref[...], spread_ref[:, cols], (((0,), (0,)), ((), ())), preferred_element_type=F32)
        part[:, :, cols] = res.astype(BF16).reshape(part.shape[0], depth, width)

    chunks(spread_ref.shape[1], 2 * STEP, product)
    core = lax.axis_index("chan") % 2
    for j in range(keep_ref.shape[0]):
        keep_ref[j] = part[2 * j + core]
        send_ref[j] = part[2 * j + 1 - core]


def join_body(order, counts, *refs):
    pieces = len(order)
    wide_ref, a_ref, b_ref = refs[pieces:]
    depth = refs[0].shape[0]
    for bits, ref in zip(order, refs[:pieces]):
        place = lax.axis_index("chan") ^ bits
        wide_ref[pl.ds(pl.multiple_of(place * depth, depth), depth), :] = ref[...]
    a, b = near_rim(counts)
    a_ref[...] = wide_ref[:, pl.ds(a, RIM)]
    b_ref[...] = wide_ref[:, pl.ds(b, RIM)]


def conv_body(layer, tab, w_ref, wide_ref, a_ref, b_ref, *refs):
    count = 2 if layer == 1 else 1
    outs, ext, prod, sums = refs[:count], refs[count], refs[count + 1], refs[count + 2 :]
    extend(ext, wide_ref, a_ref, b_ref)

    def product(start, width):
        cols = pl.ds(start, width)
        prod[:, cols] = jnp.dot(w_ref[...], ext[:, cols], preferred_element_type=F32)

    chunks(ext.shape[1], 2 * STEP, product)
    collect(tab, prod, sums)
    for b in range(sums[0].shape[0] - 1):
        z = sums[0][b]
        for acc in sums[1:]:
            z = z + acc[b]
        cols = slice(b * BLK, (b + 1) * BLK)
        if layer == 1:
            outs[0][:, cols] = z
            outs[1][:, cols] = (z / (1.0 + jnp.exp(-z))).astype(BF16)
        else:
            outs[0][:, cols] = z.astype(BF16)


def halve_body(axis, keep_ref, got_ref, mine_ref, *send_refs):
    place = lax.axis_index(axis) // 2
    mine_ref[...] = keep_ref[place].astype(F32) + got_ref[place].astype(F32)
    for j, ref in enumerate(send_refs):
        other = place ^ (j + 1)
        ref[...] = (keep_ref[other].astype(F32) + got_ref[other].astype(F32)).astype(BF16)


def rims_body(count, mine_ref, *refs):
    gots, (inner_ref, a_ref, b_ref) = refs[:count], refs[count:]
    total = mine_ref[...]
    for ref in gots:
        total = total + ref[...].astype(F32)
    rows = inner_ref.shape[1]
    inner_ref[...] = total[:, :rows]
    a_ref[...] = total[:, rows : rows + RIM].astype(BF16)
    b_ref[...] = total[:, rows + RIM :].astype(BF16)


def weight_grad(ext, spread_ref, total, keep_ref, send_ref):
    shares, width_in = total.shape[0], total.shape[1]

    def product(start, width):
        part = pl.ds(start, width)
        res = lax.dot_general(ext[...], spread_ref[part, :], (((1,), (1,)), ((), ())), preferred_element_type=F32)
        total[:, :, part] = res.reshape(shares, width_in, width)

    chunks(spread_ref.shape[0], 2 * STEP, product)
    parity = lax.axis_index("space") % 2
    for j in range(shares // 2):
        keep_ref[j] = total[2 * j + parity]
        send_ref[j] = total[2 * j + 1 - parity].astype(BF16)


def grad_two_body(wide_ref, a_ref, b_ref, spread_ref, keep_ref, send_ref, ext, total):
    extend(ext, wide_ref, a_ref, b_ref)
    weight_grad(ext, spread_ref, total, keep_ref, send_ref)


def grad_one_body(
    counts, tab, z_ref, inner_ref, from_a, from_b, wide_ref, a_ref, b_ref,
    keep_ref, send_ref, grads, blocks, spread_ref, ext, total
):
    extend(ext, wide_ref, a_ref, b_ref)
    grads[...] = inner_ref[...]
    a, b = near_rim(counts)
    for start, ref in ((a, from_a), (b, from_b)):
        grads[:, pl.ds(start, RIM)] = grads[:, pl.ds(start, RIM)] + ref[...].astype(F32)
    nblocks = blocks.shape[0] - 1
    for i in range(nblocks):
        cols = slice(i * BLK, (i + 1) * BLK)
        z = z_ref[:, cols]
        gate = 1.0 / (1.0 + jnp.exp(-z))
        value = grads[:, cols] * gate * (1.0 + z * (1.0 - gate))
        blocks[i] = value.astype(BF16).astype(F32)
    blocks[nblocks] = jnp.zeros_like(blocks[nblocks])
    spread(tab, blocks, spread_ref)
    weight_grad(ext, spread_ref, total, keep_ref, send_ref)


def finish_body(count, mine_ref, *refs):
    gots, out_ref = refs[:count], refs[count]
    total = mine_ref[...]
    for ref in gots:
        total = total + ref[...].astype(F32)
    depth = out_ref.shape[2]
    for k in range(out_ref.shape[0]):
        out_ref[k] = total[:, k * depth : (k + 1) * depth]


def swap(value, axis, bits):
    return lax.ppermute(value, axis, [(i, i ^ bits) for i in range(lax.axis_size(axis))])


def swap_other(value):
    pairs = [(i, i + 1) for i in range(1, lax.axis_size("space") - 1, 2)]
    return lax.ppermute(value, "space", pairs + [(j, i) for i, j in pairs])


def local(features, kernel_map, block_count, weight_one, weight_two, cotangent):
    slabs, parts = lax.axis_size("space"), lax.axis_size("chan")
    pairs = parts // 2
    rows, depth = features.shape
    nblocks = rows // BLK
    reach = (nblocks + 2 * HB) * BLK
    offsets, entries = kernel_map.shape[1:3]
    wide = weight_one.shape[2]
    flat = offsets * depth
    share = wide // slabs
    order = [0, 1] + [v for j in range(1, pairs) for v in (2 * j, 2 * j + 1)]
    work = 2 * flat * wide * reach
    blocks = pltpu.VMEM((nblocks + 1, depth, BLK), F32)
    ext = pltpu.VMEM((wide, reach), BF16)

    def gather(shard_t):
        far = [swap(shard_t, "chan", 2 * j) for j in range(1, pairs)]
        pieces = [shard_t, swap(shard_t, "chan", 1)]
        for got in far:
            pieces += [got, swap(got, "chan", 1)]
        joined, a, b = call(
            functools.partial(join_body, order),
            [pltpu.VMEM((wide, rows), BF16), pltpu.VMEM((wide, RIM), BF16), pltpu.VMEM((wide, RIM), BF16)],
            [block_count] + [held(v) for v in pieces],
            traffic=2 << 20,
        )
        return joined, swap(a, "space", 1), swap_other(b)

    def convolve(layer, weights, joined, a, b):
        out = pltpu.VMEM((depth, rows), BF16)
        return call(
            functools.partial(conv_body, layer),
            [pltpu.VMEM((depth, rows), F32), out] if layer == 1 else [jax.ShapeDtypeStruct((depth, rows), BF16)],
            [tab, weights, held(joined), held(a), held(b)],
            [ext, pltpu.VMEM((flat, reach), F32)] + [blocks] * 2,
            flops=work,
            traffic=16 << 20,
        )

    def reduce_slabs(keep, send):
        got = swap(send, "space", 1)
        outs = call(
            functools.partial(halve_body, "space"),
            [pltpu.VMEM((share, flat), F32)] + [pltpu.VMEM((share, flat), BF16)] * (slabs // 2 - 1),
            [held(keep), held(got)],
            traffic=2 << 20,
        )
        gots = [swap(v, "space", 2 * (j + 1)) for j, v in enumerate(outs[1:])]
        total = call(
            functools.partial(finish_body, len(gots)),
            [jax.ShapeDtypeStruct((offsets, share, depth), F32)],
            [held(v) for v in [outs[0]] + gots],
            traffic=2 << 20,
        )[0]
        return total.transpose(0, 2, 1)

    w_one = weight_one.reshape(flat, wide)
    w_two = weight_two.reshape(flat, wide)

    x_wide, x_a, x_b = gather(features.T)

    tab, spread_two, keep, send = call(
        input_grad_body,
        [
            jax.ShapeDtypeStruct((entries, offsets), jnp.int32),
            pltpu.VMEM((flat, reach), BF16),
            pltpu.VMEM((pairs, depth, reach), BF16),
            pltpu.VMEM((pairs, depth, reach), BF16),
        ],
        [block_count, kernel_map[0].transpose(2, 1, 0), cotangent.T, w_two],
        [
            blocks,
            pltpu.VMEM((parts, depth, reach), BF16),
            pltpu.SMEM((entries, offsets), jnp.int32),
            pltpu.SemaphoreType.DMA,
        ],
        flops=work,
        traffic=16 << 20,
    )
    got = swap(send, "chan", 1)
    mine, *sends = call(
        functools.partial(halve_body, "chan"),
        [pltpu.VMEM((depth, reach), F32)] + [pltpu.VMEM((depth, reach), BF16)] * (pairs - 1),
        [held(keep), held(got)],
        traffic=2 << 20,
    )
    gots = [swap(v, "chan", 2 * (j + 1)) for j, v in enumerate(sends)]

    z_one, hidden = convolve(1, w_one, x_wide, x_a, x_b)
    h_wide, h_a, h_b = gather(hidden)

    inner, to_a, to_b = call(
        functools.partial(rims_body, len(gots)),
        [pltpu.VMEM((depth, rows), F32), pltpu.VMEM((depth, RIM), BF16), pltpu.VMEM((depth, RIM), BF16)],
        [held(v) for v in [mine] + gots],
        traffic=2 << 20,
    )
    from_a, from_b = swap(to_a, "space", 1), swap_other(to_b)

    grad_outs = [pltpu.VMEM((slabs // 2, share, flat), F32), pltpu.VMEM((slabs // 2, share, flat), BF16)]
    total_scratch = pltpu.VMEM((slabs, share, flat), F32)
    keep_one, send_one = call(
        grad_one_body,
        grad_outs,
        [block_count, tab] + [held(v) for v in (z_one, inner, from_a, from_b, x_wide, x_a, x_b)],
        [pltpu.VMEM((depth, rows), F32), blocks, pltpu.VMEM((flat, reach), BF16), ext, total_scratch],
        flops=work,
        traffic=16 << 20,
    )
    grad_one = reduce_slabs(keep_one, send_one)

    keep_two, send_two = call(
        grad_two_body,
        grad_outs,
        [held(v) for v in (h_wide, h_a, h_b, spread_two)],
        [ext, total_scratch],
        flops=work,
        traffic=8 << 20,
    )
    grad_two = reduce_slabs(keep_two, send_two)
    (output,) = convolve(2, w_two, h_wide, h_a, h_b)
    return output.T, grad_one, grad_two


def solution(mesh):
    return jax.shard_map(
        local,
        mesh=mesh,
        in_specs=(
            P("space", "chan"),
            P("space", None, None, None),
            P(),
            P(None, "chan", None),
            P(None, "chan", None),
            P("space", "chan"),
        ),
        out_specs=(P("space", "chan"), P(None, "chan", "space"), P(None, "chan", "space")),
        check_vma=False,
    )
```

time: 144 us -> 104 us (0.72)
  Pallas kernels: 76.4 us -> 34.8 us
  waiting for transfers between devices: 13.1 us -> 31.9 us
  local copies, waits for them, and re-layouts: 14 us -> 4.47 us
  starting transfers between devices: 36.1 us -> 31.7 us
  other arithmetic: 2.59 us -> 0 us
    pallas_call x15 -> x13, Pallas kernels: 76.4 us -> 34.8 us  [call(): pl.pallas_call(body, out_shape=outs, in_specs=specs, out_specs=[VMEM] * l...]
    ppermute x16 -> x19, waiting for transfers between devices: 13.1 us -> 31.9 us  [swap(): lax.ppermute(value, axis, [(i, i ^ bits) for i in range(lax.axis_size(axi...]
    ppermute x6 -> x3, starting transfers between devices: 16.5 us -> 1.96 us  [swap_other(): return lax.ppermute(value, 'space', pairs + [(j, i) for i, j in pairs])]
    ppermute x16 -> x19, starting transfers between devices: 19.7 us -> 29.7 us  [swap(): lax.ppermute(value, axis, [(i, i ^ bits) for i in range(lax.axis_size(axi...]
    unnamed x44 -> x16, local copies, waits for them, and re-layouts: 9.88 us -> 4.47 us
  transfers between devices with their start and end apart: 22 -> 22, of which waited for: 4 -> 7; matrix products, arithmetic and copies ran while one was open for 5% -> 0% of each run, Pallas kernels for 52% -> 33%
where the time goes in v2:
time: 104 us
  Pallas kernels  34.8 us (33%)
  waiting for transfers between devices  31.9 us (31%)
  starting transfers between devices  31.7 us (30%)
  local copies, waits for them, and re-layouts  4.47 us (4%)
    pallas_call x13, Pallas kernels, call(): pl.pallas_call(body, out_shape=outs, in_specs=specs, out_specs=[VMEM] * l...  34.8 us
    ppermute x19, waiting for transfers between devices, swap(): lax.ppermute(value, axis, [(i, i ^ bits) for i in range(lax.axis_size(axi...  31.9 us
    ppermute x19, starting transfers between devices, swap(): lax.ppermute(value, axis, [(i, i ^ bits) for i in range(lax.axis_size(axi...  29.7 us
    unnamed x16, local copies, waits for them, and re-layouts  4.47 us
  transfers between devices with their start and end apart: 22, of which 7 were waited for; matrix products, arithmetic and copies ran while one was open for 0% of the time, Pallas kernels for 33%

profile of v2, /device:TPU:0, one launch (start us, length us, event | category | flops | bytes accessed | tf_op | source)
XLA Modules:
  0.0 103.7 jit_solution(11754305802998301009)
XLA Ops:
  0.6 3.0 %collective-permute-start.1 = (bf16[64,2048]{1,0:T(8,128)(2,1)}, bf16[64,2048]{1,0:T(8,128)(2,1)S(1)}, u32[]{:S(2)}, u32[]{:S(2)}) collective-permute-start(bf16[64,2048]{1,0:T(8,128)(2,1)} %bitcast.10), channel_id=1, source_target_pairs={{0,2},{1,3},{2,0},{3,1},{4,6},{5,7},{6,4},{7,5},{8,10},{9,11},{10,... | collective-permute-start | bytes 786440 | tf_op jit(solution)/shard_map/ppermute | solution.py:252
  3.6 0.0 collective-permute-start
  3.6 6.5 %collective-permute-done.1.refs_2_ = bf16[64,2048]{1,0:T(8,128)(2,1)S(1)} collective-permute-done((bf16[64,2048]{1,0:T(8,128)(2,1)}, bf16[64,2048]{1,0:T(8,128)(2,1)S(1)}, u32[]{:S(2)}, u32[]{:S(2)}) %collective-permute-start.1) | collective-permute-done | bytes 262176 | tf_op jit(solution)/shard_map/ppermute | solution.py:252
  10.2 0.0 collective-permute-start.2
  10.2 0.7 copy-done.1
  10.8 1.2 %copy-done.4 = bf16[27,64,256]{2,1,0:T(8,128)(2,1)S(1)} copy-done((bf16[27,64,256]{2,1,0:T(8,128)(2,1)S(1)}, bf16[27,64,256]{2,1,0:T(8,128)(2,1)}, u32[]{:S(2)}) %copy-start.4) | copy-done | bytes 884760
  12.0 0.9 copy-done.6
  12.9 0.7 copy-done.7
  13.7 7.4 %shard_map.85 = (s32[16,27]{1,0:T(8,128)S(1)}, bf16[1728,2560]{1,0:T(8,128)(2,1)S(1)}, bf16[2,64,2560]{2,1,0:T(8,128)(2,1)S(1)}, bf16[2,64,2560]{2,1,0:T(8,128)(2,1)S(1)}) custom-call(s32[8]{0:T(128)S(1)} %copy-done.1, s32[3,16,27]{2,1,0:T(8,128)S(1)} %bitcast.17, bf16[64,2048]{1,0:T(8,128)(2,1)S(1)} %bitcast.16, bf16[1728,256]{1,0:T(8,128)(2,1)S(1)} %bitcast.14), custom_call_target="tpu_custom_call" | custom-call | flops 2264924160 | bytes 16777216 | tf_op jit(solution)/shard_map/pallas_call | solution.py:27
  21.1 0.6 collective-permute-start.10
  21.6 0.0 collective-permute-done.refs_1_
  21.6 0.0 collective-permute-done.2.refs_3_
  21.6 0.9 copy-done
  22.6 0.7 shard_map.86
  23.3 1.8 %collective-permute-start.3 = (bf16[256,256]{1,0:T(8,128)(2,1)S(1)}, bf16[256,256]{1,0:T(8,128)(2,1)S(1)}, u32[]{:S(2)}, u32[]{:S(2)}) collective-permute-start(bf16[256,256]{1,0:T(8,128)(2,1)S(1)} %get-tuple-element.34), channel_id=1, source_target_pairs={{0,4},{4,0},{8,12},{12,8},{16,20},{20,16},{24,28},{28,24},{1,5},{5... | collective-permute-start | bytes 393224 | tf_op jit(solution)/shard_map/ppermute | solution.py:252
  25.1 0.7 collective-permute-start.4
  25.7 3.0 %collective-permute-done.3.a_ref = bf16[256,256]{1,0:T(8,128)(2,1)S(1)} collective-permute-done((bf16[256,256]{1,0:T(8,128)(2,1)S(1)}, bf16[256,256]{1,0:T(8,128)(2,1)S(1)}, u32[]{:S(2)}, u32[]{:S(2)}) %collective-permute-start.3) | collective-permute-done | bytes 131104 | tf_op jit(solution)/shard_map/ppermute | solution.py:252
  28.8 6.6 %shard_map.87 = (f32[64,2048]{1,0:T(8,128)S(1)}, bf16[64,2048]{1,0:T(8,128)(2,1)S(1)}) custom-call(s32[16,27]{1,0:T(8,128)S(1)} %get-tuple-element.32.tab, bf16[1728,256]{1,0:T(8,128)(2,1)S(1)} %bitcast.13, bf16[256,2048]{1,0:T(8,128)(2,1)S(1)} %get-tuple-element.33.wide_ref, bf16[256,256]{1,0:T(8,128)(2,1)S(1)} %collective-permute-done.3.a_ref, ...), custom_call_target="tpu_custom_call" | custom-call | flops 2264924160 | bytes 16777216 | tf_op jit(solution)/shard_map/pallas_call | solution.py:27
  35.4 1.7 %collective-permute-start.6 = (bf16[64,2048]{1,0:T(8,128)(2,1)S(1)}, bf16[64,2048]{1,0:T(8,128)(2,1)S(1)}, u32[]{:S(2)}, u32[]{:S(2)}) collective-permute-start(bf16[64,2048]{1,0:T(8,128)(2,1)S(1)} %get-tuple-element.36.refs_0_), channel_id=1, source_target_pairs={{0,2},{1,3},{2,0},{3,1},{4,6},{5,7},{6,4},{7,5},{8,10},{9,11},{10,... | collective-permute-start | bytes 786440 | tf_op jit(solution)/shard_map/ppermute | solution.py:252
  37.2 0.1 shard_map.90
  37.3 0.4 collective-permute-start.11
  37.7 7.0 %collective-permute-done.6.refs_2_ = bf16[64,2048]{1,0:T(8,128)(2,1)S(1)} collective-permute-done((bf16[64,2048]{1,0:T(8,128)(2,1)S(1)}, bf16[64,2048]{1,0:T(8,128)(2,1)S(1)}, u32[]{:S(2)}, u32[]{:S(2)}) %collective-permute-start.6) | collective-permute-done | bytes 262176 | tf_op jit(solution)/shard_map/ppermute | solution.py:252
  44.7 5.2 %collective-permute-done.11.refs_0_ = bf16[64,2560]{1,0:T(8,128)(2,1)S(1)} collective-permute-done((bf16[64,2560]{1,0:T(8,128)(2,1)S(1)}, bf16[64,2560]{1,0:T(8,128)(2,1)S(1)}, u32[]{:S(2)}, u32[]{:S(2)}) %collective-permute-start.11) | collective-permute-done | bytes 327712 | tf_op jit(solution)/shard_map/ppermute | solution.py:252
  49.9 0.1 shard_map.91
  50.0 4.5 %collective-permute-start.12 = (bf16[64,256]{1,0:T(8,128)(2,1)S(1)}, bf16[64,256]{1,0:T(8,128)(2,1)S(1)}, u32[]{:S(2)}, u32[]{:S(2)}) collective-permute-start(bf16[64,256]{1,0:T(8,128)(2,1)S(1)} %get-tuple-element.46), channel_id=1, source_target_pairs={{0,4},{4,0},{8,12},{12,8},{16,20},{20,16},{24,28},{28,24},{1,5},{5... | collective-permute-start | bytes 98312 | tf_op jit(solution)/shard_map/ppermute | solution.py:252
  54.5 0.7 collective-permute-start.13
  55.2 0.7 shard_map.88
  55.9 4.3 %collective-permute-start.8 = (bf16[256,256]{1,0:T(8,128)(2,1)S(1)}, bf16[256,256]{1,0:T(8,128)(2,1)S(1)}, u32[]{:S(2)}, u32[]{:S(2)}) collective-permute-start(bf16[256,256]{1,0:T(8,128)(2,1)S(1)} %get-tuple-element.38), channel_id=1, source_target_pairs={{0,4},{4,0},{8,12},{12,8},{16,20},{20,16},{24,28},{28,24},{1,5},{5... | collective-permute-start | bytes 393224 | tf_op jit(solution)/shard_map/ppermute | solution.py:252
  60.2 0.7 collective-permute-start.9
  60.8 0.0 copy-start.5
  60.9 6.8 %shard_map.92 = (f32[4,32,1728]{2,1,0:T(8,128)S(1)}, bf16[4,32,1728]{2,1,0:T(8,128)(2,1)S(1)}) custom-call(s32[8]{0:T(128)S(1)} %copy-done.2, s32[16,27]{1,0:T(8,128)S(1)} %get-tuple-element.32.tab, f32[64,2048]{1,0:T(8,128)S(1)} %get-tuple-element.40.z_ref, f32[64,2048]{1,0:T(8,128)S(1)} %get-tuple-element.45.inner_ref, ...), custom_call_target="tpu_custom_call" | custom-call | flops 2264924160 | bytes 16777216 | tf_op jit(solution)/shard_map/pallas_call | solution.py:27
  67.7 4.3 %collective-permute-start.14 = (bf16[4,32,1728]{2,1,0:T(8,128)(2,1)S(1)}, bf16[4,32,1728]{2,1,0:T(8,128)(2,1)S(1)}, u32[]{:S(2)}, u32[]{:S(2)}) collective-permute-start(bf16[4,32,1728]{2,1,0:T(8,128)(2,1)S(1)} %get-tuple-element.49), channel_id=1, source_target_pairs={{0,4},{4,0},{8,12},{12,8},{16,20},{20,16},{24,28},{28,24},{1,5},{5... | collective-permute-start | bytes 1327112 | tf_op jit(solution)/shard_map/ppermute | solution.py:252
  72.0 3.3 %shard_map.95 = (f32[4,32,1728]{2,1,0:T(8,128)S(1)}, bf16[4,32,1728]{2,1,0:T(8,128)(2,1)S(1)}) custom-call(bf16[256,2048]{1,0:T(8,128)(2,1)S(1)} %get-tuple-element.37.wide_ref, bf16[256,256]{1,0:T(8,128)(2,1)S(1)} %collective-permute-done.8.a_ref, bf16[256,256]{1,0:T(8,128)(2,1)S(1)} %collective-permute-done.9.b_ref, ...), custom_call_target="tpu_custom_call" | custom-call | flops 2264924160 | bytes 8388608 | tf_op jit(solution)/shard_map/pallas_call | solution.py:27
  75.3 0.1 collective-permute-start.18
  75.4 8.1 %collective-permute-done.14.got_ref = bf16[4,32,1728]{2,1,0:T(8,128)(2,1)S(1)} collective-permute-done((bf16[4,32,1728]{2,1,0:T(8,128)(2,1)S(1)}, bf16[4,32,1728]{2,1,0:T(8,128)(2,1)S(1)}, u32[]{:S(2)}, u32[]{:S(2)}) %collective-permute-start.14) | collective-permute-done | bytes 442400 | tf_op jit(solution)/shard_map/ppermute | solution.py:252
  83.4 0.1 shard_map.93
  83.6 1.2 %collective-permute-start.15 = (bf16[32,1728]{1,0:T(8,128)(2,1)S(1)}, bf16[32,1728]{1,0:T(8,128)(2,1)S(1)}, u32[]{:S(2)}, u32[]{:S(2)}) collective-permute-start(bf16[32,1728]{1,0:T(8,128)(2,1)S(1)} %get-tuple-element.51), channel_id=1, source_target_pairs={{0,8},{4,12},{8,0},{12,4},{16,24},{20,28},{24,16},{28,20},{1,9},{5... | collective-permute-start | bytes 331784 | tf_op jit(solution)/shard_map/ppermute | solution.py:252
  84.7 2.3 %collective-permute-start.16 = (bf16[32,1728]{1,0:T(8,128)(2,1)S(1)}, bf16[32,1728]{1,0:T(8,128)(2,1)S(1)}, u32[]{:S(2)}, u32[]{:S(2)}) collective-permute-start(bf16[32,1728]{1,0:T(8,128)(2,1)S(1)} %get-tuple-element.52), channel_id=1, source_target_pairs={{0,16},{4,20},{8,24},{12,28},{16,0},{20,4},{24,8},{28,12},{1,17},{... | collective-permute-start | bytes 331784 | tf_op jit(solution)/shard_map/ppermute | solution.py:252
  87.1 0.9 collective-permute-start.17
  88.0 1.3 %collective-permute-done.18.got_ref = bf16[4,32,1728]{2,1,0:T(8,128)(2,1)S(1)} collective-permute-done((bf16[4,32,1728]{2,1,0:T(8,128)(2,1)S(1)}, bf16[4,32,1728]{2,1,0:T(8,128)(2,1)S(1)}, u32[]{:S(2)}, u32[]{:S(2)}) %collective-permute-start.18) | collective-permute-done | bytes 442400 | tf_op jit(solution)/shard_map/ppermute | solution.py:252
  89.3 0.1 shard_map.96
  89.4 1.5 %collective-permute-start.19 = (bf16[32,1728]{1,0:T(8,128)(2,1)S(1)}, bf16[32,1728]{1,0:T(8,128)(2,1)S(1)}, u32[]{:S(2)}, u32[]{:S(2)}) collective-permute-start(bf16[32,1728]{1,0:T(8,128)(2,1)S(1)} %get-tuple-element.58), channel_id=1, source_target_pairs={{0,8},{4,12},{8,0},{12,4},{16,24},{20,28},{24,16},{28,20},{1,9},{5... | collective-permute-start | bytes 331784 | tf_op jit(solution)/shard_map/ppermute | solution.py:252
  90.9 1.8 %collective-permute-start.20 = (bf16[32,1728]{1,0:T(8,128)(2,1)S(1)}, bf16[32,1728]{1,0:T(8,128)(2,1)S(1)}, u32[]{:S(2)}, u32[]{:S(2)}) collective-permute-start(bf16[32,1728]{1,0:T(8,128)(2,1)S(1)} %get-tuple-element.59), channel_id=1, source_target_pairs={{0,16},{4,20},{8,24},{12,28},{16,0},{20,4},{24,8},{28,12},{1,17},{... | collective-permute-start | bytes 331784 | tf_op jit(solution)/shard_map/ppermute | solution.py:252
  92.7 1.2 %collective-permute-start.21 = (bf16[32,1728]{1,0:T(8,128)(2,1)S(1)}, bf16[32,1728]{1,0:T(8,128)(2,1)S(1)}, u32[]{:S(2)}, u32[]{:S(2)}) collective-permute-start(bf16[32,1728]{1,0:T(8,128)(2,1)S(1)} %get-tuple-element.60), channel_id=1, source_target_pairs={{0,24},{4,28},{8,16},{12,20},{16,8},{20,12},{24,0},{28,4},{1,25},{... | collective-permute-start | bytes 331784 | tf_op jit(solution)/shard_map/ppermute | solution.py:252
  93.9 7.2 %shard_map.89 = bf16[64,2048]{1,0:T(8,128)(2,1)} custom-call(s32[16,27]{1,0:T(8,128)S(1)} %get-tuple-element.32.tab, bf16[1728,256]{1,0:T(8,128)(2,1)S(1)} %bitcast.15, bf16[256,2048]{1,0:T(8,128)(2,1)S(1)} %get-tuple-element.37.wide_ref, bf16[256,256]{1,0:T(8,128)(2,1)S(1)} %collective-permute-done.8.a_ref, bf16[256,256]{1,0:T(8,128)(2,1)S(1)} %collective-permute-done.9.b_ref), custom_call_target="tpu_custom_call" | custom-call | flops 2264924160 | bytes 16777216 | tf_op jit(solution)/shard_map/pallas_call | solution.py:27
  101.1 0.9 shard_map.94
  102.0 0.8 collective-permute-done.20.refs_1_
  102.8 0.9 shard_map.97
  (25 shorter events, 0.1 us)
Async XLA Ops:
  0.6 9.5 %collective-permute-start.1 = (bf16[64,2048]{1,0:T(8,128)(2,1)}, bf16[64,2048]{1,0:T(8,128)(2,1)S(1)}, u32[]{:S(2)}, u32[]{:S(2)}) collective-permute-start(bf16[64,2048]{1,0:T(8,128)(2,1)} %bitcast.10), channel_id=1, source_target_pairs={{0,2},{1,3},{2,0},{3,1},{4,6},{5,7},{6,4},{7,5},{8,10},{9,11},{10,... | collective-permute-start | bytes 786440 | tf_op jit(solution)/shard_map/ppermute | solution.py:252
  3.6 18.0 %collective-permute-start = (bf16[64,2048]{1,0:T(8,128)(2,1)}, bf16[64,2048]{1,0:T(8,128)(2,1)S(1)}, u32[]{:S(2)}, u32[]{:S(2)}) collective-permute-start(bf16[64,2048]{1,0:T(8,128)(2,1)} %bitcast.11), channel_id=1, source_target_pairs={{0,1},{1,0},{2,3},{3,2},{4,5},{5,4},{6,7},{7,6},{8,9},{9,8},{10,11... | collective-permute-start | bytes 786440 | tf_op jit(solution)/shard_map/ppermute | solution.py:252
  10.2 11.5 %collective-permute-start.2 = (bf16[64,2048]{1,0:T(8,128)(2,1)S(1)}, bf16[64,2048]{1,0:T(8,128)(2,1)S(1)}, u32[]{:S(2)}, u32[]{:S(2)}) collective-permute-start(bf16[64,2048]{1,0:T(8,128)(2,1)S(1)} %collective-permute-done.1.refs_2_), channel_id=1, source_target_pairs={{0,1},{1,0},{2,3},{3,2},{4,5},{5,4},{6,7},{7,6},{8,9},{9,8},{10,11... | collective-permute-start | bytes 786440 | tf_op jit(solution)/shard_map/ppermute | solution.py:252
  10.2 0.7 copy-start.1
  10.8 1.2 %copy-start.4 = (bf16[27,64,256]{2,1,0:T(8,128)(2,1)S(1)}, bf16[27,64,256]{2,1,0:T(8,128)(2,1)}, u32[]{:S(2)}) copy-start(bf16[27,64,256]{2,1,0:T(8,128)(2,1)} %param.10) | copy-start | bytes 2654212
  12.0 0.9 copy-start.6
  12.9 0.7 copy-start.7
  13.7 15.1 %copy-start.3 = (bf16[27,64,256]{2,1,0:T(8,128)(2,1)S(1)}, bf16[27,64,256]{2,1,0:T(8,128)(2,1)}, u32[]{:S(2)}) copy-start(bf16[27,64,256]{2,1,0:T(8,128)(2,1)} %param.9) | copy-start | bytes 2654212
  13.7 41.5 %copy-start.2 = (s32[8]{0:T(128)S(1)}, s32[8]{0:T(128)}, u32[]{:S(2)}) copy-start(s32[8]{0:T(128)} %counts.7) | copy-start | bytes 100
  21.1 16.1 %collective-permute-start.10 = (bf16[2,64,2560]{2,1,0:T(8,128)(2,1)S(1)}, bf16[2,64,2560]{2,1,0:T(8,128)(2,1)S(1)}, u32[]{:S(2)}, u32[]{:S(2)}) collective-permute-start(bf16[2,64,2560]{2,1,0:T(8,128)(2,1)S(1)} %get-tuple-element.42), channel_id=1, source_target_pairs={{0,1},{1,0},{2,3},{3,2},{4,5},{5,4},{6,7},{7,6},{8,9},{9,8},{10,11... | collective-permute-start | bytes 1966088 | tf_op jit(solution)/shard_map/ppermute | solution.py:252
  21.6 1.0 copy-start
  23.3 5.5 %collective-permute-start.3 = (bf16[256,256]{1,0:T(8,128)(2,1)S(1)}, bf16[256,256]{1,0:T(8,128)(2,1)S(1)}, u32[]{:S(2)}, u32[]{:S(2)}) collective-permute-start(bf16[256,256]{1,0:T(8,128)(2,1)S(1)} %get-tuple-element.34), channel_id=1, source_target_pairs={{0,4},{4,0},{8,12},{12,8},{16,20},{20,16},{24,28},{28,24},{1,5},{5... | collective-permute-start | bytes 393224 | tf_op jit(solution)/shard_map/ppermute | solution.py:252
  25.1 3.7 %collective-permute-start.4 = (bf16[256,256]{1,0:T(8,128)(2,1)S(1)}, bf16[256,256]{1,0:T(8,128)(2,1)S(1)}, u32[]{:S(2)}, u32[]{:S(2)}) collective-permute-start(bf16[256,256]{1,0:T(8,128)(2,1)S(1)} %get-tuple-element.35), channel_id=1, source_target_pairs={{4,8},{12,16},{20,24},{8,4},{16,12},{24,20},{5,9},{13,17},{21,25},... | collective-permute-start | bytes 393224 | tf_op jit(solution)/shard_map/ppermute | solution.py:257
  35.4 9.3 %collective-permute-start.6 = (bf16[64,2048]{1,0:T(8,128)(2,1)S(1)}, bf16[64,2048]{1,0:T(8,128)(2,1)S(1)}, u32[]{:S(2)}, u32[]{:S(2)}) collective-permute-start(bf16[64,2048]{1,0:T(8,128)(2,1)S(1)} %get-tuple-element.36.refs_0_), channel_id=1, source_target_pairs={{0,2},{1,3},{2,0},{3,1},{4,6},{5,7},{6,4},{7,5},{8,10},{9,11},{10,... | collective-permute-start | bytes 786440 | tf_op jit(solution)/shard_map/ppermute | solution.py:252
  37.3 12.6 %collective-permute-start.11 = (bf16[64,2560]{1,0:T(8,128)(2,1)S(1)}, bf16[64,2560]{1,0:T(8,128)(2,1)S(1)}, u32[]{:S(2)}, u32[]{:S(2)}) collective-permute-start(bf16[64,2560]{1,0:T(8,128)(2,1)S(1)} %get-tuple-element.44), channel_id=1, source_target_pairs={{0,2},{1,3},{2,0},{3,1},{4,6},{5,7},{6,4},{7,5},{8,10},{9,11},{10,... | collective-permute-start | bytes 983048 | tf_op jit(solution)/shard_map/ppermute | solution.py:252
  37.7 17.5 %collective-permute-start.5 = (bf16[64,2048]{1,0:T(8,128)(2,1)S(1)}, bf16[64,2048]{1,0:T(8,128)(2,1)S(1)}, u32[]{:S(2)}, u32[]{:S(2)}) collective-permute-start(bf16[64,2048]{1,0:T(8,128)(2,1)S(1)} %get-tuple-element.36.refs_0_), channel_id=1, source_target_pairs={{0,1},{1,0},{2,3},{3,2},{4,5},{5,4},{6,7},{7,6},{8,9},{9,8},{10,11... | collective-permute-start | bytes 786440 | tf_op jit(solution)/shard_map/ppermute | solution.py:252
  44.7 10.5 %collective-permute-start.7 = (bf16[64,2048]{1,0:T(8,128)(2,1)S(1)}, bf16[64,2048]{1,0:T(8,128)(2,1)S(1)}, u32[]{:S(2)}, u32[]{:S(2)}) collective-permute-start(bf16[64,2048]{1,0:T(8,128)(2,1)S(1)} %collective-permute-done.6.refs_2_), channel_id=1, source_target_pairs={{0,1},{1,0},{2,3},{3,2},{4,5},{5,4},{6,7},{7,6},{8,9},{9,8},{10,11... | collective-permute-start | bytes 786440 | tf_op jit(solution)/shard_map/ppermute | solution.py:252
  50.0 10.8 %collective-permute-start.12 = (bf16[64,256]{1,0:T(8,128)(2,1)S(1)}, bf16[64,256]{1,0:T(8,128)(2,1)S(1)}, u32[]{:S(2)}, u32[]{:S(2)}) collective-permute-start(bf16[64,256]{1,0:T(8,128)(2,1)S(1)} %get-tuple-element.46), channel_id=1, source_target_pairs={{0,4},{4,0},{8,12},{12,8},{16,20},{20,16},{24,28},{28,24},{1,5},{5... | collective-permute-start | bytes 98312 | tf_op jit(solution)/shard_map/ppermute | solution.py:252
  54.5 6.3 %collective-permute-start.13 = (bf16[64,256]{1,0:T(8,128)(2,1)S(1)}, bf16[64,256]{1,0:T(8,128)(2,1)S(1)}, u32[]{:S(2)}, u32[]{:S(2)}) collective-permute-start(bf16[64,256]{1,0:T(8,128)(2,1)S(1)} %get-tuple-element.47), channel_id=1, source_target_pairs={{4,8},{12,16},{20,24},{8,4},{16,12},{24,20},{5,9},{13,17},{21,25},... | collective-permute-start | bytes 98312 | tf_op jit(solution)/shard_map/ppermute | solution.py:257
  55.9 16.1 %collective-permute-start.8 = (bf16[256,256]{1,0:T(8,128)(2,1)S(1)}, bf16[256,256]{1,0:T(8,128)(2,1)S(1)}, u32[]{:S(2)}, u32[]{:S(2)}) collective-permute-start(bf16[256,256]{1,0:T(8,128)(2,1)S(1)} %get-tuple-element.38), channel_id=1, source_target_pairs={{0,4},{4,0},{8,12},{12,8},{16,20},{20,16},{24,28},{28,24},{1,5},{5... | collective-permute-start | bytes 393224 | tf_op jit(solution)/shard_map/ppermute | solution.py:252
  60.2 11.8 %collective-permute-start.9 = (bf16[256,256]{1,0:T(8,128)(2,1)S(1)}, bf16[256,256]{1,0:T(8,128)(2,1)S(1)}, u32[]{:S(2)}, u32[]{:S(2)}) collective-permute-start(bf16[256,256]{1,0:T(8,128)(2,1)S(1)} %get-tuple-element.39), channel_id=1, source_target_pairs={{4,8},{12,16},{20,24},{8,4},{16,12},{24,20},{5,9},{13,17},{21,25},... | collective-permute-start | bytes 393224 | tf_op jit(solution)/shard_map/ppermute | solution.py:257
  60.8 33.0 %copy-start.5 = (bf16[27,64,256]{2,1,0:T(8,128)(2,1)S(1)}, bf16[27,64,256]{2,1,0:T(8,128)(2,1)}, u32[]{:S(2)}) copy-start(bf16[27,64,256]{2,1,0:T(8,128)(2,1)} %param.10) | copy-start | bytes 2654212
  67.7 15.8 %collective-permute-start.14 = (bf16[4,32,1728]{2,1,0:T(8,128)(2,1)S(1)}, bf16[4,32,1728]{2,1,0:T(8,128)(2,1)S(1)}, u32[]{:S(2)}, u32[]{:S(2)}) collective-permute-start(bf16[4,32,1728]{2,1,0:T(8,128)(2,1)S(1)} %get-tuple-element.49), channel_id=1, source_target_pairs={{0,4},{4,0},{8,12},{12,8},{16,20},{20,16},{24,28},{28,24},{1,5},{5... | collective-permute-start | bytes 1327112 | tf_op jit(solution)/shard_map/ppermute | solution.py:252
  75.3 14.0 %collective-permute-start.18 = (bf16[4,32,1728]{2,1,0:T(8,128)(2,1)S(1)}, bf16[4,32,1728]{2,1,0:T(8,128)(2,1)S(1)}, u32[]{:S(2)}, u32[]{:S(2)}) collective-permute-start(bf16[4,32,1728]{2,1,0:T(8,128)(2,1)S(1)} %get-tuple-element.56), channel_id=1, source_target_pairs={{0,4},{4,0},{8,12},{12,8},{16,20},{20,16},{24,28},{28,24},{1,5},{5... | collective-permute-start | bytes 1327112 | tf_op jit(solution)/shard_map/ppermute | solution.py:252
  83.6 9.1 %collective-permute-start.15 = (bf16[32,1728]{1,0:T(8,128)(2,1)S(1)}, bf16[32,1728]{1,0:T(8,128)(2,1)S(1)}, u32[]{:S(2)}, u32[]{:S(2)}) collective-permute-start(bf16[32,1728]{1,0:T(8,128)(2,1)S(1)} %get-tuple-element.51), channel_id=1, source_target_pairs={{0,8},{4,12},{8,0},{12,4},{16,24},{20,28},{24,16},{28,20},{1,9},{5... | collective-permute-start | bytes 331784 | tf_op jit(solution)/shard_map/ppermute | solution.py:252
  84.7 16.4 %collective-permute-start.16 = (bf16[32,1728]{1,0:T(8,128)(2,1)S(1)}, bf16[32,1728]{1,0:T(8,128)(2,1)S(1)}, u32[]{:S(2)}, u32[]{:S(2)}) collective-permute-start(bf16[32,1728]{1,0:T(8,128)(2,1)S(1)} %get-tuple-element.52), channel_id=1, source_target_pairs={{0,16},{4,20},{8,24},{12,28},{16,0},{20,4},{24,8},{28,12},{1,17},{... | collective-permute-start | bytes 331784 | tf_op jit(solution)/shard_map/ppermute | solution.py:252
  87.1 14.0 %collective-permute-start.17 = (bf16[32,1728]{1,0:T(8,128)(2,1)S(1)}, bf16[32,1728]{1,0:T(8,128)(2,1)S(1)}, u32[]{:S(2)}, u32[]{:S(2)}) collective-permute-start(bf16[32,1728]{1,0:T(8,128)(2,1)S(1)} %get-tuple-element.53), channel_id=1, source_target_pairs={{0,24},{4,28},{8,16},{12,20},{16,8},{20,12},{24,0},{28,4},{1,25},{... | collective-permute-start | bytes 331784 | tf_op jit(solution)/shard_map/ppermute | solution.py:252
  89.4 12.6 %collective-permute-start.19 = (bf16[32,1728]{1,0:T(8,128)(2,1)S(1)}, bf16[32,1728]{1,0:T(8,128)(2,1)S(1)}, u32[]{:S(2)}, u32[]{:S(2)}) collective-permute-start(bf16[32,1728]{1,0:T(8,128)(2,1)S(1)} %get-tuple-element.58), channel_id=1, source_target_pairs={{0,8},{4,12},{8,0},{12,4},{16,24},{20,28},{24,16},{28,20},{1,9},{5... | collective-permute-start | bytes 331784 | tf_op jit(solution)/shard_map/ppermute | solution.py:252
  90.9 11.9 %collective-permute-start.20 = (bf16[32,1728]{1,0:T(8,128)(2,1)S(1)}, bf16[32,1728]{1,0:T(8,128)(2,1)S(1)}, u32[]{:S(2)}, u32[]{:S(2)}) collective-permute-start(bf16[32,1728]{1,0:T(8,128)(2,1)S(1)} %get-tuple-element.59), channel_id=1, source_target_pairs={{0,16},{4,20},{8,24},{12,28},{16,0},{20,4},{24,8},{28,12},{1,17},{... | collective-permute-start | bytes 331784 | tf_op jit(solution)/shard_map/ppermute | solution.py:252
  92.7 10.1 %collective-permute-start.21 = (bf16[32,1728]{1,0:T(8,128)(2,1)S(1)}, bf16[32,1728]{1,0:T(8,128)(2,1)S(1)}, u32[]{:S(2)}, u32[]{:S(2)}) collective-permute-start(bf16[32,1728]{1,0:T(8,128)(2,1)S(1)} %get-tuple-element.60), channel_id=1, source_target_pairs={{0,24},{4,28},{8,16},{12,20},{16,8},{20,12},{24,0},{28,4},{1,25},{... | collective-permute-start | bytes 331784 | tf_op jit(solution)/shard_map/ppermute | solution.py:252

commit v3 on v2

--- a/solution.py
+++ b/solution.py
@@ -16,20 +16,30 @@
 
 VMEM = pl.BlockSpec(memory_space=pltpu.VMEM)
 SMEM = pl.BlockSpec(memory_space=pltpu.SMEM)
+FAR = pl.BlockSpec(memory_space=pltpu.HBM)
+PAD = 8
 
 
 def held(value):
     return pltpu.with_memory_space_constraint(value, pltpu.VMEM)
 
 
-def call(body, outs, ins, scratch=(), flops=0, traffic=0, vmem=40):
-    specs = [SMEM if a.dtype == jnp.int32 and a.ndim < 3 else VMEM for a in ins]
+def call(body, outs, ins, scratch=(), flops=0, traffic=0, vmem=6, specs=None, after=(), aliases=None):
+    specs = list(specs or [SMEM if a.dtype == jnp.int32 else VMEM for a in ins])
+    first, last = len(ins), len(ins) + len(after)
+    ins = list(ins) + [held(v) for v in after]
+    specs += [VMEM] * len(after)
+
+    def ordered(*refs):
+        body(*refs[:first], *refs[last:])
+
     return pl.pallas_call(
-        body,
+        ordered,
         out_shape=outs,
         in_specs=specs,
         out_specs=[VMEM] * len(outs),
         scratch_shapes=list(scratch),
+        input_output_aliases=aliases or {},
         compiler_params=pltpu.CompilerParams(vmem_limit_bytes=vmem << 20),
         cost_estimate=pl.CostEstimate(flops=flops, bytes_accessed=traffic, transcendentals=0),
     )(*ins)
@@ -51,11 +61,9 @@
     return code >> 6, code & 63
 
 
-def near_rim(counts):
-    shard = lax.axis_index("space")
-    tail = (counts[shard] - HB) * BLK
-    even = shard % 2 == 0
-    return pl.multiple_of(jnp.where(even, tail, 0), BLK), pl.multiple_of(jnp.where(even, 0, tail), BLK)
+def near_rim(tab):
+    row = tab.shape[0] - PAD
+    return pl.multiple_of(tab[row, 0], BLK), pl.multiple_of(tab[row, 1], BLK)
 
 
 def table(counts, map_ref, nblocks):
@@ -74,12 +82,14 @@
         row = code[e : e + 1]
         rank += ((row < code) | ((row == code) & (e < index))).astype(jnp.int32)
     rows = [jnp.sum(jnp.where(rank == e, code, 0), axis=0, keepdims=True) for e in range(entries)]
-    return jnp.concatenate(rows, axis=0)
+    tail = (own_count - HB) * BLK
+    spot = (lax.broadcasted_iota(jnp.int32, (PAD, code.shape[1]), 1) == 0) == even
+    return jnp.concatenate(rows + [jnp.where(spot, tail, 0)], axis=0)
 
 
 def spread(tab, blocks, spread_ref):
     depth = blocks.shape[1]
-    entries, offsets = tab.shape
+    entries, offsets = tab.shape[0] - PAD, tab.shape[1]
 
     def one(k, _):
         rows = pl.ds(pl.multiple_of(k * depth, depth), depth)
@@ -97,7 +107,7 @@
 
 def collect(tab, prod, sums):
     depth = sums[0].shape[1]
-    entries, offsets = tab.shape
+    entries, offsets = tab.shape[0] - PAD, tab.shape[1]
     for acc in sums:
         acc[...] = jnp.zeros_like(acc)
 
@@ -112,6 +122,13 @@
     lax.fori_loop(0, offsets, one, 0)
 
 
+def lay(ext_ref, order, refs):
+    depth = refs[0].shape[0]
+    for bits, ref in zip(order, refs):
+        place = lax.axis_index("chan") ^ bits
+        ext_ref[pl.ds(pl.multiple_of(place * depth, depth), depth), :] = ref[...]
+
+
 def extend(ext_ref, wide_ref, a_ref, b_ref):
     rows = wide_ref.shape[1]
     ext_ref[:, :rows] = wide_ref[...]
@@ -119,17 +136,29 @@
     ext_ref[:, rows + RIM :] = b_ref[...]
 
 
-def input_grad_body(counts, map_ref, cot_ref, w_ref, tab_ref, spread_ref, keep_ref, send_ref, blocks, part, tab, sem):
+def input_grad_body(
+    counts, map_hbm, cot_hbm, w_hbm, tab_ref, spread_ref, keep_ref, send_ref,
+    map_ref, cot_ref, w_ref, blocks, part, tab, sems, sem
+):
+    loads = [
+        pltpu.make_async_copy(src, dst, sems.at[i])
+        for i, (src, dst) in enumerate([(map_hbm, map_ref), (cot_hbm, cot_ref), (w_hbm, w_ref)])
+    ]
+    for load in loads:
+        load.start()
     depth, rows = cot_ref.shape
     nblocks = rows // BLK
+    loads[0].wait()
     tab_ref[...] = table(counts, map_ref, nblocks)
     copy = pltpu.make_async_copy(tab_ref, tab, sem)
     copy.start()
+    loads[1].wait()
     for b in range(nblocks):
         blocks[b] = cot_ref[:, b * BLK : (b + 1) * BLK].astype(F32)
     blocks[nblocks] = jnp.zeros_like(blocks[nblocks])
     copy.wait()
     spread(tab, blocks, spread_ref)
+    loads[2].wait()
 
     def product(start, width):
         cols = pl.ds(start, width)
@@ -143,39 +172,62 @@
         send_ref[j] = part[2 * j + 1 - core]
 
 
-def join_body(order, counts, *refs):
+def pass_body(value_ref, out_ref):
+    out_ref[...] = value_ref[...]
+
+
+def join_body(order, tab, *refs):
     pieces = len(order)
     wide_ref, a_ref, b_ref = refs[pieces:]
-    depth = refs[0].shape[0]
-    for bits, ref in zip(order, refs[:pieces]):
-        place = lax.axis_index("chan") ^ bits
-        wide_ref[pl.ds(pl.multiple_of(place * depth, depth), depth), :] = ref[...]
-    a, b = near_rim(counts)
+    lay(wide_ref, order, refs[:pieces])
+    a, b = near_rim(tab)
     a_ref[...] = wide_ref[:, pl.ds(a, RIM)]
     b_ref[...] = wide_ref[:, pl.ds(b, RIM)]
 
 
-def conv_body(layer, tab, w_ref, wide_ref, a_ref, b_ref, *refs):
-    count = 2 if layer == 1 else 1
-    outs, ext, prod, sums = refs[:count], refs[count], refs[count + 1], refs[count + 2 :]
-    extend(ext, wide_ref, a_ref, b_ref)
-
+def multiply(w_ref, value_ref, prod):
     def product(start, width):
         cols = pl.ds(start, width)
-        prod[:, cols] = jnp.dot(w_ref[...], ext[:, cols], preferred_element_type=F32)
-
-    chunks(ext.shape[1], 2 * STEP, product)
+        prod[:, cols] = jnp.dot(w_ref[...], value_ref[:, cols], preferred_element_type=F32)
+
+    chunks(value_ref.shape[1], 2 * STEP, product)
+
+
+def gather_sums(tab, prod, sums, store):
     collect(tab, prod, sums)
     for b in range(sums[0].shape[0] - 1):
-        z = sums[0][b]
+        total = sums[0][b]
         for acc in sums[1:]:
-            z = z + acc[b]
-        cols = slice(b * BLK, (b + 1) * BLK)
-        if layer == 1:
-            outs[0][:, cols] = z
-            outs[1][:, cols] = (z / (1.0 + jnp.exp(-z))).astype(BF16)
-        else:
-            outs[0][:, cols] = z.astype(BF16)
+            total = total + acc[b]
+        store(slice(b * BLK, (b + 1) * BLK), total)
+
+
+def inner_body(w_ref, wide_ref, prod_ref):
+    multiply(w_ref, wide_ref, prod_ref)
+
+
+def hidden_body(tab, w_ref, a_ref, b_ref, _, z_ref, hidden_ref, prod, *sums):
+    rows = z_ref.shape[1]
+    prod[:, rows : rows + RIM] = jnp.dot(w_ref[...], a_ref[...], preferred_element_type=F32)
+    prod[:, rows + RIM :] = jnp.dot(w_ref[...], b_ref[...], preferred_element_type=F32)
+
+    def store(cols, z):
+        z_ref[:, cols] = z
+        hidden_ref[:, cols] = (z / (1.0 + jnp.exp(-z))).astype(BF16)
+
+    gather_sums(tab, prod, sums, store)
+
+
+def output_body(order, tab, w_ref, *refs):
+    pieces = len(order)
+    out_ref, ext, prod, *sums = refs[pieces:]
+    lay(ext, order, refs[:pieces])
+
+    def store(cols, total):
+        out_ref[:, cols] = total.astype(BF16)
+
+    multiply(w_ref, ext, prod)
+    gather_sums(tab, prod, sums, store)
 
 
 def halve_body(axis, keep_ref, got_ref, mine_ref, *send_refs):
@@ -186,15 +238,32 @@
         ref[...] = (keep_ref[other].astype(F32) + got_ref[other].astype(F32)).astype(BF16)
 
 
-def rims_body(count, mine_ref, *refs):
+def turn_body(count, tab, hidden_ref, mine_ref, *refs):
     gots, (inner_ref, a_ref, b_ref) = refs[:count], refs[count:]
     total = mine_ref[...]
     for ref in gots:
         total = total + ref[...].astype(F32)
     rows = inner_ref.shape[1]
     inner_ref[...] = total[:, :rows]
-    a_ref[...] = total[:, rows : rows + RIM].astype(BF16)
-    b_ref[...] = total[:, rows + RIM :].astype(BF16)
+    a, b = near_rim(tab)
+    a_ref[0] = total[:, rows : rows + RIM].astype(BF16)
+    a_ref[1] = hidden_ref[:, pl.ds(a, RIM)]
+    b_ref[0] = total[:, rows + RIM :].astype(BF16)
+    b_ref[1] = hidden_ref[:, pl.ds(b, RIM)]
+
+
+def pack_body(hidden_ref, a_ref, b_ref, rim_ref, full_ref):
+    rows = hidden_ref.shape[1]
+    rim_ref[:, :RIM] = a_ref[1]
+    rim_ref[:, RIM:] = b_ref[1]
+    full_ref[:, :rows] = hidden_ref[...]
+    full_ref[:, rows:] = rim_ref[...]
+
+
+def append_body(wide_ref, rim_ref, full_ref):
+    rows = wide_ref.shape[1]
+    full_ref[:, :rows] = wide_ref[...]
+    full_ref[:, rows:] = rim_ref[...]
 
 
 def weight_grad(ext, spread_ref, total, keep_ref, send_ref):
@@ -212,20 +281,22 @@
         send_ref[j] = total[2 * j + 1 - parity].astype(BF16)
 
 
-def grad_two_body(wide_ref, a_ref, b_ref, spread_ref, keep_ref, send_ref, ext, total):
-    extend(ext, wide_ref, a_ref, b_ref)
+def grad_two_body(order, spread_ref, *refs):
+    pieces = len(order)
+    keep_ref, send_ref, ext, total = refs[pieces:]
+    lay(ext, order, refs[:pieces])
     weight_grad(ext, spread_ref, total, keep_ref, send_ref)
 
 
 def grad_one_body(
-    counts, tab, z_ref, inner_ref, from_a, from_b, wide_ref, a_ref, b_ref,
+    tab, z_ref, inner_ref, from_a, from_b, wide_ref, a_ref, b_ref,
     keep_ref, send_ref, grads, blocks, spread_ref, ext, total
 ):
     extend(ext, wide_ref, a_ref, b_ref)
     grads[...] = inner_ref[...]
-    a, b = near_rim(counts)
+    a, b = near_rim(tab)
     for start, ref in ((a, from_a), (b, from_b)):
-        grads[:, pl.ds(start, RIM)] = grads[:, pl.ds(start, RIM)] + ref[...].astype(F32)
+        grads[:, pl.ds(start, RIM)] = grads[:, pl.ds(start, RIM)] + ref[0].astype(F32)
     nblocks = blocks.shape[0] - 1
     for i in range(nblocks):
         cols = slice(i * BLK, (i + 1) * BLK)
@@ -271,30 +342,6 @@
     work = 2 * flat * wide * reach
     blocks = pltpu.VMEM((nblocks + 1, depth, BLK), F32)
     ext = pltpu.VMEM((wide, reach), BF16)
-
-    def gather(shard_t):
-        far = [swap(shard_t, "chan", 2 * j) for j in range(1, pairs)]
-        pieces = [shard_t, swap(shard_t, "chan", 1)]
-        for got in far:
-            pieces += [got, swap(got, "chan", 1)]
-        joined, a, b = call(
-            functools.partial(join_body, order),
-            [pltpu.VMEM((wide, rows), BF16), pltpu.VMEM((wide, RIM), BF16), pltpu.VMEM((wide, RIM), BF16)],
-            [block_count] + [held(v) for v in pieces],
-            traffic=2 << 20,
-        )
-        return joined, swap(a, "space", 1), swap_other(b)
-
-    def convolve(layer, weights, joined, a, b):
-        out = pltpu.VMEM((depth, rows), BF16)
-        return call(
-            functools.partial(conv_body, layer),
-            [pltpu.VMEM((depth, rows), F32), out] if layer == 1 else [jax.ShapeDtypeStruct((depth, rows), BF16)],
-            [tab, weights, held(joined), held(a), held(b)],
-            [ext, pltpu.VMEM((flat, reach), F32)] + [blocks] * 2,
-            flops=work,
-            traffic=16 << 20,
-        )
 
     def reduce_slabs(keep, send):
         got = swap(send, "space", 1)
@@ -316,68 +363,130 @@
     w_one = weight_one.reshape(flat, wide)
     w_two = weight_two.reshape(flat, wide)
 
-    x_wide, x_a, x_b = gather(features.T)
-
+    shard_t = features.T
+    far = [swap(shard_t, "chan", 2 * j) for j in range(1, pairs)]
+    cot = cotangent.T
     tab, spread_two, keep, send = call(
         input_grad_body,
         [
-            jax.ShapeDtypeStruct((entries, offsets), jnp.int32),
+            pltpu.VMEM((entries + PAD, offsets), jnp.int32),
             pltpu.VMEM((flat, reach), BF16),
             pltpu.VMEM((pairs, depth, reach), BF16),
             pltpu.VMEM((pairs, depth, reach), BF16),
         ],
-        [block_count, kernel_map[0].transpose(2, 1, 0), cotangent.T, w_two],
+        [pltpu.with_memory_space_constraint(v, pltpu.HBM) for v in (block_count, kernel_map[0].transpose(2, 1, 0), cot, w_two)],
         [
+            pltpu.VMEM((3, entries, offsets), jnp.int32),
+            pltpu.VMEM(cot.shape, BF16),
+            pltpu.VMEM(w_two.shape, BF16),
             blocks,
             pltpu.VMEM((parts, depth, reach), BF16),
-            pltpu.SMEM((entries, offsets), jnp.int32),
+            pltpu.SMEM((entries + PAD, offsets), jnp.int32),
+            pltpu.SemaphoreType.DMA((3,)),
             pltpu.SemaphoreType.DMA,
         ],
+        vmem=16,
         flops=work,
         traffic=16 << 20,
-    )
+        specs=[SMEM, FAR, FAR, FAR],
+    )
+    pieces = [shard_t, swap(shard_t, "chan", 1)]
+    for got in far:
+        (got,) = call(pass_body, [pltpu.VMEM(got.shape, BF16)], [held(got)], after=[send])
+        pieces += [got, swap(got, "chan", 1)]
+    x_wide, rim_a, rim_b = call(
+        functools.partial(join_body, order),
+        [pltpu.VMEM((wide, rows), BF16), pltpu.VMEM((wide, RIM), BF16), pltpu.VMEM((wide, RIM), BF16)],
+        [tab] + [held(v) for v in pieces],
+        flops=8 * work,
+        traffic=2 << 20,
+    )
+    x_a, x_b = swap(rim_a, "space", 1), swap_other(rim_b)
     got = swap(send, "chan", 1)
     mine, *sends = call(
         functools.partial(halve_body, "chan"),
         [pltpu.VMEM((depth, reach), F32)] + [pltpu.VMEM((depth, reach), BF16)] * (pairs - 1),
         [held(keep), held(got)],
         traffic=2 << 20,
+        after=[rim_a],
     )
     gots = [swap(v, "chan", 2 * (j + 1)) for j, v in enumerate(sends)]
 
-    z_one, hidden = convolve(1, w_one, x_wide, x_a, x_b)
-    h_wide, h_a, h_b = gather(hidden)
-
+    conv_scratch = [ext, pltpu.VMEM((flat, reach), F32)] + [blocks] * 2
+    (prod_one,) = call(
+        inner_body,
+        [pltpu.VMEM((flat, reach), F32)],
+        [w_one, held(x_wide)],
+        vmem=10,
+        flops=work,
+        traffic=16 << 20,
+        after=[mine],
+    )
+    z_one, hidden, _ = call(
+        hidden_body,
+        [pltpu.VMEM((depth, rows), F32), pltpu.VMEM((depth, rows), BF16), pltpu.VMEM((flat, reach), F32)],
+        [tab, w_one] + [held(v) for v in (x_a, x_b, prod_one)],
+        [blocks] * 2,
+        vmem=12,
+        flops=work,
+        traffic=16 << 20,
+        aliases={4: 2},
+    )
+    far = [swap(hidden, "chan", 2 * j) for j in range(1, pairs)]
     inner, to_a, to_b = call(
-        functools.partial(rims_body, len(gots)),
-        [pltpu.VMEM((depth, rows), F32), pltpu.VMEM((depth, RIM), BF16), pltpu.VMEM((depth, RIM), BF16)],
-        [held(v) for v in [mine] + gots],
+        functools.partial(turn_body, len(gots)),
+        [pltpu.VMEM((depth, rows), F32), pltpu.VMEM((2, depth, RIM), BF16), pltpu.VMEM((2, depth, RIM), BF16)],
+        [tab] + [held(v) for v in [hidden, mine] + gots],
         traffic=2 << 20,
     )
     from_a, from_b = swap(to_a, "space", 1), swap_other(to_b)
+    rim, full = call(
+        pack_body,
+        [pltpu.VMEM((depth, 2 * RIM), BF16), pltpu.VMEM((depth, reach), BF16)],
+        [held(v) for v in (hidden, from_a, from_b)],
+        traffic=1 << 20,
+    )
+    far_rims = [swap(rim, "chan", 2 * j) for j in range(1, pairs)]
+    full_other = swap(full, "chan", 1)
 
     grad_outs = [pltpu.VMEM((slabs // 2, share, flat), F32), pltpu.VMEM((slabs // 2, share, flat), BF16)]
     total_scratch = pltpu.VMEM((slabs, share, flat), F32)
     keep_one, send_one = call(
         grad_one_body,
         grad_outs,
-        [block_count, tab] + [held(v) for v in (z_one, inner, from_a, from_b, x_wide, x_a, x_b)],
+        [tab] + [held(v) for v in (z_one, inner, from_a, from_b, x_wide, x_a, x_b)],
         [pltpu.VMEM((depth, rows), F32), blocks, pltpu.VMEM((flat, reach), BF16), ext, total_scratch],
+        vmem=26,
         flops=work,
         traffic=16 << 20,
     )
     grad_one = reduce_slabs(keep_one, send_one)
 
+    pieces = [full, full_other]
+    for got, got_rim in zip(far, far_rims):
+        (got,) = call(
+            append_body, [pltpu.VMEM((depth, reach), BF16)], [held(got), held(got_rim)], traffic=1 << 20, after=[keep_one]
+        )
+        pieces += [got, swap(got, "chan", 1)]
     keep_two, send_two = call(
-        grad_two_body,
+        functools.partial(grad_two_body, order),
         grad_outs,
-        [held(v) for v in (h_wide, h_a, h_b, spread_two)],
+        [held(v) for v in [spread_two] + pieces],
         [ext, total_scratch],
+        vmem=14,
         flops=work,
         traffic=8 << 20,
     )
     grad_two = reduce_slabs(keep_two, send_two)
-    (output,) = convolve(2, w_two, h_wide, h_a, h_b)
+    (output,) = call(
+        functools.partial(output_body, order),
+        [jax.ShapeDtypeStruct((depth, rows), BF16)],
+        [tab, w_two] + [held(v) for v in pieces],
+        conv_scratch,
+        vmem=34,
+        flops=work,
+        traffic=16 << 20,
+    )
     return output.T, grad_one, grad_two
 
 

time: 104 us -> 84.8 us (0.82)
  waiting for transfers between devices: 31.9 us -> 14.9 us
  local copies, waits for them, and re-layouts: 4.47 us -> 0.96 us
  Pallas kernels: 34.8 us -> 36.2 us
    ppermute x19, waiting for transfers between devices: 31.9 us -> 14.9 us  [swap(): lax.ppermute(value, axis, [(i, i ^ bits) for i in range(lax.axis_size(axi...]
    unnamed x16 -> x6, local copies, waits for them, and re-layouts: 4.47 us -> 0.96 us
    pallas_call x13 -> x16, Pallas kernels: 34.8 us -> 36.2 us  [call(): pl.pallas_call(ordered, out_shape=outs, in_specs=specs, out_specs=[VMEM]...]
  transfers between devices with their start and end apart: 22 -> 21, of which waited for: 7 -> 8; matrix products, arithmetic and copies ran while one was open for 0% -> 0% of each run, Pallas kernels for 33% -> 41%
where the time goes in v3:
time: 84.8 us; the launch traced here: 84.7 us
  Pallas kernels  36.2 us (43%)
  starting transfers between devices  31.9 us (38%)
  waiting for transfers between devices  14.9 us (18%)
  local copies, waits for them, and re-layouts  0.96 us (1%)
    pallas_call x16, Pallas kernels, call(): pl.pallas_call(ordered, out_shape=outs, in_specs=specs, out_specs=[VMEM]...  36.2 us
    ppermute x19, starting transfers between devices, swap(): lax.ppermute(value, axis, [(i, i ^ bits) for i in range(lax.axis_size(axi...  30.5 us
    ppermute x19, waiting for transfers between devices, swap(): lax.ppermute(value, axis, [(i, i ^ bits) for i in range(lax.axis_size(axi...  14.9 us
  transfers between devices with their start and end apart: 21, of which 8 were waited for; matrix products, arithmetic and copies ran while one was open for 0% of the time, Pallas kernels for 41%

profile of v3, /device:TPU:0, one launch (start us, length us, event | category | flops | bytes accessed | tf_op | source)
XLA Modules:
  0.0 84.7 jit_solution(14663079504229797530)
XLA Ops:
  0.6 3.0 %collective-permute-start.1 = (bf16[64,2048]{1,0:T(8,128)(2,1)}, bf16[64,2048]{1,0:T(8,128)(2,1)S(1)}, u32[]{:S(2)}, u32[]{:S(2)}) collective-permute-start(bf16[64,2048]{1,0:T(8,128)(2,1)} %bitcast.14), channel_id=1, source_target_pairs={{0,2},{1,3},{2,0},{3,1},{4,6},{5,7},{6,4},{7,5},{8,10},{9,11},{10,... | collective-permute-start | bytes 786440 | tf_op jit(solution)/shard_map/ppermute | solution.py:323
  3.6 8.3 %shard_map.85 = (s32[24,27]{1,0:T(8,128)S(1)}, bf16[1728,2560]{1,0:T(8,128)(2,1)S(1)}, bf16[2,64,2560]{2,1,0:T(8,128)(2,1)S(1)}, bf16[2,64,2560]{2,1,0:T(8,128)(2,1)S(1)}) custom-call(s32[8]{0:T(128)} %refs_0_.1, s32[3,16,27]{2,1,0:T(8,128)} %bitcast.20, bf16[64,2048]{1,0:T(8,128)(2,1)} %bitcast.19, bf16[1728,256]{1,0:T(8,128)(2,1)} %bitcast.12), custom_call_target="tpu_custom_call" | custom-call | flops 2264924160 | bytes 16777216 | tf_op jit(solution)/shard_map/pallas_call | solution.py:36
  11.9 0.0 collective-permute-done.1.refs_0_
  11.9 0.6 collective-permute-start.2
  12.5 0.1 collective-permute-start.5
  12.6 1.1 %collective-permute-done.2.refs_4_ = bf16[64,2048]{1,0:T(8,128)(2,1)S(1)} collective-permute-done((bf16[64,2048]{1,0:T(8,128)(2,1)S(1)}, bf16[64,2048]{1,0:T(8,128)(2,1)S(1)}, u32[]{:S(2)}, u32[]{:S(2)}) %collective-permute-start.2) | collective-permute-done | bytes 262176 | tf_op jit(solution)/shard_map/ppermute | solution.py:323
  13.7 0.9 %copy-done.2 = bf16[2048,64]{0,1:T(8,128)(2,1)S(1)} copy-done((bf16[2048,64]{0,1:T(8,128)(2,1)S(1)}, bf16[2048,64]{0,1:T(8,128)(2,1)}, u32[]{:S(2)}) %copy-start.2) | copy-done | bytes 262168
  14.6 0.8 shard_map.87
  15.5 0.7 collective-permute-start.4
  16.2 4.4 %collective-permute-start.3 = (bf16[256,256]{1,0:T(8,128)(2,1)S(1)}, bf16[256,256]{1,0:T(8,128)(2,1)S(1)}, u32[]{:S(2)}, u32[]{:S(2)}) collective-permute-start(bf16[256,256]{1,0:T(8,128)(2,1)S(1)} %get-tuple-element.33.refs_2_), channel_id=1, source_target_pairs={{0,4},{4,0},{8,12},{12,8},{16,20},{20,16},{24,28},{28,24},{1,5},{5... | collective-permute-start | bytes 393224 | tf_op jit(solution)/shard_map/ppermute | solution.py:323
  20.5 0.0 collective-permute-done.5.refs_1_
  20.5 0.2 shard_map.88
  20.7 0.6 collective-permute-start.6
  21.3 2.5 %shard_map.89.refs_4_ = f32[1728,2560]{1,0:T(8,128)S(1)} custom-call(bf16[1728,256]{1,0:T(8,128)(2,1)S(1)} %bitcast.10, bf16[256,2048]{1,0:T(8,128)(2,1)S(1)} %get-tuple-element.35.refs_1_.refs_5_, f32[64,2560]{1,0:T(8,128)S(1)} %get-tuple-element.37.refs_2_), custom_call_target="tpu_custom_call" | custom-call | flops 2264924160 | bytes 16777216 | tf_op jit(solution)/shard_map/pallas_call | solution.py:36
  23.8 0.0 copy-start.1
  23.8 0.0 collective-permute-done.4.refs_3_.refs_7_
  23.8 2.1 %collective-permute-done.3.refs_2_.refs_6_ = bf16[256,256]{1,0:T(8,128)(2,1)S(1)} collective-permute-done((bf16[256,256]{1,0:T(8,128)(2,1)S(1)}, bf16[256,256]{1,0:T(8,128)(2,1)S(1)}, u32[]{:S(2)}, u32[]{:S(2)}) %collective-permute-start.3) | collective-permute-done | bytes 131104 | tf_op jit(solution)/shard_map/ppermute | solution.py:323
  25.9 4.1 %shard_map.90 = (f32[64,2048]{1,0:T(8,128)S(1)}, bf16[64,2048]{1,0:T(8,128)(2,1)S(1)}, f32[1728,2560]{1,0:T(8,128)S(1)}) custom-call(s32[24,27]{1,0:T(8,128)S(1)} %get-tuple-element.31.refs_0_, bf16[1728,256]{1,0:T(8,128)(2,1)S(1)} %bitcast.11, bf16[256,256]{1,0:T(8,128)(2,1)S(1)} %collective-permute-done.3.refs_2_.refs_6_, ...), custom_call_target="tpu_custom_call", output_to_operand_aliasing={{2}: (4, {})} | custom-call | flops 2264924160 | bytes 16777216 | tf_op jit(solution)/shard_map/pallas_call | solution.py:36
  30.0 0.2 collective-permute-done.6.refs_3_
  30.2 0.8 shard_map.91
  31.0 2.4 %collective-permute-start.7 = (bf16[2,64,256]{2,1,0:T(8,128)(2,1)S(1)}, bf16[2,64,256]{2,1,0:T(8,128)(2,1)S(1)}, u32[]{:S(2)}, u32[]{:S(2)}) collective-permute-start(bf16[2,64,256]{2,1,0:T(8,128)(2,1)S(1)} %get-tuple-element.40), channel_id=1, source_target_pairs={{0,4},{4,0},{8,12},{12,8},{16,20},{20,16},{24,28},{28,24},{1,5},{5... | collective-permute-start | bytes 196616 | tf_op jit(solution)/shard_map/ppermute | solution.py:323
  33.4 0.7 collective-permute-start.8
  34.1 0.6 collective-permute-start.10
  34.7 1.0 %collective-permute-done.7.refs_1_.refs_3_ = bf16[2,64,256]{2,1,0:T(8,128)(2,1)S(1)} collective-permute-done((bf16[2,64,256]{2,1,0:T(8,128)(2,1)S(1)}, bf16[2,64,256]{2,1,0:T(8,128)(2,1)S(1)}, u32[]{:S(2)}, u32[]{:S(2)}) %collective-permute-start.7) | collective-permute-done | bytes 65568 | tf_op jit(solution)/shard_map/ppermute | solution.py:323
  35.7 0.0 collective-permute-done.8.refs_2_.refs_4_
  35.7 0.6 collective-permute-start.11
  36.3 0.0 collective-permute-start.9
  36.3 6.9 %shard_map.93 = (f32[4,32,1728]{2,1,0:T(8,128)S(1)}, bf16[4,32,1728]{2,1,0:T(8,128)(2,1)S(1)}) custom-call(s32[24,27]{1,0:T(8,128)S(1)} %get-tuple-element.31.refs_0_, f32[64,2048]{1,0:T(8,128)S(1)} %get-tuple-element.44.refs_1_, f32[64,2048]{1,0:T(8,128)S(1)} %get-tuple-element.45.refs_2_, bf16[2,64,256]{2,1,0:T(8,128)(2,1)S(1)} %collective-permute-done.7.refs_1_.refs_3_, ...), custom_call_target="tpu_custom_call" | custom-call | flops 2264924160 | bytes 16777216 | tf_op jit(solution)/shard_map/pallas_call | solution.py:36
  43.2 0.3 collective-permute-done.11.refs_1_
  43.5 0.3 collective-permute-start.12
  43.8 4.9 %collective-permute-start.13 = (bf16[4,32,1728]{2,1,0:T(8,128)(2,1)S(1)}, bf16[4,32,1728]{2,1,0:T(8,128)(2,1)S(1)}, u32[]{:S(2)}, u32[]{:S(2)}) collective-permute-start(bf16[4,32,1728]{2,1,0:T(8,128)(2,1)S(1)} %get-tuple-element.47), channel_id=1, source_target_pairs={{0,4},{4,0},{8,12},{12,8},{16,20},{20,16},{24,28},{28,24},{1,5},{5... | collective-permute-start | bytes 1327112 | tf_op jit(solution)/shard_map/ppermute | solution.py:323
  48.7 3.3 %shard_map.98 = (f32[4,32,1728]{2,1,0:T(8,128)S(1)}, bf16[4,32,1728]{2,1,0:T(8,128)(2,1)S(1)}) custom-call(bf16[1728,2560]{1,0:T(8,128)(2,1)S(1)} %get-tuple-element.52.refs_0_, bf16[64,2560]{1,0:T(8,128)(2,1)S(1)} %get-tuple-element.42.refs_2_.refs_1_, bf16[64,2560]{1,0:T(8,128)(2,1)S(1)} %collective-permute-done.9.refs_3_.refs_2_, ...), custom_call_target="tpu_custom_call" | custom-call | flops 2264924160 | bytes 8388608 | tf_op jit(solution)/shard_map/pallas_call | solution.py:36
  52.0 1.3 %collective-permute-start.17 = (bf16[4,32,1728]{2,1,0:T(8,128)(2,1)S(1)}, bf16[4,32,1728]{2,1,0:T(8,128)(2,1)S(1)}, u32[]{:S(2)}, u32[]{:S(2)}) collective-permute-start(bf16[4,32,1728]{2,1,0:T(8,128)(2,1)S(1)} %get-tuple-element.54), channel_id=1, source_target_pairs={{0,4},{4,0},{8,12},{12,8},{16,20},{20,16},{24,28},{28,24},{1,5},{5... | collective-permute-start | bytes 1327112 | tf_op jit(solution)/shard_map/ppermute | solution.py:323
  53.3 6.7 %collective-permute-done.13.refs_1_ = bf16[4,32,1728]{2,1,0:T(8,128)(2,1)S(1)} collective-permute-done((bf16[4,32,1728]{2,1,0:T(8,128)(2,1)S(1)}, bf16[4,32,1728]{2,1,0:T(8,128)(2,1)S(1)}, u32[]{:S(2)}, u32[]{:S(2)}) %collective-permute-start.13) | collective-permute-done | bytes 442400 | tf_op jit(solution)/shard_map/ppermute | solution.py:323
  60.0 0.1 shard_map.96
  60.1 3.6 %collective-permute-start.14 = (bf16[32,1728]{1,0:T(8,128)(2,1)S(1)}, bf16[32,1728]{1,0:T(8,128)(2,1)S(1)}, u32[]{:S(2)}, u32[]{:S(2)}) collective-permute-start(bf16[32,1728]{1,0:T(8,128)(2,1)S(1)} %get-tuple-element.49), channel_id=1, source_target_pairs={{0,8},{4,12},{8,0},{12,4},{16,24},{20,28},{24,16},{28,20},{1,9},{5... | collective-permute-start | bytes 331784 | tf_op jit(solution)/shard_map/ppermute | solution.py:323
  63.7 1.1 %collective-permute-start.15 = (bf16[32,1728]{1,0:T(8,128)(2,1)S(1)}, bf16[32,1728]{1,0:T(8,128)(2,1)S(1)}, u32[]{:S(2)}, u32[]{:S(2)}) collective-permute-start(bf16[32,1728]{1,0:T(8,128)(2,1)S(1)} %get-tuple-element.50), channel_id=1, source_target_pairs={{0,16},{4,20},{8,24},{12,28},{16,0},{20,4},{24,8},{28,12},{1,17},{... | collective-permute-start | bytes 331784 | tf_op jit(solution)/shard_map/ppermute | solution.py:323
  64.8 1.4 %collective-permute-start.16 = (bf16[32,1728]{1,0:T(8,128)(2,1)S(1)}, bf16[32,1728]{1,0:T(8,128)(2,1)S(1)}, u32[]{:S(2)}, u32[]{:S(2)}) collective-permute-start(bf16[32,1728]{1,0:T(8,128)(2,1)S(1)} %get-tuple-element.51), channel_id=1, source_target_pairs={{0,24},{4,28},{8,16},{12,20},{16,8},{20,12},{24,0},{28,4},{1,25},{... | collective-permute-start | bytes 331784 | tf_op jit(solution)/shard_map/ppermute | solution.py:323
  66.1 3.1 %collective-permute-done.17.refs_1_ = bf16[4,32,1728]{2,1,0:T(8,128)(2,1)S(1)} collective-permute-done((bf16[4,32,1728]{2,1,0:T(8,128)(2,1)S(1)}, bf16[4,32,1728]{2,1,0:T(8,128)(2,1)S(1)}, u32[]{:S(2)}, u32[]{:S(2)}) %collective-permute-start.17) | collective-permute-done | bytes 442400 | tf_op jit(solution)/shard_map/ppermute | solution.py:323
  69.3 0.1 shard_map.99
  69.4 3.3 %collective-permute-start.18 = (bf16[32,1728]{1,0:T(8,128)(2,1)S(1)}, bf16[32,1728]{1,0:T(8,128)(2,1)S(1)}, u32[]{:S(2)}, u32[]{:S(2)}) collective-permute-start(bf16[32,1728]{1,0:T(8,128)(2,1)S(1)} %get-tuple-element.56), channel_id=1, source_target_pairs={{0,8},{4,12},{8,0},{12,4},{16,24},{20,28},{24,16},{28,20},{1,9},{5... | collective-permute-start | bytes 331784 | tf_op jit(solution)/shard_map/ppermute | solution.py:323
  72.6 1.1 %collective-permute-start.19 = (bf16[32,1728]{1,0:T(8,128)(2,1)S(1)}, bf16[32,1728]{1,0:T(8,128)(2,1)S(1)}, u32[]{:S(2)}, u32[]{:S(2)}) collective-permute-start(bf16[32,1728]{1,0:T(8,128)(2,1)S(1)} %get-tuple-element.57), channel_id=1, source_target_pairs={{0,16},{4,20},{8,24},{12,28},{16,0},{20,4},{24,8},{28,12},{1,17},{... | collective-permute-start | bytes 331784 | tf_op jit(solution)/shard_map/ppermute | solution.py:323
  73.7 0.0 collective-permute-done.14.refs_1_
  73.7 1.4 %collective-permute-start.20 = (bf16[32,1728]{1,0:T(8,128)(2,1)S(1)}, bf16[32,1728]{1,0:T(8,128)(2,1)S(1)}, u32[]{:S(2)}, u32[]{:S(2)}) collective-permute-start(bf16[32,1728]{1,0:T(8,128)(2,1)S(1)} %get-tuple-element.58), channel_id=1, source_target_pairs={{0,24},{4,28},{8,16},{12,20},{16,8},{20,12},{24,0},{28,4},{1,25},{... | collective-permute-start | bytes 331784 | tf_op jit(solution)/shard_map/ppermute | solution.py:323
  75.1 7.3 %shard_map.95 = bf16[64,2048]{1,0:T(8,128)(2,1)} custom-call(s32[24,27]{1,0:T(8,128)S(1)} %get-tuple-element.31.refs_0_, bf16[1728,256]{1,0:T(8,128)(2,1)S(1)} %bitcast.13, bf16[64,2560]{1,0:T(8,128)(2,1)S(1)} %get-tuple-element.42.refs_2_.refs_1_, bf16[64,2560]{1,0:T(8,128)(2,1)S(1)} %collective-permute-done.9.refs_3_.refs_2_, ...), custom_call_target="tpu_custom_call" | custom-call | flops 2264924160 | bytes 16777216 | tf_op jit(solution)/shard_map/pallas_call | solution.py:36
  82.4 0.9 %shard_map.97 = f32[27,32,64]{2,1,0:T(8,128)} custom-call(f32[32,1728]{1,0:T(8,128)S(1)} %get-tuple-element.48.refs_0_, bf16[32,1728]{1,0:T(8,128)(2,1)S(1)} %collective-permute-done.14.refs_1_, bf16[32,1728]{1,0:T(8,128)(2,1)S(1)} %collective-permute-done.15.refs_2_, bf16[32,1728]{1,0:T(8,128)(2,1)S(1)} %collective-permute-done.16.refs_3_), custom_call_target="tpu_custom_call" | custom-call | bytes 2097152 | tf_op jit(solution)/shard_map/pallas_call | solution.py:36
  83.3 0.4 collective-permute-done.19.refs_2_
  83.8 0.9 %shard_map.100 = f32[27,32,64]{2,1,0:T(8,128)} custom-call(f32[32,1728]{1,0:T(8,128)S(1)} %get-tuple-element.55.refs_0_, bf16[32,1728]{1,0:T(8,128)(2,1)S(1)} %collective-permute-done.18.refs_1_, bf16[32,1728]{1,0:T(8,128)(2,1)S(1)} %collective-permute-done.19.refs_2_, bf16[32,1728]{1,0:T(8,128)(2,1)S(1)} %collective-permute-done.20.refs_3_), custom_call_target="tpu_custom_call" | custom-call | bytes 2097152 | tf_op jit(solution)/shard_map/pallas_call | solution.py:36
  (16 shorter events, 0.1 us)
Async XLA Ops:
  0.6 11.3 %collective-permute-start.1 = (bf16[64,2048]{1,0:T(8,128)(2,1)}, bf16[64,2048]{1,0:T(8,128)(2,1)S(1)}, u32[]{:S(2)}, u32[]{:S(2)}) collective-permute-start(bf16[64,2048]{1,0:T(8,128)(2,1)} %bitcast.14), channel_id=1, source_target_pairs={{0,2},{1,3},{2,0},{3,1},{4,6},{5,7},{6,4},{7,5},{8,10},{9,11},{10,... | collective-permute-start | bytes 786440 | tf_op jit(solution)/shard_map/ppermute | solution.py:323
  3.6 9.0 %collective-permute-start = (bf16[64,2048]{1,0:T(8,128)(2,1)}, bf16[64,2048]{1,0:T(8,128)(2,1)S(1)}, u32[]{:S(2)}, u32[]{:S(2)}) collective-permute-start(bf16[64,2048]{1,0:T(8,128)(2,1)} %bitcast.15), channel_id=1, source_target_pairs={{0,1},{1,0},{2,3},{3,2},{4,5},{5,4},{6,7},{7,6},{8,9},{9,8},{10,11... | collective-permute-start | bytes 786440 | tf_op jit(solution)/shard_map/ppermute | solution.py:323
  11.9 1.7 %collective-permute-start.2 = (bf16[64,2048]{1,0:T(8,128)(2,1)S(1)}, bf16[64,2048]{1,0:T(8,128)(2,1)S(1)}, u32[]{:S(2)}, u32[]{:S(2)}) collective-permute-start(bf16[64,2048]{1,0:T(8,128)(2,1)S(1)} %shard_map.86.refs_3_), channel_id=1, source_target_pairs={{0,1},{1,0},{2,3},{3,2},{4,5},{5,4},{6,7},{7,6},{8,9},{9,8},{10,11... | collective-permute-start | bytes 786440 | tf_op jit(solution)/shard_map/ppermute | solution.py:323
  12.5 8.0 %collective-permute-start.5 = (bf16[2,64,2560]{2,1,0:T(8,128)(2,1)S(1)}, bf16[2,64,2560]{2,1,0:T(8,128)(2,1)S(1)}, u32[]{:S(2)}, u32[]{:S(2)}) collective-permute-start(bf16[2,64,2560]{2,1,0:T(8,128)(2,1)S(1)} %get-tuple-element.32.refs_1_), channel_id=1, source_target_pairs={{0,1},{1,0},{2,3},{3,2},{4,5},{5,4},{6,7},{7,6},{8,9},{9,8},{10,11... | collective-permute-start | bytes 1966088 | tf_op jit(solution)/shard_map/ppermute | solution.py:323
  13.7 0.9 %copy-start.2 = (bf16[2048,64]{0,1:T(8,128)(2,1)S(1)}, bf16[2048,64]{0,1:T(8,128)(2,1)}, u32[]{:S(2)}) copy-start(bf16[2048,64]{0,1:T(8,128)(2,1)} %param.6) | copy-start | bytes 786436
  14.6 6.7 %copy-start = (bf16[27,64,256]{2,1,0:T(8,128)(2,1)S(1)}, bf16[27,64,256]{2,1,0:T(8,128)(2,1)}, u32[]{:S(2)}) copy-start(bf16[27,64,256]{2,1,0:T(8,128)(2,1)} %param.9) | copy-start | bytes 2654212
  15.5 8.3 %collective-permute-start.4 = (bf16[256,256]{1,0:T(8,128)(2,1)S(1)}, bf16[256,256]{1,0:T(8,128)(2,1)S(1)}, u32[]{:S(2)}, u32[]{:S(2)}) collective-permute-start(bf16[256,256]{1,0:T(8,128)(2,1)S(1)} %get-tuple-element.34), channel_id=1, source_target_pairs={{4,8},{12,16},{20,24},{8,4},{16,12},{24,20},{5,9},{13,17},{21,25},... | collective-permute-start | bytes 393224 | tf_op jit(solution)/shard_map/ppermute | solution.py:328
  16.2 9.7 %collective-permute-start.3 = (bf16[256,256]{1,0:T(8,128)(2,1)S(1)}, bf16[256,256]{1,0:T(8,128)(2,1)S(1)}, u32[]{:S(2)}, u32[]{:S(2)}) collective-permute-start(bf16[256,256]{1,0:T(8,128)(2,1)S(1)} %get-tuple-element.33.refs_2_), channel_id=1, source_target_pairs={{0,4},{4,0},{8,12},{12,8},{16,20},{20,16},{24,28},{28,24},{1,5},{5... | collective-permute-start | bytes 393224 | tf_op jit(solution)/shard_map/ppermute | solution.py:323
  20.7 9.5 %collective-permute-start.6 = (bf16[64,2560]{1,0:T(8,128)(2,1)S(1)}, bf16[64,2560]{1,0:T(8,128)(2,1)S(1)}, u32[]{:S(2)}, u32[]{:S(2)}) collective-permute-start(bf16[64,2560]{1,0:T(8,128)(2,1)S(1)} %get-tuple-element.39), channel_id=1, source_target_pairs={{0,2},{1,3},{2,0},{3,1},{4,6},{5,7},{6,4},{7,5},{8,10},{9,11},{10,... | collective-permute-start | bytes 983048 | tf_op jit(solution)/shard_map/ppermute | solution.py:323
  23.8 51.3 %copy-start.1 = (bf16[27,64,256]{2,1,0:T(8,128)(2,1)S(1)}, bf16[27,64,256]{2,1,0:T(8,128)(2,1)}, u32[]{:S(2)}) copy-start(bf16[27,64,256]{2,1,0:T(8,128)(2,1)} %param.10) | copy-start | bytes 2654212
  31.0 4.7 %collective-permute-start.7 = (bf16[2,64,256]{2,1,0:T(8,128)(2,1)S(1)}, bf16[2,64,256]{2,1,0:T(8,128)(2,1)S(1)}, u32[]{:S(2)}, u32[]{:S(2)}) collective-permute-start(bf16[2,64,256]{2,1,0:T(8,128)(2,1)S(1)} %get-tuple-element.40), channel_id=1, source_target_pairs={{0,4},{4,0},{8,12},{12,8},{16,20},{20,16},{24,28},{28,24},{1,5},{5... | collective-permute-start | bytes 196616 | tf_op jit(solution)/shard_map/ppermute | solution.py:323
  33.4 2.3 %collective-permute-start.8 = (bf16[2,64,256]{2,1,0:T(8,128)(2,1)S(1)}, bf16[2,64,256]{2,1,0:T(8,128)(2,1)S(1)}, u32[]{:S(2)}, u32[]{:S(2)}) collective-permute-start(bf16[2,64,256]{2,1,0:T(8,128)(2,1)S(1)} %get-tuple-element.41), channel_id=1, source_target_pairs={{4,8},{12,16},{20,24},{8,4},{16,12},{24,20},{5,9},{13,17},{21,25},... | collective-permute-start | bytes 196616 | tf_op jit(solution)/shard_map/ppermute | solution.py:328
  34.1 9.1 %collective-permute-start.10 = (bf16[64,2048]{1,0:T(8,128)(2,1)S(1)}, bf16[64,2048]{1,0:T(8,128)(2,1)S(1)}, u32[]{:S(2)}, u32[]{:S(2)}) collective-permute-start(bf16[64,2048]{1,0:T(8,128)(2,1)S(1)} %get-tuple-element.38.refs_1_.refs_0_), channel_id=1, source_target_pairs={{0,2},{1,3},{2,0},{3,1},{4,6},{5,7},{6,4},{7,5},{8,10},{9,11},{10,... | collective-permute-start | bytes 786440 | tf_op jit(solution)/shard_map/ppermute | solution.py:323
  35.7 7.8 %collective-permute-start.11 = (bf16[64,512]{1,0:T(8,128)(2,1)S(1)}, bf16[64,512]{1,0:T(8,128)(2,1)S(1)}, u32[]{:S(2)}, u32[]{:S(2)}) collective-permute-start(bf16[64,512]{1,0:T(8,128)(2,1)S(1)} %get-tuple-element.43), channel_id=1, source_target_pairs={{0,2},{1,3},{2,0},{3,1},{4,6},{5,7},{6,4},{7,5},{8,10},{9,11},{10,... | collective-permute-start | bytes 196616 | tf_op jit(solution)/shard_map/ppermute | solution.py:323
  36.3 12.4 %collective-permute-start.9 = (bf16[64,2560]{1,0:T(8,128)(2,1)S(1)}, bf16[64,2560]{1,0:T(8,128)(2,1)S(1)}, u32[]{:S(2)}, u32[]{:S(2)}) collective-permute-start(bf16[64,2560]{1,0:T(8,128)(2,1)S(1)} %get-tuple-element.42.refs_2_.refs_1_), channel_id=1, source_target_pairs={{0,1},{1,0},{2,3},{3,2},{4,5},{5,4},{6,7},{7,6},{8,9},{9,8},{10,11... | collective-permute-start | bytes 983048 | tf_op jit(solution)/shard_map/ppermute | solution.py:323
  43.5 5.2 %collective-permute-start.12 = (bf16[64,2560]{1,0:T(8,128)(2,1)S(1)}, bf16[64,2560]{1,0:T(8,128)(2,1)S(1)}, u32[]{:S(2)}, u32[]{:S(2)}) collective-permute-start(bf16[64,2560]{1,0:T(8,128)(2,1)S(1)} %shard_map.94.refs_4_.refs_3_), channel_id=1, source_target_pairs={{0,1},{1,0},{2,3},{3,2},{4,5},{5,4},{6,7},{7,6},{8,9},{9,8},{10,11... | collective-permute-start | bytes 983048 | tf_op jit(solution)/shard_map/ppermute | solution.py:323
  43.8 16.2 %collective-permute-start.13 = (bf16[4,32,1728]{2,1,0:T(8,128)(2,1)S(1)}, bf16[4,32,1728]{2,1,0:T(8,128)(2,1)S(1)}, u32[]{:S(2)}, u32[]{:S(2)}) collective-permute-start(bf16[4,32,1728]{2,1,0:T(8,128)(2,1)S(1)} %get-tuple-element.47), channel_id=1, source_target_pairs={{0,4},{4,0},{8,12},{12,8},{16,20},{20,16},{24,28},{28,24},{1,5},{5... | collective-permute-start | bytes 1327112 | tf_op jit(solution)/shard_map/ppermute | solution.py:323
  52.0 17.3 %collective-permute-start.17 = (bf16[4,32,1728]{2,1,0:T(8,128)(2,1)S(1)}, bf16[4,32,1728]{2,1,0:T(8,128)(2,1)S(1)}, u32[]{:S(2)}, u32[]{:S(2)}) collective-permute-start(bf16[4,32,1728]{2,1,0:T(8,128)(2,1)S(1)} %get-tuple-element.54), channel_id=1, source_target_pairs={{0,4},{4,0},{8,12},{12,8},{16,20},{20,16},{24,28},{28,24},{1,5},{5... | collective-permute-start | bytes 1327112 | tf_op jit(solution)/shard_map/ppermute | solution.py:323
  60.1 13.6 %collective-permute-start.14 = (bf16[32,1728]{1,0:T(8,128)(2,1)S(1)}, bf16[32,1728]{1,0:T(8,128)(2,1)S(1)}, u32[]{:S(2)}, u32[]{:S(2)}) collective-permute-start(bf16[32,1728]{1,0:T(8,128)(2,1)S(1)} %get-tuple-element.49), channel_id=1, source_target_pairs={{0,8},{4,12},{8,0},{12,4},{16,24},{20,28},{24,16},{28,20},{1,9},{5... | collective-permute-start | bytes 331784 | tf_op jit(solution)/shard_map/ppermute | solution.py:323
  63.7 18.8 %collective-permute-start.15 = (bf16[32,1728]{1,0:T(8,128)(2,1)S(1)}, bf16[32,1728]{1,0:T(8,128)(2,1)S(1)}, u32[]{:S(2)}, u32[]{:S(2)}) collective-permute-start(bf16[32,1728]{1,0:T(8,128)(2,1)S(1)} %get-tuple-element.50), channel_id=1, source_target_pairs={{0,16},{4,20},{8,24},{12,28},{16,0},{20,4},{24,8},{28,12},{1,17},{... | collective-permute-start | bytes 331784 | tf_op jit(solution)/shard_map/ppermute | solution.py:323
  64.8 17.7 %collective-permute-start.16 = (bf16[32,1728]{1,0:T(8,128)(2,1)S(1)}, bf16[32,1728]{1,0:T(8,128)(2,1)S(1)}, u32[]{:S(2)}, u32[]{:S(2)}) collective-permute-start(bf16[32,1728]{1,0:T(8,128)(2,1)S(1)} %get-tuple-element.51), channel_id=1, source_target_pairs={{0,24},{4,28},{8,16},{12,20},{16,8},{20,12},{24,0},{28,4},{1,25},{... | collective-permute-start | bytes 331784 | tf_op jit(solution)/shard_map/ppermute | solution.py:323
  69.4 14.0 %collective-permute-start.18 = (bf16[32,1728]{1,0:T(8,128)(2,1)S(1)}, bf16[32,1728]{1,0:T(8,128)(2,1)S(1)}, u32[]{:S(2)}, u32[]{:S(2)}) collective-permute-start(bf16[32,1728]{1,0:T(8,128)(2,1)S(1)} %get-tuple-element.56), channel_id=1, source_target_pairs={{0,8},{4,12},{8,0},{12,4},{16,24},{20,28},{24,16},{28,20},{1,9},{5... | collective-permute-start | bytes 331784 | tf_op jit(solution)/shard_map/ppermute | solution.py:323
  72.6 11.1 %collective-permute-start.19 = (bf16[32,1728]{1,0:T(8,128)(2,1)S(1)}, bf16[32,1728]{1,0:T(8,128)(2,1)S(1)}, u32[]{:S(2)}, u32[]{:S(2)}) collective-permute-start(bf16[32,1728]{1,0:T(8,128)(2,1)S(1)} %get-tuple-element.57), channel_id=1, source_target_pairs={{0,16},{4,20},{8,24},{12,28},{16,0},{20,4},{24,8},{28,12},{1,17},{... | collective-permute-start | bytes 331784 | tf_op jit(solution)/shard_map/ppermute | solution.py:323
  73.7 10.0 %collective-permute-start.20 = (bf16[32,1728]{1,0:T(8,128)(2,1)S(1)}, bf16[32,1728]{1,0:T(8,128)(2,1)S(1)}, u32[]{:S(2)}, u32[]{:S(2)}) collective-permute-start(bf16[32,1728]{1,0:T(8,128)(2,1)S(1)} %get-tuple-element.58), channel_id=1, source_target_pairs={{0,24},{4,28},{8,16},{12,20},{16,8},{20,12},{24,0},{28,4},{1,25},{... | collective-permute-start | bytes 331784 | tf_op jit(solution)/shard_map/ppermute | solution.py:323

commit v4 on v3

--- a/solution.py
+++ b/solution.py
@@ -9,6 +9,7 @@
 
 BLK = 128
 HB = 2
+Y_FIRST = 20
 RIM = HB * BLK
 STEP = 256
 F32 = jnp.float32
@@ -33,7 +34,8 @@
     def ordered(*refs):
         body(*refs[:first], *refs[last:])
 
-    return pl.pallas_call(
+    name = getattr(body, "func", body).__name__
+    kernel = pl.pallas_call(
         ordered,
         out_shape=outs,
         in_specs=specs,
@@ -42,7 +44,9 @@
         input_output_aliases=aliases or {},
         compiler_params=pltpu.CompilerParams(vmem_limit_bytes=vmem << 20),
         cost_estimate=pl.CostEstimate(flops=flops, bytes_accessed=traffic, transcendentals=0),
-    )(*ins)
+    )
+    with jax.named_scope(name):
+        return kernel(*ins)
 
 
 def chunks(total, step, body):
@@ -93,12 +97,12 @@
 
     def one(k, _):
         rows = pl.ds(pl.multiple_of(k * depth, depth), depth)
-        spread_ref[rows, :] = jnp.zeros((depth, spread_ref.shape[1]), BF16)
+        spread_ref[:, rows, :] = jnp.zeros((spread_ref.shape[0], depth, BLK), BF16)
         before, acc = -1, jnp.zeros((depth, BLK), F32)
         for e in range(entries):
             s, t = cell(tab[e, k])
             acc = jnp.where(s == before, acc, 0.0) + blocks[t]
-            spread_ref[rows, pl.ds(pl.multiple_of(s * BLK, BLK), BLK)] = acc.astype(BF16)
+            spread_ref[s, rows, :] = acc.astype(BF16)
             before = s
         return 0
 
@@ -116,7 +120,7 @@
         for e in range(entries):
             acc = sums[e % len(sums)]
             s, t = cell(tab[e, k])
-            acc[t] = acc[t] + prod[rows, pl.ds(pl.multiple_of(s * BLK, BLK), BLK)]
+            acc[t] = acc[t] + prod[s, rows, :]
         return 0
 
     lax.fori_loop(0, offsets, one, 0)
@@ -137,13 +141,11 @@
 
 
 def input_grad_body(
-    counts, map_hbm, cot_hbm, w_hbm, tab_ref, spread_ref, keep_ref, send_ref,
-    map_ref, cot_ref, w_ref, blocks, part, tab, sems, sem
+    counts, map_hbm, cot_hbm, w_hbm, feat_hbm, tab_ref, spread_ref, keep_ref, send_ref,
+    own_ref, map_ref, cot_ref, w_ref, blocks, part, tab, sems, sem
 ):
-    loads = [
-        pltpu.make_async_copy(src, dst, sems.at[i])
-        for i, (src, dst) in enumerate([(map_hbm, map_ref), (cot_hbm, cot_ref), (w_hbm, w_ref)])
-    ]
+    ways = [(map_hbm, map_ref), (cot_hbm, cot_ref), (w_hbm, w_ref), (feat_hbm, own_ref)]
+    loads = [pltpu.make_async_copy(src, dst, sems.at[i]) for i, (src, dst) in enumerate(ways)]
     for load in loads:
         load.start()
     depth, rows = cot_ref.shape
@@ -160,16 +162,21 @@
     spread(tab, blocks, spread_ref)
     loads[2].wait()
 
-    def product(start, width):
-        cols = pl.ds(start, width)
-        res = lax.dot_general(w_ref[...], spread_ref[:, cols], (((0,), (0,)), ((), ())), preferred_element_type=F32)
-        part[:, :, cols] = res.astype(BF16).reshape(part.shape[0], depth, width)
-
-    chunks(spread_ref.shape[1], 2 * STEP, product)
+    half = spread_ref.shape[0] // 2
+
+    def product(i, _):
+        table = jnp.concatenate([spread_ref[i * half + j] for j in range(half)], axis=1)
+        res = lax.dot_general(w_ref[...], table, (((0,), (0,)), ((), ())), preferred_element_type=F32)
+        cols = pl.ds(pl.multiple_of(i * half * BLK, BLK), half * BLK)
+        part[:, :, cols] = res.astype(BF16).reshape(part.shape[0], depth, half * BLK)
+        return 0
+
+    lax.fori_loop(0, 2, product, 0)
     core = lax.axis_index("chan") % 2
     for j in range(keep_ref.shape[0]):
         keep_ref[j] = part[2 * j + core]
         send_ref[j] = part[2 * j + 1 - core]
+    loads[3].wait()
 
 
 def pass_body(value_ref, out_ref):
@@ -185,12 +192,10 @@
     b_ref[...] = wide_ref[:, pl.ds(b, RIM)]
 
 
-def multiply(w_ref, value_ref, prod):
-    def product(start, width):
-        cols = pl.ds(start, width)
-        prod[:, cols] = jnp.dot(w_ref[...], value_ref[:, cols], preferred_element_type=F32)
-
-    chunks(value_ref.shape[1], 2 * STEP, product)
+def multiply(w_ref, value, prod, first):
+    res = jnp.dot(w_ref[...], value, preferred_element_type=F32)
+    for j in range(value.shape[1] // BLK):
+        prod[first + j] = res[:, j * BLK : (j + 1) * BLK]
 
 
 def gather_sums(tab, prod, sums, store):
@@ -203,13 +208,12 @@
 
 
 def inner_body(w_ref, wide_ref, prod_ref):
-    multiply(w_ref, wide_ref, prod_ref)
+    multiply(w_ref, wide_ref[...], prod_ref, 0)
 
 
 def hidden_body(tab, w_ref, a_ref, b_ref, _, z_ref, hidden_ref, prod, *sums):
-    rows = z_ref.shape[1]
-    prod[:, rows : rows + RIM] = jnp.dot(w_ref[...], a_ref[...], preferred_element_type=F32)
-    prod[:, rows + RIM :] = jnp.dot(w_ref[...], b_ref[...], preferred_element_type=F32)
+    nblocks = z_ref.shape[1] // BLK
+    multiply(w_ref, jnp.concatenate([a_ref[...], b_ref[...]], axis=1), prod, nblocks)
 
     def store(cols, z):
         z_ref[:, cols] = z
@@ -220,13 +224,16 @@
 
 def output_body(order, tab, w_ref, *refs):
     pieces = len(order)
-    out_ref, ext, prod, *sums = refs[pieces:]
+    out_ref, done_ref, ext, prod, *sums = refs[pieces:]
+    done_ref[...] = jnp.zeros_like(done_ref)
     lay(ext, order, refs[:pieces])
 
     def store(cols, total):
         out_ref[:, cols] = total.astype(BF16)
 
-    multiply(w_ref, ext, prod)
+    half = prod.shape[0] // 2
+    for i in range(2):
+        multiply(w_ref, ext[:, i * half * BLK : (i + 1) * half * BLK], prod, i * half)
     gather_sums(tab, prod, sums, store)
 
 
@@ -266,26 +273,45 @@
     full_ref[:, rows:] = rim_ref[...]
 
 
-def weight_grad(ext, spread_ref, total, keep_ref, send_ref):
-    shares, width_in = total.shape[0], total.shape[1]
+def weight_grad(ext, spread_ref, total):
+    reach = spread_ref.shape[0]
 
     def product(start, width):
         part = pl.ds(start, width)
-        res = lax.dot_general(ext[...], spread_ref[part, :], (((1,), (1,)), ((), ())), preferred_element_type=F32)
-        total[:, :, part] = res.reshape(shares, width_in, width)
-
-    chunks(spread_ref.shape[0], 2 * STEP, product)
+        table = jnp.concatenate([spread_ref[s, part, :] for s in range(reach)], axis=1)
+        res = lax.dot_general(ext[...], table, (((1,), (1,)), ((), ())), preferred_element_type=F32)
+        total[:, :, :, part] = res.reshape(total.shape[:3] + (width,))
+
+    chunks(spread_ref.shape[1], 7 * BLK, product)
+
+
+def part_slabs(total, keep_ref, send_ref):
     parity = lax.axis_index("space") % 2
-    for j in range(shares // 2):
-        keep_ref[j] = total[2 * j + parity]
-        send_ref[j] = total[2 * j + 1 - parity].astype(BF16)
+    keep_ref[...] = total[:, parity]
+    send_ref[...] = total[:, 1 - parity].astype(BF16)
 
 
 def grad_two_body(order, spread_ref, *refs):
     pieces = len(order)
-    keep_ref, send_ref, ext, total = refs[pieces:]
+    keep_ref, send_ref, mine_ref, *send_refs, ext, total = refs[pieces:]
     lay(ext, order, refs[:pieces])
-    weight_grad(ext, spread_ref, total, keep_ref, send_ref)
+    weight_grad(ext, spread_ref, total)
+    cut = keep_ref.shape[2]
+    part_slabs(total.at[:, :, :, :cut], keep_ref, send_ref)
+    place = lax.axis_index("space") // 2
+    mine_ref[...] = total[place, :, :, cut:]
+    for j, ref in enumerate(send_refs):
+        ref[...] = total[place ^ (j + 1), :, :, cut:].astype(BF16)
+
+
+def split_body(count, mine_ref, *refs):
+    gots, (keep_ref, send_ref) = refs[:count], refs[count:]
+    parity = lax.axis_index("space") % 2
+    for ref, place in ((keep_ref, parity), (send_ref, 1 - parity)):
+        total = mine_ref[place]
+        for got in gots:
+            total = total + got[place].astype(F32)
+        ref[...] = total.astype(ref.dtype)
 
 
 def grad_one_body(
@@ -306,17 +332,22 @@
         blocks[i] = value.astype(BF16).astype(F32)
     blocks[nblocks] = jnp.zeros_like(blocks[nblocks])
     spread(tab, blocks, spread_ref)
-    weight_grad(ext, spread_ref, total, keep_ref, send_ref)
-
-
-def finish_body(count, mine_ref, *refs):
-    gots, out_ref = refs[:count], refs[count]
-    total = mine_ref[...]
-    for ref in gots:
-        total = total + ref[...].astype(F32)
+    weight_grad(ext, spread_ref, total)
+    part_slabs(total, keep_ref, send_ref)
+
+
+def finish_body(counts, *refs):
+    out_ref = refs[-1]
     depth = out_ref.shape[2]
-    for k in range(out_ref.shape[0]):
-        out_ref[k] = total[:, k * depth : (k + 1) * depth]
+    k = first = 0
+    for count in counts:
+        total = refs[first][...]
+        for ref in refs[first + 1 : first + count]:
+            total = total + ref[...].astype(F32)
+        first += count
+        for i in range(total.shape[1] // depth):
+            out_ref[k] = total[:, i * depth : (i + 1) * depth]
+            k += 1
 
 
 def swap(value, axis, bits):
@@ -342,39 +373,47 @@
     work = 2 * flat * wide * reach
     blocks = pltpu.VMEM((nblocks + 1, depth, BLK), F32)
     ext = pltpu.VMEM((wide, reach), BF16)
-
-    def reduce_slabs(keep, send):
-        got = swap(send, "space", 1)
-        outs = call(
-            functools.partial(halve_body, "space"),
-            [pltpu.VMEM((share, flat), F32)] + [pltpu.VMEM((share, flat), BF16)] * (slabs // 2 - 1),
-            [held(keep), held(got)],
-            traffic=2 << 20,
-        )
-        gots = [swap(v, "space", 2 * (j + 1)) for j, v in enumerate(outs[1:])]
+    spread_shape = (nblocks + 2 * HB, flat, BLK)
+
+    def finish(*groups):
         total = call(
-            functools.partial(finish_body, len(gots)),
+            functools.partial(finish_body, [len(g) for g in groups]),
             [jax.ShapeDtypeStruct((offsets, share, depth), F32)],
-            [held(v) for v in [outs[0]] + gots],
+            [held(v) for g in groups for v in g],
             traffic=2 << 20,
         )[0]
         return total.transpose(0, 2, 1)
 
+    def reduce_far(keep, got, after):
+        width = keep.shape[2]
+        mine, *sends = call(
+            functools.partial(halve_body, "space"),
+            [pltpu.VMEM((share, width), F32)] + [pltpu.VMEM((share, width), BF16)] * (slabs // 2 - 1),
+            [held(keep), held(got)],
+            traffic=2 << 20,
+            after=after,
+        )
+        return [mine] + [swap(v, "space", 2 * (j + 1)) for j, v in enumerate(sends)]
+
     w_one = weight_one.reshape(flat, wide)
     w_two = weight_two.reshape(flat, wide)
 
     shard_t = features.T
     far = [swap(shard_t, "chan", 2 * j) for j in range(1, pairs)]
     cot = cotangent.T
-    tab, spread_two, keep, send = call(
+    tab, spread_two, keep, send, own = call(
         input_grad_body,
         [
             pltpu.VMEM((entries + PAD, offsets), jnp.int32),
-            pltpu.VMEM((flat, reach), BF16),
+            pltpu.VMEM(spread_shape, BF16),
             pltpu.VMEM((pairs, depth, reach), BF16),
             pltpu.VMEM((pairs, depth, reach), BF16),
+            pltpu.VMEM((depth, rows), BF16),
         ],
-        [pltpu.with_memory_space_constraint(v, pltpu.HBM) for v in (block_count, kernel_map[0].transpose(2, 1, 0), cot, w_two)],
+        [
+            pltpu.with_memory_space_constraint(v, pltpu.HBM)
+            for v in (block_count, kernel_map[0].transpose(2, 1, 0), cot, w_two, shard_t)
+        ],
         [
             pltpu.VMEM((3, entries, offsets), jnp.int32),
             pltpu.VMEM(cot.shape, BF16),
@@ -382,15 +421,15 @@
             blocks,
             pltpu.VMEM((parts, depth, reach), BF16),
             pltpu.SMEM((entries + PAD, offsets), jnp.int32),
-            pltpu.SemaphoreType.DMA((3,)),
+            pltpu.SemaphoreType.DMA((4,)),
             pltpu.SemaphoreType.DMA,
         ],
         vmem=16,
         flops=work,
         traffic=16 << 20,
-        specs=[SMEM, FAR, FAR, FAR],
-    )
-    pieces = [shard_t, swap(shard_t, "chan", 1)]
+        specs=[SMEM] + [FAR] * 4,
+    )
+    pieces = [own, swap(shard_t, "chan", 1)]
     for got in far:
         (got,) = call(pass_body, [pltpu.VMEM(got.shape, BF16)], [held(got)], after=[send])
         pieces += [got, swap(got, "chan", 1)]
@@ -412,10 +451,10 @@
     )
     gots = [swap(v, "chan", 2 * (j + 1)) for j, v in enumerate(sends)]
 
-    conv_scratch = [ext, pltpu.VMEM((flat, reach), F32)] + [blocks] * 2
+    conv_scratch = [ext, pltpu.VMEM(spread_shape, F32)] + [blocks] * 2
     (prod_one,) = call(
         inner_body,
-        [pltpu.VMEM((flat, reach), F32)],
+        [pltpu.VMEM(spread_shape, F32)],
         [w_one, held(x_wide)],
         vmem=10,
         flops=work,
@@ -424,7 +463,7 @@
     )
     z_one, hidden, _ = call(
         hidden_body,
-        [pltpu.VMEM((depth, rows), F32), pltpu.VMEM((depth, rows), BF16), pltpu.VMEM((flat, reach), F32)],
+        [pltpu.VMEM((depth, rows), F32), pltpu.VMEM((depth, rows), BF16), pltpu.VMEM(spread_shape, F32)],
         [tab, w_one] + [held(v) for v in (x_a, x_b, prod_one)],
         [blocks] * 2,
         vmem=12,
@@ -449,18 +488,17 @@
     far_rims = [swap(rim, "chan", 2 * j) for j in range(1, pairs)]
     full_other = swap(full, "chan", 1)
 
-    grad_outs = [pltpu.VMEM((slabs // 2, share, flat), F32), pltpu.VMEM((slabs // 2, share, flat), BF16)]
-    total_scratch = pltpu.VMEM((slabs, share, flat), F32)
+    total = pltpu.VMEM((slabs // 2, 2, share, flat), F32)
     keep_one, send_one = call(
         grad_one_body,
-        grad_outs,
+        [pltpu.VMEM((slabs // 2, share, flat), F32), pltpu.VMEM((slabs // 2, share, flat), BF16)],
         [tab] + [held(v) for v in (z_one, inner, from_a, from_b, x_wide, x_a, x_b)],
-        [pltpu.VMEM((depth, rows), F32), blocks, pltpu.VMEM((flat, reach), BF16), ext, total_scratch],
+        [pltpu.VMEM((depth, rows), F32), blocks, pltpu.VMEM(spread_shape, BF16), ext, total],
         vmem=26,
         flops=work,
         traffic=16 << 20,
     )
-    grad_one = reduce_slabs(keep_one, send_one)
+    got_one = swap(send_one, "space", 1)
 
     pieces = [full, full_other]
     for got, got_rim in zip(far, far_rims):
@@ -468,25 +506,46 @@
             append_body, [pltpu.VMEM((depth, reach), BF16)], [held(got), held(got_rim)], traffic=1 << 20, after=[keep_one]
         )
         pieces += [got, swap(got, "chan", 1)]
-    keep_two, send_two = call(
+    cut = min(Y_FIRST, offsets) * depth
+    far_part = (2, share, flat - cut)
+    keep_two, send_two, mine_far, *sends_far = call(
         functools.partial(grad_two_body, order),
-        grad_outs,
+        [
+            pltpu.VMEM((slabs // 2, share, cut), F32),
+            pltpu.VMEM((slabs // 2, share, cut), BF16),
+            pltpu.VMEM(far_part, F32),
+        ]
+        + [pltpu.VMEM(far_part, BF16)] * (slabs // 2 - 1),
         [held(v) for v in [spread_two] + pieces],
-        [ext, total_scratch],
+        [ext, total],
         vmem=14,
         flops=work,
         traffic=8 << 20,
     )
-    grad_two = reduce_slabs(keep_two, send_two)
-    (output,) = call(
+    gots_far = [swap(v, "space", 2 * (j + 1)) for j, v in enumerate(sends_far)]
+    got_two = swap(send_two, "space", 1)
+    group_one = reduce_far(keep_one, got_one, [])
+    output, done = call(
         functools.partial(output_body, order),
-        [jax.ShapeDtypeStruct((depth, rows), BF16)],
+        [jax.ShapeDtypeStruct((depth, rows), BF16), pltpu.VMEM((8, BLK), F32)],
         [tab, w_two] + [held(v) for v in pieces],
         conv_scratch,
         vmem=34,
-        flops=work,
+        flops=8 * work,
         traffic=16 << 20,
-    )
+        after=[group_one[0]],
+    )
+    keep_far, send_far = call(
+        functools.partial(split_body, len(gots_far)),
+        [pltpu.VMEM(far_part[1:], F32), pltpu.VMEM(far_part[1:], BF16)],
+        [held(v) for v in [mine_far] + gots_far],
+        traffic=1 << 20,
+        after=[done],
+    )
+    got_far = swap(send_far, "space", 1)
+    group_two = reduce_far(keep_two, got_two, [keep_far])
+    grad_one = finish(group_one)
+    grad_two = finish(group_two, [keep_far, got_far])
     return output.T, grad_one, grad_two
 
 

time: 84.8 us -> 80.7 us (0.952)
  Pallas kernels: 36.2 us -> 32.7 us
  starting transfers between devices: 31.9 us -> 35.2 us
  waiting for transfers between devices: 14.9 us -> 11.8 us
  local copies, waits for them, and re-layouts: 0.96 us -> 0.01 us
    pallas_call x16 -> x17, Pallas kernels: 36.2 us -> 32.7 us  [call(): return kernel(*ins)]
    ppermute x19 -> x23, starting transfers between devices: 30.5 us -> 33.7 us  [swap(): lax.ppermute(value, axis, [(i, i ^ bits) for i in range(lax.axis_size(axi...]
    ppermute x19 -> x23, waiting for transfers between devices: 14.9 us -> 11.8 us  [swap(): lax.ppermute(value, axis, [(i, i ^ bits) for i in range(lax.axis_size(axi...]
    unnamed x6 -> x4, local copies, waits for them, and re-layouts: 0.96 us -> 0.01 us
  transfers between devices with their start and end apart: 21 -> 25, of which waited for: 8 -> 7; matrix products, arithmetic and copies ran while one was open for 0% -> 0% of each run, Pallas kernels for 41% -> 39%
where the time goes in v4:
time: 80.7 us; the launch traced here: 80.6 us
  starting transfers between devices  35.2 us (44%)
  Pallas kernels  32.7 us (41%)
  waiting for transfers between devices  11.8 us (15%)
    ppermute x23, starting transfers between devices, swap(): lax.ppermute(value, axis, [(i, i ^ bits) for i in range(lax.axis_size(axi...  33.7 us
    pallas_call x17, Pallas kernels, call(): return kernel(*ins)  32.7 us
    ppermute x23, waiting for transfers between devices, swap(): lax.ppermute(value, axis, [(i, i ^ bits) for i in range(lax.axis_size(axi...  11.8 us
  transfers between devices with their start and end apart: 25, of which 7 were waited for; matrix products, arithmetic and copies ran while one was open for 0% of the time, Pallas kernels for 39%

profile of v4, /device:TPU:0, one launch (start us, length us, event | category | flops | bytes accessed | tf_op | source)
XLA Modules:
  0.0 80.6 jit_solution(8329387169254374570)
XLA Ops:
  0.6 3.0 %collective-permute-start.1 = (bf16[64,2048]{1,0:T(8,128)(2,1)}, bf16[64,2048]{1,0:T(8,128)(2,1)S(1)}, u32[]{:S(2)}, u32[]{:S(2)}) collective-permute-start(bf16[64,2048]{1,0:T(8,128)(2,1)} %bitcast.17), channel_id=1, source_target_pairs={{0,2},{1,3},{2,0},{3,1},{4,6},{5,7},{6,4},{7,5},{8,10},{9,11},{10,... | collective-permute-start | bytes 786440 | tf_op jit(solution)/shard_map/ppermute | solution.py:354
  3.6 0.0 collective-permute-start
  3.6 7.8 %input_grad_body.1 = (s32[24,27]{1,0:T(8,128)S(1)}, bf16[20,1728,128]{2,1,0:T(8,128)(2,1)S(1)}, bf16[2,64,2560]{2,1,0:T(8,128)(2,1)S(1)}, bf16[2,64,2560]{2,1,0:T(8,128)(2,1)S(1)}, bf16[64,2048]{1,0:T(8,128)(2,1)S(1)}) custom-call(s32[8]{0:T(128)} %refs_0_.1, s32[3,16,27]{2,1,0:T(8,128)} %bitcast.20, bf16[64,2048]{1,0:T(8,128)(2,1)} %bitcast.16, ...), custom_call_target="tpu_custom_call" | custom-call | flops 2264924160 | bytes 16777216 | tf_op jit(solution)/shard_map/input_grad_body/pallas_call | solution.py:49
  11.5 0.0 collective-permute-done.1.refs_0_
  11.5 0.6 collective-permute-start.2
  12.1 0.1 collective-permute-start.5
  12.2 0.0 collective-permute-done.refs_2_
  12.2 1.1 %collective-permute-done.2.refs_4_ = bf16[64,2048]{1,0:T(8,128)(2,1)S(1)} collective-permute-done((bf16[64,2048]{1,0:T(8,128)(2,1)S(1)}, bf16[64,2048]{1,0:T(8,128)(2,1)S(1)}, u32[]{:S(2)}, u32[]{:S(2)}) %collective-permute-start.2) | collective-permute-done | bytes 262176 | tf_op jit(solution)/shard_map/ppermute | solution.py:354
  13.2 0.8 %join_body.1 = (bf16[256,2048]{1,0:T(8,128)(2,1)S(1)}, bf16[256,256]{1,0:T(8,128)(2,1)S(1)}, bf16[256,256]{1,0:T(8,128)(2,1)S(1)}) custom-call(s32[24,27]{1,0:T(8,128)S(1)} %get-tuple-element.40.refs_0_, bf16[64,2048]{1,0:T(8,128)(2,1)S(1)} %get-tuple-element.41.refs_1_, bf16[64,2048]{1,0:T(8,128)(2,1)S(1)} %collective-permute-done.refs_2_, ...), custom_call_target="tpu_custom_call" | custom-call | flops 18119393280 | bytes 2097152 | tf_op jit(solution)/shard_map/join_body/pallas_call | solution.py:49
  14.1 0.7 collective-permute-start.4
  14.8 4.4 %collective-permute-start.3 = (bf16[256,256]{1,0:T(8,128)(2,1)S(1)}, bf16[256,256]{1,0:T(8,128)(2,1)S(1)}, u32[]{:S(2)}, u32[]{:S(2)}) collective-permute-start(bf16[256,256]{1,0:T(8,128)(2,1)S(1)} %get-tuple-element.43.refs_2_), channel_id=1, source_target_pairs={{0,4},{4,0},{8,12},{12,8},{16,20},{20,16},{24,28},{28,24},{1,5},{5... | collective-permute-start | bytes 393224 | tf_op jit(solution)/shard_map/ppermute | solution.py:354
  19.1 0.0 collective-permute-done.5.refs_1_
  19.1 0.2 halve_body.3
  19.3 0.6 collective-permute-start.6
  19.9 2.0 %inner_body.1.refs_4_ = f32[20,1728,128]{2,1,0:T(8,128)S(1)} custom-call(bf16[1728,256]{1,0:T(8,128)(2,1)S(1)} %bitcast.10, bf16[256,2048]{1,0:T(8,128)(2,1)S(1)} %get-tuple-element.45.refs_1_.refs_5_, f32[64,2560]{1,0:T(8,128)S(1)} %get-tuple-element.47.refs_2_), custom_call_target="tpu_custom_call" | custom-call | flops 2264924160 | bytes 16777216 | tf_op jit(solution)/shard_map/inner_body/pallas_call | solution.py:49
  21.9 0.0 copy-start.1
  21.9 2.6 %collective-permute-done.3.refs_2_.refs_6_ = bf16[256,256]{1,0:T(8,128)(2,1)S(1)} collective-permute-done((bf16[256,256]{1,0:T(8,128)(2,1)S(1)}, bf16[256,256]{1,0:T(8,128)(2,1)S(1)}, u32[]{:S(2)}, u32[]{:S(2)}) %collective-permute-start.3) | collective-permute-done | bytes 131104 | tf_op jit(solution)/shard_map/ppermute | solution.py:354
  24.5 3.2 %hidden_body.1 = (f32[64,2048]{1,0:T(8,128)S(1)}, bf16[64,2048]{1,0:T(8,128)(2,1)S(1)}, f32[20,1728,128]{2,1,0:T(8,128)S(1)}) custom-call(s32[24,27]{1,0:T(8,128)S(1)} %get-tuple-element.40.refs_0_, bf16[1728,256]{1,0:T(8,128)(2,1)S(1)} %bitcast.11, bf16[256,256]{1,0:T(8,128)(2,1)S(1)} %collective-permute-done.3.refs_2_.refs_6_, ...), custom_call_target="tpu_custom_call", output_to_operand_aliasing={{2}: (4, {})} | custom-call | flops 2264924160 | bytes 16777216 | tf_op jit(solution)/shard_map/hidden_body/pallas_call | solution.py:49
  27.7 1.0 %collective-permute-done.6.refs_3_ = bf16[64,2560]{1,0:T(8,128)(2,1)S(1)} collective-permute-done((bf16[64,2560]{1,0:T(8,128)(2,1)S(1)}, bf16[64,2560]{1,0:T(8,128)(2,1)S(1)}, u32[]{:S(2)}, u32[]{:S(2)}) %collective-permute-start.6) | collective-permute-done | bytes 327712 | tf_op jit(solution)/shard_map/ppermute | solution.py:354
  28.8 0.8 turn_body.1
  29.6 1.5 %collective-permute-start.7 = (bf16[2,64,256]{2,1,0:T(8,128)(2,1)S(1)}, bf16[2,64,256]{2,1,0:T(8,128)(2,1)S(1)}, u32[]{:S(2)}, u32[]{:S(2)}) collective-permute-start(bf16[2,64,256]{2,1,0:T(8,128)(2,1)S(1)} %get-tuple-element.50), channel_id=1, source_target_pairs={{0,4},{4,0},{8,12},{12,8},{16,20},{20,16},{24,28},{28,24},{1,5},{5... | collective-permute-start | bytes 196616 | tf_op jit(solution)/shard_map/ppermute | solution.py:354
  31.1 0.8 %collective-permute-start.8 = (bf16[2,64,256]{2,1,0:T(8,128)(2,1)S(1)}, bf16[2,64,256]{2,1,0:T(8,128)(2,1)S(1)}, u32[]{:S(2)}, u32[]{:S(2)}) collective-permute-start(bf16[2,64,256]{2,1,0:T(8,128)(2,1)S(1)} %get-tuple-element.51), channel_id=1, source_target_pairs={{4,8},{12,16},{20,24},{8,4},{16,12},{24,20},{5,9},{13,17},{21,25},... | collective-permute-start | bytes 196616 | tf_op jit(solution)/shard_map/ppermute | solution.py:359
  32.0 0.6 collective-permute-start.10
  32.6 1.3 %collective-permute-done.7.refs_1_.refs_3_ = bf16[2,64,256]{2,1,0:T(8,128)(2,1)S(1)} collective-permute-done((bf16[2,64,256]{2,1,0:T(8,128)(2,1)S(1)}, bf16[2,64,256]{2,1,0:T(8,128)(2,1)S(1)}, u32[]{:S(2)}, u32[]{:S(2)}) %collective-permute-start.7) | collective-permute-done | bytes 65568 | tf_op jit(solution)/shard_map/ppermute | solution.py:354
  33.9 0.6 collective-permute-start.11
  34.5 6.8 %grad_one_body.1 = (f32[4,32,1728]{2,1,0:T(8,128)S(1)}, bf16[4,32,1728]{2,1,0:T(8,128)(2,1)S(1)}) custom-call(s32[24,27]{1,0:T(8,128)S(1)} %get-tuple-element.40.refs_0_, f32[64,2048]{1,0:T(8,128)S(1)} %get-tuple-element.54.refs_1_, f32[64,2048]{1,0:T(8,128)S(1)} %get-tuple-element.55.refs_2_, ...), custom_call_target="tpu_custom_call" | custom-call | flops 2264924160 | bytes 16777216 | tf_op jit(solution)/shard_map/grad_one_body/pallas_call | solution.py:49
  41.4 0.6 collective-permute-start.12
  42.0 4.8 %collective-permute-start.13 = (bf16[4,32,1728]{2,1,0:T(8,128)(2,1)S(1)}, bf16[4,32,1728]{2,1,0:T(8,128)(2,1)S(1)}, u32[]{:S(2)}, u32[]{:S(2)}) collective-permute-start(bf16[4,32,1728]{2,1,0:T(8,128)(2,1)S(1)} %get-tuple-element.57), channel_id=1, source_target_pairs={{0,4},{4,0},{8,12},{12,8},{16,20},{20,16},{24,28},{28,24},{1,5},{5... | collective-permute-start | bytes 1327112 | tf_op jit(solution)/shard_map/ppermute | solution.py:354
  46.8 3.2 %grad_two_body.1 = (f32[4,32,1280]{2,1,0:T(8,128)S(1)}, bf16[4,32,1280]{2,1,0:T(8,128)(2,1)S(1)}, f32[2,32,448]{2,1,0:T(8,128)S(1)}, bf16[2,32,448]{2,1,0:T(8,12...) custom-call(bf16[20,1728,128]{2,1,0:T(8,128)(2,1)S(1)} %get-tuple-element.63.refs_0_, ...), custom_call_target="tpu_custom_call" | custom-call | flops 2264924160 | bytes 8388608 | tf_op jit(solution)/shard_map/grad_two_body/pallas_call | solution.py:49
  50.0 2.4 %collective-permute-start.18 = (bf16[2,32,448]{2,1,0:T(8,128)(2,1)S(1)}, bf16[2,32,448]{2,1,0:T(8,128)(2,1)S(1)}, u32[]{:S(2)}, u32[]{:S(2)}) collective-permute-start(bf16[2,32,448]{2,1,0:T(8,128)(2,1)S(1)} %get-tuple-element.67), channel_id=1, source_target_pairs={{0,8},{4,12},{8,0},{12,4},{16,24},{20,28},{24,16},{28,20},{1,9},{5... | collective-permute-start | bytes 172040 | tf_op jit(solution)/shard_map/ppermute | solution.py:354
  52.3 1.5 %collective-permute-start.19 = (bf16[2,32,448]{2,1,0:T(8,128)(2,1)S(1)}, bf16[2,32,448]{2,1,0:T(8,128)(2,1)S(1)}, u32[]{:S(2)}, u32[]{:S(2)}) collective-permute-start(bf16[2,32,448]{2,1,0:T(8,128)(2,1)S(1)} %get-tuple-element.68), channel_id=1, source_target_pairs={{0,16},{4,20},{8,24},{12,28},{16,0},{20,4},{24,8},{28,12},{1,17},{... | collective-permute-start | bytes 172040 | tf_op jit(solution)/shard_map/ppermute | solution.py:354
  53.9 1.0 %collective-permute-start.20 = (bf16[2,32,448]{2,1,0:T(8,128)(2,1)S(1)}, bf16[2,32,448]{2,1,0:T(8,128)(2,1)S(1)}, u32[]{:S(2)}, u32[]{:S(2)}) collective-permute-start(bf16[2,32,448]{2,1,0:T(8,128)(2,1)S(1)} %get-tuple-element.69), channel_id=1, source_target_pairs={{0,24},{4,28},{8,16},{12,20},{16,8},{20,12},{24,0},{28,4},{1,25},{... | collective-permute-start | bytes 172040 | tf_op jit(solution)/shard_map/ppermute | solution.py:354
  54.8 0.9 %collective-permute-start.17 = (bf16[4,32,1280]{2,1,0:T(8,128)(2,1)S(1)}, bf16[4,32,1280]{2,1,0:T(8,128)(2,1)S(1)}, u32[]{:S(2)}, u32[]{:S(2)}) collective-permute-start(bf16[4,32,1280]{2,1,0:T(8,128)(2,1)S(1)} %get-tuple-element.65), channel_id=1, source_target_pairs={{0,4},{4,0},{8,12},{12,8},{16,20},{20,16},{24,28},{28,24},{1,5},{5... | collective-permute-start | bytes 983048 | tf_op jit(solution)/shard_map/ppermute | solution.py:354
  55.7 2.2 %collective-permute-done.13.refs_1_ = bf16[4,32,1728]{2,1,0:T(8,128)(2,1)S(1)} collective-permute-done((bf16[4,32,1728]{2,1,0:T(8,128)(2,1)S(1)}, bf16[4,32,1728]{2,1,0:T(8,128)(2,1)S(1)}, u32[]{:S(2)}, u32[]{:S(2)}) %collective-permute-start.13) | collective-permute-done | bytes 442400 | tf_op jit(solution)/shard_map/ppermute | solution.py:354
  57.9 0.1 halve_body.4
  58.0 3.4 %collective-permute-start.14 = (bf16[32,1728]{1,0:T(8,128)(2,1)S(1)}, bf16[32,1728]{1,0:T(8,128)(2,1)S(1)}, u32[]{:S(2)}, u32[]{:S(2)}) collective-permute-start(bf16[32,1728]{1,0:T(8,128)(2,1)S(1)} %get-tuple-element.60), channel_id=1, source_target_pairs={{0,8},{4,12},{8,0},{12,4},{16,24},{20,28},{24,16},{28,20},{1,9},{5... | collective-permute-start | bytes 331784 | tf_op jit(solution)/shard_map/ppermute | solution.py:354
  61.4 1.5 %collective-permute-start.15 = (bf16[32,1728]{1,0:T(8,128)(2,1)S(1)}, bf16[32,1728]{1,0:T(8,128)(2,1)S(1)}, u32[]{:S(2)}, u32[]{:S(2)}) collective-permute-start(bf16[32,1728]{1,0:T(8,128)(2,1)S(1)} %get-tuple-element.61), channel_id=1, source_target_pairs={{0,16},{4,20},{8,24},{12,28},{16,0},{20,4},{24,8},{28,12},{1,17},{... | collective-permute-start | bytes 331784 | tf_op jit(solution)/shard_map/ppermute | solution.py:354
  62.9 1.0 %collective-permute-start.16 = (bf16[32,1728]{1,0:T(8,128)(2,1)S(1)}, bf16[32,1728]{1,0:T(8,128)(2,1)S(1)}, u32[]{:S(2)}, u32[]{:S(2)}) collective-permute-start(bf16[32,1728]{1,0:T(8,128)(2,1)S(1)} %get-tuple-element.62), channel_id=1, source_target_pairs={{0,24},{4,28},{8,16},{12,20},{16,8},{20,12},{24,0},{28,4},{1,25},{... | collective-permute-start | bytes 331784 | tf_op jit(solution)/shard_map/ppermute | solution.py:354
  63.9 5.8 %output_body.1 = (bf16[64,2048]{1,0:T(8,128)(2,1)}, f32[8,128]{1,0:T(8,128)S(1)}) custom-call(s32[24,27]{1,0:T(8,128)S(1)} %get-tuple-element.40.refs_0_, bf16[1728,256]{1,0:T(8,128)(2,1)S(1)} %bitcast.13, bf16[64,2560]{1,0:T(8,128)(2,1)S(1)} %get-tuple-element.52.refs_2_.refs_1_, bf16[64,2560]{1,0:T(8,128)(2,1)S(1)} %collective-permute-done.9.refs_3_.refs_2_, ...), custom_call_target="tpu_custom_call" | custom-call | flops 18119393280 | bytes 16777216 | tf_op jit(solution)/shard_map/output_body/pallas_call | solution.py:49
  69.8 0.1 halve_body.5
  69.9 1.0 %collective-permute-start.21 = (bf16[32,1280]{1,0:T(8,128)(2,1)S(1)}, bf16[32,1280]{1,0:T(8,128)(2,1)S(1)}, u32[]{:S(2)}, u32[]{:S(2)}) collective-permute-start(bf16[32,1280]{1,0:T(8,128)(2,1)S(1)} %get-tuple-element.73), channel_id=1, source_target_pairs={{0,8},{4,12},{8,0},{12,4},{16,24},{20,28},{24,16},{28,20},{1,9},{5... | collective-permute-start | bytes 245768 | tf_op jit(solution)/shard_map/ppermute | solution.py:354
  70.9 2.4 %collective-permute-start.22 = (bf16[32,1280]{1,0:T(8,128)(2,1)S(1)}, bf16[32,1280]{1,0:T(8,128)(2,1)S(1)}, u32[]{:S(2)}, u32[]{:S(2)}) collective-permute-start(bf16[32,1280]{1,0:T(8,128)(2,1)S(1)} %get-tuple-element.74), channel_id=1, source_target_pairs={{0,16},{4,20},{8,24},{12,28},{16,0},{20,4},{24,8},{28,12},{1,17},{... | collective-permute-start | bytes 245768 | tf_op jit(solution)/shard_map/ppermute | solution.py:354
  73.3 1.0 %collective-permute-start.23 = (bf16[32,1280]{1,0:T(8,128)(2,1)S(1)}, bf16[32,1280]{1,0:T(8,128)(2,1)S(1)}, u32[]{:S(2)}, u32[]{:S(2)}) collective-permute-start(bf16[32,1280]{1,0:T(8,128)(2,1)S(1)} %get-tuple-element.75), channel_id=1, source_target_pairs={{0,24},{4,28},{8,16},{12,20},{16,8},{20,12},{24,0},{28,4},{1,25},{... | collective-permute-start | bytes 245768 | tf_op jit(solution)/shard_map/ppermute | solution.py:354
  74.3 0.8 %collective-permute-start.24 = (bf16[32,448]{1,0:T(8,128)(2,1)S(1)}, bf16[32,448]{1,0:T(8,128)(2,1)S(1)}, u32[]{:S(2)}, u32[]{:S(2)}) collective-permute-start(bf16[32,448]{1,0:T(8,128)(2,1)S(1)} %get-tuple-element.76), channel_id=1, source_target_pairs={{0,4},{4,0},{8,12},{12,8},{16,20},{20,16},{24,28},{28,24},{1,5},{5... | collective-permute-start | bytes 86024 | tf_op jit(solution)/shard_map/ppermute | solution.py:354
  75.2 0.9 %finish_body.2 = f32[27,32,64]{2,1,0:T(8,128)} custom-call(f32[32,1728]{1,0:T(8,128)S(1)} %get-tuple-element.58.refs_6_.refs_0_, bf16[32,1728]{1,0:T(8,128)(2,1)S(1)} %collective-permute-done.14.refs_1_, bf16[32,1728]{1,0:T(8,128)(2,1)S(1)} %collective-permute-done.15.refs_2_, bf16[32,1728]{1,0:T(8,128)(2,1)S(1)} %collective-permute-done.16.refs_3_), custom_call_target="tpu_custom_call" | custom-call | bytes 2097152 | tf_op jit(solution)/shard_map/finish_body/pallas_call | solution.py:49
  76.1 2.2 %collective-permute-done.24.refs_5_ = bf16[32,448]{1,0:T(8,128)(2,1)S(1)} collective-permute-done((bf16[32,448]{1,0:T(8,128)(2,1)S(1)}, bf16[32,448]{1,0:T(8,128)(2,1)S(1)}, u32[]{:S(2)}, u32[]{:S(2)}) %collective-permute-start.24) | collective-permute-done | bytes 28704 | tf_op jit(solution)/shard_map/ppermute | solution.py:354
  78.3 1.4 %collective-permute-done.23.refs_3_ = bf16[32,1280]{1,0:T(8,128)(2,1)S(1)} collective-permute-done((bf16[32,1280]{1,0:T(8,128)(2,1)S(1)}, bf16[32,1280]{1,0:T(8,128)(2,1)S(1)}, u32[]{:S(2)}, u32[]{:S(2)}) %collective-permute-start.23) | collective-permute-done | bytes 81952 | tf_op jit(solution)/shard_map/ppermute | solution.py:354
  79.7 0.9 %finish_body.3 = f32[27,32,64]{2,1,0:T(8,128)} custom-call(f32[32,1280]{1,0:T(8,128)S(1)} %get-tuple-element.72.refs_0_, bf16[32,1280]{1,0:T(8,128)(2,1)S(1)} %collective-permute-done.21.refs_1_, bf16[32,1280]{1,0:T(8,128)(2,1)S(1)} %collective-permute-done.22.refs_2_, bf16[32,1280]{1,0:T(8,128)(2,1)S(1)} %collective-permute-done.23.refs_3_, ...), custom_call_target="tpu_custom_call" | custom-call | bytes 2097152 | tf_op jit(solution)/shard_map/finish_body/pallas_call | solution.py:49
  (23 shorter events, 0.1 us)
Async XLA Ops:
  0.6 10.8 %collective-permute-start.1 = (bf16[64,2048]{1,0:T(8,128)(2,1)}, bf16[64,2048]{1,0:T(8,128)(2,1)S(1)}, u32[]{:S(2)}, u32[]{:S(2)}) collective-permute-start(bf16[64,2048]{1,0:T(8,128)(2,1)} %bitcast.17), channel_id=1, source_target_pairs={{0,2},{1,3},{2,0},{3,1},{4,6},{5,7},{6,4},{7,5},{8,10},{9,11},{10,... | collective-permute-start | bytes 786440 | tf_op jit(solution)/shard_map/ppermute | solution.py:354
  3.6 8.5 %collective-permute-start = (bf16[64,2048]{1,0:T(8,128)(2,1)}, bf16[64,2048]{1,0:T(8,128)(2,1)S(1)}, u32[]{:S(2)}, u32[]{:S(2)}) collective-permute-start(bf16[64,2048]{1,0:T(8,128)(2,1)} %bitcast.18), channel_id=1, source_target_pairs={{0,1},{1,0},{2,3},{3,2},{4,5},{5,4},{6,7},{7,6},{8,9},{9,8},{10,11... | collective-permute-start | bytes 786440 | tf_op jit(solution)/shard_map/ppermute | solution.py:354
  11.5 1.7 %collective-permute-start.2 = (bf16[64,2048]{1,0:T(8,128)(2,1)S(1)}, bf16[64,2048]{1,0:T(8,128)(2,1)S(1)}, u32[]{:S(2)}, u32[]{:S(2)}) collective-permute-start(bf16[64,2048]{1,0:T(8,128)(2,1)S(1)} %pass_body.1.refs_3_), channel_id=1, source_target_pairs={{0,1},{1,0},{2,3},{3,2},{4,5},{5,4},{6,7},{7,6},{8,9},{9,8},{10,11... | collective-permute-start | bytes 786440 | tf_op jit(solution)/shard_map/ppermute | solution.py:354
  12.1 7.0 %collective-permute-start.5 = (bf16[2,64,2560]{2,1,0:T(8,128)(2,1)S(1)}, bf16[2,64,2560]{2,1,0:T(8,128)(2,1)S(1)}, u32[]{:S(2)}, u32[]{:S(2)}) collective-permute-start(bf16[2,64,2560]{2,1,0:T(8,128)(2,1)S(1)} %get-tuple-element.42.refs_1_), channel_id=1, source_target_pairs={{0,1},{1,0},{2,3},{3,2},{4,5},{5,4},{6,7},{7,6},{8,9},{9,8},{10,11... | collective-permute-start | bytes 1966088 | tf_op jit(solution)/shard_map/ppermute | solution.py:354
  13.2 6.7 %copy-start = (bf16[27,64,256]{2,1,0:T(8,128)(2,1)S(1)}, bf16[27,64,256]{2,1,0:T(8,128)(2,1)}, u32[]{:S(2)}) copy-start(bf16[27,64,256]{2,1,0:T(8,128)(2,1)} %param.9) | copy-start | bytes 2654212
  14.1 7.8 %collective-permute-start.4 = (bf16[256,256]{1,0:T(8,128)(2,1)S(1)}, bf16[256,256]{1,0:T(8,128)(2,1)S(1)}, u32[]{:S(2)}, u32[]{:S(2)}) collective-permute-start(bf16[256,256]{1,0:T(8,128)(2,1)S(1)} %get-tuple-element.44), channel_id=1, source_target_pairs={{4,8},{12,16},{20,24},{8,4},{16,12},{24,20},{5,9},{13,17},{21,25},... | collective-permute-start | bytes 393224 | tf_op jit(solution)/shard_map/ppermute | solution.py:359
  14.8 9.7 %collective-permute-start.3 = (bf16[256,256]{1,0:T(8,128)(2,1)S(1)}, bf16[256,256]{1,0:T(8,128)(2,1)S(1)}, u32[]{:S(2)}, u32[]{:S(2)}) collective-permute-start(bf16[256,256]{1,0:T(8,128)(2,1)S(1)} %get-tuple-element.43.refs_2_), channel_id=1, source_target_pairs={{0,4},{4,0},{8,12},{12,8},{16,20},{20,16},{24,28},{28,24},{1,5},{5... | collective-permute-start | bytes 393224 | tf_op jit(solution)/shard_map/ppermute | solution.py:354
  19.3 9.5 %collective-permute-start.6 = (bf16[64,2560]{1,0:T(8,128)(2,1)S(1)}, bf16[64,2560]{1,0:T(8,128)(2,1)S(1)}, u32[]{:S(2)}, u32[]{:S(2)}) collective-permute-start(bf16[64,2560]{1,0:T(8,128)(2,1)S(1)} %get-tuple-element.49), channel_id=1, source_target_pairs={{0,2},{1,3},{2,0},{3,1},{4,6},{5,7},{6,4},{7,5},{8,10},{9,11},{10,... | collective-permute-start | bytes 983048 | tf_op jit(solution)/shard_map/ppermute | solution.py:354
  21.9 42.0 %copy-start.1 = (bf16[27,64,256]{2,1,0:T(8,128)(2,1)S(1)}, bf16[27,64,256]{2,1,0:T(8,128)(2,1)}, u32[]{:S(2)}) copy-start(bf16[27,64,256]{2,1,0:T(8,128)(2,1)} %param.10) | copy-start | bytes 2654212
  29.6 4.3 %collective-permute-start.7 = (bf16[2,64,256]{2,1,0:T(8,128)(2,1)S(1)}, bf16[2,64,256]{2,1,0:T(8,128)(2,1)S(1)}, u32[]{:S(2)}, u32[]{:S(2)}) collective-permute-start(bf16[2,64,256]{2,1,0:T(8,128)(2,1)S(1)} %get-tuple-element.50), channel_id=1, source_target_pairs={{0,4},{4,0},{8,12},{12,8},{16,20},{20,16},{24,28},{28,24},{1,5},{5... | collective-permute-start | bytes 196616 | tf_op jit(solution)/shard_map/ppermute | solution.py:354
  31.1 2.8 %collective-permute-start.8 = (bf16[2,64,256]{2,1,0:T(8,128)(2,1)S(1)}, bf16[2,64,256]{2,1,0:T(8,128)(2,1)S(1)}, u32[]{:S(2)}, u32[]{:S(2)}) collective-permute-start(bf16[2,64,256]{2,1,0:T(8,128)(2,1)S(1)} %get-tuple-element.51), channel_id=1, source_target_pairs={{4,8},{12,16},{20,24},{8,4},{16,12},{24,20},{5,9},{13,17},{21,25},... | collective-permute-start | bytes 196616 | tf_op jit(solution)/shard_map/ppermute | solution.py:359
  32.0 9.4 %collective-permute-start.10 = (bf16[64,2048]{1,0:T(8,128)(2,1)S(1)}, bf16[64,2048]{1,0:T(8,128)(2,1)S(1)}, u32[]{:S(2)}, u32[]{:S(2)}) collective-permute-start(bf16[64,2048]{1,0:T(8,128)(2,1)S(1)} %get-tuple-element.48.refs_1_.refs_0_), channel_id=1, source_target_pairs={{0,2},{1,3},{2,0},{3,1},{4,6},{5,7},{6,4},{7,5},{8,10},{9,11},{10,... | collective-permute-start | bytes 786440 | tf_op jit(solution)/shard_map/ppermute | solution.py:354
  33.9 7.5 %collective-permute-start.11 = (bf16[64,512]{1,0:T(8,128)(2,1)S(1)}, bf16[64,512]{1,0:T(8,128)(2,1)S(1)}, u32[]{:S(2)}, u32[]{:S(2)}) collective-permute-start(bf16[64,512]{1,0:T(8,128)(2,1)S(1)} %get-tuple-element.53), channel_id=1, source_target_pairs={{0,2},{1,3},{2,0},{3,1},{4,6},{5,7},{6,4},{7,5},{8,10},{9,11},{10,... | collective-permute-start | bytes 196616 | tf_op jit(solution)/shard_map/ppermute | solution.py:354
  34.5 12.3 %collective-permute-start.9 = (bf16[64,2560]{1,0:T(8,128)(2,1)S(1)}, bf16[64,2560]{1,0:T(8,128)(2,1)S(1)}, u32[]{:S(2)}, u32[]{:S(2)}) collective-permute-start(bf16[64,2560]{1,0:T(8,128)(2,1)S(1)} %get-tuple-element.52.refs_2_.refs_1_), channel_id=1, source_target_pairs={{0,1},{1,0},{2,3},{3,2},{4,5},{5,4},{6,7},{7,6},{8,9},{9,8},{10,11... | collective-permute-start | bytes 983048 | tf_op jit(solution)/shard_map/ppermute | solution.py:354
  41.4 5.4 %collective-permute-start.12 = (bf16[64,2560]{1,0:T(8,128)(2,1)S(1)}, bf16[64,2560]{1,0:T(8,128)(2,1)S(1)}, u32[]{:S(2)}, u32[]{:S(2)}) collective-permute-start(bf16[64,2560]{1,0:T(8,128)(2,1)S(1)} %append_body.1.refs_4_.refs_3_), channel_id=1, source_target_pairs={{0,1},{1,0},{2,3},{3,2},{4,5},{5,4},{6,7},{7,6},{8,9},{9,8},{10,11... | collective-permute-start | bytes 983048 | tf_op jit(solution)/shard_map/ppermute | solution.py:354
  42.0 15.9 %collective-permute-start.13 = (bf16[4,32,1728]{2,1,0:T(8,128)(2,1)S(1)}, bf16[4,32,1728]{2,1,0:T(8,128)(2,1)S(1)}, u32[]{:S(2)}, u32[]{:S(2)}) collective-permute-start(bf16[4,32,1728]{2,1,0:T(8,128)(2,1)S(1)} %get-tuple-element.57), channel_id=1, source_target_pairs={{0,4},{4,0},{8,12},{12,8},{16,20},{20,16},{24,28},{28,24},{1,5},{5... | collective-permute-start | bytes 1327112 | tf_op jit(solution)/shard_map/ppermute | solution.py:354
  50.0 11.4 %collective-permute-start.18 = (bf16[2,32,448]{2,1,0:T(8,128)(2,1)S(1)}, bf16[2,32,448]{2,1,0:T(8,128)(2,1)S(1)}, u32[]{:S(2)}, u32[]{:S(2)}) collective-permute-start(bf16[2,32,448]{2,1,0:T(8,128)(2,1)S(1)} %get-tuple-element.67), channel_id=1, source_target_pairs={{0,8},{4,12},{8,0},{12,4},{16,24},{20,28},{24,16},{28,20},{1,9},{5... | collective-permute-start | bytes 172040 | tf_op jit(solution)/shard_map/ppermute | solution.py:354
  52.3 10.6 %collective-permute-start.19 = (bf16[2,32,448]{2,1,0:T(8,128)(2,1)S(1)}, bf16[2,32,448]{2,1,0:T(8,128)(2,1)S(1)}, u32[]{:S(2)}, u32[]{:S(2)}) collective-permute-start(bf16[2,32,448]{2,1,0:T(8,128)(2,1)S(1)} %get-tuple-element.68), channel_id=1, source_target_pairs={{0,16},{4,20},{8,24},{12,28},{16,0},{20,4},{24,8},{28,12},{1,17},{... | collective-permute-start | bytes 172040 | tf_op jit(solution)/shard_map/ppermute | solution.py:354
  53.9 15.9 %collective-permute-start.20 = (bf16[2,32,448]{2,1,0:T(8,128)(2,1)S(1)}, bf16[2,32,448]{2,1,0:T(8,128)(2,1)S(1)}, u32[]{:S(2)}, u32[]{:S(2)}) collective-permute-start(bf16[2,32,448]{2,1,0:T(8,128)(2,1)S(1)} %get-tuple-element.69), channel_id=1, source_target_pairs={{0,24},{4,28},{8,16},{12,20},{16,8},{20,12},{24,0},{28,4},{1,25},{... | collective-permute-start | bytes 172040 | tf_op jit(solution)/shard_map/ppermute | solution.py:354
  54.8 15.0 %collective-permute-start.17 = (bf16[4,32,1280]{2,1,0:T(8,128)(2,1)S(1)}, bf16[4,32,1280]{2,1,0:T(8,128)(2,1)S(1)}, u32[]{:S(2)}, u32[]{:S(2)}) collective-permute-start(bf16[4,32,1280]{2,1,0:T(8,128)(2,1)S(1)} %get-tuple-element.65), channel_id=1, source_target_pairs={{0,4},{4,0},{8,12},{12,8},{16,20},{20,16},{24,28},{28,24},{1,5},{5... | collective-permute-start | bytes 983048 | tf_op jit(solution)/shard_map/ppermute | solution.py:354
  58.0 15.3 %collective-permute-start.14 = (bf16[32,1728]{1,0:T(8,128)(2,1)S(1)}, bf16[32,1728]{1,0:T(8,128)(2,1)S(1)}, u32[]{:S(2)}, u32[]{:S(2)}) collective-permute-start(bf16[32,1728]{1,0:T(8,128)(2,1)S(1)} %get-tuple-element.60), channel_id=1, source_target_pairs={{0,8},{4,12},{8,0},{12,4},{16,24},{20,28},{24,16},{28,20},{1,9},{5... | collective-permute-start | bytes 331784 | tf_op jit(solution)/shard_map/ppermute | solution.py:354
  61.4 12.9 %collective-permute-start.15 = (bf16[32,1728]{1,0:T(8,128)(2,1)S(1)}, bf16[32,1728]{1,0:T(8,128)(2,1)S(1)}, u32[]{:S(2)}, u32[]{:S(2)}) collective-permute-start(bf16[32,1728]{1,0:T(8,128)(2,1)S(1)} %get-tuple-element.61), channel_id=1, source_target_pairs={{0,16},{4,20},{8,24},{12,28},{16,0},{20,4},{24,8},{28,12},{1,17},{... | collective-permute-start | bytes 331784 | tf_op jit(solution)/shard_map/ppermute | solution.py:354
  62.9 12.3 %collective-permute-start.16 = (bf16[32,1728]{1,0:T(8,128)(2,1)S(1)}, bf16[32,1728]{1,0:T(8,128)(2,1)S(1)}, u32[]{:S(2)}, u32[]{:S(2)}) collective-permute-start(bf16[32,1728]{1,0:T(8,128)(2,1)S(1)} %get-tuple-element.62), channel_id=1, source_target_pairs={{0,24},{4,28},{8,16},{12,20},{16,8},{20,12},{24,0},{28,4},{1,25},{... | collective-permute-start | bytes 331784 | tf_op jit(solution)/shard_map/ppermute | solution.py:354
  69.9 8.4 %collective-permute-start.21 = (bf16[32,1280]{1,0:T(8,128)(2,1)S(1)}, bf16[32,1280]{1,0:T(8,128)(2,1)S(1)}, u32[]{:S(2)}, u32[]{:S(2)}) collective-permute-start(bf16[32,1280]{1,0:T(8,128)(2,1)S(1)} %get-tuple-element.73), channel_id=1, source_target_pairs={{0,8},{4,12},{8,0},{12,4},{16,24},{20,28},{24,16},{28,20},{1,9},{5... | collective-permute-start | bytes 245768 | tf_op jit(solution)/shard_map/ppermute | solution.py:354
  70.9 7.4 %collective-permute-start.22 = (bf16[32,1280]{1,0:T(8,128)(2,1)S(1)}, bf16[32,1280]{1,0:T(8,128)(2,1)S(1)}, u32[]{:S(2)}, u32[]{:S(2)}) collective-permute-start(bf16[32,1280]{1,0:T(8,128)(2,1)S(1)} %get-tuple-element.74), channel_id=1, source_target_pairs={{0,16},{4,20},{8,24},{12,28},{16,0},{20,4},{24,8},{28,12},{1,17},{... | collective-permute-start | bytes 245768 | tf_op jit(solution)/shard_map/ppermute | solution.py:354
  73.3 6.3 %collective-permute-start.23 = (bf16[32,1280]{1,0:T(8,128)(2,1)S(1)}, bf16[32,1280]{1,0:T(8,128)(2,1)S(1)}, u32[]{:S(2)}, u32[]{:S(2)}) collective-permute-start(bf16[32,1280]{1,0:T(8,128)(2,1)S(1)} %get-tuple-element.75), channel_id=1, source_target_pairs={{0,24},{4,28},{8,16},{12,20},{16,8},{20,12},{24,0},{28,4},{1,25},{... | collective-permute-start | bytes 245768 | tf_op jit(solution)/shard_map/ppermute | solution.py:354
  74.3 3.9 %collective-permute-start.24 = (bf16[32,448]{1,0:T(8,128)(2,1)S(1)}, bf16[32,448]{1,0:T(8,128)(2,1)S(1)}, u32[]{:S(2)}, u32[]{:S(2)}) collective-permute-start(bf16[32,448]{1,0:T(8,128)(2,1)S(1)} %get-tuple-element.76), channel_id=1, source_target_pairs={{0,4},{4,0},{8,12},{12,8},{16,20},{20,16},{24,28},{28,24},{1,5},{5... | collective-permute-start | bytes 86024 | tf_op jit(solution)/shard_map/ppermute | solution.py:354

commit v5 on v4

--- a/solution.py
+++ b/solution.py
@@ -95,8 +95,8 @@
     depth = blocks.shape[1]
     entries, offsets = tab.shape[0] - PAD, tab.shape[1]
 
-    def one(k, _):
-        rows = pl.ds(pl.multiple_of(k * depth, depth), depth)
+    def one(k):
+        rows = slice(k * depth, (k + 1) * depth)
         spread_ref[:, rows, :] = jnp.zeros((spread_ref.shape[0], depth, BLK), BF16)
         before, acc = -1, jnp.zeros((depth, BLK), F32)
         for e in range(entries):
@@ -104,9 +104,9 @@
             acc = jnp.where(s == before, acc, 0.0) + blocks[t]
             spread_ref[s, rows, :] = acc.astype(BF16)
             before = s
-        return 0
-
-    lax.fori_loop(0, offsets, one, 0)
+
+    for k in range(offsets):
+        one(k)
 
 
 def collect(tab, prod, sums):
@@ -131,13 +131,6 @@
     for bits, ref in zip(order, refs):
         place = lax.axis_index("chan") ^ bits
         ext_ref[pl.ds(pl.multiple_of(place * depth, depth), depth), :] = ref[...]
-
-
-def extend(ext_ref, wide_ref, a_ref, b_ref):
-    rows = wide_ref.shape[1]
-    ext_ref[:, :rows] = wide_ref[...]
-    ext_ref[:, rows : rows + RIM] = a_ref[...]
-    ext_ref[:, rows + RIM :] = b_ref[...]
 
 
 def input_grad_body(
@@ -183,13 +176,16 @@
     out_ref[...] = value_ref[...]
 
 
-def join_body(order, tab, *refs):
+def cut_body(order, tab, *refs):
     pieces = len(order)
-    wide_ref, a_ref, b_ref = refs[pieces:]
-    lay(wide_ref, order, refs[:pieces])
-    a, b = near_rim(tab)
-    a_ref[...] = wide_ref[:, pl.ds(a, RIM)]
-    b_ref[...] = wide_ref[:, pl.ds(b, RIM)]
+    a_ref, b_ref, rims = refs[pieces:]
+    depth, half = refs[0].shape[0], a_ref.shape[0]
+    own = pl.ds(pl.multiple_of(lax.axis_index("chan") % 2 * half, half), half)
+    for start, out_ref in zip(near_rim(tab), (a_ref, b_ref)):
+        for bits, ref in zip(order, refs[:pieces]):
+            place = lax.axis_index("chan") ^ bits
+            rims[pl.ds(pl.multiple_of(place * depth, depth), depth), :] = ref[:, pl.ds(start, RIM)]
+        out_ref[...] = rims[own, :]
 
 
 def multiply(w_ref, value, prod, first):
@@ -207,13 +203,23 @@
         store(slice(b * BLK, (b + 1) * BLK), total)
 
 
-def inner_body(w_ref, wide_ref, prod_ref):
+def inner_body(order, w_ref, *refs):
+    pieces = len(order)
+    prod_ref, wide_ref = refs[pieces:]
+    lay(wide_ref, order, refs[:pieces])
     multiply(w_ref, wide_ref[...], prod_ref, 0)
 
 
-def hidden_body(tab, w_ref, a_ref, b_ref, _, z_ref, hidden_ref, prod, *sums):
-    nblocks = z_ref.shape[1] // BLK
-    multiply(w_ref, jnp.concatenate([a_ref[...], b_ref[...]], axis=1), prod, nblocks)
+def stack_body(a_ref, b_ref, out_ref):
+    out_ref[:, :RIM] = a_ref[...]
+    out_ref[:, RIM:] = b_ref[...]
+
+
+def hidden_body(tab, w_ref, own_ref, other_ref, _, z_ref, hidden_ref, rims_ref, prod, *sums):
+    core, half = lax.axis_index("chan") % 2, own_ref.shape[0]
+    for place, ref in ((core, own_ref), (1 - core, other_ref)):
+        rims_ref[pl.ds(pl.multiple_of(place * half, half), half), :] = ref[...]
+    multiply(w_ref, rims_ref[...], prod, z_ref.shape[1] // BLK)
 
     def store(cols, z):
         z_ref[:, cols] = z
@@ -246,17 +252,15 @@
 
 
 def turn_body(count, tab, hidden_ref, mine_ref, *refs):
-    gots, (inner_ref, a_ref, b_ref) = refs[:count], refs[count:]
-    total = mine_ref[...]
-    for ref in gots:
-        total = total + ref[...].astype(F32)
-    rows = inner_ref.shape[1]
-    inner_ref[...] = total[:, :rows]
-    a, b = near_rim(tab)
-    a_ref[0] = total[:, rows : rows + RIM].astype(BF16)
-    a_ref[1] = hidden_ref[:, pl.ds(a, RIM)]
-    b_ref[0] = total[:, rows + RIM :].astype(BF16)
-    b_ref[1] = hidden_ref[:, pl.ds(b, RIM)]
+    gots, outs = refs[:count], refs[count:]
+    rows = hidden_ref.shape[1]
+    for i, (start, out_ref) in enumerate(zip(near_rim(tab), outs)):
+        cols = slice(rows + i * RIM, rows + (i + 1) * RIM)
+        total = mine_ref[:, cols]
+        for ref in gots:
+            total = total + ref[:, cols].astype(F32)
+        out_ref[0] = total.astype(BF16)
+        out_ref[1] = hidden_ref[:, pl.ds(start, RIM)]
 
 
 def pack_body(hidden_ref, a_ref, b_ref, rim_ref, full_ref):
@@ -273,35 +277,37 @@
     full_ref[:, rows:] = rim_ref[...]
 
 
-def weight_grad(ext, spread_ref, total):
-    reach = spread_ref.shape[0]
+def weight_grad(ext_ref, spread_ref, start, width):
+    part = pl.ds(start, width)
+    table = jnp.concatenate([spread_ref[s, part, :] for s in range(spread_ref.shape[0])], axis=1)
+    res = lax.dot_general(ext_ref[...], table, (((1,), (1,)), ((), ())), preferred_element_type=F32)
+    slabs = lax.axis_size("space")
+    return res.reshape(slabs // 2, 2, res.shape[0] // slabs, width)
+
+
+def part_slabs(ext_ref, spread_ref, keep_ref, send_ref, step):
+    even = lax.axis_index("space") % 2 == 0
 
     def product(start, width):
+        res = weight_grad(ext_ref, spread_ref, start, width)
         part = pl.ds(start, width)
-        table = jnp.concatenate([spread_ref[s, part, :] for s in range(reach)], axis=1)
-        res = lax.dot_general(ext[...], table, (((1,), (1,)), ((), ())), preferred_element_type=F32)
-        total[:, :, :, part] = res.reshape(total.shape[:3] + (width,))
-
-    chunks(spread_ref.shape[1], 7 * BLK, product)
-
-
-def part_slabs(total, keep_ref, send_ref):
-    parity = lax.axis_index("space") % 2
-    keep_ref[...] = total[:, parity]
-    send_ref[...] = total[:, 1 - parity].astype(BF16)
+        keep_ref[:, :, part] = jnp.where(even, res[:, 0], res[:, 1])
+        send_ref[:, :, part] = jnp.where(even, res[:, 1], res[:, 0]).astype(BF16)
+
+    chunks(keep_ref.shape[2], step, product)
 
 
 def grad_two_body(order, spread_ref, *refs):
     pieces = len(order)
     keep_ref, send_ref, mine_ref, *send_refs, ext, total = refs[pieces:]
     lay(ext, order, refs[:pieces])
-    weight_grad(ext, spread_ref, total)
     cut = keep_ref.shape[2]
-    part_slabs(total.at[:, :, :, :cut], keep_ref, send_ref)
+    part_slabs(ext, spread_ref, keep_ref, send_ref, cut)
+    total[...] = weight_grad(ext, spread_ref, cut, mine_ref.shape[2])
     place = lax.axis_index("space") // 2
-    mine_ref[...] = total[place, :, :, cut:]
+    mine_ref[...] = total[place]
     for j, ref in enumerate(send_refs):
-        ref[...] = total[place ^ (j + 1), :, :, cut:].astype(BF16)
+        ref[...] = total[place ^ (j + 1)].astype(BF16)
 
 
 def split_body(count, mine_ref, *refs):
@@ -314,26 +320,32 @@
         ref[...] = total.astype(ref.dtype)
 
 
-def grad_one_body(
-    tab, z_ref, inner_ref, from_a, from_b, wide_ref, a_ref, b_ref,
-    keep_ref, send_ref, grads, blocks, spread_ref, ext, total
-):
-    extend(ext, wide_ref, a_ref, b_ref)
-    grads[...] = inner_ref[...]
+def prepare_body(z_ref, wide_ref, rims_ref, slope_ref, ext_ref):
+    rows = wide_ref.shape[1]
+    ext_ref[:, :rows] = wide_ref[...]
+    ext_ref[:, rows:] = rims_ref[...]
+    z = z_ref[...]
+    gate = 1.0 / (1.0 + jnp.exp(-z))
+    slope_ref[...] = gate * (1.0 + z * (1.0 - gate))
+
+
+def grad_one_body(count, tab, slope_ref, from_a, from_b, ext_ref, mine_ref, *refs):
+    gots, (keep_ref, send_ref, grads, blocks, spread_ref) = refs[:count], refs[count:]
+    rows = slope_ref.shape[1]
+    inner = mine_ref[:, :rows]
+    for ref in gots:
+        inner = inner + ref[:, :rows].astype(F32)
+    grads[...] = inner
     a, b = near_rim(tab)
     for start, ref in ((a, from_a), (b, from_b)):
         grads[:, pl.ds(start, RIM)] = grads[:, pl.ds(start, RIM)] + ref[0].astype(F32)
     nblocks = blocks.shape[0] - 1
     for i in range(nblocks):
         cols = slice(i * BLK, (i + 1) * BLK)
-        z = z_ref[:, cols]
-        gate = 1.0 / (1.0 + jnp.exp(-z))
-        value = grads[:, cols] * gate * (1.0 + z * (1.0 - gate))
-        blocks[i] = value.astype(BF16).astype(F32)
+        blocks[i] = (grads[:, cols] * slope_ref[:, cols]).astype(BF16).astype(F32)
     blocks[nblocks] = jnp.zeros_like(blocks[nblocks])
     spread(tab, blocks, spread_ref)
-    weight_grad(ext, spread_ref, total)
-    part_slabs(total, keep_ref, send_ref)
+    part_slabs(ext_ref, spread_ref, keep_ref, send_ref, 7 * BLK)
 
 
 def finish_body(counts, *refs):
@@ -433,12 +445,13 @@
     for got in far:
         (got,) = call(pass_body, [pltpu.VMEM(got.shape, BF16)], [held(got)], after=[send])
         pieces += [got, swap(got, "chan", 1)]
-    x_wide, rim_a, rim_b = call(
-        functools.partial(join_body, order),
-        [pltpu.VMEM((wide, rows), BF16), pltpu.VMEM((wide, RIM), BF16), pltpu.VMEM((wide, RIM), BF16)],
+    half_rim = pltpu.VMEM((wide // 2, RIM), BF16)
+    rim_a, rim_b = call(
+        functools.partial(cut_body, order),
+        [half_rim, half_rim],
         [tab] + [held(v) for v in pieces],
+        [pltpu.VMEM((wide, RIM), BF16)],
         flops=8 * work,
-        traffic=2 << 20,
     )
     x_a, x_b = swap(rim_a, "space", 1), swap_other(rim_b)
     got = swap(send, "chan", 1)
@@ -452,29 +465,30 @@
     gots = [swap(v, "chan", 2 * (j + 1)) for j, v in enumerate(sends)]
 
     conv_scratch = [ext, pltpu.VMEM(spread_shape, F32)] + [blocks] * 2
-    (prod_one,) = call(
-        inner_body,
-        [pltpu.VMEM(spread_shape, F32)],
-        [w_one, held(x_wide)],
+    prod_one, x_wide = call(
+        functools.partial(inner_body, order),
+        [pltpu.VMEM(spread_shape, F32), pltpu.VMEM((wide, rows), BF16)],
+        [w_one] + [held(v) for v in pieces],
         vmem=10,
         flops=work,
         traffic=16 << 20,
         after=[mine],
     )
-    z_one, hidden, _ = call(
+    (x_half,) = call(
+        stack_body, [pltpu.VMEM((wide // 2, 2 * RIM), BF16)], [held(x_a), held(x_b)], after=[x_wide]
+    )
+    z_one, hidden, x_rims, _ = call(
         hidden_body,
-        [pltpu.VMEM((depth, rows), F32), pltpu.VMEM((depth, rows), BF16), pltpu.VMEM(spread_shape, F32)],
-        [tab, w_one] + [held(v) for v in (x_a, x_b, prod_one)],
+        [pltpu.VMEM((depth, rows), F32), pltpu.VMEM((depth, rows), BF16), pltpu.VMEM((wide, 2 * RIM), BF16), pltpu.VMEM(spread_shape, F32)],
+        [tab, w_one] + [held(v) for v in (x_half, swap(x_half, "chan", 1), prod_one)],
         [blocks] * 2,
         vmem=12,
-        flops=work,
-        traffic=16 << 20,
-        aliases={4: 2},
+        aliases={4: 3},
     )
     far = [swap(hidden, "chan", 2 * j) for j in range(1, pairs)]
-    inner, to_a, to_b = call(
+    to_a, to_b = call(
         functools.partial(turn_body, len(gots)),
-        [pltpu.VMEM((depth, rows), F32), pltpu.VMEM((2, depth, RIM), BF16), pltpu.VMEM((2, depth, RIM), BF16)],
+        [pltpu.VMEM((2, depth, RIM), BF16), pltpu.VMEM((2, depth, RIM), BF16)],
         [tab] + [held(v) for v in [hidden, mine] + gots],
         traffic=2 << 20,
     )
@@ -488,13 +502,18 @@
     far_rims = [swap(rim, "chan", 2 * j) for j in range(1, pairs)]
     full_other = swap(full, "chan", 1)
 
-    total = pltpu.VMEM((slabs // 2, 2, share, flat), F32)
+    slope, x_ext = call(
+        prepare_body,
+        [pltpu.VMEM((depth, rows), F32), pltpu.VMEM((wide, reach), BF16)],
+        [held(v) for v in (z_one, x_wide, x_rims)],
+        after=[to_a],
+    )
     keep_one, send_one = call(
-        grad_one_body,
+        functools.partial(grad_one_body, len(gots)),
         [pltpu.VMEM((slabs // 2, share, flat), F32), pltpu.VMEM((slabs // 2, share, flat), BF16)],
-        [tab] + [held(v) for v in (z_one, inner, from_a, from_b, x_wide, x_a, x_b)],
-        [pltpu.VMEM((depth, rows), F32), blocks, pltpu.VMEM(spread_shape, BF16), ext, total],
-        vmem=26,
+        [tab] + [held(v) for v in [slope, from_a, from_b, x_ext, mine] + gots],
+        [pltpu.VMEM((depth, rows), F32), blocks, pltpu.VMEM(spread_shape, BF16)],
+        vmem=24,
         flops=work,
         traffic=16 << 20,
     )
@@ -517,10 +536,8 @@
         ]
         + [pltpu.VMEM(far_part, BF16)] * (slabs // 2 - 1),
         [held(v) for v in [spread_two] + pieces],
-        [ext, total],
+        [ext, pltpu.VMEM((slabs // 2,) + far_part, F32)],
         vmem=14,
-        flops=work,
-        traffic=8 << 20,
     )
     gots_far = [swap(v, "space", 2 * (j + 1)) for j, v in enumerate(sends_far)]
     got_two = swap(send_two, "space", 1)

time: 80.7 us -> 78.6 us (0.974)
  Pallas kernels: 32.7 us -> 31.4 us
    pallas_call x17 -> x19, Pallas kernels: 32.7 us -> 31.4 us  [call(): return kernel(*ins)]
    ppermute x23 -> x24, starting transfers between devices: 33.7 us -> 33 us  [swap(): lax.ppermute(value, axis, [(i, i ^ bits) for i in range(lax.axis_size(axi...]
    ppermute x23 -> x24, waiting for transfers between devices: 11.8 us -> 11.7 us  [swap(): lax.ppermute(value, axis, [(i, i ^ bits) for i in range(lax.axis_size(axi...]
  transfers between devices with their start and end apart: 25 -> 26, of which waited for: 7 -> 9; matrix products, arithmetic and copies ran while one was open for 0% -> 0% of each run, Pallas kernels for 39% -> 38%
where the time goes in v5:
time: 78.6 us; the launch traced here: 78.4 us
  starting transfers between devices  34.5 us (44%)
  Pallas kernels  31.4 us (40%)
  waiting for transfers between devices  11.7 us (15%)
  between operations  0.82 us (1%)
    ppermute x24, starting transfers between devices, swap(): lax.ppermute(value, axis, [(i, i ^ bits) for i in range(lax.axis_size(axi...  33 us
    pallas_call x19, Pallas kernels, call(): return kernel(*ins)  31.4 us
    ppermute x24, waiting for transfers between devices, swap(): lax.ppermute(value, axis, [(i, i ^ bits) for i in range(lax.axis_size(axi...  11.7 us
  transfers between devices with their start and end apart: 26, of which 9 were waited for; matrix products, arithmetic and copies ran while one was open for 0% of the time, Pallas kernels for 38%

profile of v5, /device:TPU:0, one launch (start us, length us, event | category | flops | bytes accessed | tf_op | source)
XLA Modules:
  0.0 78.4 jit_solution(1014862179808796196)
XLA Ops:
  0.6 3.0 %collective-permute-start.1 = (bf16[64,2048]{1,0:T(8,128)(2,1)}, bf16[64,2048]{1,0:T(8,128)(2,1)S(1)}, u32[]{:S(2)}, u32[]{:S(2)}) collective-permute-start(bf16[64,2048]{1,0:T(8,128)(2,1)} %bitcast.17), channel_id=1, source_target_pairs={{0,2},{1,3},{2,0},{3,1},{4,6},{5,7},{6,4},{7,5},{8,10},{9,11},{10,... | collective-permute-start | bytes 786440 | tf_op jit(solution)/shard_map/ppermute | solution.py:366
  3.6 7.5 %input_grad_body.1 = (s32[24,27]{1,0:T(8,128)S(1)}, bf16[20,1728,128]{2,1,0:T(8,128)(2,1)S(1)}, bf16[2,64,2560]{2,1,0:T(8,128)(2,1)S(1)}, bf16[2,64,2560]{2,1,0:T(8,128)(2,1)S(1)}, bf16[64,2048]{1,0:T(8,128)(2,1)S(1)}) custom-call(s32[8]{0:T(128)} %refs_0_.1, s32[3,16,27]{2,1,0:T(8,128)} %bitcast.20, bf16[64,2048]{1,0:T(8,128)(2,1)} %bitcast.16, ...), custom_call_target="tpu_custom_call" | custom-call | flops 2264924160 | bytes 16777216 | tf_op jit(solution)/shard_map/input_grad_body/pallas_call | solution.py:49
  11.2 0.6 collective-permute-start.2
  11.7 0.1 collective-permute-start.5
  11.8 1.1 %collective-permute-done.2.refs_4_ = bf16[64,2048]{1,0:T(8,128)(2,1)S(1)} collective-permute-done((bf16[64,2048]{1,0:T(8,128)(2,1)S(1)}, bf16[64,2048]{1,0:T(8,128)(2,1)S(1)}, u32[]{:S(2)}, u32[]{:S(2)}) %collective-permute-start.2) | collective-permute-done | bytes 262176 | tf_op jit(solution)/shard_map/ppermute | solution.py:366
  12.9 0.8 %cut_body.1 = (bf16[128,256]{1,0:T(8,128)(2,1)S(1)}, bf16[128,256]{1,0:T(8,128)(2,1)S(1)}) custom-call(s32[24,27]{1,0:T(8,128)S(1)} %get-tuple-element.43.refs_0_, bf16[64,2048]{1,0:T(8,128)(2,1)S(1)} %get-tuple-element.44.refs_1_, bf16[64,2048]{1,0:T(8,128)(2,1)S(1)} %collective-permute-done.refs_2_, bf16[64,2048]{1,0:T(8,128)(2,1)S(1)} %pass_body.1.refs_3_, ...), custom_call_target="tpu_custom_call" | custom-call | flops 18119393280 | tf_op jit(solution)/shard_map/cut_body/pallas_call | solution.py:49
  13.7 0.7 collective-permute-start.4
  14.4 4.4 %collective-permute-start.3 = (bf16[128,256]{1,0:T(8,128)(2,1)S(1)}, bf16[128,256]{1,0:T(8,128)(2,1)S(1)}, u32[]{:S(2)}, u32[]{:S(2)}) collective-permute-start(bf16[128,256]{1,0:T(8,128)(2,1)S(1)} %get-tuple-element.46.refs_2_), channel_id=1, source_target_pairs={{0,4},{4,0},{8,12},{12,8},{16,20},{20,16},{24,28},{28,24},{1,5},{5... | collective-permute-start | bytes 196616 | tf_op jit(solution)/shard_map/ppermute | solution.py:366
  18.7 0.2 halve_body.3
  18.9 0.7 collective-permute-start.7
  19.6 2.1 %inner_body.1 = (f32[20,1728,128]{2,1,0:T(8,128)S(1)}, bf16[256,2048]{1,0:T(8,128)(2,1)S(1)}) custom-call(bf16[1728,256]{1,0:T(8,128)(2,1)S(1)} %bitcast.10, bf16[64,2048]{1,0:T(8,128)(2,1)S(1)} %get-tuple-element.44.refs_1_, bf16[64,2048]{1,0:T(8,128)(2,1)S(1)} %collective-permute-done.refs_2_, bf16[64,2048]{1,0:T(8,128)(2,1)S(1)} %pass_body.1.refs_3_, ...), custom_call_target="tpu_custom_call" | custom-call | flops 2264924160 | bytes 16777216 | tf_op jit(solution)/shard_map/inner_body/pallas_call | solution.py:49
  21.7 0.1 collective-permute-start.6
  21.8 1.3 %collective-permute-done.6.refs_3_ = bf16[128,512]{1,0:T(8,128)(2,1)S(1)} collective-permute-done((bf16[128,512]{1,0:T(8,128)(2,1)S(1)}, bf16[128,512]{1,0:T(8,128)(2,1)S(1)}, u32[]{:S(2)}, u32[]{:S(2)}) %collective-permute-start.6) | collective-permute-done | bytes 131104 | tf_op jit(solution)/shard_map/ppermute | solution.py:366
  23.1 3.3 %hidden_body.1 = (f32[64,2048]{1,0:T(8,128)S(1)}, bf16[64,2048]{1,0:T(8,128)(2,1)S(1)}, bf16[256,512]{1,0:T(8,128)(2,1)S(1)}, f32[20,1728,128]{2,1,0:T(8,128)S(1)}) custom-call(s32[24,27]{1,0:T(8,128)S(1)} %get-tuple-element.43.refs_0_, bf16[1728,256]{1,0:T(8,128)(2,1)S(1)} %bitcast.11, ...), custom_call_target="tpu_custom_call", output_to_operand_aliasing={{3}: (4, {})} | custom-call | tf_op jit(solution)/shard_map/hidden_body/pallas_call | solution.py:49
  26.4 2.0 %collective-permute-done.7.refs_3_.refs_6_ = bf16[64,2560]{1,0:T(8,128)(2,1)S(1)} collective-permute-done((bf16[64,2560]{1,0:T(8,128)(2,1)S(1)}, bf16[64,2560]{1,0:T(8,128)(2,1)S(1)}, u32[]{:S(2)}, u32[]{:S(2)}) %collective-permute-start.7) | collective-permute-done | bytes 327712 | tf_op jit(solution)/shard_map/ppermute | solution.py:366
  28.4 0.8 turn_body.1
  29.2 0.8 %collective-permute-start.9 = (bf16[2,64,256]{2,1,0:T(8,128)(2,1)S(1)}, bf16[2,64,256]{2,1,0:T(8,128)(2,1)S(1)}, u32[]{:S(2)}, u32[]{:S(2)}) collective-permute-start(bf16[2,64,256]{2,1,0:T(8,128)(2,1)S(1)} %get-tuple-element.55), channel_id=1, source_target_pairs={{4,8},{12,16},{20,24},{8,4},{16,12},{24,20},{5,9},{13,17},{21,25},... | collective-permute-start | bytes 196616 | tf_op jit(solution)/shard_map/ppermute | solution.py:371
  30.0 4.3 %collective-permute-start.8 = (bf16[2,64,256]{2,1,0:T(8,128)(2,1)S(1)}, bf16[2,64,256]{2,1,0:T(8,128)(2,1)S(1)}, u32[]{:S(2)}, u32[]{:S(2)}) collective-permute-start(bf16[2,64,256]{2,1,0:T(8,128)(2,1)S(1)} %get-tuple-element.54.refs_3_), channel_id=1, source_target_pairs={{0,4},{4,0},{8,12},{12,8},{16,20},{20,16},{24,28},{28,24},{1,5},{5... | collective-permute-start | bytes 196616 | tf_op jit(solution)/shard_map/ppermute | solution.py:366
  34.4 0.5 collective-permute-start.11
  34.9 0.3 prepare_body.1
  35.2 1.4 %collective-permute-done.8.refs_1_.refs_2_ = bf16[2,64,256]{2,1,0:T(8,128)(2,1)S(1)} collective-permute-done((bf16[2,64,256]{2,1,0:T(8,128)(2,1)S(1)}, bf16[2,64,256]{2,1,0:T(8,128)(2,1)S(1)}, u32[]{:S(2)}, u32[]{:S(2)}) %collective-permute-start.8) | collective-permute-done | bytes 65568 | tf_op jit(solution)/shard_map/ppermute | solution.py:366
  36.6 0.6 collective-permute-start.12
  37.2 6.0 %grad_one_body.1 = (f32[4,32,1728]{2,1,0:T(8,128)S(1)}, bf16[4,32,1728]{2,1,0:T(8,128)(2,1)S(1)}) custom-call(s32[24,27]{1,0:T(8,128)S(1)} %get-tuple-element.43.refs_0_, f32[64,2048]{1,0:T(8,128)S(1)} %get-tuple-element.60.refs_1_, bf16[2,64,256]{2,1,0:T(8,128)(2,1)S(1)} %collective-permute-done.8.refs_1_.refs_2_, ...), custom_call_target="tpu_custom_call" | custom-call | flops 2264924160 | bytes 16777216 | tf_op jit(solution)/shard_map/grad_one_body/pallas_call | solution.py:49
  43.3 2.1 %collective-permute-start.14 = (bf16[4,32,1728]{2,1,0:T(8,128)(2,1)S(1)}, bf16[4,32,1728]{2,1,0:T(8,128)(2,1)S(1)}, u32[]{:S(2)}, u32[]{:S(2)}) collective-permute-start(bf16[4,32,1728]{2,1,0:T(8,128)(2,1)S(1)} %get-tuple-element.63), channel_id=1, source_target_pairs={{0,4},{4,0},{8,12},{12,8},{16,20},{20,16},{24,28},{28,24},{1,5},{5... | collective-permute-start | bytes 1327112 | tf_op jit(solution)/shard_map/ppermute | solution.py:366
  45.4 0.6 collective-permute-start.13
  46.0 1.0 %collective-permute-done.10.refs_3_.refs_2_ = bf16[64,2560]{1,0:T(8,128)(2,1)S(1)} collective-permute-done((bf16[64,2560]{1,0:T(8,128)(2,1)S(1)}, bf16[64,2560]{1,0:T(8,128)(2,1)S(1)}, u32[]{:S(2)}, u32[]{:S(2)}) %collective-permute-start.10) | collective-permute-done | bytes 327712 | tf_op jit(solution)/shard_map/ppermute | solution.py:366
  47.0 0.5 collective-permute-done.13.refs_5_.refs_4_
  47.5 2.7 %grad_two_body.1 = (f32[4,32,1280]{2,1,0:T(8,128)S(1)}, bf16[4,32,1280]{2,1,0:T(8,128)(2,1)S(1)}, f32[2,32,448]{2,1,0:T(8,128)S(1)}, bf16[2,32,448]{2,1,0:T(8,12...) custom-call(bf16[20,1728,128]{2,1,0:T(8,128)(2,1)S(1)} %get-tuple-element.69.refs_0_, ...), custom_call_target="tpu_custom_call" | custom-call | tf_op jit(solution)/shard_map/grad_two_body/pallas_call | solution.py:49
  50.1 1.6 %collective-permute-start.19 = (bf16[2,32,448]{2,1,0:T(8,128)(2,1)S(1)}, bf16[2,32,448]{2,1,0:T(8,128)(2,1)S(1)}, u32[]{:S(2)}, u32[]{:S(2)}) collective-permute-start(bf16[2,32,448]{2,1,0:T(8,128)(2,1)S(1)} %get-tuple-element.73), channel_id=1, source_target_pairs={{0,8},{4,12},{8,0},{12,4},{16,24},{20,28},{24,16},{28,20},{1,9},{5... | collective-permute-start | bytes 172040 | tf_op jit(solution)/shard_map/ppermute | solution.py:366
  51.8 0.1 collective-permute-start.20
  51.9 2.7 %collective-permute-start.21 = (bf16[2,32,448]{2,1,0:T(8,128)(2,1)S(1)}, bf16[2,32,448]{2,1,0:T(8,128)(2,1)S(1)}, u32[]{:S(2)}, u32[]{:S(2)}) collective-permute-start(bf16[2,32,448]{2,1,0:T(8,128)(2,1)S(1)} %get-tuple-element.75), channel_id=1, source_target_pairs={{0,24},{4,28},{8,16},{12,20},{16,8},{20,12},{24,0},{28,4},{1,25},{... | collective-permute-start | bytes 172040 | tf_op jit(solution)/shard_map/ppermute | solution.py:366
  54.6 0.1 collective-permute-start.18
  54.7 0.1 halve_body.4
  54.8 1.1 %collective-permute-start.15 = (bf16[32,1728]{1,0:T(8,128)(2,1)S(1)}, bf16[32,1728]{1,0:T(8,128)(2,1)S(1)}, u32[]{:S(2)}, u32[]{:S(2)}) collective-permute-start(bf16[32,1728]{1,0:T(8,128)(2,1)S(1)} %get-tuple-element.66), channel_id=1, source_target_pairs={{0,8},{4,12},{8,0},{12,4},{16,24},{20,28},{24,16},{28,20},{1,9},{5... | collective-permute-start | bytes 331784 | tf_op jit(solution)/shard_map/ppermute | solution.py:366
  55.9 3.3 %collective-permute-start.16 = (bf16[32,1728]{1,0:T(8,128)(2,1)S(1)}, bf16[32,1728]{1,0:T(8,128)(2,1)S(1)}, u32[]{:S(2)}, u32[]{:S(2)}) collective-permute-start(bf16[32,1728]{1,0:T(8,128)(2,1)S(1)} %get-tuple-element.67), channel_id=1, source_target_pairs={{0,16},{4,20},{8,24},{12,28},{16,0},{20,4},{24,8},{28,12},{1,17},{... | collective-permute-start | bytes 331784 | tf_op jit(solution)/shard_map/ppermute | solution.py:366
  59.2 1.6 %collective-permute-done.20.refs_2_ = bf16[2,32,448]{2,1,0:T(8,128)(2,1)S(1)} collective-permute-done((bf16[2,32,448]{2,1,0:T(8,128)(2,1)S(1)}, bf16[2,32,448]{2,1,0:T(8,128)(2,1)S(1)}, u32[]{:S(2)}, u32[]{:S(2)}) %collective-permute-start.20) | collective-permute-done | bytes 57376 | tf_op jit(solution)/shard_map/ppermute | solution.py:366
  60.8 0.7 collective-permute-start.17
  61.5 5.8 %output_body.1 = (bf16[64,2048]{1,0:T(8,128)(2,1)}, f32[8,128]{1,0:T(8,128)S(1)}) custom-call(s32[24,27]{1,0:T(8,128)S(1)} %get-tuple-element.43.refs_0_, bf16[1728,256]{1,0:T(8,128)(2,1)S(1)} %bitcast.13, bf16[64,2560]{1,0:T(8,128)(2,1)S(1)} %get-tuple-element.56.refs_2_.refs_1_, bf16[64,2560]{1,0:T(8,128)(2,1)S(1)} %collective-permute-done.10.refs_3_.refs_2_, ...), custom_call_target="tpu_custom_call" | custom-call | flops 18119393280 | bytes 16777216 | tf_op jit(solution)/shard_map/output_body/pallas_call | solution.py:49
  67.3 0.1 halve_body.5
  67.4 0.1 collective-permute-start.22
  67.5 3.7 %collective-permute-start.23 = (bf16[32,1280]{1,0:T(8,128)(2,1)S(1)}, bf16[32,1280]{1,0:T(8,128)(2,1)S(1)}, u32[]{:S(2)}, u32[]{:S(2)}) collective-permute-start(bf16[32,1280]{1,0:T(8,128)(2,1)S(1)} %get-tuple-element.80), channel_id=1, source_target_pairs={{0,16},{4,20},{8,24},{12,28},{16,0},{20,4},{24,8},{28,12},{1,17},{... | collective-permute-start | bytes 245768 | tf_op jit(solution)/shard_map/ppermute | solution.py:366
  71.2 0.7 collective-permute-start.24
  71.9 2.0 %collective-permute-start.25 = (bf16[32,448]{1,0:T(8,128)(2,1)S(1)}, bf16[32,448]{1,0:T(8,128)(2,1)S(1)}, u32[]{:S(2)}, u32[]{:S(2)}) collective-permute-start(bf16[32,448]{1,0:T(8,128)(2,1)S(1)} %get-tuple-element.82), channel_id=1, source_target_pairs={{0,4},{4,0},{8,12},{12,8},{16,20},{20,16},{24,28},{28,24},{1,5},{5... | collective-permute-start | bytes 86024 | tf_op jit(solution)/shard_map/ppermute | solution.py:366
  73.9 0.9 %finish_body.2 = f32[27,32,64]{2,1,0:T(8,128)} custom-call(f32[32,1728]{1,0:T(8,128)S(1)} %get-tuple-element.64.refs_6_.refs_0_, bf16[32,1728]{1,0:T(8,128)(2,1)S(1)} %collective-permute-done.15.refs_1_, bf16[32,1728]{1,0:T(8,128)(2,1)S(1)} %collective-permute-done.16.refs_2_, bf16[32,1728]{1,0:T(8,128)(2,1)S(1)} %collective-permute-done.17.refs_3_), custom_call_target="tpu_custom_call" | custom-call | bytes 2097152 | tf_op jit(solution)/shard_map/finish_body/pallas_call | solution.py:49
  74.8 1.0 %collective-permute-done.25.refs_5_ = bf16[32,448]{1,0:T(8,128)(2,1)S(1)} collective-permute-done((bf16[32,448]{1,0:T(8,128)(2,1)S(1)}, bf16[32,448]{1,0:T(8,128)(2,1)S(1)}, u32[]{:S(2)}, u32[]{:S(2)}) %collective-permute-start.25) | collective-permute-done | bytes 28704 | tf_op jit(solution)/shard_map/ppermute | solution.py:366
  75.8 0.0 collective-permute-done.23.refs_2_
  75.8 1.7 %collective-permute-done.24.refs_3_ = bf16[32,1280]{1,0:T(8,128)(2,1)S(1)} collective-permute-done((bf16[32,1280]{1,0:T(8,128)(2,1)S(1)}, bf16[32,1280]{1,0:T(8,128)(2,1)S(1)}, u32[]{:S(2)}, u32[]{:S(2)}) %collective-permute-start.24) | collective-permute-done | bytes 81952 | tf_op jit(solution)/shard_map/ppermute | solution.py:366
  77.5 0.9 %finish_body.3 = f32[27,32,64]{2,1,0:T(8,128)} custom-call(f32[32,1280]{1,0:T(8,128)S(1)} %get-tuple-element.78.refs_0_, bf16[32,1280]{1,0:T(8,128)(2,1)S(1)} %collective-permute-done.22.refs_1_, bf16[32,1280]{1,0:T(8,128)(2,1)S(1)} %collective-permute-done.23.refs_2_, bf16[32,1280]{1,0:T(8,128)(2,1)S(1)} %collective-permute-done.24.refs_3_, ...), custom_call_target="tpu_custom_call" | custom-call | bytes 2097152 | tf_op jit(solution)/shard_map/finish_body/pallas_call | solution.py:49
  (27 shorter events, 0.2 us)
Async XLA Ops:
  0.6 10.5 %collective-permute-start.1 = (bf16[64,2048]{1,0:T(8,128)(2,1)}, bf16[64,2048]{1,0:T(8,128)(2,1)S(1)}, u32[]{:S(2)}, u32[]{:S(2)}) collective-permute-start(bf16[64,2048]{1,0:T(8,128)(2,1)} %bitcast.17), channel_id=1, source_target_pairs={{0,2},{1,3},{2,0},{3,1},{4,6},{5,7},{6,4},{7,5},{8,10},{9,11},{10,... | collective-permute-start | bytes 786440 | tf_op jit(solution)/shard_map/ppermute | solution.py:366
  3.6 8.2 %collective-permute-start = (bf16[64,2048]{1,0:T(8,128)(2,1)}, bf16[64,2048]{1,0:T(8,128)(2,1)S(1)}, u32[]{:S(2)}, u32[]{:S(2)}) collective-permute-start(bf16[64,2048]{1,0:T(8,128)(2,1)} %bitcast.18), channel_id=1, source_target_pairs={{0,1},{1,0},{2,3},{3,2},{4,5},{5,4},{6,7},{7,6},{8,9},{9,8},{10,11... | collective-permute-start | bytes 786440 | tf_op jit(solution)/shard_map/ppermute | solution.py:366
  11.2 1.7 %collective-permute-start.2 = (bf16[64,2048]{1,0:T(8,128)(2,1)S(1)}, bf16[64,2048]{1,0:T(8,128)(2,1)S(1)}, u32[]{:S(2)}, u32[]{:S(2)}) collective-permute-start(bf16[64,2048]{1,0:T(8,128)(2,1)S(1)} %pass_body.1.refs_3_), channel_id=1, source_target_pairs={{0,1},{1,0},{2,3},{3,2},{4,5},{5,4},{6,7},{7,6},{8,9},{9,8},{10,11... | collective-permute-start | bytes 786440 | tf_op jit(solution)/shard_map/ppermute | solution.py:366
  11.7 7.0 %collective-permute-start.5 = (bf16[2,64,2560]{2,1,0:T(8,128)(2,1)S(1)}, bf16[2,64,2560]{2,1,0:T(8,128)(2,1)S(1)}, u32[]{:S(2)}, u32[]{:S(2)}) collective-permute-start(bf16[2,64,2560]{2,1,0:T(8,128)(2,1)S(1)} %get-tuple-element.45.refs_1_), channel_id=1, source_target_pairs={{0,1},{1,0},{2,3},{3,2},{4,5},{5,4},{6,7},{7,6},{8,9},{9,8},{10,11... | collective-permute-start | bytes 1966088 | tf_op jit(solution)/shard_map/ppermute | solution.py:366
  12.9 6.7 %copy-start = (bf16[27,64,256]{2,1,0:T(8,128)(2,1)S(1)}, bf16[27,64,256]{2,1,0:T(8,128)(2,1)}, u32[]{:S(2)}) copy-start(bf16[27,64,256]{2,1,0:T(8,128)(2,1)} %param.9) | copy-start | bytes 2654212
  13.7 8.0 %collective-permute-start.4 = (bf16[128,256]{1,0:T(8,128)(2,1)S(1)}, bf16[128,256]{1,0:T(8,128)(2,1)S(1)}, u32[]{:S(2)}, u32[]{:S(2)}) collective-permute-start(bf16[128,256]{1,0:T(8,128)(2,1)S(1)} %get-tuple-element.47), channel_id=1, source_target_pairs={{4,8},{12,16},{20,24},{8,4},{16,12},{24,20},{5,9},{13,17},{21,25},... | collective-permute-start | bytes 196616 | tf_op jit(solution)/shard_map/ppermute | solution.py:371
  14.4 7.3 %collective-permute-start.3 = (bf16[128,256]{1,0:T(8,128)(2,1)S(1)}, bf16[128,256]{1,0:T(8,128)(2,1)S(1)}, u32[]{:S(2)}, u32[]{:S(2)}) collective-permute-start(bf16[128,256]{1,0:T(8,128)(2,1)S(1)} %get-tuple-element.46.refs_2_), channel_id=1, source_target_pairs={{0,4},{4,0},{8,12},{12,8},{16,20},{20,16},{24,28},{28,24},{1,5},{5... | collective-permute-start | bytes 196616 | tf_op jit(solution)/shard_map/ppermute | solution.py:366
  18.9 9.5 %collective-permute-start.7 = (bf16[64,2560]{1,0:T(8,128)(2,1)S(1)}, bf16[64,2560]{1,0:T(8,128)(2,1)S(1)}, u32[]{:S(2)}, u32[]{:S(2)}) collective-permute-start(bf16[64,2560]{1,0:T(8,128)(2,1)S(1)} %get-tuple-element.53), channel_id=1, source_target_pairs={{0,2},{1,3},{2,0},{3,1},{4,6},{5,7},{6,4},{7,5},{8,10},{9,11},{10,... | collective-permute-start | bytes 983048 | tf_op jit(solution)/shard_map/ppermute | solution.py:366
  21.7 1.4 %collective-permute-start.6 = (bf16[128,512]{1,0:T(8,128)(2,1)S(1)}, bf16[128,512]{1,0:T(8,128)(2,1)S(1)}, u32[]{:S(2)}, u32[]{:S(2)}) collective-permute-start(bf16[128,512]{1,0:T(8,128)(2,1)S(1)} %stack_body.1.refs_2_), channel_id=1, source_target_pairs={{0,1},{1,0},{2,3},{3,2},{4,5},{5,4},{6,7},{7,6},{8,9},{9,8},{10,11... | collective-permute-start | bytes 393224 | tf_op jit(solution)/shard_map/ppermute | solution.py:366
  23.1 38.3 %copy-start.1 = (bf16[27,64,256]{2,1,0:T(8,128)(2,1)S(1)}, bf16[27,64,256]{2,1,0:T(8,128)(2,1)}, u32[]{:S(2)}) copy-start(bf16[27,64,256]{2,1,0:T(8,128)(2,1)} %param.10) | copy-start | bytes 2654212
  29.2 6.0 %collective-permute-start.9 = (bf16[2,64,256]{2,1,0:T(8,128)(2,1)S(1)}, bf16[2,64,256]{2,1,0:T(8,128)(2,1)S(1)}, u32[]{:S(2)}, u32[]{:S(2)}) collective-permute-start(bf16[2,64,256]{2,1,0:T(8,128)(2,1)S(1)} %get-tuple-element.55), channel_id=1, source_target_pairs={{4,8},{12,16},{20,24},{8,4},{16,12},{24,20},{5,9},{13,17},{21,25},... | collective-permute-start | bytes 196616 | tf_op jit(solution)/shard_map/ppermute | solution.py:371
  30.0 6.6 %collective-permute-start.8 = (bf16[2,64,256]{2,1,0:T(8,128)(2,1)S(1)}, bf16[2,64,256]{2,1,0:T(8,128)(2,1)S(1)}, u32[]{:S(2)}, u32[]{:S(2)}) collective-permute-start(bf16[2,64,256]{2,1,0:T(8,128)(2,1)S(1)} %get-tuple-element.54.refs_3_), channel_id=1, source_target_pairs={{0,4},{4,0},{8,12},{12,8},{16,20},{20,16},{24,28},{28,24},{1,5},{5... | collective-permute-start | bytes 196616 | tf_op jit(solution)/shard_map/ppermute | solution.py:366
  34.4 11.0 %collective-permute-start.11 = (bf16[64,2048]{1,0:T(8,128)(2,1)S(1)}, bf16[64,2048]{1,0:T(8,128)(2,1)S(1)}, u32[]{:S(2)}, u32[]{:S(2)}) collective-permute-start(bf16[64,2048]{1,0:T(8,128)(2,1)S(1)} %get-tuple-element.52.refs_1_.refs_0_), channel_id=1, source_target_pairs={{0,2},{1,3},{2,0},{3,1},{4,6},{5,7},{6,4},{7,5},{8,10},{9,11},{10,... | collective-permute-start | bytes 786440 | tf_op jit(solution)/shard_map/ppermute | solution.py:366
  36.6 8.7 %collective-permute-start.12 = (bf16[64,512]{1,0:T(8,128)(2,1)S(1)}, bf16[64,512]{1,0:T(8,128)(2,1)S(1)}, u32[]{:S(2)}, u32[]{:S(2)}) collective-permute-start(bf16[64,512]{1,0:T(8,128)(2,1)S(1)} %get-tuple-element.57), channel_id=1, source_target_pairs={{0,2},{1,3},{2,0},{3,1},{4,6},{5,7},{6,4},{7,5},{8,10},{9,11},{10,... | collective-permute-start | bytes 196616 | tf_op jit(solution)/shard_map/ppermute | solution.py:366
  43.3 11.4 %collective-permute-start.14 = (bf16[4,32,1728]{2,1,0:T(8,128)(2,1)S(1)}, bf16[4,32,1728]{2,1,0:T(8,128)(2,1)S(1)}, u32[]{:S(2)}, u32[]{:S(2)}) collective-permute-start(bf16[4,32,1728]{2,1,0:T(8,128)(2,1)S(1)} %get-tuple-element.63), channel_id=1, source_target_pairs={{0,4},{4,0},{8,12},{12,8},{16,20},{20,16},{24,28},{28,24},{1,5},{5... | collective-permute-start | bytes 1327112 | tf_op jit(solution)/shard_map/ppermute | solution.py:366
  45.4 1.6 %collective-permute-start.10 = (bf16[64,2560]{1,0:T(8,128)(2,1)S(1)}, bf16[64,2560]{1,0:T(8,128)(2,1)S(1)}, u32[]{:S(2)}, u32[]{:S(2)}) collective-permute-start(bf16[64,2560]{1,0:T(8,128)(2,1)S(1)} %get-tuple-element.56.refs_2_.refs_1_), channel_id=1, source_target_pairs={{0,1},{1,0},{2,3},{3,2},{4,5},{5,4},{6,7},{7,6},{8,9},{9,8},{10,11... | collective-permute-start | bytes 983048 | tf_op jit(solution)/shard_map/ppermute | solution.py:366
  45.4 2.1 %collective-permute-start.13 = (bf16[64,2560]{1,0:T(8,128)(2,1)S(1)}, bf16[64,2560]{1,0:T(8,128)(2,1)S(1)}, u32[]{:S(2)}, u32[]{:S(2)}) collective-permute-start(bf16[64,2560]{1,0:T(8,128)(2,1)S(1)} %append_body.1.refs_4_.refs_3_), channel_id=1, source_target_pairs={{0,1},{1,0},{2,3},{3,2},{4,5},{5,4},{6,7},{7,6},{8,9},{9,8},{10,11... | collective-permute-start | bytes 983048 | tf_op jit(solution)/shard_map/ppermute | solution.py:366
  50.1 5.7 %collective-permute-start.19 = (bf16[2,32,448]{2,1,0:T(8,128)(2,1)S(1)}, bf16[2,32,448]{2,1,0:T(8,128)(2,1)S(1)}, u32[]{:S(2)}, u32[]{:S(2)}) collective-permute-start(bf16[2,32,448]{2,1,0:T(8,128)(2,1)S(1)} %get-tuple-element.73), channel_id=1, source_target_pairs={{0,8},{4,12},{8,0},{12,4},{16,24},{20,28},{24,16},{28,20},{1,9},{5... | collective-permute-start | bytes 172040 | tf_op jit(solution)/shard_map/ppermute | solution.py:366
  51.8 9.0 %collective-permute-start.20 = (bf16[2,32,448]{2,1,0:T(8,128)(2,1)S(1)}, bf16[2,32,448]{2,1,0:T(8,128)(2,1)S(1)}, u32[]{:S(2)}, u32[]{:S(2)}) collective-permute-start(bf16[2,32,448]{2,1,0:T(8,128)(2,1)S(1)} %get-tuple-element.74), channel_id=1, source_target_pairs={{0,16},{4,20},{8,24},{12,28},{16,0},{20,4},{24,8},{28,12},{1,17},{... | collective-permute-start | bytes 172040 | tf_op jit(solution)/shard_map/ppermute | solution.py:366
  51.9 15.4 %collective-permute-start.21 = (bf16[2,32,448]{2,1,0:T(8,128)(2,1)S(1)}, bf16[2,32,448]{2,1,0:T(8,128)(2,1)S(1)}, u32[]{:S(2)}, u32[]{:S(2)}) collective-permute-start(bf16[2,32,448]{2,1,0:T(8,128)(2,1)S(1)} %get-tuple-element.75), channel_id=1, source_target_pairs={{0,24},{4,28},{8,16},{12,20},{16,8},{20,12},{24,0},{28,4},{1,25},{... | collective-permute-start | bytes 172040 | tf_op jit(solution)/shard_map/ppermute | solution.py:366
  54.6 12.7 %collective-permute-start.18 = (bf16[4,32,1280]{2,1,0:T(8,128)(2,1)S(1)}, bf16[4,32,1280]{2,1,0:T(8,128)(2,1)S(1)}, u32[]{:S(2)}, u32[]{:S(2)}) collective-permute-start(bf16[4,32,1280]{2,1,0:T(8,128)(2,1)S(1)} %get-tuple-element.71), channel_id=1, source_target_pairs={{0,4},{4,0},{8,12},{12,8},{16,20},{20,16},{24,28},{28,24},{1,5},{5... | collective-permute-start | bytes 983048 | tf_op jit(solution)/shard_map/ppermute | solution.py:366
  54.8 16.4 %collective-permute-start.15 = (bf16[32,1728]{1,0:T(8,128)(2,1)S(1)}, bf16[32,1728]{1,0:T(8,128)(2,1)S(1)}, u32[]{:S(2)}, u32[]{:S(2)}) collective-permute-start(bf16[32,1728]{1,0:T(8,128)(2,1)S(1)} %get-tuple-element.66), channel_id=1, source_target_pairs={{0,8},{4,12},{8,0},{12,4},{16,24},{20,28},{24,16},{28,20},{1,9},{5... | collective-permute-start | bytes 331784 | tf_op jit(solution)/shard_map/ppermute | solution.py:366
  55.9 16.0 %collective-permute-start.16 = (bf16[32,1728]{1,0:T(8,128)(2,1)S(1)}, bf16[32,1728]{1,0:T(8,128)(2,1)S(1)}, u32[]{:S(2)}, u32[]{:S(2)}) collective-permute-start(bf16[32,1728]{1,0:T(8,128)(2,1)S(1)} %get-tuple-element.67), channel_id=1, source_target_pairs={{0,16},{4,20},{8,24},{12,28},{16,0},{20,4},{24,8},{28,12},{1,17},{... | collective-permute-start | bytes 331784 | tf_op jit(solution)/shard_map/ppermute | solution.py:366
  60.8 13.1 %collective-permute-start.17 = (bf16[32,1728]{1,0:T(8,128)(2,1)S(1)}, bf16[32,1728]{1,0:T(8,128)(2,1)S(1)}, u32[]{:S(2)}, u32[]{:S(2)}) collective-permute-start(bf16[32,1728]{1,0:T(8,128)(2,1)S(1)} %get-tuple-element.68), channel_id=1, source_target_pairs={{0,24},{4,28},{8,16},{12,20},{16,8},{20,12},{24,0},{28,4},{1,25},{... | collective-permute-start | bytes 331784 | tf_op jit(solution)/shard_map/ppermute | solution.py:366
  67.4 8.4 %collective-permute-start.22 = (bf16[32,1280]{1,0:T(8,128)(2,1)S(1)}, bf16[32,1280]{1,0:T(8,128)(2,1)S(1)}, u32[]{:S(2)}, u32[]{:S(2)}) collective-permute-start(bf16[32,1280]{1,0:T(8,128)(2,1)S(1)} %get-tuple-element.79), channel_id=1, source_target_pairs={{0,8},{4,12},{8,0},{12,4},{16,24},{20,28},{24,16},{28,20},{1,9},{5... | collective-permute-start | bytes 245768 | tf_op jit(solution)/shard_map/ppermute | solution.py:366
  67.5 8.3 %collective-permute-start.23 = (bf16[32,1280]{1,0:T(8,128)(2,1)S(1)}, bf16[32,1280]{1,0:T(8,128)(2,1)S(1)}, u32[]{:S(2)}, u32[]{:S(2)}) collective-permute-start(bf16[32,1280]{1,0:T(8,128)(2,1)S(1)} %get-tuple-element.80), channel_id=1, source_target_pairs={{0,16},{4,20},{8,24},{12,28},{16,0},{20,4},{24,8},{28,12},{1,17},{... | collective-permute-start | bytes 245768 | tf_op jit(solution)/shard_map/ppermute | solution.py:366
  71.2 6.3 %collective-permute-start.24 = (bf16[32,1280]{1,0:T(8,128)(2,1)S(1)}, bf16[32,1280]{1,0:T(8,128)(2,1)S(1)}, u32[]{:S(2)}, u32[]{:S(2)}) collective-permute-start(bf16[32,1280]{1,0:T(8,128)(2,1)S(1)} %get-tuple-element.81), channel_id=1, source_target_pairs={{0,24},{4,28},{8,16},{12,20},{16,8},{20,12},{24,0},{28,4},{1,25},{... | collective-permute-start | bytes 245768 | tf_op jit(solution)/shard_map/ppermute | solution.py:366
  71.9 3.9 %collective-permute-start.25 = (bf16[32,448]{1,0:T(8,128)(2,1)S(1)}, bf16[32,448]{1,0:T(8,128)(2,1)S(1)}, u32[]{:S(2)}, u32[]{:S(2)}) collective-permute-start(bf16[32,448]{1,0:T(8,128)(2,1)S(1)} %get-tuple-element.82), channel_id=1, source_target_pairs={{0,4},{4,0},{8,12},{12,8},{16,20},{20,16},{24,28},{28,24},{1,5},{5... | collective-permute-start | bytes 86024 | tf_op jit(solution)/shard_map/ppermute | solution.py:366

commit v6 on v5

--- a/solution.py
+++ b/solution.py
@@ -9,7 +9,7 @@
 
 BLK = 128
 HB = 2
-Y_FIRST = 20
+Y_FIRST = 24
 RIM = HB * BLK
 STEP = 256
 F32 = jnp.float32
@@ -538,6 +538,7 @@
         [held(v) for v in [spread_two] + pieces],
         [ext, pltpu.VMEM((slabs // 2,) + far_part, F32)],
         vmem=14,
+        flops=work // 4,
     )
     gots_far = [swap(v, "space", 2 * (j + 1)) for j, v in enumerate(sends_far)]
     got_two = swap(send_two, "space", 1)

time: 78.6 us -> 77.2 us (0.982)
  transfers between devices with their start and end apart: 26 -> 26, of which waited for: 9 -> 9; matrix products, arithmetic and copies ran while one was open for 0% -> 0% of each run, Pallas kernels for 38% -> 39%
where the time goes in v6:
time: 77.2 us; the launch traced here: 77 us
  starting transfers between devices  33.8 us (44%)
  Pallas kernels  31.4 us (41%)
  waiting for transfers between devices  11 us (14%)
  between operations  0.82 us (1%)
    ppermute x24, starting transfers between devices, swap(): lax.ppermute(value, axis, [(i, i ^ bits) for i in range(lax.axis_size(axi...  32.3 us
    pallas_call x19, Pallas kernels, call(): return kernel(*ins)  31.4 us
    ppermute x24, waiting for transfers between devices, swap(): lax.ppermute(value, axis, [(i, i ^ bits) for i in range(lax.axis_size(axi...  11 us
  transfers between devices with their start and end apart: 26, of which 9 were waited for; matrix products, arithmetic and copies ran while one was open for 0% of the time, Pallas kernels for 39%

profile of v6, /device:TPU:0, one launch (start us, length us, event | category | flops | bytes accessed | tf_op | source)
XLA Modules:
  0.0 77.0 jit_solution(3005794792990305288)
XLA Ops:
  0.6 3.0 %collective-permute-start.1 = (bf16[64,2048]{1,0:T(8,128)(2,1)}, bf16[64,2048]{1,0:T(8,128)(2,1)S(1)}, u32[]{:S(2)}, u32[]{:S(2)}) collective-permute-start(bf16[64,2048]{1,0:T(8,128)(2,1)} %bitcast.17), channel_id=1, source_target_pairs={{0,2},{1,3},{2,0},{3,1},{4,6},{5,7},{6,4},{7,5},{8,10},{9,11},{10,... | collective-permute-start | bytes 786440 | tf_op jit(solution)/shard_map/ppermute | solution.py:366
  3.6 7.5 %input_grad_body.1 = (s32[24,27]{1,0:T(8,128)S(1)}, bf16[20,1728,128]{2,1,0:T(8,128)(2,1)S(1)}, bf16[2,64,2560]{2,1,0:T(8,128)(2,1)S(1)}, bf16[2,64,2560]{2,1,0:T(8,128)(2,1)S(1)}, bf16[64,2048]{1,0:T(8,128)(2,1)S(1)}) custom-call(s32[8]{0:T(128)} %refs_0_.1, s32[3,16,27]{2,1,0:T(8,128)} %bitcast.20, bf16[64,2048]{1,0:T(8,128)(2,1)} %bitcast.16, ...), custom_call_target="tpu_custom_call" | custom-call | flops 2264924160 | bytes 16777216 | tf_op jit(solution)/shard_map/input_grad_body/pallas_call | solution.py:49
  11.2 0.6 collective-permute-start.2
  11.7 0.1 collective-permute-start.5
  11.8 0.0 collective-permute-done.refs_2_
  11.8 1.1 %collective-permute-done.2.refs_4_ = bf16[64,2048]{1,0:T(8,128)(2,1)S(1)} collective-permute-done((bf16[64,2048]{1,0:T(8,128)(2,1)S(1)}, bf16[64,2048]{1,0:T(8,128)(2,1)S(1)}, u32[]{:S(2)}, u32[]{:S(2)}) %collective-permute-start.2) | collective-permute-done | bytes 262176 | tf_op jit(solution)/shard_map/ppermute | solution.py:366
  12.9 0.8 %cut_body.1 = (bf16[128,256]{1,0:T(8,128)(2,1)S(1)}, bf16[128,256]{1,0:T(8,128)(2,1)S(1)}) custom-call(s32[24,27]{1,0:T(8,128)S(1)} %get-tuple-element.43.refs_0_, bf16[64,2048]{1,0:T(8,128)(2,1)S(1)} %get-tuple-element.44.refs_1_, bf16[64,2048]{1,0:T(8,128)(2,1)S(1)} %collective-permute-done.refs_2_, bf16[64,2048]{1,0:T(8,128)(2,1)S(1)} %pass_body.1.refs_3_, ...), custom_call_target="tpu_custom_call" | custom-call | flops 18119393280 | tf_op jit(solution)/shard_map/cut_body/pallas_call | solution.py:49
  13.7 0.7 collective-permute-start.4
  14.4 4.4 %collective-permute-start.3 = (bf16[128,256]{1,0:T(8,128)(2,1)S(1)}, bf16[128,256]{1,0:T(8,128)(2,1)S(1)}, u32[]{:S(2)}, u32[]{:S(2)}) collective-permute-start(bf16[128,256]{1,0:T(8,128)(2,1)S(1)} %get-tuple-element.46.refs_2_), channel_id=1, source_target_pairs={{0,4},{4,0},{8,12},{12,8},{16,20},{20,16},{24,28},{28,24},{1,5},{5... | collective-permute-start | bytes 196616 | tf_op jit(solution)/shard_map/ppermute | solution.py:366
  18.7 0.2 halve_body.3
  18.9 0.7 collective-permute-start.7
  19.6 2.1 %inner_body.1 = (f32[20,1728,128]{2,1,0:T(8,128)S(1)}, bf16[256,2048]{1,0:T(8,128)(2,1)S(1)}) custom-call(bf16[1728,256]{1,0:T(8,128)(2,1)S(1)} %bitcast.10, bf16[64,2048]{1,0:T(8,128)(2,1)S(1)} %get-tuple-element.44.refs_1_, bf16[64,2048]{1,0:T(8,128)(2,1)S(1)} %collective-permute-done.refs_2_, bf16[64,2048]{1,0:T(8,128)(2,1)S(1)} %pass_body.1.refs_3_, ...), custom_call_target="tpu_custom_call" | custom-call | flops 2264924160 | bytes 16777216 | tf_op jit(solution)/shard_map/inner_body/pallas_call | solution.py:49
  21.7 0.1 collective-permute-start.6
  21.8 1.3 %collective-permute-done.6.refs_3_ = bf16[128,512]{1,0:T(8,128)(2,1)S(1)} collective-permute-done((bf16[128,512]{1,0:T(8,128)(2,1)S(1)}, bf16[128,512]{1,0:T(8,128)(2,1)S(1)}, u32[]{:S(2)}, u32[]{:S(2)}) %collective-permute-start.6) | collective-permute-done | bytes 131104 | tf_op jit(solution)/shard_map/ppermute | solution.py:366
  23.1 3.3 %hidden_body.1 = (f32[64,2048]{1,0:T(8,128)S(1)}, bf16[64,2048]{1,0:T(8,128)(2,1)S(1)}, bf16[256,512]{1,0:T(8,128)(2,1)S(1)}, f32[20,1728,128]{2,1,0:T(8,128)S(1)}) custom-call(s32[24,27]{1,0:T(8,128)S(1)} %get-tuple-element.43.refs_0_, bf16[1728,256]{1,0:T(8,128)(2,1)S(1)} %bitcast.11, ...), custom_call_target="tpu_custom_call", output_to_operand_aliasing={{3}: (4, {})} | custom-call | tf_op jit(solution)/shard_map/hidden_body/pallas_call | solution.py:49
  26.4 2.0 %collective-permute-done.7.refs_3_.refs_6_ = bf16[64,2560]{1,0:T(8,128)(2,1)S(1)} collective-permute-done((bf16[64,2560]{1,0:T(8,128)(2,1)S(1)}, bf16[64,2560]{1,0:T(8,128)(2,1)S(1)}, u32[]{:S(2)}, u32[]{:S(2)}) %collective-permute-start.7) | collective-permute-done | bytes 327712 | tf_op jit(solution)/shard_map/ppermute | solution.py:366
  28.4 0.8 turn_body.1
  29.2 0.8 %collective-permute-start.9 = (bf16[2,64,256]{2,1,0:T(8,128)(2,1)S(1)}, bf16[2,64,256]{2,1,0:T(8,128)(2,1)S(1)}, u32[]{:S(2)}, u32[]{:S(2)}) collective-permute-start(bf16[2,64,256]{2,1,0:T(8,128)(2,1)S(1)} %get-tuple-element.55), channel_id=1, source_target_pairs={{4,8},{12,16},{20,24},{8,4},{16,12},{24,20},{5,9},{13,17},{21,25},... | collective-permute-start | bytes 196616 | tf_op jit(solution)/shard_map/ppermute | solution.py:371
  30.0 4.3 %collective-permute-start.8 = (bf16[2,64,256]{2,1,0:T(8,128)(2,1)S(1)}, bf16[2,64,256]{2,1,0:T(8,128)(2,1)S(1)}, u32[]{:S(2)}, u32[]{:S(2)}) collective-permute-start(bf16[2,64,256]{2,1,0:T(8,128)(2,1)S(1)} %get-tuple-element.54.refs_3_), channel_id=1, source_target_pairs={{0,4},{4,0},{8,12},{12,8},{16,20},{20,16},{24,28},{28,24},{1,5},{5... | collective-permute-start | bytes 196616 | tf_op jit(solution)/shard_map/ppermute | solution.py:366
  34.4 0.5 collective-permute-start.11
  34.9 0.3 prepare_body.1
  35.2 1.4 %collective-permute-done.8.refs_1_.refs_2_ = bf16[2,64,256]{2,1,0:T(8,128)(2,1)S(1)} collective-permute-done((bf16[2,64,256]{2,1,0:T(8,128)(2,1)S(1)}, bf16[2,64,256]{2,1,0:T(8,128)(2,1)S(1)}, u32[]{:S(2)}, u32[]{:S(2)}) %collective-permute-start.8) | collective-permute-done | bytes 65568 | tf_op jit(solution)/shard_map/ppermute | solution.py:366
  36.6 0.6 collective-permute-start.12
  37.2 6.0 %grad_one_body.1 = (f32[4,32,1728]{2,1,0:T(8,128)S(1)}, bf16[4,32,1728]{2,1,0:T(8,128)(2,1)S(1)}) custom-call(s32[24,27]{1,0:T(8,128)S(1)} %get-tuple-element.43.refs_0_, f32[64,2048]{1,0:T(8,128)S(1)} %get-tuple-element.60.refs_1_, bf16[2,64,256]{2,1,0:T(8,128)(2,1)S(1)} %collective-permute-done.8.refs_1_.refs_2_, ...), custom_call_target="tpu_custom_call" | custom-call | flops 2264924160 | bytes 16777216 | tf_op jit(solution)/shard_map/grad_one_body/pallas_call | solution.py:49
  43.3 2.1 %collective-permute-start.14 = (bf16[4,32,1728]{2,1,0:T(8,128)(2,1)S(1)}, bf16[4,32,1728]{2,1,0:T(8,128)(2,1)S(1)}, u32[]{:S(2)}, u32[]{:S(2)}) collective-permute-start(bf16[4,32,1728]{2,1,0:T(8,128)(2,1)S(1)} %get-tuple-element.63), channel_id=1, source_target_pairs={{0,4},{4,0},{8,12},{12,8},{16,20},{20,16},{24,28},{28,24},{1,5},{5... | collective-permute-start | bytes 1327112 | tf_op jit(solution)/shard_map/ppermute | solution.py:366
  45.4 0.6 collective-permute-start.13
  46.0 1.0 %collective-permute-done.10.refs_3_.refs_2_ = bf16[64,2560]{1,0:T(8,128)(2,1)S(1)} collective-permute-done((bf16[64,2560]{1,0:T(8,128)(2,1)S(1)}, bf16[64,2560]{1,0:T(8,128)(2,1)S(1)}, u32[]{:S(2)}, u32[]{:S(2)}) %collective-permute-start.10) | collective-permute-done | bytes 327712 | tf_op jit(solution)/shard_map/ppermute | solution.py:366
  47.0 0.5 collective-permute-done.13.refs_5_.refs_4_
  47.5 2.7 %grad_two_body.1 = (f32[4,32,1536]{2,1,0:T(8,128)S(1)}, bf16[4,32,1536]{2,1,0:T(8,128)(2,1)S(1)}, f32[2,32,192]{2,1,0:T(8,128)S(1)}, bf16[2,32,192]{2,1,0:T(8,12...) custom-call(bf16[20,1728,128]{2,1,0:T(8,128)(2,1)S(1)} %get-tuple-element.69.refs_0_, ...), custom_call_target="tpu_custom_call" | custom-call | flops 566231040 | tf_op jit(solution)/shard_map/grad_two_body/pallas_call | solution.py:49
  50.1 1.7 %collective-permute-start.19 = (bf16[2,32,192]{2,1,0:T(8,128)(2,1)S(1)}, bf16[2,32,192]{2,1,0:T(8,128)(2,1)S(1)}, u32[]{:S(2)}, u32[]{:S(2)}) collective-permute-start(bf16[2,32,192]{2,1,0:T(8,128)(2,1)S(1)} %get-tuple-element.73), channel_id=1, source_target_pairs={{0,8},{4,12},{8,0},{12,4},{16,24},{20,28},{24,16},{28,20},{1,9},{5... | collective-permute-start | bytes 73736 | tf_op jit(solution)/shard_map/ppermute | solution.py:366
  51.8 0.1 collective-permute-start.20
  51.9 2.7 %collective-permute-start.21 = (bf16[2,32,192]{2,1,0:T(8,128)(2,1)S(1)}, bf16[2,32,192]{2,1,0:T(8,128)(2,1)S(1)}, u32[]{:S(2)}, u32[]{:S(2)}) collective-permute-start(bf16[2,32,192]{2,1,0:T(8,128)(2,1)S(1)} %get-tuple-element.75), channel_id=1, source_target_pairs={{0,24},{4,28},{8,16},{12,20},{16,8},{20,12},{24,0},{28,4},{1,25},{... | collective-permute-start | bytes 73736 | tf_op jit(solution)/shard_map/ppermute | solution.py:366
  54.6 0.1 collective-permute-start.18
  54.7 0.1 halve_body.4
  54.8 1.1 %collective-permute-start.15 = (bf16[32,1728]{1,0:T(8,128)(2,1)S(1)}, bf16[32,1728]{1,0:T(8,128)(2,1)S(1)}, u32[]{:S(2)}, u32[]{:S(2)}) collective-permute-start(bf16[32,1728]{1,0:T(8,128)(2,1)S(1)} %get-tuple-element.66), channel_id=1, source_target_pairs={{0,8},{4,12},{8,0},{12,4},{16,24},{20,28},{24,16},{28,20},{1,9},{5... | collective-permute-start | bytes 331784 | tf_op jit(solution)/shard_map/ppermute | solution.py:366
  55.8 3.4 %collective-permute-start.16 = (bf16[32,1728]{1,0:T(8,128)(2,1)S(1)}, bf16[32,1728]{1,0:T(8,128)(2,1)S(1)}, u32[]{:S(2)}, u32[]{:S(2)}) collective-permute-start(bf16[32,1728]{1,0:T(8,128)(2,1)S(1)} %get-tuple-element.67), channel_id=1, source_target_pairs={{0,16},{4,20},{8,24},{12,28},{16,0},{20,4},{24,8},{28,12},{1,17},{... | collective-permute-start | bytes 331784 | tf_op jit(solution)/shard_map/ppermute | solution.py:366
  59.2 0.0 collective-permute-start.17
  59.2 5.8 %output_body.1 = (bf16[64,2048]{1,0:T(8,128)(2,1)}, f32[8,128]{1,0:T(8,128)S(1)}) custom-call(s32[24,27]{1,0:T(8,128)S(1)} %get-tuple-element.43.refs_0_, bf16[1728,256]{1,0:T(8,128)(2,1)S(1)} %bitcast.13, bf16[64,2560]{1,0:T(8,128)(2,1)S(1)} %get-tuple-element.56.refs_2_.refs_1_, bf16[64,2560]{1,0:T(8,128)(2,1)S(1)} %collective-permute-done.10.refs_3_.refs_2_, ...), custom_call_target="tpu_custom_call" | custom-call | flops 18119393280 | bytes 16777216 | tf_op jit(solution)/shard_map/output_body/pallas_call | solution.py:49
  65.1 0.1 halve_body.5
  65.2 0.7 collective-permute-start.22
  65.9 3.8 %collective-permute-start.23 = (bf16[32,1536]{1,0:T(8,128)(2,1)S(1)}, bf16[32,1536]{1,0:T(8,128)(2,1)S(1)}, u32[]{:S(2)}, u32[]{:S(2)}) collective-permute-start(bf16[32,1536]{1,0:T(8,128)(2,1)S(1)} %get-tuple-element.80), channel_id=1, source_target_pairs={{0,16},{4,20},{8,24},{12,28},{16,0},{20,4},{24,8},{28,12},{1,17},{... | collective-permute-start | bytes 294920 | tf_op jit(solution)/shard_map/ppermute | solution.py:366
  69.6 0.0 collective-permute-start.24
  69.7 2.0 %collective-permute-start.25 = (bf16[32,192]{1,0:T(8,128)(2,1)S(1)}, bf16[32,192]{1,0:T(8,128)(2,1)S(1)}, u32[]{:S(2)}, u32[]{:S(2)}) collective-permute-start(bf16[32,192]{1,0:T(8,128)(2,1)S(1)} %get-tuple-element.82), channel_id=1, source_target_pairs={{0,4},{4,0},{8,12},{12,8},{16,20},{20,16},{24,28},{28,24},{1,5},{5... | collective-permute-start | bytes 36872 | tf_op jit(solution)/shard_map/ppermute | solution.py:366
  71.6 0.9 %finish_body.2 = f32[27,32,64]{2,1,0:T(8,128)} custom-call(f32[32,1728]{1,0:T(8,128)S(1)} %get-tuple-element.64.refs_6_.refs_0_, bf16[32,1728]{1,0:T(8,128)(2,1)S(1)} %collective-permute-done.15.refs_1_, bf16[32,1728]{1,0:T(8,128)(2,1)S(1)} %collective-permute-done.16.refs_2_, bf16[32,1728]{1,0:T(8,128)(2,1)S(1)} %collective-permute-done.17.refs_3_), custom_call_target="tpu_custom_call" | custom-call | bytes 2097152 | tf_op jit(solution)/shard_map/finish_body/pallas_call | solution.py:49
  72.5 0.9 %collective-permute-done.25.refs_5_ = bf16[32,192]{1,0:T(8,128)(2,1)S(1)} collective-permute-done((bf16[32,192]{1,0:T(8,128)(2,1)S(1)}, bf16[32,192]{1,0:T(8,128)(2,1)S(1)}, u32[]{:S(2)}, u32[]{:S(2)}) %collective-permute-start.25) | collective-permute-done | bytes 12320 | tf_op jit(solution)/shard_map/ppermute | solution.py:366
  73.4 0.8 collective-permute-done.23.refs_2_
  74.2 2.0 %collective-permute-done.24.refs_3_ = bf16[32,1536]{1,0:T(8,128)(2,1)S(1)} collective-permute-done((bf16[32,1536]{1,0:T(8,128)(2,1)S(1)}, bf16[32,1536]{1,0:T(8,128)(2,1)S(1)}, u32[]{:S(2)}, u32[]{:S(2)}) %collective-permute-start.24) | collective-permute-done | bytes 98336 | tf_op jit(solution)/shard_map/ppermute | solution.py:366
  76.1 0.9 %finish_body.3 = f32[27,32,64]{2,1,0:T(8,128)} custom-call(f32[32,1536]{1,0:T(8,128)S(1)} %get-tuple-element.78.refs_0_, bf16[32,1536]{1,0:T(8,128)(2,1)S(1)} %collective-permute-done.22.refs_1_, bf16[32,1536]{1,0:T(8,128)(2,1)S(1)} %collective-permute-done.23.refs_2_, bf16[32,1536]{1,0:T(8,128)(2,1)S(1)} %collective-permute-done.24.refs_3_, ...), custom_call_target="tpu_custom_call" | custom-call | bytes 2097152 | tf_op jit(solution)/shard_map/finish_body/pallas_call | solution.py:49
  (27 shorter events, 0.2 us)
Async XLA Ops:
  0.6 10.5 %collective-permute-start.1 = (bf16[64,2048]{1,0:T(8,128)(2,1)}, bf16[64,2048]{1,0:T(8,128)(2,1)S(1)}, u32[]{:S(2)}, u32[]{:S(2)}) collective-permute-start(bf16[64,2048]{1,0:T(8,128)(2,1)} %bitcast.17), channel_id=1, source_target_pairs={{0,2},{1,3},{2,0},{3,1},{4,6},{5,7},{6,4},{7,5},{8,10},{9,11},{10,... | collective-permute-start | bytes 786440 | tf_op jit(solution)/shard_map/ppermute | solution.py:366
  3.6 8.2 %collective-permute-start = (bf16[64,2048]{1,0:T(8,128)(2,1)}, bf16[64,2048]{1,0:T(8,128)(2,1)S(1)}, u32[]{:S(2)}, u32[]{:S(2)}) collective-permute-start(bf16[64,2048]{1,0:T(8,128)(2,1)} %bitcast.18), channel_id=1, source_target_pairs={{0,1},{1,0},{2,3},{3,2},{4,5},{5,4},{6,7},{7,6},{8,9},{9,8},{10,11... | collective-permute-start | bytes 786440 | tf_op jit(solution)/shard_map/ppermute | solution.py:366
  11.2 1.7 %collective-permute-start.2 = (bf16[64,2048]{1,0:T(8,128)(2,1)S(1)}, bf16[64,2048]{1,0:T(8,128)(2,1)S(1)}, u32[]{:S(2)}, u32[]{:S(2)}) collective-permute-start(bf16[64,2048]{1,0:T(8,128)(2,1)S(1)} %pass_body.1.refs_3_), channel_id=1, source_target_pairs={{0,1},{1,0},{2,3},{3,2},{4,5},{5,4},{6,7},{7,6},{8,9},{9,8},{10,11... | collective-permute-start | bytes 786440 | tf_op jit(solution)/shard_map/ppermute | solution.py:366
  11.7 7.0 %collective-permute-start.5 = (bf16[2,64,2560]{2,1,0:T(8,128)(2,1)S(1)}, bf16[2,64,2560]{2,1,0:T(8,128)(2,1)S(1)}, u32[]{:S(2)}, u32[]{:S(2)}) collective-permute-start(bf16[2,64,2560]{2,1,0:T(8,128)(2,1)S(1)} %get-tuple-element.45.refs_1_), channel_id=1, source_target_pairs={{0,1},{1,0},{2,3},{3,2},{4,5},{5,4},{6,7},{7,6},{8,9},{9,8},{10,11... | collective-permute-start | bytes 1966088 | tf_op jit(solution)/shard_map/ppermute | solution.py:366
  12.9 6.7 %copy-start = (bf16[27,64,256]{2,1,0:T(8,128)(2,1)S(1)}, bf16[27,64,256]{2,1,0:T(8,128)(2,1)}, u32[]{:S(2)}) copy-start(bf16[27,64,256]{2,1,0:T(8,128)(2,1)} %param.9) | copy-start | bytes 2654212
  13.7 8.0 %collective-permute-start.4 = (bf16[128,256]{1,0:T(8,128)(2,1)S(1)}, bf16[128,256]{1,0:T(8,128)(2,1)S(1)}, u32[]{:S(2)}, u32[]{:S(2)}) collective-permute-start(bf16[128,256]{1,0:T(8,128)(2,1)S(1)} %get-tuple-element.47), channel_id=1, source_target_pairs={{4,8},{12,16},{20,24},{8,4},{16,12},{24,20},{5,9},{13,17},{21,25},... | collective-permute-start | bytes 196616 | tf_op jit(solution)/shard_map/ppermute | solution.py:371
  14.4 7.3 %collective-permute-start.3 = (bf16[128,256]{1,0:T(8,128)(2,1)S(1)}, bf16[128,256]{1,0:T(8,128)(2,1)S(1)}, u32[]{:S(2)}, u32[]{:S(2)}) collective-permute-start(bf16[128,256]{1,0:T(8,128)(2,1)S(1)} %get-tuple-element.46.refs_2_), channel_id=1, source_target_pairs={{0,4},{4,0},{8,12},{12,8},{16,20},{20,16},{24,28},{28,24},{1,5},{5... | collective-permute-start | bytes 196616 | tf_op jit(solution)/shard_map/ppermute | solution.py:366
  18.9 9.5 %collective-permute-start.7 = (bf16[64,2560]{1,0:T(8,128)(2,1)S(1)}, bf16[64,2560]{1,0:T(8,128)(2,1)S(1)}, u32[]{:S(2)}, u32[]{:S(2)}) collective-permute-start(bf16[64,2560]{1,0:T(8,128)(2,1)S(1)} %get-tuple-element.53), channel_id=1, source_target_pairs={{0,2},{1,3},{2,0},{3,1},{4,6},{5,7},{6,4},{7,5},{8,10},{9,11},{10,... | collective-permute-start | bytes 983048 | tf_op jit(solution)/shard_map/ppermute | solution.py:366
  21.7 1.4 %collective-permute-start.6 = (bf16[128,512]{1,0:T(8,128)(2,1)S(1)}, bf16[128,512]{1,0:T(8,128)(2,1)S(1)}, u32[]{:S(2)}, u32[]{:S(2)}) collective-permute-start(bf16[128,512]{1,0:T(8,128)(2,1)S(1)} %stack_body.1.refs_2_), channel_id=1, source_target_pairs={{0,1},{1,0},{2,3},{3,2},{4,5},{5,4},{6,7},{7,6},{8,9},{9,8},{10,11... | collective-permute-start | bytes 393224 | tf_op jit(solution)/shard_map/ppermute | solution.py:366
  23.1 36.1 %copy-start.1 = (bf16[27,64,256]{2,1,0:T(8,128)(2,1)S(1)}, bf16[27,64,256]{2,1,0:T(8,128)(2,1)}, u32[]{:S(2)}) copy-start(bf16[27,64,256]{2,1,0:T(8,128)(2,1)} %param.10) | copy-start | bytes 2654212
  29.2 6.0 %collective-permute-start.9 = (bf16[2,64,256]{2,1,0:T(8,128)(2,1)S(1)}, bf16[2,64,256]{2,1,0:T(8,128)(2,1)S(1)}, u32[]{:S(2)}, u32[]{:S(2)}) collective-permute-start(bf16[2,64,256]{2,1,0:T(8,128)(2,1)S(1)} %get-tuple-element.55), channel_id=1, source_target_pairs={{4,8},{12,16},{20,24},{8,4},{16,12},{24,20},{5,9},{13,17},{21,25},... | collective-permute-start | bytes 196616 | tf_op jit(solution)/shard_map/ppermute | solution.py:371
  30.0 6.6 %collective-permute-start.8 = (bf16[2,64,256]{2,1,0:T(8,128)(2,1)S(1)}, bf16[2,64,256]{2,1,0:T(8,128)(2,1)S(1)}, u32[]{:S(2)}, u32[]{:S(2)}) collective-permute-start(bf16[2,64,256]{2,1,0:T(8,128)(2,1)S(1)} %get-tuple-element.54.refs_3_), channel_id=1, source_target_pairs={{0,4},{4,0},{8,12},{12,8},{16,20},{20,16},{24,28},{28,24},{1,5},{5... | collective-permute-start | bytes 196616 | tf_op jit(solution)/shard_map/ppermute | solution.py:366
  34.4 11.0 %collective-permute-start.11 = (bf16[64,2048]{1,0:T(8,128)(2,1)S(1)}, bf16[64,2048]{1,0:T(8,128)(2,1)S(1)}, u32[]{:S(2)}, u32[]{:S(2)}) collective-permute-start(bf16[64,2048]{1,0:T(8,128)(2,1)S(1)} %get-tuple-element.52.refs_1_.refs_0_), channel_id=1, source_target_pairs={{0,2},{1,3},{2,0},{3,1},{4,6},{5,7},{6,4},{7,5},{8,10},{9,11},{10,... | collective-permute-start | bytes 786440 | tf_op jit(solution)/shard_map/ppermute | solution.py:366
  36.6 8.7 %collective-permute-start.12 = (bf16[64,512]{1,0:T(8,128)(2,1)S(1)}, bf16[64,512]{1,0:T(8,128)(2,1)S(1)}, u32[]{:S(2)}, u32[]{:S(2)}) collective-permute-start(bf16[64,512]{1,0:T(8,128)(2,1)S(1)} %get-tuple-element.57), channel_id=1, source_target_pairs={{0,2},{1,3},{2,0},{3,1},{4,6},{5,7},{6,4},{7,5},{8,10},{9,11},{10,... | collective-permute-start | bytes 196616 | tf_op jit(solution)/shard_map/ppermute | solution.py:366
  43.3 11.4 %collective-permute-start.14 = (bf16[4,32,1728]{2,1,0:T(8,128)(2,1)S(1)}, bf16[4,32,1728]{2,1,0:T(8,128)(2,1)S(1)}, u32[]{:S(2)}, u32[]{:S(2)}) collective-permute-start(bf16[4,32,1728]{2,1,0:T(8,128)(2,1)S(1)} %get-tuple-element.63), channel_id=1, source_target_pairs={{0,4},{4,0},{8,12},{12,8},{16,20},{20,16},{24,28},{28,24},{1,5},{5... | collective-permute-start | bytes 1327112 | tf_op jit(solution)/shard_map/ppermute | solution.py:366
  45.4 1.6 %collective-permute-start.10 = (bf16[64,2560]{1,0:T(8,128)(2,1)S(1)}, bf16[64,2560]{1,0:T(8,128)(2,1)S(1)}, u32[]{:S(2)}, u32[]{:S(2)}) collective-permute-start(bf16[64,2560]{1,0:T(8,128)(2,1)S(1)} %get-tuple-element.56.refs_2_.refs_1_), channel_id=1, source_target_pairs={{0,1},{1,0},{2,3},{3,2},{4,5},{5,4},{6,7},{7,6},{8,9},{9,8},{10,11... | collective-permute-start | bytes 983048 | tf_op jit(solution)/shard_map/ppermute | solution.py:366
  45.4 2.1 %collective-permute-start.13 = (bf16[64,2560]{1,0:T(8,128)(2,1)S(1)}, bf16[64,2560]{1,0:T(8,128)(2,1)S(1)}, u32[]{:S(2)}, u32[]{:S(2)}) collective-permute-start(bf16[64,2560]{1,0:T(8,128)(2,1)S(1)} %append_body.1.refs_4_.refs_3_), channel_id=1, source_target_pairs={{0,1},{1,0},{2,3},{3,2},{4,5},{5,4},{6,7},{7,6},{8,9},{9,8},{10,11... | collective-permute-start | bytes 983048 | tf_op jit(solution)/shard_map/ppermute | solution.py:366
  50.1 5.7 %collective-permute-start.19 = (bf16[2,32,192]{2,1,0:T(8,128)(2,1)S(1)}, bf16[2,32,192]{2,1,0:T(8,128)(2,1)S(1)}, u32[]{:S(2)}, u32[]{:S(2)}) collective-permute-start(bf16[2,32,192]{2,1,0:T(8,128)(2,1)S(1)} %get-tuple-element.73), channel_id=1, source_target_pairs={{0,8},{4,12},{8,0},{12,4},{16,24},{20,28},{24,16},{28,20},{1,9},{5... | collective-permute-start | bytes 73736 | tf_op jit(solution)/shard_map/ppermute | solution.py:366
  51.8 7.4 %collective-permute-start.20 = (bf16[2,32,192]{2,1,0:T(8,128)(2,1)S(1)}, bf16[2,32,192]{2,1,0:T(8,128)(2,1)S(1)}, u32[]{:S(2)}, u32[]{:S(2)}) collective-permute-start(bf16[2,32,192]{2,1,0:T(8,128)(2,1)S(1)} %get-tuple-element.74), channel_id=1, source_target_pairs={{0,16},{4,20},{8,24},{12,28},{16,0},{20,4},{24,8},{28,12},{1,17},{... | collective-permute-start | bytes 73736 | tf_op jit(solution)/shard_map/ppermute | solution.py:366
  51.9 13.2 %collective-permute-start.21 = (bf16[2,32,192]{2,1,0:T(8,128)(2,1)S(1)}, bf16[2,32,192]{2,1,0:T(8,128)(2,1)S(1)}, u32[]{:S(2)}, u32[]{:S(2)}) collective-permute-start(bf16[2,32,192]{2,1,0:T(8,128)(2,1)S(1)} %get-tuple-element.75), channel_id=1, source_target_pairs={{0,24},{4,28},{8,16},{12,20},{16,8},{20,12},{24,0},{28,4},{1,25},{... | collective-permute-start | bytes 73736 | tf_op jit(solution)/shard_map/ppermute | solution.py:366
  54.6 10.5 %collective-permute-start.18 = (bf16[4,32,1536]{2,1,0:T(8,128)(2,1)S(1)}, bf16[4,32,1536]{2,1,0:T(8,128)(2,1)S(1)}, u32[]{:S(2)}, u32[]{:S(2)}) collective-permute-start(bf16[4,32,1536]{2,1,0:T(8,128)(2,1)S(1)} %get-tuple-element.71), channel_id=1, source_target_pairs={{0,4},{4,0},{8,12},{12,8},{16,20},{20,16},{24,28},{28,24},{1,5},{5... | collective-permute-start | bytes 1179656 | tf_op jit(solution)/shard_map/ppermute | solution.py:366
  54.8 14.8 %collective-permute-start.15 = (bf16[32,1728]{1,0:T(8,128)(2,1)S(1)}, bf16[32,1728]{1,0:T(8,128)(2,1)S(1)}, u32[]{:S(2)}, u32[]{:S(2)}) collective-permute-start(bf16[32,1728]{1,0:T(8,128)(2,1)S(1)} %get-tuple-element.66), channel_id=1, source_target_pairs={{0,8},{4,12},{8,0},{12,4},{16,24},{20,28},{24,16},{28,20},{1,9},{5... | collective-permute-start | bytes 331784 | tf_op jit(solution)/shard_map/ppermute | solution.py:366
  55.8 13.8 %collective-permute-start.16 = (bf16[32,1728]{1,0:T(8,128)(2,1)S(1)}, bf16[32,1728]{1,0:T(8,128)(2,1)S(1)}, u32[]{:S(2)}, u32[]{:S(2)}) collective-permute-start(bf16[32,1728]{1,0:T(8,128)(2,1)S(1)} %get-tuple-element.67), channel_id=1, source_target_pairs={{0,16},{4,20},{8,24},{12,28},{16,0},{20,4},{24,8},{28,12},{1,17},{... | collective-permute-start | bytes 331784 | tf_op jit(solution)/shard_map/ppermute | solution.py:366
  59.2 12.4 %collective-permute-start.17 = (bf16[32,1728]{1,0:T(8,128)(2,1)S(1)}, bf16[32,1728]{1,0:T(8,128)(2,1)S(1)}, u32[]{:S(2)}, u32[]{:S(2)}) collective-permute-start(bf16[32,1728]{1,0:T(8,128)(2,1)S(1)} %get-tuple-element.68), channel_id=1, source_target_pairs={{0,24},{4,28},{8,16},{12,20},{16,8},{20,12},{24,0},{28,4},{1,25},{... | collective-permute-start | bytes 331784 | tf_op jit(solution)/shard_map/ppermute | solution.py:366
  65.2 8.2 %collective-permute-start.22 = (bf16[32,1536]{1,0:T(8,128)(2,1)S(1)}, bf16[32,1536]{1,0:T(8,128)(2,1)S(1)}, u32[]{:S(2)}, u32[]{:S(2)}) collective-permute-start(bf16[32,1536]{1,0:T(8,128)(2,1)S(1)} %get-tuple-element.79), channel_id=1, source_target_pairs={{0,8},{4,12},{8,0},{12,4},{16,24},{20,28},{24,16},{28,20},{1,9},{5... | collective-permute-start | bytes 294920 | tf_op jit(solution)/shard_map/ppermute | solution.py:366
  65.9 8.3 %collective-permute-start.23 = (bf16[32,1536]{1,0:T(8,128)(2,1)S(1)}, bf16[32,1536]{1,0:T(8,128)(2,1)S(1)}, u32[]{:S(2)}, u32[]{:S(2)}) collective-permute-start(bf16[32,1536]{1,0:T(8,128)(2,1)S(1)} %get-tuple-element.80), channel_id=1, source_target_pairs={{0,16},{4,20},{8,24},{12,28},{16,0},{20,4},{24,8},{28,12},{1,17},{... | collective-permute-start | bytes 294920 | tf_op jit(solution)/shard_map/ppermute | solution.py:366
  69.6 6.5 %collective-permute-start.24 = (bf16[32,1536]{1,0:T(8,128)(2,1)S(1)}, bf16[32,1536]{1,0:T(8,128)(2,1)S(1)}, u32[]{:S(2)}, u32[]{:S(2)}) collective-permute-start(bf16[32,1536]{1,0:T(8,128)(2,1)S(1)} %get-tuple-element.81), channel_id=1, source_target_pairs={{0,24},{4,28},{8,16},{12,20},{16,8},{20,12},{24,0},{28,4},{1,25},{... | collective-permute-start | bytes 294920 | tf_op jit(solution)/shard_map/ppermute | solution.py:366
  69.7 3.8 %collective-permute-start.25 = (bf16[32,192]{1,0:T(8,128)(2,1)S(1)}, bf16[32,192]{1,0:T(8,128)(2,1)S(1)}, u32[]{:S(2)}, u32[]{:S(2)}) collective-permute-start(bf16[32,192]{1,0:T(8,128)(2,1)S(1)} %get-tuple-element.82), channel_id=1, source_target_pairs={{0,4},{4,0},{8,12},{12,8},{16,20},{20,16},{24,28},{28,24},{1,5},{5... | collective-permute-start | bytes 36872 | tf_op jit(solution)/shard_map/ppermute | solution.py:366

commit v7 on v6

--- a/solution.py
+++ b/solution.py
@@ -26,7 +26,7 @@
 
 
 def call(body, outs, ins, scratch=(), flops=0, traffic=0, vmem=6, specs=None, after=(), aliases=None):
-    specs = list(specs or [SMEM if a.dtype == jnp.int32 else VMEM for a in ins])
+    specs = list(specs or [VMEM] * len(ins))
     first, last = len(ins), len(ins) + len(after)
     ins = list(ins) + [held(v) for v in after]
     specs += [VMEM] * len(after)
@@ -68,6 +68,11 @@
 def near_rim(tab):
     row = tab.shape[0] - PAD
     return pl.multiple_of(tab[row, 0], BLK), pl.multiple_of(tab[row, 1], BLK)
+
+
+def held_rim(tab_ref):
+    row = tab_ref.shape[0] - PAD
+    return tuple(pl.multiple_of(jnp.max(tab_ref[row:, i : i + 1]), BLK) for i in range(2))
 
 
 def table(counts, map_ref, nblocks):
@@ -181,7 +186,7 @@
     a_ref, b_ref, rims = refs[pieces:]
     depth, half = refs[0].shape[0], a_ref.shape[0]
     own = pl.ds(pl.multiple_of(lax.axis_index("chan") % 2 * half, half), half)
-    for start, out_ref in zip(near_rim(tab), (a_ref, b_ref)):
+    for start, out_ref in zip(held_rim(tab), (a_ref, b_ref)):
         for bits, ref in zip(order, refs[:pieces]):
             place = lax.axis_index("chan") ^ bits
             rims[pl.ds(pl.multiple_of(place * depth, depth), depth), :] = ref[:, pl.ds(start, RIM)]
@@ -215,11 +220,14 @@
     out_ref[:, RIM:] = b_ref[...]
 
 
-def hidden_body(tab, w_ref, own_ref, other_ref, _, z_ref, hidden_ref, rims_ref, prod, *sums):
+def hidden_body(tab_ref, w_ref, own_ref, other_ref, _, z_ref, hidden_ref, rims_ref, prod, tab, sem, *sums):
+    fetch = pltpu.make_async_copy(tab_ref, tab, sem)
+    fetch.start()
     core, half = lax.axis_index("chan") % 2, own_ref.shape[0]
     for place, ref in ((core, own_ref), (1 - core, other_ref)):
         rims_ref[pl.ds(pl.multiple_of(place * half, half), half), :] = ref[...]
     multiply(w_ref, rims_ref[...], prod, z_ref.shape[1] // BLK)
+    fetch.wait()
 
     def store(cols, z):
         z_ref[:, cols] = z
@@ -228,9 +236,11 @@
     gather_sums(tab, prod, sums, store)
 
 
-def output_body(order, tab, w_ref, *refs):
+def output_body(order, tab_ref, w_ref, *refs):
     pieces = len(order)
-    out_ref, done_ref, ext, prod, *sums = refs[pieces:]
+    out_ref, done_ref, ext, prod, tab, sem, *sums = refs[pieces:]
+    fetch = pltpu.make_async_copy(tab_ref, tab, sem)
+    fetch.start()
     done_ref[...] = jnp.zeros_like(done_ref)
     lay(ext, order, refs[:pieces])
 
@@ -240,6 +250,7 @@
     half = prod.shape[0] // 2
     for i in range(2):
         multiply(w_ref, ext[:, i * half * BLK : (i + 1) * half * BLK], prod, i * half)
+    fetch.wait()
     gather_sums(tab, prod, sums, store)
 
 
@@ -254,7 +265,7 @@
 def turn_body(count, tab, hidden_ref, mine_ref, *refs):
     gots, outs = refs[:count], refs[count:]
     rows = hidden_ref.shape[1]
-    for i, (start, out_ref) in enumerate(zip(near_rim(tab), outs)):
+    for i, (start, out_ref) in enumerate(zip(held_rim(tab), outs)):
         cols = slice(rows + i * RIM, rows + (i + 1) * RIM)
         total = mine_ref[:, cols]
         for ref in gots:
@@ -329,13 +340,16 @@
     slope_ref[...] = gate * (1.0 + z * (1.0 - gate))
 
 
-def grad_one_body(count, tab, slope_ref, from_a, from_b, ext_ref, mine_ref, *refs):
-    gots, (keep_ref, send_ref, grads, blocks, spread_ref) = refs[:count], refs[count:]
+def grad_one_body(count, tab_ref, slope_ref, from_a, from_b, ext_ref, mine_ref, *refs):
+    gots, (keep_ref, send_ref, grads, blocks, spread_ref, tab, sem) = refs[:count], refs[count:]
+    fetch = pltpu.make_async_copy(tab_ref, tab, sem)
+    fetch.start()
     rows = slope_ref.shape[1]
     inner = mine_ref[:, :rows]
     for ref in gots:
         inner = inner + ref[:, :rows].astype(F32)
     grads[...] = inner
+    fetch.wait()
     a, b = near_rim(tab)
     for start, ref in ((a, from_a), (b, from_b)):
         grads[:, pl.ds(start, RIM)] = grads[:, pl.ds(start, RIM)] + ref[0].astype(F32)
@@ -449,7 +463,7 @@
     rim_a, rim_b = call(
         functools.partial(cut_body, order),
         [half_rim, half_rim],
-        [tab] + [held(v) for v in pieces],
+        [held(tab)] + [held(v) for v in pieces],
         [pltpu.VMEM((wide, RIM), BF16)],
         flops=8 * work,
     )
@@ -464,7 +478,8 @@
     )
     gots = [swap(v, "chan", 2 * (j + 1)) for j, v in enumerate(sends)]
 
-    conv_scratch = [ext, pltpu.VMEM(spread_shape, F32)] + [blocks] * 2
+    table_scratch = [pltpu.SMEM((entries + PAD, offsets), jnp.int32), pltpu.SemaphoreType.DMA]
+    conv_scratch = [ext, pltpu.VMEM(spread_shape, F32)] + table_scratch + [blocks] * 2
     prod_one, x_wide = call(
         functools.partial(inner_body, order),
         [pltpu.VMEM(spread_shape, F32), pltpu.VMEM((wide, rows), BF16)],
@@ -480,8 +495,8 @@
     z_one, hidden, x_rims, _ = call(
         hidden_body,
         [pltpu.VMEM((depth, rows), F32), pltpu.VMEM((depth, rows), BF16), pltpu.VMEM((wide, 2 * RIM), BF16), pltpu.VMEM(spread_shape, F32)],
-        [tab, w_one] + [held(v) for v in (x_half, swap(x_half, "chan", 1), prod_one)],
-        [blocks] * 2,
+        [held(tab), w_one] + [held(v) for v in (x_half, swap(x_half, "chan", 1), prod_one)],
+        table_scratch + [blocks] * 2,
         vmem=12,
         aliases={4: 3},
     )
@@ -489,7 +504,7 @@
     to_a, to_b = call(
         functools.partial(turn_body, len(gots)),
         [pltpu.VMEM((2, depth, RIM), BF16), pltpu.VMEM((2, depth, RIM), BF16)],
-        [tab] + [held(v) for v in [hidden, mine] + gots],
+        [held(tab)] + [held(v) for v in [hidden, mine] + gots],
         traffic=2 << 20,
     )
     from_a, from_b = swap(to_a, "space", 1), swap_other(to_b)
@@ -511,8 +526,8 @@
     keep_one, send_one = call(
         functools.partial(grad_one_body, len(gots)),
         [pltpu.VMEM((slabs // 2, share, flat), F32), pltpu.VMEM((slabs // 2, share, flat), BF16)],
-        [tab] + [held(v) for v in [slope, from_a, from_b, x_ext, mine] + gots],
-        [pltpu.VMEM((depth, rows), F32), blocks, pltpu.VMEM(spread_shape, BF16)],
+        [held(tab)] + [held(v) for v in [slope, from_a, from_b, x_ext, mine] + gots],
+        [pltpu.VMEM((depth, rows), F32), blocks, pltpu.VMEM(spread_shape, BF16)] + table_scratch,
         vmem=24,
         flops=work,
         traffic=16 << 20,
@@ -546,7 +561,7 @@
     output, done = call(
         functools.partial(output_body, order),
         [jax.ShapeDtypeStruct((depth, rows), BF16), pltpu.VMEM((8, BLK), F32)],
-        [tab, w_two] + [held(v) for v in pieces],
+        [held(tab), w_two] + [held(v) for v in pieces],
         conv_scratch,
         vmem=34,
         flops=8 * work,

time: 77.2 us -> 75.3 us (0.975)
  Pallas kernels: 31.4 us -> 29 us
  waiting for transfers between devices: 11 us -> 11.8 us
    pallas_call x19, Pallas kernels: 31.4 us -> 29 us  [call(): return kernel(*ins)]
    ppermute x24, waiting for transfers between devices: 11 us -> 11.8 us  [swap(): lax.ppermute(value, axis, [(i, i ^ bits) for i in range(lax.axis_size(axi...]
  transfers between devices with their start and end apart: 26 -> 26, of which waited for: 9 -> 9; matrix products, arithmetic and copies ran while one was open for 0% -> 0% of each run, Pallas kernels for 39% -> 37%
where the time goes in v7:
time: 75.3 us; the launch traced here: 75.1 us
  starting transfers between devices  33.5 us (44%)
  Pallas kernels  29 us (39%)
  waiting for transfers between devices  11.8 us (16%)
  between operations  0.83 us (1%)
    ppermute x24, starting transfers between devices, swap(): lax.ppermute(value, axis, [(i, i ^ bits) for i in range(lax.axis_size(axi...  31.8 us
    pallas_call x19, Pallas kernels, call(): return kernel(*ins)  29 us
    ppermute x24, waiting for transfers between devices, swap(): lax.ppermute(value, axis, [(i, i ^ bits) for i in range(lax.axis_size(axi...  11.8 us
    ppermute x2, starting transfers between devices, swap_other(): return lax.ppermute(value, 'space', pairs + [(j, i) for i, j in pairs])  1.64 us
  transfers between devices with their start and end apart: 26, of which 9 were waited for; matrix products, arithmetic and copies ran while one was open for 0% of the time, Pallas kernels for 37%

profile of v7, /device:TPU:0, one launch (start us, length us, event | category | flops | bytes accessed | tf_op | source)
XLA Modules:
  0.0 75.1 jit_solution(7890353770486712008)
XLA Ops:
  0.6 3.0 %collective-permute-start.1 = (bf16[64,2048]{1,0:T(8,128)(2,1)}, bf16[64,2048]{1,0:T(8,128)(2,1)S(1)}, u32[]{:S(2)}, u32[]{:S(2)}) collective-permute-start(bf16[64,2048]{1,0:T(8,128)(2,1)} %bitcast.17), channel_id=1, source_target_pairs={{0,2},{1,3},{2,0},{3,1},{4,6},{5,7},{6,4},{7,5},{8,10},{9,11},{10,... | collective-permute-start | bytes 786440 | tf_op jit(solution)/shard_map/ppermute | solution.py:380
  3.6 7.5 %input_grad_body.1 = (s32[24,27]{1,0:T(8,128)S(1)}, bf16[20,1728,128]{2,1,0:T(8,128)(2,1)S(1)}, bf16[2,64,2560]{2,1,0:T(8,128)(2,1)S(1)}, bf16[2,64,2560]{2,1,0:T(8,128)(2,1)S(1)}, bf16[64,2048]{1,0:T(8,128)(2,1)S(1)}) custom-call(s32[8]{0:T(128)} %refs_0_.1, s32[3,16,27]{2,1,0:T(8,128)} %bitcast.20, bf16[64,2048]{1,0:T(8,128)(2,1)} %bitcast.16, ...), custom_call_target="tpu_custom_call" | custom-call | flops 2264924160 | bytes 16777216 | tf_op jit(solution)/shard_map/input_grad_body/pallas_call | solution.py:49
  11.1 0.0 collective-permute-done.1.refs_0_
  11.2 0.6 collective-permute-start.2
  11.7 0.1 collective-permute-start.5
  11.8 0.0 collective-permute-done.refs_2_
  11.8 1.1 %collective-permute-done.2.refs_4_ = bf16[64,2048]{1,0:T(8,128)(2,1)S(1)} collective-permute-done((bf16[64,2048]{1,0:T(8,128)(2,1)S(1)}, bf16[64,2048]{1,0:T(8,128)(2,1)S(1)}, u32[]{:S(2)}, u32[]{:S(2)}) %collective-permute-start.2) | collective-permute-done | bytes 262176 | tf_op jit(solution)/shard_map/ppermute | solution.py:380
  12.9 0.2 cut_body.1
  13.2 0.8 %collective-permute-start.4 = (bf16[128,256]{1,0:T(8,128)(2,1)S(1)}, bf16[128,256]{1,0:T(8,128)(2,1)S(1)}, u32[]{:S(2)}, u32[]{:S(2)}) collective-permute-start(bf16[128,256]{1,0:T(8,128)(2,1)S(1)} %get-tuple-element.47), channel_id=1, source_target_pairs={{4,8},{12,16},{20,24},{8,4},{16,12},{24,20},{5,9},{13,17},{21,25},... | collective-permute-start | bytes 196616 | tf_op jit(solution)/shard_map/ppermute | solution.py:385
  14.0 4.4 %collective-permute-start.3 = (bf16[128,256]{1,0:T(8,128)(2,1)S(1)}, bf16[128,256]{1,0:T(8,128)(2,1)S(1)}, u32[]{:S(2)}, u32[]{:S(2)}) collective-permute-start(bf16[128,256]{1,0:T(8,128)(2,1)S(1)} %get-tuple-element.46.refs_2_), channel_id=1, source_target_pairs={{0,4},{4,0},{8,12},{12,8},{16,20},{20,16},{24,28},{28,24},{1,5},{5... | collective-permute-start | bytes 196616 | tf_op jit(solution)/shard_map/ppermute | solution.py:380
  18.3 0.2 halve_body.3
  18.5 0.7 collective-permute-start.7
  19.2 2.1 %inner_body.1 = (f32[20,1728,128]{2,1,0:T(8,128)S(1)}, bf16[256,2048]{1,0:T(8,128)(2,1)S(1)}) custom-call(bf16[1728,256]{1,0:T(8,128)(2,1)S(1)} %bitcast.10, bf16[64,2048]{1,0:T(8,128)(2,1)S(1)} %get-tuple-element.44.refs_1_, bf16[64,2048]{1,0:T(8,128)(2,1)S(1)} %collective-permute-done.refs_2_, bf16[64,2048]{1,0:T(8,128)(2,1)S(1)} %pass_body.1.refs_3_, ...), custom_call_target="tpu_custom_call" | custom-call | flops 2264924160 | bytes 16777216 | tf_op jit(solution)/shard_map/inner_body/pallas_call | solution.py:49
  21.3 0.1 collective-permute-start.6
  21.4 1.3 %collective-permute-done.6.refs_3_ = bf16[128,512]{1,0:T(8,128)(2,1)S(1)} collective-permute-done((bf16[128,512]{1,0:T(8,128)(2,1)S(1)}, bf16[128,512]{1,0:T(8,128)(2,1)S(1)}, u32[]{:S(2)}, u32[]{:S(2)}) %collective-permute-start.6) | collective-permute-done | bytes 131104 | tf_op jit(solution)/shard_map/ppermute | solution.py:380
  22.7 2.7 %hidden_body.1 = (f32[64,2048]{1,0:T(8,128)S(1)}, bf16[64,2048]{1,0:T(8,128)(2,1)S(1)}, bf16[256,512]{1,0:T(8,128)(2,1)S(1)}, f32[20,1728,128]{2,1,0:T(8,128)S(1)}) custom-call(s32[24,27]{1,0:T(8,128)S(1)} %get-tuple-element.43.refs_0_, bf16[1728,256]{1,0:T(8,128)(2,1)S(1)} %bitcast.11, ...), custom_call_target="tpu_custom_call", output_to_operand_aliasing={{3}: (4, {})} | custom-call | tf_op jit(solution)/shard_map/hidden_body/pallas_call | solution.py:49
  25.4 2.6 %collective-permute-done.7.refs_3_.refs_6_ = bf16[64,2560]{1,0:T(8,128)(2,1)S(1)} collective-permute-done((bf16[64,2560]{1,0:T(8,128)(2,1)S(1)}, bf16[64,2560]{1,0:T(8,128)(2,1)S(1)}, u32[]{:S(2)}, u32[]{:S(2)}) %collective-permute-start.7) | collective-permute-done | bytes 327712 | tf_op jit(solution)/shard_map/ppermute | solution.py:380
  28.0 0.2 turn_body.1
  28.2 0.8 %collective-permute-start.9 = (bf16[2,64,256]{2,1,0:T(8,128)(2,1)S(1)}, bf16[2,64,256]{2,1,0:T(8,128)(2,1)S(1)}, u32[]{:S(2)}, u32[]{:S(2)}) collective-permute-start(bf16[2,64,256]{2,1,0:T(8,128)(2,1)S(1)} %get-tuple-element.55), channel_id=1, source_target_pairs={{4,8},{12,16},{20,24},{8,4},{16,12},{24,20},{5,9},{13,17},{21,25},... | collective-permute-start | bytes 196616 | tf_op jit(solution)/shard_map/ppermute | solution.py:385
  29.1 4.3 %collective-permute-start.8 = (bf16[2,64,256]{2,1,0:T(8,128)(2,1)S(1)}, bf16[2,64,256]{2,1,0:T(8,128)(2,1)S(1)}, u32[]{:S(2)}, u32[]{:S(2)}) collective-permute-start(bf16[2,64,256]{2,1,0:T(8,128)(2,1)S(1)} %get-tuple-element.54.refs_3_), channel_id=1, source_target_pairs={{0,4},{4,0},{8,12},{12,8},{16,20},{20,16},{24,28},{28,24},{1,5},{5... | collective-permute-start | bytes 196616 | tf_op jit(solution)/shard_map/ppermute | solution.py:380
  33.4 0.5 collective-permute-start.11
  33.9 0.3 prepare_body.1
  34.2 1.4 %collective-permute-done.8.refs_1_.refs_2_ = bf16[2,64,256]{2,1,0:T(8,128)(2,1)S(1)} collective-permute-done((bf16[2,64,256]{2,1,0:T(8,128)(2,1)S(1)}, bf16[2,64,256]{2,1,0:T(8,128)(2,1)S(1)}, u32[]{:S(2)}, u32[]{:S(2)}) %collective-permute-start.8) | collective-permute-done | bytes 65568 | tf_op jit(solution)/shard_map/ppermute | solution.py:380
  35.7 0.6 collective-permute-start.12
  36.3 6.0 %grad_one_body.1 = (f32[4,32,1728]{2,1,0:T(8,128)S(1)}, bf16[4,32,1728]{2,1,0:T(8,128)(2,1)S(1)}) custom-call(s32[24,27]{1,0:T(8,128)S(1)} %get-tuple-element.43.refs_0_, f32[64,2048]{1,0:T(8,128)S(1)} %get-tuple-element.60.refs_1_, bf16[2,64,256]{2,1,0:T(8,128)(2,1)S(1)} %collective-permute-done.8.refs_1_.refs_2_, ...), custom_call_target="tpu_custom_call" | custom-call | flops 2264924160 | bytes 16777216 | tf_op jit(solution)/shard_map/grad_one_body/pallas_call | solution.py:49
  42.2 2.1 %collective-permute-start.14 = (bf16[4,32,1728]{2,1,0:T(8,128)(2,1)S(1)}, bf16[4,32,1728]{2,1,0:T(8,128)(2,1)S(1)}, u32[]{:S(2)}, u32[]{:S(2)}) collective-permute-start(bf16[4,32,1728]{2,1,0:T(8,128)(2,1)S(1)} %get-tuple-element.63), channel_id=1, source_target_pairs={{0,4},{4,0},{8,12},{12,8},{16,20},{20,16},{24,28},{28,24},{1,5},{5... | collective-permute-start | bytes 1327112 | tf_op jit(solution)/shard_map/ppermute | solution.py:380
  44.4 0.6 collective-permute-start.13
  44.9 1.0 %collective-permute-done.10.refs_3_.refs_2_ = bf16[64,2560]{1,0:T(8,128)(2,1)S(1)} collective-permute-done((bf16[64,2560]{1,0:T(8,128)(2,1)S(1)}, bf16[64,2560]{1,0:T(8,128)(2,1)S(1)}, u32[]{:S(2)}, u32[]{:S(2)}) %collective-permute-start.10) | collective-permute-done | bytes 327712 | tf_op jit(solution)/shard_map/ppermute | solution.py:380
  45.9 0.5 collective-permute-done.13.refs_5_.refs_4_
  46.4 2.7 %grad_two_body.1 = (f32[4,32,1536]{2,1,0:T(8,128)S(1)}, bf16[4,32,1536]{2,1,0:T(8,128)(2,1)S(1)}, f32[2,32,192]{2,1,0:T(8,128)S(1)}, bf16[2,32,192]{2,1,0:T(8,12...) custom-call(bf16[20,1728,128]{2,1,0:T(8,128)(2,1)S(1)} %get-tuple-element.69.refs_0_, ...), custom_call_target="tpu_custom_call" | custom-call | flops 566231040 | tf_op jit(solution)/shard_map/grad_two_body/pallas_call | solution.py:49
  49.1 1.7 %collective-permute-start.19 = (bf16[2,32,192]{2,1,0:T(8,128)(2,1)S(1)}, bf16[2,32,192]{2,1,0:T(8,128)(2,1)S(1)}, u32[]{:S(2)}, u32[]{:S(2)}) collective-permute-start(bf16[2,32,192]{2,1,0:T(8,128)(2,1)S(1)} %get-tuple-element.73), channel_id=1, source_target_pairs={{0,8},{4,12},{8,0},{12,4},{16,24},{20,28},{24,16},{28,20},{1,9},{5... | collective-permute-start | bytes 73736 | tf_op jit(solution)/shard_map/ppermute | solution.py:380
  50.7 2.8 %collective-permute-start.21 = (bf16[2,32,192]{2,1,0:T(8,128)(2,1)S(1)}, bf16[2,32,192]{2,1,0:T(8,128)(2,1)S(1)}, u32[]{:S(2)}, u32[]{:S(2)}) collective-permute-start(bf16[2,32,192]{2,1,0:T(8,128)(2,1)S(1)} %get-tuple-element.75), channel_id=1, source_target_pairs={{0,24},{4,28},{8,16},{12,20},{16,8},{20,12},{24,0},{28,4},{1,25},{... | collective-permute-start | bytes 73736 | tf_op jit(solution)/shard_map/ppermute | solution.py:380
  53.5 0.1 collective-permute-start.18
  53.6 0.1 halve_body.4
  53.7 1.0 %collective-permute-start.15 = (bf16[32,1728]{1,0:T(8,128)(2,1)S(1)}, bf16[32,1728]{1,0:T(8,128)(2,1)S(1)}, u32[]{:S(2)}, u32[]{:S(2)}) collective-permute-start(bf16[32,1728]{1,0:T(8,128)(2,1)S(1)} %get-tuple-element.66), channel_id=1, source_target_pairs={{0,8},{4,12},{8,0},{12,4},{16,24},{20,28},{24,16},{28,20},{1,9},{5... | collective-permute-start | bytes 331784 | tf_op jit(solution)/shard_map/ppermute | solution.py:380
  54.7 2.4 %collective-permute-start.16 = (bf16[32,1728]{1,0:T(8,128)(2,1)S(1)}, bf16[32,1728]{1,0:T(8,128)(2,1)S(1)}, u32[]{:S(2)}, u32[]{:S(2)}) collective-permute-start(bf16[32,1728]{1,0:T(8,128)(2,1)S(1)} %get-tuple-element.67), channel_id=1, source_target_pairs={{0,16},{4,20},{8,24},{12,28},{16,0},{20,4},{24,8},{28,12},{1,17},{... | collective-permute-start | bytes 331784 | tf_op jit(solution)/shard_map/ppermute | solution.py:380
  57.2 1.0 %collective-permute-start.17 = (bf16[32,1728]{1,0:T(8,128)(2,1)S(1)}, bf16[32,1728]{1,0:T(8,128)(2,1)S(1)}, u32[]{:S(2)}, u32[]{:S(2)}) collective-permute-start(bf16[32,1728]{1,0:T(8,128)(2,1)S(1)} %get-tuple-element.68), channel_id=1, source_target_pairs={{0,24},{4,28},{8,16},{12,20},{16,8},{20,12},{24,0},{28,4},{1,25},{... | collective-permute-start | bytes 331784 | tf_op jit(solution)/shard_map/ppermute | solution.py:380
  58.2 5.1 %output_body.1 = (bf16[64,2048]{1,0:T(8,128)(2,1)}, f32[8,128]{1,0:T(8,128)S(1)}) custom-call(s32[24,27]{1,0:T(8,128)S(1)} %get-tuple-element.43.refs_0_, bf16[1728,256]{1,0:T(8,128)(2,1)S(1)} %bitcast.13, bf16[64,2560]{1,0:T(8,128)(2,1)S(1)} %get-tuple-element.56.refs_2_.refs_1_, bf16[64,2560]{1,0:T(8,128)(2,1)S(1)} %collective-permute-done.10.refs_3_.refs_2_, ...), custom_call_target="tpu_custom_call" | custom-call | flops 18119393280 | bytes 16777216 | tf_op jit(solution)/shard_map/output_body/pallas_call | solution.py:49
  63.4 0.5 collective-permute-done.18.refs_1_
  63.9 0.1 halve_body.5
  63.9 0.8 %collective-permute-start.22 = (bf16[32,1536]{1,0:T(8,128)(2,1)S(1)}, bf16[32,1536]{1,0:T(8,128)(2,1)S(1)}, u32[]{:S(2)}, u32[]{:S(2)}) collective-permute-start(bf16[32,1536]{1,0:T(8,128)(2,1)S(1)} %get-tuple-element.79), channel_id=1, source_target_pairs={{0,8},{4,12},{8,0},{12,4},{16,24},{20,28},{24,16},{28,20},{1,9},{5... | collective-permute-start | bytes 294920 | tf_op jit(solution)/shard_map/ppermute | solution.py:380
  64.7 2.2 %collective-permute-start.23 = (bf16[32,1536]{1,0:T(8,128)(2,1)S(1)}, bf16[32,1536]{1,0:T(8,128)(2,1)S(1)}, u32[]{:S(2)}, u32[]{:S(2)}) collective-permute-start(bf16[32,1536]{1,0:T(8,128)(2,1)S(1)} %get-tuple-element.80), channel_id=1, source_target_pairs={{0,16},{4,20},{8,24},{12,28},{16,0},{20,4},{24,8},{28,12},{1,17},{... | collective-permute-start | bytes 294920 | tf_op jit(solution)/shard_map/ppermute | solution.py:380
  66.9 1.5 %collective-permute-start.24 = (bf16[32,1536]{1,0:T(8,128)(2,1)S(1)}, bf16[32,1536]{1,0:T(8,128)(2,1)S(1)}, u32[]{:S(2)}, u32[]{:S(2)}) collective-permute-start(bf16[32,1536]{1,0:T(8,128)(2,1)S(1)} %get-tuple-element.81), channel_id=1, source_target_pairs={{0,24},{4,28},{8,16},{12,20},{16,8},{20,12},{24,0},{28,4},{1,25},{... | collective-permute-start | bytes 294920 | tf_op jit(solution)/shard_map/ppermute | solution.py:380
  68.4 1.5 %collective-permute-start.25 = (bf16[32,192]{1,0:T(8,128)(2,1)S(1)}, bf16[32,192]{1,0:T(8,128)(2,1)S(1)}, u32[]{:S(2)}, u32[]{:S(2)}) collective-permute-start(bf16[32,192]{1,0:T(8,128)(2,1)S(1)} %get-tuple-element.82), channel_id=1, source_target_pairs={{0,4},{4,0},{8,12},{12,8},{16,20},{20,16},{24,28},{28,24},{1,5},{5... | collective-permute-start | bytes 36872 | tf_op jit(solution)/shard_map/ppermute | solution.py:380
  69.9 0.9 %finish_body.2 = f32[27,32,64]{2,1,0:T(8,128)} custom-call(f32[32,1728]{1,0:T(8,128)S(1)} %get-tuple-element.64.refs_6_.refs_0_, bf16[32,1728]{1,0:T(8,128)(2,1)S(1)} %collective-permute-done.15.refs_1_, bf16[32,1728]{1,0:T(8,128)(2,1)S(1)} %collective-permute-done.16.refs_2_, bf16[32,1728]{1,0:T(8,128)(2,1)S(1)} %collective-permute-done.17.refs_3_), custom_call_target="tpu_custom_call" | custom-call | bytes 2097152 | tf_op jit(solution)/shard_map/finish_body/pallas_call | solution.py:49
  70.8 1.3 %collective-permute-done.25.refs_5_ = bf16[32,192]{1,0:T(8,128)(2,1)S(1)} collective-permute-done((bf16[32,192]{1,0:T(8,128)(2,1)S(1)}, bf16[32,192]{1,0:T(8,128)(2,1)S(1)}, u32[]{:S(2)}, u32[]{:S(2)}) %collective-permute-start.25) | collective-permute-done | bytes 12320 | tf_op jit(solution)/shard_map/ppermute | solution.py:380
  72.1 2.1 %collective-permute-done.23.refs_2_ = bf16[32,1536]{1,0:T(8,128)(2,1)S(1)} collective-permute-done((bf16[32,1536]{1,0:T(8,128)(2,1)S(1)}, bf16[32,1536]{1,0:T(8,128)(2,1)S(1)}, u32[]{:S(2)}, u32[]{:S(2)}) %collective-permute-start.23) | collective-permute-done | bytes 98336 | tf_op jit(solution)/shard_map/ppermute | solution.py:380
  74.2 0.9 %finish_body.3 = f32[27,32,64]{2,1,0:T(8,128)} custom-call(f32[32,1536]{1,0:T(8,128)S(1)} %get-tuple-element.78.refs_0_, bf16[32,1536]{1,0:T(8,128)(2,1)S(1)} %collective-permute-done.22.refs_1_, bf16[32,1536]{1,0:T(8,128)(2,1)S(1)} %collective-permute-done.23.refs_2_, bf16[32,1536]{1,0:T(8,128)(2,1)S(1)} %collective-permute-done.24.refs_3_, ...), custom_call_target="tpu_custom_call" | custom-call | bytes 2097152 | tf_op jit(solution)/shard_map/finish_body/pallas_call | solution.py:49
  (27 shorter events, 0.2 us)
Async XLA Ops:
  0.6 10.5 %collective-permute-start.1 = (bf16[64,2048]{1,0:T(8,128)(2,1)}, bf16[64,2048]{1,0:T(8,128)(2,1)S(1)}, u32[]{:S(2)}, u32[]{:S(2)}) collective-permute-start(bf16[64,2048]{1,0:T(8,128)(2,1)} %bitcast.17), channel_id=1, source_target_pairs={{0,2},{1,3},{2,0},{3,1},{4,6},{5,7},{6,4},{7,5},{8,10},{9,11},{10,... | collective-permute-start | bytes 786440 | tf_op jit(solution)/shard_map/ppermute | solution.py:380
  3.6 8.2 %collective-permute-start = (bf16[64,2048]{1,0:T(8,128)(2,1)}, bf16[64,2048]{1,0:T(8,128)(2,1)S(1)}, u32[]{:S(2)}, u32[]{:S(2)}) collective-permute-start(bf16[64,2048]{1,0:T(8,128)(2,1)} %bitcast.18), channel_id=1, source_target_pairs={{0,1},{1,0},{2,3},{3,2},{4,5},{5,4},{6,7},{7,6},{8,9},{9,8},{10,11... | collective-permute-start | bytes 786440 | tf_op jit(solution)/shard_map/ppermute | solution.py:380
  11.2 1.7 %collective-permute-start.2 = (bf16[64,2048]{1,0:T(8,128)(2,1)S(1)}, bf16[64,2048]{1,0:T(8,128)(2,1)S(1)}, u32[]{:S(2)}, u32[]{:S(2)}) collective-permute-start(bf16[64,2048]{1,0:T(8,128)(2,1)S(1)} %pass_body.1.refs_3_), channel_id=1, source_target_pairs={{0,1},{1,0},{2,3},{3,2},{4,5},{5,4},{6,7},{7,6},{8,9},{9,8},{10,11... | collective-permute-start | bytes 786440 | tf_op jit(solution)/shard_map/ppermute | solution.py:380
  11.7 6.6 %collective-permute-start.5 = (bf16[2,64,2560]{2,1,0:T(8,128)(2,1)S(1)}, bf16[2,64,2560]{2,1,0:T(8,128)(2,1)S(1)}, u32[]{:S(2)}, u32[]{:S(2)}) collective-permute-start(bf16[2,64,2560]{2,1,0:T(8,128)(2,1)S(1)} %get-tuple-element.45.refs_1_), channel_id=1, source_target_pairs={{0,1},{1,0},{2,3},{3,2},{4,5},{5,4},{6,7},{7,6},{8,9},{9,8},{10,11... | collective-permute-start | bytes 1966088 | tf_op jit(solution)/shard_map/ppermute | solution.py:380
  12.9 6.3 %copy-start = (bf16[27,64,256]{2,1,0:T(8,128)(2,1)S(1)}, bf16[27,64,256]{2,1,0:T(8,128)(2,1)}, u32[]{:S(2)}) copy-start(bf16[27,64,256]{2,1,0:T(8,128)(2,1)} %param.9) | copy-start | bytes 2654212
  13.2 8.1 %collective-permute-start.4 = (bf16[128,256]{1,0:T(8,128)(2,1)S(1)}, bf16[128,256]{1,0:T(8,128)(2,1)S(1)}, u32[]{:S(2)}, u32[]{:S(2)}) collective-permute-start(bf16[128,256]{1,0:T(8,128)(2,1)S(1)} %get-tuple-element.47), channel_id=1, source_target_pairs={{4,8},{12,16},{20,24},{8,4},{16,12},{24,20},{5,9},{13,17},{21,25},... | collective-permute-start | bytes 196616 | tf_op jit(solution)/shard_map/ppermute | solution.py:385
  14.0 7.3 %collective-permute-start.3 = (bf16[128,256]{1,0:T(8,128)(2,1)S(1)}, bf16[128,256]{1,0:T(8,128)(2,1)S(1)}, u32[]{:S(2)}, u32[]{:S(2)}) collective-permute-start(bf16[128,256]{1,0:T(8,128)(2,1)S(1)} %get-tuple-element.46.refs_2_), channel_id=1, source_target_pairs={{0,4},{4,0},{8,12},{12,8},{16,20},{20,16},{24,28},{28,24},{1,5},{5... | collective-permute-start | bytes 196616 | tf_op jit(solution)/shard_map/ppermute | solution.py:380
  18.5 9.5 %collective-permute-start.7 = (bf16[64,2560]{1,0:T(8,128)(2,1)S(1)}, bf16[64,2560]{1,0:T(8,128)(2,1)S(1)}, u32[]{:S(2)}, u32[]{:S(2)}) collective-permute-start(bf16[64,2560]{1,0:T(8,128)(2,1)S(1)} %get-tuple-element.53), channel_id=1, source_target_pairs={{0,2},{1,3},{2,0},{3,1},{4,6},{5,7},{6,4},{7,5},{8,10},{9,11},{10,... | collective-permute-start | bytes 983048 | tf_op jit(solution)/shard_map/ppermute | solution.py:380
  21.3 1.4 %collective-permute-start.6 = (bf16[128,512]{1,0:T(8,128)(2,1)S(1)}, bf16[128,512]{1,0:T(8,128)(2,1)S(1)}, u32[]{:S(2)}, u32[]{:S(2)}) collective-permute-start(bf16[128,512]{1,0:T(8,128)(2,1)S(1)} %stack_body.1.refs_2_), channel_id=1, source_target_pairs={{0,1},{1,0},{2,3},{3,2},{4,5},{5,4},{6,7},{7,6},{8,9},{9,8},{10,11... | collective-permute-start | bytes 393224 | tf_op jit(solution)/shard_map/ppermute | solution.py:380
  22.7 35.5 %copy-start.1 = (bf16[27,64,256]{2,1,0:T(8,128)(2,1)S(1)}, bf16[27,64,256]{2,1,0:T(8,128)(2,1)}, u32[]{:S(2)}) copy-start(bf16[27,64,256]{2,1,0:T(8,128)(2,1)} %param.10) | copy-start | bytes 2654212
  28.2 6.0 %collective-permute-start.9 = (bf16[2,64,256]{2,1,0:T(8,128)(2,1)S(1)}, bf16[2,64,256]{2,1,0:T(8,128)(2,1)S(1)}, u32[]{:S(2)}, u32[]{:S(2)}) collective-permute-start(bf16[2,64,256]{2,1,0:T(8,128)(2,1)S(1)} %get-tuple-element.55), channel_id=1, source_target_pairs={{4,8},{12,16},{20,24},{8,4},{16,12},{24,20},{5,9},{13,17},{21,25},... | collective-permute-start | bytes 196616 | tf_op jit(solution)/shard_map/ppermute | solution.py:385
  29.1 6.6 %collective-permute-start.8 = (bf16[2,64,256]{2,1,0:T(8,128)(2,1)S(1)}, bf16[2,64,256]{2,1,0:T(8,128)(2,1)S(1)}, u32[]{:S(2)}, u32[]{:S(2)}) collective-permute-start(bf16[2,64,256]{2,1,0:T(8,128)(2,1)S(1)} %get-tuple-element.54.refs_3_), channel_id=1, source_target_pairs={{0,4},{4,0},{8,12},{12,8},{16,20},{20,16},{24,28},{28,24},{1,5},{5... | collective-permute-start | bytes 196616 | tf_op jit(solution)/shard_map/ppermute | solution.py:380
  33.4 10.9 %collective-permute-start.11 = (bf16[64,2048]{1,0:T(8,128)(2,1)S(1)}, bf16[64,2048]{1,0:T(8,128)(2,1)S(1)}, u32[]{:S(2)}, u32[]{:S(2)}) collective-permute-start(bf16[64,2048]{1,0:T(8,128)(2,1)S(1)} %get-tuple-element.52.refs_1_.refs_0_), channel_id=1, source_target_pairs={{0,2},{1,3},{2,0},{3,1},{4,6},{5,7},{6,4},{7,5},{8,10},{9,11},{10,... | collective-permute-start | bytes 786440 | tf_op jit(solution)/shard_map/ppermute | solution.py:380
  35.7 8.6 %collective-permute-start.12 = (bf16[64,512]{1,0:T(8,128)(2,1)S(1)}, bf16[64,512]{1,0:T(8,128)(2,1)S(1)}, u32[]{:S(2)}, u32[]{:S(2)}) collective-permute-start(bf16[64,512]{1,0:T(8,128)(2,1)S(1)} %get-tuple-element.57), channel_id=1, source_target_pairs={{0,2},{1,3},{2,0},{3,1},{4,6},{5,7},{6,4},{7,5},{8,10},{9,11},{10,... | collective-permute-start | bytes 196616 | tf_op jit(solution)/shard_map/ppermute | solution.py:380
  42.2 11.4 %collective-permute-start.14 = (bf16[4,32,1728]{2,1,0:T(8,128)(2,1)S(1)}, bf16[4,32,1728]{2,1,0:T(8,128)(2,1)S(1)}, u32[]{:S(2)}, u32[]{:S(2)}) collective-permute-start(bf16[4,32,1728]{2,1,0:T(8,128)(2,1)S(1)} %get-tuple-element.63), channel_id=1, source_target_pairs={{0,4},{4,0},{8,12},{12,8},{16,20},{20,16},{24,28},{28,24},{1,5},{5... | collective-permute-start | bytes 1327112 | tf_op jit(solution)/shard_map/ppermute | solution.py:380
  44.3 1.6 %collective-permute-start.10 = (bf16[64,2560]{1,0:T(8,128)(2,1)S(1)}, bf16[64,2560]{1,0:T(8,128)(2,1)S(1)}, u32[]{:S(2)}, u32[]{:S(2)}) collective-permute-start(bf16[64,2560]{1,0:T(8,128)(2,1)S(1)} %get-tuple-element.56.refs_2_.refs_1_), channel_id=1, source_target_pairs={{0,1},{1,0},{2,3},{3,2},{4,5},{5,4},{6,7},{7,6},{8,9},{9,8},{10,11... | collective-permute-start | bytes 983048 | tf_op jit(solution)/shard_map/ppermute | solution.py:380
  44.4 2.1 %collective-permute-start.13 = (bf16[64,2560]{1,0:T(8,128)(2,1)S(1)}, bf16[64,2560]{1,0:T(8,128)(2,1)S(1)}, u32[]{:S(2)}, u32[]{:S(2)}) collective-permute-start(bf16[64,2560]{1,0:T(8,128)(2,1)S(1)} %append_body.1.refs_4_.refs_3_), channel_id=1, source_target_pairs={{0,1},{1,0},{2,3},{3,2},{4,5},{5,4},{6,7},{7,6},{8,9},{9,8},{10,11... | collective-permute-start | bytes 983048 | tf_op jit(solution)/shard_map/ppermute | solution.py:380
  49.1 5.7 %collective-permute-start.19 = (bf16[2,32,192]{2,1,0:T(8,128)(2,1)S(1)}, bf16[2,32,192]{2,1,0:T(8,128)(2,1)S(1)}, u32[]{:S(2)}, u32[]{:S(2)}) collective-permute-start(bf16[2,32,192]{2,1,0:T(8,128)(2,1)S(1)} %get-tuple-element.73), channel_id=1, source_target_pairs={{0,8},{4,12},{8,0},{12,4},{16,24},{20,28},{24,16},{28,20},{1,9},{5... | collective-permute-start | bytes 73736 | tf_op jit(solution)/shard_map/ppermute | solution.py:380
  50.7 6.4 %collective-permute-start.20 = (bf16[2,32,192]{2,1,0:T(8,128)(2,1)S(1)}, bf16[2,32,192]{2,1,0:T(8,128)(2,1)S(1)}, u32[]{:S(2)}, u32[]{:S(2)}) collective-permute-start(bf16[2,32,192]{2,1,0:T(8,128)(2,1)S(1)} %get-tuple-element.74), channel_id=1, source_target_pairs={{0,16},{4,20},{8,24},{12,28},{16,0},{20,4},{24,8},{28,12},{1,17},{... | collective-permute-start | bytes 73736 | tf_op jit(solution)/shard_map/ppermute | solution.py:380
  50.7 12.6 %collective-permute-start.21 = (bf16[2,32,192]{2,1,0:T(8,128)(2,1)S(1)}, bf16[2,32,192]{2,1,0:T(8,128)(2,1)S(1)}, u32[]{:S(2)}, u32[]{:S(2)}) collective-permute-start(bf16[2,32,192]{2,1,0:T(8,128)(2,1)S(1)} %get-tuple-element.75), channel_id=1, source_target_pairs={{0,24},{4,28},{8,16},{12,20},{16,8},{20,12},{24,0},{28,4},{1,25},{... | collective-permute-start | bytes 73736 | tf_op jit(solution)/shard_map/ppermute | solution.py:380
  53.5 10.3 %collective-permute-start.18 = (bf16[4,32,1536]{2,1,0:T(8,128)(2,1)S(1)}, bf16[4,32,1536]{2,1,0:T(8,128)(2,1)S(1)}, u32[]{:S(2)}, u32[]{:S(2)}) collective-permute-start(bf16[4,32,1536]{2,1,0:T(8,128)(2,1)S(1)} %get-tuple-element.71), channel_id=1, source_target_pairs={{0,4},{4,0},{8,12},{12,8},{16,20},{20,16},{24,28},{28,24},{1,5},{5... | collective-permute-start | bytes 1179656 | tf_op jit(solution)/shard_map/ppermute | solution.py:380
  53.7 13.2 %collective-permute-start.15 = (bf16[32,1728]{1,0:T(8,128)(2,1)S(1)}, bf16[32,1728]{1,0:T(8,128)(2,1)S(1)}, u32[]{:S(2)}, u32[]{:S(2)}) collective-permute-start(bf16[32,1728]{1,0:T(8,128)(2,1)S(1)} %get-tuple-element.66), channel_id=1, source_target_pairs={{0,8},{4,12},{8,0},{12,4},{16,24},{20,28},{24,16},{28,20},{1,9},{5... | collective-permute-start | bytes 331784 | tf_op jit(solution)/shard_map/ppermute | solution.py:380
  54.7 13.6 %collective-permute-start.16 = (bf16[32,1728]{1,0:T(8,128)(2,1)S(1)}, bf16[32,1728]{1,0:T(8,128)(2,1)S(1)}, u32[]{:S(2)}, u32[]{:S(2)}) collective-permute-start(bf16[32,1728]{1,0:T(8,128)(2,1)S(1)} %get-tuple-element.67), channel_id=1, source_target_pairs={{0,16},{4,20},{8,24},{12,28},{16,0},{20,4},{24,8},{28,12},{1,17},{... | collective-permute-start | bytes 331784 | tf_op jit(solution)/shard_map/ppermute | solution.py:380
  57.2 12.7 %collective-permute-start.17 = (bf16[32,1728]{1,0:T(8,128)(2,1)S(1)}, bf16[32,1728]{1,0:T(8,128)(2,1)S(1)}, u32[]{:S(2)}, u32[]{:S(2)}) collective-permute-start(bf16[32,1728]{1,0:T(8,128)(2,1)S(1)} %get-tuple-element.68), channel_id=1, source_target_pairs={{0,24},{4,28},{8,16},{12,20},{16,8},{20,12},{24,0},{28,4},{1,25},{... | collective-permute-start | bytes 331784 | tf_op jit(solution)/shard_map/ppermute | solution.py:380
  63.9 8.2 %collective-permute-start.22 = (bf16[32,1536]{1,0:T(8,128)(2,1)S(1)}, bf16[32,1536]{1,0:T(8,128)(2,1)S(1)}, u32[]{:S(2)}, u32[]{:S(2)}) collective-permute-start(bf16[32,1536]{1,0:T(8,128)(2,1)S(1)} %get-tuple-element.79), channel_id=1, source_target_pairs={{0,8},{4,12},{8,0},{12,4},{16,24},{20,28},{24,16},{28,20},{1,9},{5... | collective-permute-start | bytes 294920 | tf_op jit(solution)/shard_map/ppermute | solution.py:380
  64.7 9.5 %collective-permute-start.23 = (bf16[32,1536]{1,0:T(8,128)(2,1)S(1)}, bf16[32,1536]{1,0:T(8,128)(2,1)S(1)}, u32[]{:S(2)}, u32[]{:S(2)}) collective-permute-start(bf16[32,1536]{1,0:T(8,128)(2,1)S(1)} %get-tuple-element.80), channel_id=1, source_target_pairs={{0,16},{4,20},{8,24},{12,28},{16,0},{20,4},{24,8},{28,12},{1,17},{... | collective-permute-start | bytes 294920 | tf_op jit(solution)/shard_map/ppermute | solution.py:380
  66.9 7.3 %collective-permute-start.24 = (bf16[32,1536]{1,0:T(8,128)(2,1)S(1)}, bf16[32,1536]{1,0:T(8,128)(2,1)S(1)}, u32[]{:S(2)}, u32[]{:S(2)}) collective-permute-start(bf16[32,1536]{1,0:T(8,128)(2,1)S(1)} %get-tuple-element.81), channel_id=1, source_target_pairs={{0,24},{4,28},{8,16},{12,20},{16,8},{20,12},{24,0},{28,4},{1,25},{... | collective-permute-start | bytes 294920 | tf_op jit(solution)/shard_map/ppermute | solution.py:380
  68.4 3.7 %collective-permute-start.25 = (bf16[32,192]{1,0:T(8,128)(2,1)S(1)}, bf16[32,192]{1,0:T(8,128)(2,1)S(1)}, u32[]{:S(2)}, u32[]{:S(2)}) collective-permute-start(bf16[32,192]{1,0:T(8,128)(2,1)S(1)} %get-tuple-element.82), channel_id=1, source_target_pairs={{0,4},{4,0},{8,12},{12,8},{16,20},{20,16},{24,28},{28,24},{1,5},{5... | collective-permute-start | bytes 36872 | tf_op jit(solution)/shard_map/ppermute | solution.py:380

commit v8 on v7

--- a/solution.py
+++ b/solution.py
@@ -139,16 +139,17 @@
 
 
 def input_grad_body(
-    counts, map_hbm, cot_hbm, w_hbm, feat_hbm, tab_ref, spread_ref, keep_ref, send_ref,
-    own_ref, map_ref, cot_ref, w_ref, blocks, part, tab, sems, sem
+    counts_hbm, map_hbm, cot_hbm, w_hbm, feat_hbm, tab_ref, spread_ref, keep_ref, send_ref,
+    own_ref, map_ref, cot_ref, w_ref, blocks, part, tab, counts, sems, sem
 ):
-    ways = [(map_hbm, map_ref), (cot_hbm, cot_ref), (w_hbm, w_ref), (feat_hbm, own_ref)]
+    ways = [(map_hbm, map_ref), (cot_hbm, cot_ref), (w_hbm, w_ref), (feat_hbm, own_ref), (counts_hbm, counts)]
     loads = [pltpu.make_async_copy(src, dst, sems.at[i]) for i, (src, dst) in enumerate(ways)]
     for load in loads:
         load.start()
     depth, rows = cot_ref.shape
     nblocks = rows // BLK
     loads[0].wait()
+    loads[4].wait()
     tab_ref[...] = table(counts, map_ref, nblocks)
     copy = pltpu.make_async_copy(tab_ref, tab, sem)
     copy.start()
@@ -447,13 +448,14 @@
             blocks,
             pltpu.VMEM((parts, depth, reach), BF16),
             pltpu.SMEM((entries + PAD, offsets), jnp.int32),
-            pltpu.SemaphoreType.DMA((4,)),
+            pltpu.SMEM(block_count.shape, jnp.int32),
+            pltpu.SemaphoreType.DMA((5,)),
             pltpu.SemaphoreType.DMA,
         ],
         vmem=16,
         flops=work,
         traffic=16 << 20,
-        specs=[SMEM] + [FAR] * 4,
+        specs=[FAR] * 5,
     )
     pieces = [own, swap(shard_t, "chan", 1)]
     for got in far:

time: 75.3 us -> 75.1 us (level)
  starting transfers between devices: 33.5 us -> 34.9 us
  waiting for transfers between devices: 11.8 us -> 10.8 us
    ppermute x24, starting transfers between devices: 31.8 us -> 33.3 us  [swap(): lax.ppermute(value, axis, [(i, i ^ bits) for i in range(lax.axis_size(axi...]
    ppermute x24, waiting for transfers between devices: 11.8 us -> 10.8 us  [swap(): lax.ppermute(value, axis, [(i, i ^ bits) for i in range(lax.axis_size(axi...]
  transfers between devices with their start and end apart: 26 -> 26, of which waited for: 9 -> 9; matrix products, arithmetic and copies ran while one was open for 0% -> 0% of each run, Pallas kernels for 37% -> 36%
where the time goes in v8:
time: 75.1 us; the launch traced here: 74.9 us
  starting transfers between devices  34.9 us (46%)
  Pallas kernels  28.4 us (38%)
  waiting for transfers between devices  10.8 us (14%)
  between operations  0.83 us (1%)
    ppermute x24, starting transfers between devices, swap(): lax.ppermute(value, axis, [(i, i ^ bits) for i in range(lax.axis_size(axi...  33.3 us
    pallas_call x19, Pallas kernels, call(): return kernel(*ins)  28.4 us
    ppermute x24, waiting for transfers between devices, swap(): lax.ppermute(value, axis, [(i, i ^ bits) for i in range(lax.axis_size(axi...  10.8 us
    ppermute x2, starting transfers between devices, swap_other(): return lax.ppermute(value, 'space', pairs + [(j, i) for i, j in pairs])  1.64 us
  transfers between devices with their start and end apart: 26, of which 9 were waited for; matrix products, arithmetic and copies ran while one was open for 0% of the time, Pallas kernels for 36%

profile of v8, /device:TPU:0, one launch (start us, length us, event | category | flops | bytes accessed | tf_op | source)
XLA Modules:
  0.0 74.9 jit_solution(3317544192876565140)
XLA Ops:
  0.6 3.0 %collective-permute-start.1 = (bf16[64,2048]{1,0:T(8,128)(2,1)}, bf16[64,2048]{1,0:T(8,128)(2,1)S(1)}, u32[]{:S(2)}, u32[]{:S(2)}) collective-permute-start(bf16[64,2048]{1,0:T(8,128)(2,1)} %bitcast.17), channel_id=1, source_target_pairs={{0,2},{1,3},{2,0},{3,1},{4,6},{5,7},{6,4},{7,5},{8,10},{9,11},{10,... | collective-permute-start | bytes 786440 | tf_op jit(solution)/shard_map/ppermute | solution.py:381
  3.6 6.9 %input_grad_body.1 = (s32[24,27]{1,0:T(8,128)S(1)}, bf16[20,1728,128]{2,1,0:T(8,128)(2,1)S(1)}, bf16[2,64,2560]{2,1,0:T(8,128)(2,1)S(1)}, bf16[2,64,2560]{2,1,0:T(8,128)(2,1)S(1)}, bf16[64,2048]{1,0:T(8,128)(2,1)S(1)}) custom-call(s32[8]{0:T(128)} %refs_0_.1, s32[3,16,27]{2,1,0:T(8,128)} %bitcast.20, bf16[64,2048]{1,0:T(8,128)(2,1)} %bitcast.16, ...), custom_call_target="tpu_custom_call" | custom-call | flops 2264924160 | bytes 16777216 | tf_op jit(solution)/shard_map/input_grad_body/pallas_call | solution.py:49
  10.6 0.6 collective-permute-start.2
  11.2 0.1 collective-permute-start.5
  11.2 1.1 %collective-permute-done.2.refs_4_ = bf16[64,2048]{1,0:T(8,128)(2,1)S(1)} collective-permute-done((bf16[64,2048]{1,0:T(8,128)(2,1)S(1)}, bf16[64,2048]{1,0:T(8,128)(2,1)S(1)}, u32[]{:S(2)}, u32[]{:S(2)}) %collective-permute-start.2) | collective-permute-done | bytes 262176 | tf_op jit(solution)/shard_map/ppermute | solution.py:381
  12.3 0.2 cut_body.1
  12.6 0.8 %collective-permute-start.4 = (bf16[128,256]{1,0:T(8,128)(2,1)S(1)}, bf16[128,256]{1,0:T(8,128)(2,1)S(1)}, u32[]{:S(2)}, u32[]{:S(2)}) collective-permute-start(bf16[128,256]{1,0:T(8,128)(2,1)S(1)} %get-tuple-element.47), channel_id=1, source_target_pairs={{4,8},{12,16},{20,24},{8,4},{16,12},{24,20},{5,9},{13,17},{21,25},... | collective-permute-start | bytes 196616 | tf_op jit(solution)/shard_map/ppermute | solution.py:386
  13.4 4.4 %collective-permute-start.3 = (bf16[128,256]{1,0:T(8,128)(2,1)S(1)}, bf16[128,256]{1,0:T(8,128)(2,1)S(1)}, u32[]{:S(2)}, u32[]{:S(2)}) collective-permute-start(bf16[128,256]{1,0:T(8,128)(2,1)S(1)} %get-tuple-element.46.refs_2_), channel_id=1, source_target_pairs={{0,4},{4,0},{8,12},{12,8},{16,20},{20,16},{24,28},{28,24},{1,5},{5... | collective-permute-start | bytes 196616 | tf_op jit(solution)/shard_map/ppermute | solution.py:381
  17.7 0.0 collective-permute-done.5.refs_1_
  17.7 0.2 halve_body.3
  17.9 1.3 %collective-permute-start.7 = (bf16[64,2560]{1,0:T(8,128)(2,1)S(1)}, bf16[64,2560]{1,0:T(8,128)(2,1)S(1)}, u32[]{:S(2)}, u32[]{:S(2)}) collective-permute-start(bf16[64,2560]{1,0:T(8,128)(2,1)S(1)} %get-tuple-element.53), channel_id=1, source_target_pairs={{0,2},{1,3},{2,0},{3,1},{4,6},{5,7},{6,4},{7,5},{8,10},{9,11},{10,... | collective-permute-start | bytes 983048 | tf_op jit(solution)/shard_map/ppermute | solution.py:381
  19.2 2.1 %inner_body.1 = (f32[20,1728,128]{2,1,0:T(8,128)S(1)}, bf16[256,2048]{1,0:T(8,128)(2,1)S(1)}) custom-call(bf16[1728,256]{1,0:T(8,128)(2,1)S(1)} %bitcast.10, bf16[64,2048]{1,0:T(8,128)(2,1)S(1)} %get-tuple-element.44.refs_1_, bf16[64,2048]{1,0:T(8,128)(2,1)S(1)} %collective-permute-done.refs_2_, bf16[64,2048]{1,0:T(8,128)(2,1)S(1)} %pass_body.1.refs_3_, ...), custom_call_target="tpu_custom_call" | custom-call | flops 2264924160 | bytes 16777216 | tf_op jit(solution)/shard_map/inner_body/pallas_call | solution.py:49
  21.2 0.0 collective-permute-done.4.refs_1_
  21.3 0.1 collective-permute-start.6
  21.4 1.3 %collective-permute-done.6.refs_3_ = bf16[128,512]{1,0:T(8,128)(2,1)S(1)} collective-permute-done((bf16[128,512]{1,0:T(8,128)(2,1)S(1)}, bf16[128,512]{1,0:T(8,128)(2,1)S(1)}, u32[]{:S(2)}, u32[]{:S(2)}) %collective-permute-start.6) | collective-permute-done | bytes 131104 | tf_op jit(solution)/shard_map/ppermute | solution.py:381
  22.7 2.7 %hidden_body.1 = (f32[64,2048]{1,0:T(8,128)S(1)}, bf16[64,2048]{1,0:T(8,128)(2,1)S(1)}, bf16[256,512]{1,0:T(8,128)(2,1)S(1)}, f32[20,1728,128]{2,1,0:T(8,128)S(1)}) custom-call(s32[24,27]{1,0:T(8,128)S(1)} %get-tuple-element.43.refs_0_, bf16[1728,256]{1,0:T(8,128)(2,1)S(1)} %bitcast.11, ...), custom_call_target="tpu_custom_call", output_to_operand_aliasing={{3}: (4, {})} | custom-call | tf_op jit(solution)/shard_map/hidden_body/pallas_call | solution.py:49
  25.4 2.0 %collective-permute-done.7.refs_3_.refs_6_ = bf16[64,2560]{1,0:T(8,128)(2,1)S(1)} collective-permute-done((bf16[64,2560]{1,0:T(8,128)(2,1)S(1)}, bf16[64,2560]{1,0:T(8,128)(2,1)S(1)}, u32[]{:S(2)}, u32[]{:S(2)}) %collective-permute-start.7) | collective-permute-done | bytes 327712 | tf_op jit(solution)/shard_map/ppermute | solution.py:381
  27.4 0.2 turn_body.1
  27.6 0.8 %collective-permute-start.9 = (bf16[2,64,256]{2,1,0:T(8,128)(2,1)S(1)}, bf16[2,64,256]{2,1,0:T(8,128)(2,1)S(1)}, u32[]{:S(2)}, u32[]{:S(2)}) collective-permute-start(bf16[2,64,256]{2,1,0:T(8,128)(2,1)S(1)} %get-tuple-element.55), channel_id=1, source_target_pairs={{4,8},{12,16},{20,24},{8,4},{16,12},{24,20},{5,9},{13,17},{21,25},... | collective-permute-start | bytes 196616 | tf_op jit(solution)/shard_map/ppermute | solution.py:386
  28.5 4.3 %collective-permute-start.8 = (bf16[2,64,256]{2,1,0:T(8,128)(2,1)S(1)}, bf16[2,64,256]{2,1,0:T(8,128)(2,1)S(1)}, u32[]{:S(2)}, u32[]{:S(2)}) collective-permute-start(bf16[2,64,256]{2,1,0:T(8,128)(2,1)S(1)} %get-tuple-element.54.refs_3_), channel_id=1, source_target_pairs={{0,4},{4,0},{8,12},{12,8},{16,20},{20,16},{24,28},{28,24},{1,5},{5... | collective-permute-start | bytes 196616 | tf_op jit(solution)/shard_map/ppermute | solution.py:381
  32.8 1.0 %collective-permute-start.11 = (bf16[64,2048]{1,0:T(8,128)(2,1)S(1)}, bf16[64,2048]{1,0:T(8,128)(2,1)S(1)}, u32[]{:S(2)}, u32[]{:S(2)}) collective-permute-start(bf16[64,2048]{1,0:T(8,128)(2,1)S(1)} %get-tuple-element.52.refs_1_.refs_0_), channel_id=1, source_target_pairs={{0,2},{1,3},{2,0},{3,1},{4,6},{5,7},{6,4},{7,5},{8,10},{9,11},{10,... | collective-permute-start | bytes 786440 | tf_op jit(solution)/shard_map/ppermute | solution.py:381
  33.8 0.3 prepare_body.1
  34.1 1.0 %collective-permute-done.8.refs_1_.refs_2_ = bf16[2,64,256]{2,1,0:T(8,128)(2,1)S(1)} collective-permute-done((bf16[2,64,256]{2,1,0:T(8,128)(2,1)S(1)}, bf16[2,64,256]{2,1,0:T(8,128)(2,1)S(1)}, u32[]{:S(2)}, u32[]{:S(2)}) %collective-permute-start.8) | collective-permute-done | bytes 65568 | tf_op jit(solution)/shard_map/ppermute | solution.py:381
  35.1 1.0 %collective-permute-start.12 = (bf16[64,512]{1,0:T(8,128)(2,1)S(1)}, bf16[64,512]{1,0:T(8,128)(2,1)S(1)}, u32[]{:S(2)}, u32[]{:S(2)}) collective-permute-start(bf16[64,512]{1,0:T(8,128)(2,1)S(1)} %get-tuple-element.57), channel_id=1, source_target_pairs={{0,2},{1,3},{2,0},{3,1},{4,6},{5,7},{6,4},{7,5},{8,10},{9,11},{10,... | collective-permute-start | bytes 196616 | tf_op jit(solution)/shard_map/ppermute | solution.py:381
  36.1 6.0 %grad_one_body.1 = (f32[4,32,1728]{2,1,0:T(8,128)S(1)}, bf16[4,32,1728]{2,1,0:T(8,128)(2,1)S(1)}) custom-call(s32[24,27]{1,0:T(8,128)S(1)} %get-tuple-element.43.refs_0_, f32[64,2048]{1,0:T(8,128)S(1)} %get-tuple-element.60.refs_1_, bf16[2,64,256]{2,1,0:T(8,128)(2,1)S(1)} %collective-permute-done.8.refs_1_.refs_2_, ...), custom_call_target="tpu_custom_call" | custom-call | flops 2264924160 | bytes 16777216 | tf_op jit(solution)/shard_map/grad_one_body/pallas_call | solution.py:49
  42.1 2.1 %collective-permute-start.14 = (bf16[4,32,1728]{2,1,0:T(8,128)(2,1)S(1)}, bf16[4,32,1728]{2,1,0:T(8,128)(2,1)S(1)}, u32[]{:S(2)}, u32[]{:S(2)}) collective-permute-start(bf16[4,32,1728]{2,1,0:T(8,128)(2,1)S(1)} %get-tuple-element.63), channel_id=1, source_target_pairs={{0,4},{4,0},{8,12},{12,8},{16,20},{20,16},{24,28},{28,24},{1,5},{5... | collective-permute-start | bytes 1327112 | tf_op jit(solution)/shard_map/ppermute | solution.py:381
  44.2 0.6 collective-permute-start.13
  44.8 1.0 %collective-permute-done.10.refs_3_.refs_2_ = bf16[64,2560]{1,0:T(8,128)(2,1)S(1)} collective-permute-done((bf16[64,2560]{1,0:T(8,128)(2,1)S(1)}, bf16[64,2560]{1,0:T(8,128)(2,1)S(1)}, u32[]{:S(2)}, u32[]{:S(2)}) %collective-permute-start.10) | collective-permute-done | bytes 327712 | tf_op jit(solution)/shard_map/ppermute | solution.py:381
  45.8 0.5 collective-permute-done.13.refs_5_.refs_4_
  46.3 2.7 %grad_two_body.1 = (f32[4,32,1536]{2,1,0:T(8,128)S(1)}, bf16[4,32,1536]{2,1,0:T(8,128)(2,1)S(1)}, f32[2,32,192]{2,1,0:T(8,128)S(1)}, bf16[2,32,192]{2,1,0:T(8,12...) custom-call(bf16[20,1728,128]{2,1,0:T(8,128)(2,1)S(1)} %get-tuple-element.69.refs_0_, ...), custom_call_target="tpu_custom_call" | custom-call | flops 566231040 | tf_op jit(solution)/shard_map/grad_two_body/pallas_call | solution.py:49
  48.9 1.6 %collective-permute-start.19 = (bf16[2,32,192]{2,1,0:T(8,128)(2,1)S(1)}, bf16[2,32,192]{2,1,0:T(8,128)(2,1)S(1)}, u32[]{:S(2)}, u32[]{:S(2)}) collective-permute-start(bf16[2,32,192]{2,1,0:T(8,128)(2,1)S(1)} %get-tuple-element.73), channel_id=1, source_target_pairs={{0,8},{4,12},{8,0},{12,4},{16,24},{20,28},{24,16},{28,20},{1,9},{5... | collective-permute-start | bytes 73736 | tf_op jit(solution)/shard_map/ppermute | solution.py:381
  50.6 2.8 %collective-permute-start.21 = (bf16[2,32,192]{2,1,0:T(8,128)(2,1)S(1)}, bf16[2,32,192]{2,1,0:T(8,128)(2,1)S(1)}, u32[]{:S(2)}, u32[]{:S(2)}) collective-permute-start(bf16[2,32,192]{2,1,0:T(8,128)(2,1)S(1)} %get-tuple-element.75), channel_id=1, source_target_pairs={{0,24},{4,28},{8,16},{12,20},{16,8},{20,12},{24,0},{28,4},{1,25},{... | collective-permute-start | bytes 73736 | tf_op jit(solution)/shard_map/ppermute | solution.py:381
  53.4 0.1 collective-permute-start.18
  53.5 0.1 halve_body.4
  53.6 1.0 %collective-permute-start.15 = (bf16[32,1728]{1,0:T(8,128)(2,1)S(1)}, bf16[32,1728]{1,0:T(8,128)(2,1)S(1)}, u32[]{:S(2)}, u32[]{:S(2)}) collective-permute-start(bf16[32,1728]{1,0:T(8,128)(2,1)S(1)} %get-tuple-element.66), channel_id=1, source_target_pairs={{0,8},{4,12},{8,0},{12,4},{16,24},{20,28},{24,16},{28,20},{1,9},{5... | collective-permute-start | bytes 331784 | tf_op jit(solution)/shard_map/ppermute | solution.py:381
  54.6 2.4 %collective-permute-start.16 = (bf16[32,1728]{1,0:T(8,128)(2,1)S(1)}, bf16[32,1728]{1,0:T(8,128)(2,1)S(1)}, u32[]{:S(2)}, u32[]{:S(2)}) collective-permute-start(bf16[32,1728]{1,0:T(8,128)(2,1)S(1)} %get-tuple-element.67), channel_id=1, source_target_pairs={{0,16},{4,20},{8,24},{12,28},{16,0},{20,4},{24,8},{28,12},{1,17},{... | collective-permute-start | bytes 331784 | tf_op jit(solution)/shard_map/ppermute | solution.py:381
  57.0 1.0 %collective-permute-start.17 = (bf16[32,1728]{1,0:T(8,128)(2,1)S(1)}, bf16[32,1728]{1,0:T(8,128)(2,1)S(1)}, u32[]{:S(2)}, u32[]{:S(2)}) collective-permute-start(bf16[32,1728]{1,0:T(8,128)(2,1)S(1)} %get-tuple-element.68), channel_id=1, source_target_pairs={{0,24},{4,28},{8,16},{12,20},{16,8},{20,12},{24,0},{28,4},{1,25},{... | collective-permute-start | bytes 331784 | tf_op jit(solution)/shard_map/ppermute | solution.py:381
  58.1 5.1 %output_body.1 = (bf16[64,2048]{1,0:T(8,128)(2,1)}, f32[8,128]{1,0:T(8,128)S(1)}) custom-call(s32[24,27]{1,0:T(8,128)S(1)} %get-tuple-element.43.refs_0_, bf16[1728,256]{1,0:T(8,128)(2,1)S(1)} %bitcast.13, bf16[64,2560]{1,0:T(8,128)(2,1)S(1)} %get-tuple-element.56.refs_2_.refs_1_, bf16[64,2560]{1,0:T(8,128)(2,1)S(1)} %collective-permute-done.10.refs_3_.refs_2_, ...), custom_call_target="tpu_custom_call" | custom-call | flops 18119393280 | bytes 16777216 | tf_op jit(solution)/shard_map/output_body/pallas_call | solution.py:49
  63.2 0.5 collective-permute-done.18.refs_1_
  63.7 0.1 halve_body.5
  63.8 0.7 collective-permute-start.22
  64.5 2.2 %collective-permute-start.23 = (bf16[32,1536]{1,0:T(8,128)(2,1)S(1)}, bf16[32,1536]{1,0:T(8,128)(2,1)S(1)}, u32[]{:S(2)}, u32[]{:S(2)}) collective-permute-start(bf16[32,1536]{1,0:T(8,128)(2,1)S(1)} %get-tuple-element.80), channel_id=1, source_target_pairs={{0,16},{4,20},{8,24},{12,28},{16,0},{20,4},{24,8},{28,12},{1,17},{... | collective-permute-start | bytes 294920 | tf_op jit(solution)/shard_map/ppermute | solution.py:381
  66.7 1.5 %collective-permute-start.24 = (bf16[32,1536]{1,0:T(8,128)(2,1)S(1)}, bf16[32,1536]{1,0:T(8,128)(2,1)S(1)}, u32[]{:S(2)}, u32[]{:S(2)}) collective-permute-start(bf16[32,1536]{1,0:T(8,128)(2,1)S(1)} %get-tuple-element.81), channel_id=1, source_target_pairs={{0,24},{4,28},{8,16},{12,20},{16,8},{20,12},{24,0},{28,4},{1,25},{... | collective-permute-start | bytes 294920 | tf_op jit(solution)/shard_map/ppermute | solution.py:381
  68.2 1.5 %collective-permute-start.25 = (bf16[32,192]{1,0:T(8,128)(2,1)S(1)}, bf16[32,192]{1,0:T(8,128)(2,1)S(1)}, u32[]{:S(2)}, u32[]{:S(2)}) collective-permute-start(bf16[32,192]{1,0:T(8,128)(2,1)S(1)} %get-tuple-element.82), channel_id=1, source_target_pairs={{0,4},{4,0},{8,12},{12,8},{16,20},{20,16},{24,28},{28,24},{1,5},{5... | collective-permute-start | bytes 36872 | tf_op jit(solution)/shard_map/ppermute | solution.py:381
  69.8 0.9 %finish_body.2 = f32[27,32,64]{2,1,0:T(8,128)} custom-call(f32[32,1728]{1,0:T(8,128)S(1)} %get-tuple-element.64.refs_6_.refs_0_, bf16[32,1728]{1,0:T(8,128)(2,1)S(1)} %collective-permute-done.15.refs_1_, bf16[32,1728]{1,0:T(8,128)(2,1)S(1)} %collective-permute-done.16.refs_2_, bf16[32,1728]{1,0:T(8,128)(2,1)S(1)} %collective-permute-done.17.refs_3_), custom_call_target="tpu_custom_call" | custom-call | bytes 2097152 | tf_op jit(solution)/shard_map/finish_body/pallas_call | solution.py:49
  70.7 1.3 %collective-permute-done.25.refs_5_ = bf16[32,192]{1,0:T(8,128)(2,1)S(1)} collective-permute-done((bf16[32,192]{1,0:T(8,128)(2,1)S(1)}, bf16[32,192]{1,0:T(8,128)(2,1)S(1)}, u32[]{:S(2)}, u32[]{:S(2)}) %collective-permute-start.25) | collective-permute-done | bytes 12320 | tf_op jit(solution)/shard_map/ppermute | solution.py:381
  72.0 2.0 %collective-permute-done.23.refs_2_ = bf16[32,1536]{1,0:T(8,128)(2,1)S(1)} collective-permute-done((bf16[32,1536]{1,0:T(8,128)(2,1)S(1)}, bf16[32,1536]{1,0:T(8,128)(2,1)S(1)}, u32[]{:S(2)}, u32[]{:S(2)}) %collective-permute-start.23) | collective-permute-done | bytes 98336 | tf_op jit(solution)/shard_map/ppermute | solution.py:381
  74.0 0.9 %finish_body.3 = f32[27,32,64]{2,1,0:T(8,128)} custom-call(f32[32,1536]{1,0:T(8,128)S(1)} %get-tuple-element.78.refs_0_, bf16[32,1536]{1,0:T(8,128)(2,1)S(1)} %collective-permute-done.22.refs_1_, bf16[32,1536]{1,0:T(8,128)(2,1)S(1)} %collective-permute-done.23.refs_2_, bf16[32,1536]{1,0:T(8,128)(2,1)S(1)} %collective-permute-done.24.refs_3_, ...), custom_call_target="tpu_custom_call" | custom-call | bytes 2097152 | tf_op jit(solution)/shard_map/finish_body/pallas_call | solution.py:49
  (27 shorter events, 0.2 us)
Async XLA Ops:
  0.6 9.9 %collective-permute-start.1 = (bf16[64,2048]{1,0:T(8,128)(2,1)}, bf16[64,2048]{1,0:T(8,128)(2,1)S(1)}, u32[]{:S(2)}, u32[]{:S(2)}) collective-permute-start(bf16[64,2048]{1,0:T(8,128)(2,1)} %bitcast.17), channel_id=1, source_target_pairs={{0,2},{1,3},{2,0},{3,1},{4,6},{5,7},{6,4},{7,5},{8,10},{9,11},{10,... | collective-permute-start | bytes 786440 | tf_op jit(solution)/shard_map/ppermute | solution.py:381
  3.6 7.6 %collective-permute-start = (bf16[64,2048]{1,0:T(8,128)(2,1)}, bf16[64,2048]{1,0:T(8,128)(2,1)S(1)}, u32[]{:S(2)}, u32[]{:S(2)}) collective-permute-start(bf16[64,2048]{1,0:T(8,128)(2,1)} %bitcast.18), channel_id=1, source_target_pairs={{0,1},{1,0},{2,3},{3,2},{4,5},{5,4},{6,7},{7,6},{8,9},{9,8},{10,11... | collective-permute-start | bytes 786440 | tf_op jit(solution)/shard_map/ppermute | solution.py:381
  10.6 1.7 %collective-permute-start.2 = (bf16[64,2048]{1,0:T(8,128)(2,1)S(1)}, bf16[64,2048]{1,0:T(8,128)(2,1)S(1)}, u32[]{:S(2)}, u32[]{:S(2)}) collective-permute-start(bf16[64,2048]{1,0:T(8,128)(2,1)S(1)} %pass_body.1.refs_3_), channel_id=1, source_target_pairs={{0,1},{1,0},{2,3},{3,2},{4,5},{5,4},{6,7},{7,6},{8,9},{9,8},{10,11... | collective-permute-start | bytes 786440 | tf_op jit(solution)/shard_map/ppermute | solution.py:381
  11.2 6.6 %collective-permute-start.5 = (bf16[2,64,2560]{2,1,0:T(8,128)(2,1)S(1)}, bf16[2,64,2560]{2,1,0:T(8,128)(2,1)S(1)}, u32[]{:S(2)}, u32[]{:S(2)}) collective-permute-start(bf16[2,64,2560]{2,1,0:T(8,128)(2,1)S(1)} %get-tuple-element.45.refs_1_), channel_id=1, source_target_pairs={{0,1},{1,0},{2,3},{3,2},{4,5},{5,4},{6,7},{7,6},{8,9},{9,8},{10,11... | collective-permute-start | bytes 1966088 | tf_op jit(solution)/shard_map/ppermute | solution.py:381
  12.3 6.9 %copy-start = (bf16[27,64,256]{2,1,0:T(8,128)(2,1)S(1)}, bf16[27,64,256]{2,1,0:T(8,128)(2,1)}, u32[]{:S(2)}) copy-start(bf16[27,64,256]{2,1,0:T(8,128)(2,1)} %param.9) | copy-start | bytes 2654212
  12.6 8.7 %collective-permute-start.4 = (bf16[128,256]{1,0:T(8,128)(2,1)S(1)}, bf16[128,256]{1,0:T(8,128)(2,1)S(1)}, u32[]{:S(2)}, u32[]{:S(2)}) collective-permute-start(bf16[128,256]{1,0:T(8,128)(2,1)S(1)} %get-tuple-element.47), channel_id=1, source_target_pairs={{4,8},{12,16},{20,24},{8,4},{16,12},{24,20},{5,9},{13,17},{21,25},... | collective-permute-start | bytes 196616 | tf_op jit(solution)/shard_map/ppermute | solution.py:386
  13.4 7.9 %collective-permute-start.3 = (bf16[128,256]{1,0:T(8,128)(2,1)S(1)}, bf16[128,256]{1,0:T(8,128)(2,1)S(1)}, u32[]{:S(2)}, u32[]{:S(2)}) collective-permute-start(bf16[128,256]{1,0:T(8,128)(2,1)S(1)} %get-tuple-element.46.refs_2_), channel_id=1, source_target_pairs={{0,4},{4,0},{8,12},{12,8},{16,20},{20,16},{24,28},{28,24},{1,5},{5... | collective-permute-start | bytes 196616 | tf_op jit(solution)/shard_map/ppermute | solution.py:381
  17.9 9.5 %collective-permute-start.7 = (bf16[64,2560]{1,0:T(8,128)(2,1)S(1)}, bf16[64,2560]{1,0:T(8,128)(2,1)S(1)}, u32[]{:S(2)}, u32[]{:S(2)}) collective-permute-start(bf16[64,2560]{1,0:T(8,128)(2,1)S(1)} %get-tuple-element.53), channel_id=1, source_target_pairs={{0,2},{1,3},{2,0},{3,1},{4,6},{5,7},{6,4},{7,5},{8,10},{9,11},{10,... | collective-permute-start | bytes 983048 | tf_op jit(solution)/shard_map/ppermute | solution.py:381
  21.3 1.4 %collective-permute-start.6 = (bf16[128,512]{1,0:T(8,128)(2,1)S(1)}, bf16[128,512]{1,0:T(8,128)(2,1)S(1)}, u32[]{:S(2)}, u32[]{:S(2)}) collective-permute-start(bf16[128,512]{1,0:T(8,128)(2,1)S(1)} %stack_body.1.refs_2_), channel_id=1, source_target_pairs={{0,1},{1,0},{2,3},{3,2},{4,5},{5,4},{6,7},{7,6},{8,9},{9,8},{10,11... | collective-permute-start | bytes 393224 | tf_op jit(solution)/shard_map/ppermute | solution.py:381
  22.7 35.4 %copy-start.1 = (bf16[27,64,256]{2,1,0:T(8,128)(2,1)S(1)}, bf16[27,64,256]{2,1,0:T(8,128)(2,1)}, u32[]{:S(2)}) copy-start(bf16[27,64,256]{2,1,0:T(8,128)(2,1)} %param.10) | copy-start | bytes 2654212
  27.6 6.4 %collective-permute-start.9 = (bf16[2,64,256]{2,1,0:T(8,128)(2,1)S(1)}, bf16[2,64,256]{2,1,0:T(8,128)(2,1)S(1)}, u32[]{:S(2)}, u32[]{:S(2)}) collective-permute-start(bf16[2,64,256]{2,1,0:T(8,128)(2,1)S(1)} %get-tuple-element.55), channel_id=1, source_target_pairs={{4,8},{12,16},{20,24},{8,4},{16,12},{24,20},{5,9},{13,17},{21,25},... | collective-permute-start | bytes 196616 | tf_op jit(solution)/shard_map/ppermute | solution.py:386
  28.5 6.6 %collective-permute-start.8 = (bf16[2,64,256]{2,1,0:T(8,128)(2,1)S(1)}, bf16[2,64,256]{2,1,0:T(8,128)(2,1)S(1)}, u32[]{:S(2)}, u32[]{:S(2)}) collective-permute-start(bf16[2,64,256]{2,1,0:T(8,128)(2,1)S(1)} %get-tuple-element.54.refs_3_), channel_id=1, source_target_pairs={{0,4},{4,0},{8,12},{12,8},{16,20},{20,16},{24,28},{28,24},{1,5},{5... | collective-permute-start | bytes 196616 | tf_op jit(solution)/shard_map/ppermute | solution.py:381
  32.8 11.4 %collective-permute-start.11 = (bf16[64,2048]{1,0:T(8,128)(2,1)S(1)}, bf16[64,2048]{1,0:T(8,128)(2,1)S(1)}, u32[]{:S(2)}, u32[]{:S(2)}) collective-permute-start(bf16[64,2048]{1,0:T(8,128)(2,1)S(1)} %get-tuple-element.52.refs_1_.refs_0_), channel_id=1, source_target_pairs={{0,2},{1,3},{2,0},{3,1},{4,6},{5,7},{6,4},{7,5},{8,10},{9,11},{10,... | collective-permute-start | bytes 786440 | tf_op jit(solution)/shard_map/ppermute | solution.py:381
  35.1 9.1 %collective-permute-start.12 = (bf16[64,512]{1,0:T(8,128)(2,1)S(1)}, bf16[64,512]{1,0:T(8,128)(2,1)S(1)}, u32[]{:S(2)}, u32[]{:S(2)}) collective-permute-start(bf16[64,512]{1,0:T(8,128)(2,1)S(1)} %get-tuple-element.57), channel_id=1, source_target_pairs={{0,2},{1,3},{2,0},{3,1},{4,6},{5,7},{6,4},{7,5},{8,10},{9,11},{10,... | collective-permute-start | bytes 196616 | tf_op jit(solution)/shard_map/ppermute | solution.py:381
  42.1 11.4 %collective-permute-start.14 = (bf16[4,32,1728]{2,1,0:T(8,128)(2,1)S(1)}, bf16[4,32,1728]{2,1,0:T(8,128)(2,1)S(1)}, u32[]{:S(2)}, u32[]{:S(2)}) collective-permute-start(bf16[4,32,1728]{2,1,0:T(8,128)(2,1)S(1)} %get-tuple-element.63), channel_id=1, source_target_pairs={{0,4},{4,0},{8,12},{12,8},{16,20},{20,16},{24,28},{28,24},{1,5},{5... | collective-permute-start | bytes 1327112 | tf_op jit(solution)/shard_map/ppermute | solution.py:381
  44.2 1.6 %collective-permute-start.10 = (bf16[64,2560]{1,0:T(8,128)(2,1)S(1)}, bf16[64,2560]{1,0:T(8,128)(2,1)S(1)}, u32[]{:S(2)}, u32[]{:S(2)}) collective-permute-start(bf16[64,2560]{1,0:T(8,128)(2,1)S(1)} %get-tuple-element.56.refs_2_.refs_1_), channel_id=1, source_target_pairs={{0,1},{1,0},{2,3},{3,2},{4,5},{5,4},{6,7},{7,6},{8,9},{9,8},{10,11... | collective-permute-start | bytes 983048 | tf_op jit(solution)/shard_map/ppermute | solution.py:381
  44.2 2.1 %collective-permute-start.13 = (bf16[64,2560]{1,0:T(8,128)(2,1)S(1)}, bf16[64,2560]{1,0:T(8,128)(2,1)S(1)}, u32[]{:S(2)}, u32[]{:S(2)}) collective-permute-start(bf16[64,2560]{1,0:T(8,128)(2,1)S(1)} %append_body.1.refs_4_.refs_3_), channel_id=1, source_target_pairs={{0,1},{1,0},{2,3},{3,2},{4,5},{5,4},{6,7},{7,6},{8,9},{9,8},{10,11... | collective-permute-start | bytes 983048 | tf_op jit(solution)/shard_map/ppermute | solution.py:381
  48.9 5.6 %collective-permute-start.19 = (bf16[2,32,192]{2,1,0:T(8,128)(2,1)S(1)}, bf16[2,32,192]{2,1,0:T(8,128)(2,1)S(1)}, u32[]{:S(2)}, u32[]{:S(2)}) collective-permute-start(bf16[2,32,192]{2,1,0:T(8,128)(2,1)S(1)} %get-tuple-element.73), channel_id=1, source_target_pairs={{0,8},{4,12},{8,0},{12,4},{16,24},{20,28},{24,16},{28,20},{1,9},{5... | collective-permute-start | bytes 73736 | tf_op jit(solution)/shard_map/ppermute | solution.py:381
  50.6 6.4 %collective-permute-start.20 = (bf16[2,32,192]{2,1,0:T(8,128)(2,1)S(1)}, bf16[2,32,192]{2,1,0:T(8,128)(2,1)S(1)}, u32[]{:S(2)}, u32[]{:S(2)}) collective-permute-start(bf16[2,32,192]{2,1,0:T(8,128)(2,1)S(1)} %get-tuple-element.74), channel_id=1, source_target_pairs={{0,16},{4,20},{8,24},{12,28},{16,0},{20,4},{24,8},{28,12},{1,17},{... | collective-permute-start | bytes 73736 | tf_op jit(solution)/shard_map/ppermute | solution.py:381
  50.6 12.6 %collective-permute-start.21 = (bf16[2,32,192]{2,1,0:T(8,128)(2,1)S(1)}, bf16[2,32,192]{2,1,0:T(8,128)(2,1)S(1)}, u32[]{:S(2)}, u32[]{:S(2)}) collective-permute-start(bf16[2,32,192]{2,1,0:T(8,128)(2,1)S(1)} %get-tuple-element.75), channel_id=1, source_target_pairs={{0,24},{4,28},{8,16},{12,20},{16,8},{20,12},{24,0},{28,4},{1,25},{... | collective-permute-start | bytes 73736 | tf_op jit(solution)/shard_map/ppermute | solution.py:381
  53.4 10.3 %collective-permute-start.18 = (bf16[4,32,1536]{2,1,0:T(8,128)(2,1)S(1)}, bf16[4,32,1536]{2,1,0:T(8,128)(2,1)S(1)}, u32[]{:S(2)}, u32[]{:S(2)}) collective-permute-start(bf16[4,32,1536]{2,1,0:T(8,128)(2,1)S(1)} %get-tuple-element.71), channel_id=1, source_target_pairs={{0,4},{4,0},{8,12},{12,8},{16,20},{20,16},{24,28},{28,24},{1,5},{5... | collective-permute-start | bytes 1179656 | tf_op jit(solution)/shard_map/ppermute | solution.py:381
  53.6 13.2 %collective-permute-start.15 = (bf16[32,1728]{1,0:T(8,128)(2,1)S(1)}, bf16[32,1728]{1,0:T(8,128)(2,1)S(1)}, u32[]{:S(2)}, u32[]{:S(2)}) collective-permute-start(bf16[32,1728]{1,0:T(8,128)(2,1)S(1)} %get-tuple-element.66), channel_id=1, source_target_pairs={{0,8},{4,12},{8,0},{12,4},{16,24},{20,28},{24,16},{28,20},{1,9},{5... | collective-permute-start | bytes 331784 | tf_op jit(solution)/shard_map/ppermute | solution.py:381
  54.6 13.7 %collective-permute-start.16 = (bf16[32,1728]{1,0:T(8,128)(2,1)S(1)}, bf16[32,1728]{1,0:T(8,128)(2,1)S(1)}, u32[]{:S(2)}, u32[]{:S(2)}) collective-permute-start(bf16[32,1728]{1,0:T(8,128)(2,1)S(1)} %get-tuple-element.67), channel_id=1, source_target_pairs={{0,16},{4,20},{8,24},{12,28},{16,0},{20,4},{24,8},{28,12},{1,17},{... | collective-permute-start | bytes 331784 | tf_op jit(solution)/shard_map/ppermute | solution.py:381
  57.0 12.7 %collective-permute-start.17 = (bf16[32,1728]{1,0:T(8,128)(2,1)S(1)}, bf16[32,1728]{1,0:T(8,128)(2,1)S(1)}, u32[]{:S(2)}, u32[]{:S(2)}) collective-permute-start(bf16[32,1728]{1,0:T(8,128)(2,1)S(1)} %get-tuple-element.68), channel_id=1, source_target_pairs={{0,24},{4,28},{8,16},{12,20},{16,8},{20,12},{24,0},{28,4},{1,25},{... | collective-permute-start | bytes 331784 | tf_op jit(solution)/shard_map/ppermute | solution.py:381
  63.8 8.2 %collective-permute-start.22 = (bf16[32,1536]{1,0:T(8,128)(2,1)S(1)}, bf16[32,1536]{1,0:T(8,128)(2,1)S(1)}, u32[]{:S(2)}, u32[]{:S(2)}) collective-permute-start(bf16[32,1536]{1,0:T(8,128)(2,1)S(1)} %get-tuple-element.79), channel_id=1, source_target_pairs={{0,8},{4,12},{8,0},{12,4},{16,24},{20,28},{24,16},{28,20},{1,9},{5... | collective-permute-start | bytes 294920 | tf_op jit(solution)/shard_map/ppermute | solution.py:381
  64.5 9.5 %collective-permute-start.23 = (bf16[32,1536]{1,0:T(8,128)(2,1)S(1)}, bf16[32,1536]{1,0:T(8,128)(2,1)S(1)}, u32[]{:S(2)}, u32[]{:S(2)}) collective-permute-start(bf16[32,1536]{1,0:T(8,128)(2,1)S(1)} %get-tuple-element.80), channel_id=1, source_target_pairs={{0,16},{4,20},{8,24},{12,28},{16,0},{20,4},{24,8},{28,12},{1,17},{... | collective-permute-start | bytes 294920 | tf_op jit(solution)/shard_map/ppermute | solution.py:381
  66.7 7.3 %collective-permute-start.24 = (bf16[32,1536]{1,0:T(8,128)(2,1)S(1)}, bf16[32,1536]{1,0:T(8,128)(2,1)S(1)}, u32[]{:S(2)}, u32[]{:S(2)}) collective-permute-start(bf16[32,1536]{1,0:T(8,128)(2,1)S(1)} %get-tuple-element.81), channel_id=1, source_target_pairs={{0,24},{4,28},{8,16},{12,20},{16,8},{20,12},{24,0},{28,4},{1,25},{... | collective-permute-start | bytes 294920 | tf_op jit(solution)/shard_map/ppermute | solution.py:381
  68.2 3.7 %collective-permute-start.25 = (bf16[32,192]{1,0:T(8,128)(2,1)S(1)}, bf16[32,192]{1,0:T(8,128)(2,1)S(1)}, u32[]{:S(2)}, u32[]{:S(2)}) collective-permute-start(bf16[32,192]{1,0:T(8,128)(2,1)S(1)} %get-tuple-element.82), channel_id=1, source_target_pairs={{0,4},{4,0},{8,12},{12,8},{16,20},{20,16},{24,28},{28,24},{1,5},{5... | collective-permute-start | bytes 36872 | tf_op jit(solution)/shard_map/ppermute | solution.py:381
